TPU v7x, 32 devices: a whole 2x2x4 slice. The times are simulated.
32 devices in a mesh: dp: 8 (over y, x, core), head: 4 (over z).
Axes of the slice: x: 2, y: 2, z: 4, core: 2. Of those that a mesh axis runs over, the one named last changes fastest.
Arguments:
- inputs: bfloat16 [16384, 768], P(('dp', 'head')), may hold values from -6 to 6
- segment_ids: int32 [8, 2048], P('dp'), may hold values from 0 to 47, never falling along the last dimension, each value on 1 to 64 neighbouring positions
- features: bfloat16 [2, 12, 32, 64], P(None, 'head'), may hold values from -4 to 4
- norm_gain: float32 [2, 2, 768], replicated, may hold values from 0.5 to 1.5
- query_key_value: bfloat16 [2, 3, 768, 768], P(None, None, 'dp', 'head'), may hold values from -0.21875 to 0.21875
- output_weight: bfloat16 [2, 768, 768], P(None, 'dp', 'head'), may hold values from -0.875 to 0.875
- up_weight: bfloat16 [2, 3072, 768], P(None, 'dp', 'head'), may hold values from -0.21875 to 0.21875
- down_weight: bfloat16 [2, 3072, 768], P(None, 'dp', 'head'), may hold values from -0.15625 to 0.15625
- cotangent: bfloat16 [16384, 768], P(('dp', 'head')), may hold values from -6 to 6
Outputs:
- outputs: bfloat16 [16384, 768], P(('dp', 'head'))
- input_grad: float32 [16384, 768], P(('dp', 'head'))
- gain_grad: float32 [2, 768], replicated
- middle_gain_grad: float32 [2, 768], replicated
- query_key_value_grad: float32 [2, 3, 768, 768], P(None, None, 'dp', 'head')
- output_weight_grad: float32 [2, 768, 768], P(None, 'dp', 'head')
- up_weight_grad: float32 [2, 3072, 768], P(None, 'dp', 'head')
- down_weight_grad: float32 [2, 3072, 768], P(None, 'dp', 'head')
Inputs may be any that keep to these rules, and one draw needn't show every extreme that they name: `segment_ids`: along each packed sequence the ids never fall; each of 0 to 47 labels one run of 1 to 64 rows, and some run has exactly 64 rows.
All inputs are finite; a program needn't handle non-finite values.
Results may differ from a plain program's by a relative error of at most 0.04.
The roundings to bfloat16 on the way count: a program that leaves them out, or rounds other values in their place, can miss the bound.
Values may be sent and summed in bfloat16 or wider, within the bound.
No kernel may reach another device: no remote copies, remote signals or barrier semaphores. Data moves between devices by JAX's collectives and lax.ppermute only.
A program may use at most 256 MiB of HBM per device.

v0:
```python
import math

import jax
import jax.numpy as jnp
from jax import lax
from jax.sharding import PartitionSpec as P

MOST = 64


EPSILON = 1e-05
FINEST_PRECISION = lax.Precision.HIGHEST


def in_blocks(array, dim, size):
    before, after = (array.shape[:dim], array.shape[dim + 1 :])
    return jnp.moveaxis(array.reshape(*before, size, -1, *after), dim, 0)


def summed_on_arrival(array, axis, dim):
    blocks = in_blocks(array, dim, lax.axis_size(axis))
    arrived = lax.all_to_all(blocks, axis, split_axis=0, concat_axis=0, tiled=True)
    return arrived.astype(jnp.float32).sum(axis=0)


def layer_norm(values, gain_row):
    centred = values - jnp.mean(values, axis=-1, keepdims=True)
    inverse = lax.rsqrt(jnp.mean(centred * centred, axis=-1, keepdims=True) + EPSILON)
    normed = centred * inverse
    return (normed * gain_row, normed, inverse)


def layer_norm_back(grad_out, gain_row, normed, inverse):
    scaled = grad_out * gain_row
    first_mean = jnp.mean(scaled, axis=-1, keepdims=True)
    second_mean = jnp.mean(scaled * normed, axis=-1, keepdims=True)
    return (
        inverse * (scaled - first_mean - normed * second_mean),
        jnp.sum(grad_out * normed, axis=0),
    )


def rotary_tables(segment_ids, head_width):
    seq_count, seq_width = segment_ids.shape
    places = jnp.arange(seq_width, dtype=jnp.int32)
    starts = jnp.concatenate(
        [jnp.ones((seq_count, 1), jnp.bool_), segment_ids[:, 1:] != segment_ids[:, :-1]], axis=1
    )
    first_place = lax.cummax(jnp.where(starts, places[None, :], 0), axis=1)
    position = (places[None, :] - first_place).astype(jnp.float32).reshape(-1)
    halves = head_width // 2
    frequency = jnp.exp(
        jnp.arange(halves, dtype=jnp.float32) * (-2.0 * math.log(10000.0) / head_width)
    )
    angles = position[:, None] * frequency[None, :]
    cosine = jnp.concatenate([jnp.cos(angles), jnp.cos(angles)], axis=1)[:, None, :]
    sine_table = jnp.concatenate([jnp.sin(angles), jnp.sin(angles)], axis=1)[:, None, :]
    return (cosine, sine_table)


def rotate(values, cosine, sine_table):
    halves = values.shape[-1] // 2
    turned = jnp.concatenate([-values[..., halves:], values[..., :halves]], axis=-1)
    return values * cosine + turned * sine_table


def rotate_back(gradient, cosine, sine_table):
    halves = gradient.shape[-1] // 2
    weighted_values = gradient * sine_table
    turned = jnp.concatenate(
        [weighted_values[..., halves:], -weighted_values[..., :halves]], axis=-1
    )
    return gradient * cosine + turned


def feature_map(row_values, random_feature_table):
    score_logits = jnp.einsum(
        "raw,axw->rax",
        row_values,
        random_feature_table.astype(jnp.float32),
        precision=FINEST_PRECISION,
    )
    squares = jnp.sum(row_values * row_values, axis=-1, keepdims=True)
    return jnp.exp(score_logits - 0.5 * squares) / math.sqrt(random_feature_table.shape[1])


def feature_back(grad_phi, phi_full, row_values, random_feature_table):
    weighted_values = grad_phi * phi_full
    along = jnp.einsum(
        "quy,uyi->qui",
        weighted_values,
        random_feature_table.astype(jnp.float32),
        precision=FINEST_PRECISION,
    )
    return along - row_values * jnp.sum(weighted_values, axis=-1, keepdims=True)


def query_back(grad_phi, row_values, random_feature_table, query_scale, cosine, sine_table):
    phi_full = feature_map(row_values, random_feature_table)
    grad_rows = feature_back(grad_phi, phi_full, row_values, random_feature_table)
    return rotate_back(grad_rows * query_scale, cosine, sine_table).astype(jnp.bfloat16)


def gelu_slope(hidden):
    return 0.5 * (1.0 + lax.erf(hidden / math.sqrt(2.0))) + hidden * jnp.exp(
        -0.5 * hidden * hidden
    ) / math.sqrt(2.0 * math.pi)


def to_blocks(source, seq_count, seq_width, block_rows):
    return source.reshape((seq_count * (seq_width // block_rows), block_rows) + source.shape[1:])


def windows(source, seq_count, seq_width, block_rows, fill_value):
    block_count = seq_width // block_rows
    shaped = source.reshape((seq_count, block_count, block_rows) + source.shape[1:])
    edge_fill = jnp.full_like(shaped[:, :1, :MOST], fill_value)
    before_part = jnp.concatenate([edge_fill, shaped[:, :-1, block_rows - MOST :]], axis=1)
    after_part = jnp.concatenate([shaped[:, 1:, :MOST], edge_fill], axis=1)
    joined = jnp.concatenate([before_part, shaped, after_part], axis=2)
    return joined.reshape((seq_count * block_count, block_rows + 2 * MOST) + source.shape[1:])


def fold_windows(window_rows, seq_count, seq_width, block_rows):
    block_count = seq_width // block_rows
    shaped = window_rows.reshape(
        (seq_count, block_count, block_rows + 2 * MOST) + window_rows.shape[2:]
    )
    middle_rows = shaped[:, :, MOST : MOST + block_rows]
    empty_rows = jnp.zeros_like(shaped[:, :1, :MOST])
    into_tail = jnp.concatenate([shaped[:, 1:, :MOST], empty_rows], axis=1)
    split_into_heads = jnp.concatenate([empty_rows, shaped[:, :-1, MOST + block_rows :]], axis=1)
    padding = jnp.zeros_like(shaped[:, :, : block_rows - MOST])
    middle_rows = (
        middle_rows
        + jnp.concatenate([split_into_heads, padding], axis=2)
        + jnp.concatenate([padding, into_tail], axis=2)
    )
    return middle_rows.reshape((seq_count * seq_width,) + window_rows.shape[2:])


def block_forward(pieces):
    phi_query, phi_key, value_rows, query_ids, key_ids = pieces
    same_segment = (query_ids[:, None] == key_ids[None, :]).astype(jnp.float32)
    scores = (
        jnp.einsum("qhm,khm->hqk", phi_query, phi_key, preferred_element_type=jnp.float32)
        * same_segment[None]
    )
    totals = jnp.sum(scores, axis=-1)
    weights = (scores / totals[..., None]).astype(jnp.bfloat16)
    mixed_heads = jnp.einsum(
        "hqk,khd->qhd", weights, value_rows, preferred_element_type=jnp.float32
    )
    return (mixed_heads.astype(jnp.bfloat16), totals)


def block_backward(pieces):
    phi_query, phi_key, value_rows, query_ids, key_ids, grad_mixed, totals = pieces
    same_segment = (query_ids[:, None] == key_ids[None, :]).astype(jnp.float32)
    scores = (
        jnp.einsum("qhm,khm->hqk", phi_query, phi_key, preferred_element_type=jnp.float32)
        * same_segment[None]
    )
    weights = scores / totals[..., None]
    grad_weights = jnp.einsum(
        "qhd,khd->hqk", grad_mixed, value_rows, preferred_element_type=jnp.float32
    )
    grad_values = jnp.einsum(
        "hqk,qhd->khd", weights.astype(jnp.bfloat16), grad_mixed, preferred_element_type=jnp.float32
    )
    inner_sum = jnp.sum(grad_weights * weights, axis=-1, keepdims=True)
    grad_scores = ((grad_weights - inner_sum) / totals[..., None] * same_segment[None]).astype(
        jnp.bfloat16
    )
    grad_query = jnp.einsum(
        "hqk,khm->qhm", grad_scores, phi_key, preferred_element_type=jnp.float32
    )
    grad_key = jnp.einsum(
        "hqk,qhm->khm", grad_scores, phi_query, preferred_element_type=jnp.float32
    )
    return (grad_query, grad_key, grad_values)


def gather_rows(values):
    return lax.all_gather(values, "head", axis=0, tiled=True)


def sum_rows(values):
    return lax.psum_scatter(
        values.astype(jnp.bfloat16), "head", scatter_dimension=0, tiled=True
    ).astype(jnp.float32)


def body(
    inputs,
    segment_ids,
    features,
    norm_gain,
    query_key_value,
    output_weight,
    up_weight,
    down_weight,
    cotangent,
):
    layer_count = norm_gain.shape[0]
    seq_count, seq_width = segment_ids.shape
    group_rows = seq_count * seq_width
    head_width = features.shape[3]
    query_scale = head_width ** (-0.25)
    cosine, sine_table = rotary_tables(segment_ids, head_width)
    contract_last = (((1,), (1,)), ((), ()))
    contract_first = (((0,), (0,)), ((), ()))
    block_rows = min(512, seq_width)
    flat_ids = segment_ids.reshape(-1)
    id_blocks = to_blocks(flat_ids, seq_count, seq_width, block_rows)
    id_windows = windows(flat_ids, seq_count, seq_width, block_rows, -1)
    residual = inputs.astype(jnp.float32)
    stored = []
    for layer_index in range(layer_count):
        gain_pair = norm_gain[layer_index]
        normed_a, hat_a, inverse_a = layer_norm(residual, gain_pair[0])
        qkv_part, out_part = (
            lax.all_gather(query_key_value[layer_index], "dp", axis=1, tiled=True),
            lax.all_gather(output_weight[layer_index], "dp", axis=0, tiled=True),
        )
        attn_input = gather_rows(normed_a.astype(jnp.bfloat16))
        qkv_used, out_used, active_feature_table = (qkv_part, out_part, features[layer_index])
        heads_used = active_feature_table.shape[0]
        projected = jnp.einsum(
            "td,cde->cte", attn_input, qkv_used, preferred_element_type=jnp.float32
        )
        projected = projected.reshape(3, group_rows, heads_used, head_width)
        queries = rotate(projected[0], cosine, sine_table) * query_scale
        keys_turned = rotate(projected[1], cosine, sine_table) * query_scale
        values = projected[2].astype(jnp.bfloat16)
        phi_full_query = feature_map(queries, active_feature_table).astype(jnp.bfloat16)
        phi_full_key = feature_map(keys_turned, active_feature_table).astype(jnp.bfloat16)
        phi_query = to_blocks(phi_full_query, seq_count, seq_width, block_rows)
        phi_key = windows(phi_full_key, seq_count, seq_width, block_rows, 0)
        value_windows = windows(values, seq_count, seq_width, block_rows, 0)
        mixed_heads, totals = lax.map(
            block_forward, (phi_query, phi_key, value_windows, id_blocks, id_windows)
        )
        mixed_heads = mixed_heads.reshape(group_rows, heads_used * head_width)
        partial_out = lax.dot_general(
            mixed_heads, out_used, contract_last, preferred_element_type=jnp.float32
        )
        middle = residual + sum_rows(partial_out)
        normed_c, hat_c, inverse_c = layer_norm(middle, gain_pair[1])
        ffn_rows = normed_c.astype(jnp.bfloat16)
        up_cols, down_cols = (
            lax.all_gather(up_weight[layer_index], "head", axis=1, tiled=True),
            lax.all_gather(down_weight[layer_index], "head", axis=1, tiled=True),
        )
        up_full, down_full = (
            lax.all_gather(up_cols, "dp", axis=0, tiled=True),
            lax.all_gather(down_cols, "dp", axis=0, tiled=True),
        )
        hidden = lax.dot_general(
            ffn_rows, up_full, contract_last, preferred_element_type=jnp.float32
        )
        activated = jax.nn.gelu(hidden, approximate=False).astype(jnp.bfloat16)
        branch = jnp.dot(activated, down_full, preferred_element_type=jnp.float32)
        stored.append(
            (
                hat_a,
                inverse_a,
                attn_input,
                qkv_used,
                out_used,
                active_feature_table,
                queries,
                keys_turned,
                phi_query,
                phi_key,
                value_windows,
                mixed_heads,
                totals,
                hat_c,
                inverse_c,
                ffn_rows,
                up_full,
                down_full,
                hidden,
                activated,
            )
        )
        residual = middle + branch
    gradient = cotangent.astype(jnp.float32)
    gain_parts = []
    qkv_parts = []
    out_parts = []
    up_parts = []
    down_parts = []
    for layer_index in reversed(range(layer_count)):
        (
            hat_a,
            inverse_a,
            attn_input,
            qkv_used,
            out_used,
            active_feature_table,
            queries,
            keys_turned,
            phi_query,
            phi_key,
            value_windows,
            mixed_heads,
            totals,
            hat_c,
            inverse_c,
            ffn_rows,
            up_full,
            down_full,
            hidden,
            activated,
        ) = stored[layer_index]
        gain_pair = norm_gain[layer_index]
        heads_used = active_feature_table.shape[0]
        branch_rows = gradient.astype(jnp.bfloat16)
        grad_act = lax.dot_general(
            branch_rows, down_full, contract_last, preferred_element_type=jnp.float32
        )
        grad_hidden = (grad_act * gelu_slope(hidden)).astype(jnp.bfloat16)
        grad_down = lax.dot_general(
            activated, branch_rows, contract_first, preferred_element_type=jnp.float32
        )
        grad_up = lax.dot_general(
            grad_hidden, ffn_rows, contract_first, preferred_element_type=jnp.float32
        )
        grad_normed_c = jnp.dot(grad_hidden, up_full, preferred_element_type=jnp.float32)
        up_rows_sum, down_rows_sum = (
            lax.psum_scatter(grad_up, "dp", scatter_dimension=0, tiled=True),
            lax.psum_scatter(grad_down, "dp", scatter_dimension=0, tiled=True),
        )
        up_share, down_share = (
            lax.psum_scatter(
                up_rows_sum.astype(jnp.bfloat16), "head", scatter_dimension=1, tiled=True
            ).astype(jnp.float32),
            lax.psum_scatter(
                down_rows_sum.astype(jnp.bfloat16), "head", scatter_dimension=1, tiled=True
            ).astype(jnp.float32),
        )
        back_c, gain_c = layer_norm_back(grad_normed_c, gain_pair[1], hat_c, inverse_c)
        grad_middle = gradient + back_c
        attn_rows = gather_rows(grad_middle.astype(jnp.bfloat16))
        grad_mixed = jnp.dot(attn_rows, out_used, preferred_element_type=jnp.float32).astype(
            jnp.bfloat16
        )
        grad_out = lax.dot_general(
            attn_rows, mixed_heads, contract_first, preferred_element_type=jnp.float32
        )
        grad_blocks = grad_mixed.reshape(phi_query.shape[:3] + (head_width,))
        grad_phi_query, key_window_gradient, grad_value_windows = lax.map(
            block_backward,
            (phi_query, phi_key, value_windows, id_blocks, id_windows, grad_blocks, totals),
        )
        grad_phi_query = grad_phi_query.reshape(group_rows, heads_used, -1)
        grad_phi_key = fold_windows(key_window_gradient, seq_count, seq_width, block_rows)
        grad_values = fold_windows(grad_value_windows, seq_count, seq_width, block_rows).astype(
            jnp.bfloat16
        )
        grad_queries = query_back(
            grad_phi_query, queries, active_feature_table, query_scale, cosine, sine_table
        )
        grad_keys = query_back(
            grad_phi_key, keys_turned, active_feature_table, query_scale, cosine, sine_table
        )
        grad_projected = jnp.stack([grad_queries, grad_keys, grad_values]).reshape(
            3, group_rows, heads_used * head_width
        )
        grad_qkv = jnp.einsum(
            "td,cte->cde", attn_input, grad_projected, preferred_element_type=jnp.float32
        )
        grad_normed_a = jnp.einsum(
            "cte,cde->td", grad_projected, qkv_used, preferred_element_type=jnp.float32
        )
        summed_a = sum_rows(grad_normed_a)
        qkv_share, out_share = (
            summed_on_arrival(grad_qkv.astype(jnp.bfloat16), "dp", 1),
            summed_on_arrival(grad_out.astype(jnp.bfloat16), "dp", 0),
        )
        back_a, gain_a = layer_norm_back(summed_a, gain_pair[0], hat_a, inverse_a)
        gradient = grad_middle + back_a
        gain_parts.append(jnp.stack([gain_a, gain_c]))
        qkv_parts.append(qkv_share)
        out_parts.append(out_share)
        up_parts.append(up_share)
        down_parts.append(down_share)
    gain_total = lax.psum(jnp.stack(gain_parts[::-1]), ("dp", "head"))
    return (
        residual.astype(jnp.bfloat16),
        gradient,
        gain_total[:, 0],
        gain_total[:, 1],
        jnp.stack(qkv_parts[::-1]),
        jnp.stack(out_parts[::-1]),
        jnp.stack(up_parts[::-1]),
        jnp.stack(down_parts[::-1]),
    )


def solution(mesh):
    in_specs = (
        P(("dp", "head"), None),
        P("dp", None),
        P(None, "head", None, None),
        P(),
        P(None, None, "dp", "head"),
        P(None, "dp", "head"),
        P(None, "dp", "head"),
        P(None, "dp", "head"),
        P(("dp", "head"), None),
    )
    out_specs = (
        P(("dp", "head"), None),
        P(("dp", "head"), None),
        P(),
        P(),
        P(None, None, "dp", "head"),
        P(None, "dp", "head"),
        P(None, "dp", "head"),
        P(None, "dp", "head"),
    )
    return jax.shard_map(body, mesh=mesh, in_specs=in_specs, out_specs=out_specs, check_vma=False)
```

profile of v0, /device:TPU:0, one launch (start us, length us, event | category | flops | bytes accessed | tf_op | source)
XLA Modules:
  0.0 1323.9 jit_solution(876881945593562120)
XLA Ops:
  14.5 14.8 %all-gather = bf16[1,3,768,192]{3,1,0,2:T(4,128)(2,1)S(1)} all-gather(bf16[1,3,96,192]{3,1,0,2:T(4,128)(2,1)S(1)} %copy.133), channel_id=2, replica_groups=mesh['dp'=8,'head'=4] {'dp'}, dimensions={2}, use_global_device_ids=true | all-gather | bytes 995328 | tf_op jit(solution)/shard_map/all_gather | solution.py:223
  34.1 9.6 all-gather.1
  46.2 33.8 %all-gather.21.cloned.1.call-done = bf16[2048,768]{1,0:T(8,128)(2,1)} async-done(((bf16[512,768]{1,0:T(8,128)(2,1)}), bf16[2048,768]{1,0:T(8,128)(2,1)}) %all-gather.21.cloned.1.call-update) | async-done | bytes 3145744 | tf_op jit(solution)/shard_map/all_gather | solution.py:185
  99.8 8.0 while.52
  113.9 22.1 %all-gather.2 = bf16[1,384,768]{1,2,0:T(8,128)(2,1)} all-gather(bf16[1,384,192]{1,2,0:T(8,128)(2,1)S(1)} %get-tuple-element.521), channel_id=4, replica_groups=mesh['dp'=8,'head'=4] {'head'}, dimensions={2}, use_global_device_ids=true | all-gather | bytes 737280 | tf_op jit(solution)/shard_map/all_gather | solution.py:252
  136.8 24.5 %all-gather.4 = bf16[1,384,768]{1,2,0:T(8,128)(2,1)} all-gather(bf16[1,384,192]{1,2,0:T(8,128)(2,1)S(1)} %get-tuple-element.519), channel_id=6, replica_groups=mesh['dp'=8,'head'=4] {'head'}, dimensions={2}, use_global_device_ids=true | all-gather | bytes 737280 | tf_op jit(solution)/shard_map/all_gather | solution.py:253
  161.4 26.7 %reduce-scatter.21.cloned.1.call-done = bf16[512,768]{1,0:T(8,128)(2,1)} async-done(((bf16[2048,768]{1,0:T(8,128)(2,1)}), bf16[512,768]{1,0:T(8,128)(2,1)}) %reduce-scatter.21.cloned.1.call-update) | async-done | bytes 786448 | tf_op jit(solution)/shard_map/reduce_scatter | solution.py:189
  190.1 19.4 %fusion.106 = (bf16[512,3072]{1,0:T(8,128)(2,1)}, f32[512,3072]{1,0:T(8,128)}) fusion(bf16[1,3072,768]{1,2,0:T(8,128)(2,1)} %all-gather.29.cloned.1.call-done, f32[768]{0:T(1024)S(1)} %get-tuple-element.373, f32[512]{0:T(512)S(1)} %add_rsqrt_fusion.2, f32[512]{0:T(512)S(1)} %broadcast_multiply_fusion.24, bf16[512,768]{1,0:T(8,128)(2,1)S(1)} %copy-done.35, ...), kind=kOutput, calls=%fused_computation.120 | convolution fusion | flops 2520907776 | bytes 15735808 | tf_op jit(solution)/shard_map/dot_general | solution.py:259
  209.5 7.6 all-gather.31.cloned.1.call-done
  217.1 6.0 fusion.318
  224.9 14.2 %all-gather.6 = bf16[1,3,768,192]{3,1,0,2:T(4,128)(2,1)} all-gather(bf16[1,3,96,192]{3,1,0,2:T(4,128)(2,1)S(1)} %copy.134), channel_id=8, replica_groups=mesh['dp'=8,'head'=4] {'dp'}, dimensions={2}, use_global_device_ids=true | all-gather | bytes 995328 | tf_op jit(solution)/shard_map/all_gather | solution.py:223
  241.7 10.7 all-gather.7
  252.4 35.9 %all-gather.23.cloned.1.call-done = bf16[2048,768]{1,0:T(8,128)(2,1)} async-done(((bf16[512,768]{1,0:T(8,128)(2,1)}), bf16[2048,768]{1,0:T(8,128)(2,1)}) %all-gather.23.cloned.1.call-update) | async-done | bytes 3145744 | tf_op jit(solution)/shard_map/all_gather | solution.py:185
  307.9 14.4 %while.53 = (s32[]{:T(128)}, bf16[4,512,3,64]{1,3,2,0:T(8,128)(2,1)}, f32[4,3,512]{2,1,0:T(4,128)S(1)}, bf16[4,640,3,64]{1,3,2,0:T(8,128)(2,1)S(1)}, bf16[4,512,...) while((s32[]{:T(128)}, ...), condition=%wide.region_18.19_spmd, body=%wide.region_16.18_spmd.sunk | while | flops 194411008 | bytes 12506737 | solution.py:241
  329.2 21.0 %all-gather.8 = bf16[1,384,768]{1,2,0:T(8,128)(2,1)} all-gather(bf16[1,384,192]{1,2,0:T(8,128)(2,1)S(1)} %copy-done.86), channel_id=10, replica_groups=mesh['dp'=8,'head'=4] {'head'}, dimensions={2}, use_global_device_ids=true | all-gather | bytes 737280 | tf_op jit(solution)/shard_map/all_gather | solution.py:252
  350.3 24.6 %all-gather.10 = bf16[1,384,768]{1,2,0:T(8,128)(2,1)} all-gather(bf16[1,384,192]{1,2,0:T(8,128)(2,1)S(1)} %copy-done.87), channel_id=12, replica_groups=mesh['dp'=8,'head'=4] {'head'}, dimensions={2}, use_global_device_ids=true | all-gather | bytes 737280 | tf_op jit(solution)/shard_map/all_gather | solution.py:253
  375.2 28.3 %reduce-scatter.23.cloned.1.call-done = bf16[512,768]{1,0:T(8,128)(2,1)} async-done(((bf16[2048,768]{1,0:T(8,128)(2,1)}), bf16[512,768]{1,0:T(8,128)(2,1)}) %reduce-scatter.23.cloned.1.call-update) | async-done | bytes 786448 | tf_op jit(solution)/shard_map/reduce_scatter | solution.py:189
  406.3 19.9 %fusion.109 = (bf16[512,3072]{1,0:T(8,128)(2,1)}, f32[512,3072]{1,0:T(8,128)}) fusion(bf16[1,3072,768]{1,2,0:T(8,128)(2,1)} %all-gather.33.cloned.1.call-done, f32[512,768]{1,0:T(8,128)} %copy-done.6, f32[768]{0:T(1024)S(1)} %copy-done.113, f32[512]{0:T(512)S(1)} %add_rsqrt_fusion, f32[512]{0:T(512)S(1)} %broadcast_multiply_fusion.22), kind=kOutput, calls=%fused_computation.123 | convolution fusion | flops 2519728128 | bytes 15735808 | tf_op jit(solution)/shard_map/dot_general | solution.py:259
  426.2 5.9 all-gather.35.cloned.1.call-done
  432.2 6.9 fusion.115
  444.7 63.6 %all-gather.25.cloned.1.call-done = bf16[2048,768]{1,0:T(8,128)(2,1)} async-done(((bf16[512,768]{1,0:T(8,128)(2,1)}), bf16[2048,768]{1,0:T(8,128)(2,1)}) %all-gather.25.cloned.1.call-update) | async-done | bytes 3145744 | tf_op jit(solution)/shard_map/all_gather | solution.py:185
  517.6 122.2 %while.54 = (s32[]{:T(128)}, f32[4,512,3,32]{1,0,3,2:T(4,128)}, f32[4,640,3,32]{1,3,2,0:T(8,128)}, f32[4,640,3,64]{1,3,2,0:T(8,128)}, bf16[4,640,3,32]{1,3,2,0:T...) while((s32[]{:T(128)}, f32[4,512,3,32]{1,0,3,2:T(4,128)}, ...), condition=%wide.region_26.27_spmd, body=%wide.region_24.26_spmd.sunk | while | flops 453841152 | bytes 49774288 | solution.py:354
  536.5 8.1 fusion.391
  556.0 5.9 convolution_bitcast_fusion.14
  567.1 8.1 fusion.391
  597.6 8.1 fusion.391
  628.1 8.1 fusion.391
  671.5 8.3 fusion.289
  680.9 8.2 fusion.323
  689.2 41.3 %reduce-scatter.25.cloned.1.call-done = bf16[512,768]{1,0:T(8,128)(2,1)} async-done(((bf16[2048,768]{1,0:T(8,128)(2,1)}), bf16[512,768]{1,0:T(8,128)(2,1)}) %reduce-scatter.25.cloned.1.call-update) | async-done | bytes 786448 | tf_op jit(solution)/shard_map/reduce_scatter | solution.py:189
  733.7 7.4 fusion.121
  746.5 9.0 fusion.261
  756.0 54.5 %reduce-scatter.31.cloned.1.call-done = f32[384,768]{1,0:T(8,128)} async-done(((f32[3072,768]{1,0:T(8,128)}), f32[384,768]{1,0:T(8,128)}) %reduce-scatter.31.cloned.1.call-update) | async-done | bytes 1179664 | tf_op jit(solution)/shard_map/reduce_scatter | solution.py:333
  813.0 77.5 %reduce-scatter.35.cloned.1.call-done = f32[384,768]{1,0:T(8,128)} async-done(((f32[3072,768]{1,0:T(8,128)}), f32[384,768]{1,0:T(8,128)}) %reduce-scatter.35.cloned.1.call-update) | async-done | bytes 1179664 | tf_op jit(solution)/shard_map/reduce_scatter | solution.py:334
  893.0 63.2 %all-gather.27.cloned.1.call-done = bf16[2048,768]{1,0:T(8,128)(2,1)} async-done(((bf16[512,768]{1,0:T(8,128)(2,1)}), bf16[2048,768]{1,0:T(8,128)(2,1)}) %all-gather.27.cloned.1.call-update) | async-done | bytes 3145744 | tf_op jit(solution)/shard_map/all_gather | solution.py:185
  963.5 125.8 %while.55 = (s32[]{:T(128)}, f32[4,512,3,32]{1,0,3,2:T(4,128)}, f32[4,640,3,32]{1,3,2,0:T(8,128)}, f32[4,640,3,64]{1,3,2,0:T(8,128)}, bf16[4,640,3,32]{1,3,2,0:T...) while((s32[]{:T(128)}, f32[4,512,3,32]{1,0,3,2:T(4,128)}, ...), condition=%wide.region_36.37_spmd, body=%wide.region_34.36_spmd.sunk | while | flops 453841152 | bytes 43482776 | solution.py:354
  972.5 6.8 convolution_bitcast_fusion.15
  984.5 8.1 fusion.404
  1004.3 6.0 convolution_bitcast_fusion.15
  1015.5 8.8 fusion.404
  1047.1 8.1 fusion.404
  1066.7 5.9 convolution_bitcast_fusion.15
  1077.8 8.1 fusion.404
  1126.5 8.2 fusion.254
  1160.7 12.8 all-to-all-done.1
  1193.6 7.7 add_convert_fusion
  1217.1 48.1 %reduce-scatter.33.cloned.1.call-done = f32[384,768]{1,0:T(8,128)} async-done(((f32[3072,768]{1,0:T(8,128)}), f32[384,768]{1,0:T(8,128)}) %reduce-scatter.33.cloned.1.call-update) | async-done | bytes 1179664 | tf_op jit(solution)/shard_map/reduce_scatter | solution.py:334
  1269.6 39.9 %psum.7 = f32[2,2,768]{2,0,1:T(2,128)S(1)} all-reduce(f32[2,2,768]{2,0,1:T(2,128)S(1)} %pad_maximum_fusion.10), channel_id=1, replica_groups=mesh['dp'=8,'head'=4] {'dp','head'}, use_global_device_ids=true, to_apply=%region_46.47 | all-reduce | flops 3072 | bytes 24576 | tf_op jit(solution)/shard_map/psum | solution.py:390
  (639 shorter events, 433.7 us)
Async XLA Ops:
  8.0 71.9 %all-gather.21.cloned.1.call-start = ((), (), s32[]{:S(2)}) async-start(), calls=%async_computation.16 | async-start | bytes 3932160 | tf_op jit(solution)/shard_map/all_gather | solution.py:185
  9.5 180.6 %copy-start.110 = (f32[768]{0:T(1024)}, f32[768]{0:T(1024)S(1)}, u32[]{:S(2)}) copy-start(f32[768]{0:T(1024)S(1)} %get-tuple-element.373) | copy-start | bytes 9220
  9.5 214.0 %copy-start.95 = (f32[768]{0:T(1024)}, f32[768]{0:T(1024)S(1)}, u32[]{:S(2)}) copy-start(f32[768]{0:T(1024)S(1)} %get-tuple-element.375) | copy-start | bytes 9220
  13.6 174.5 %reduce-scatter.21.cloned.1.call-start = ((), (), s32[]{:S(2)}) async-start(), calls=%async_computation.17 | async-start | bytes 3932160 | tf_op jit(solution)/shard_map/reduce_scatter | solution.py:189
  14.5 16.9 %copy-start.93 = (s32[1,2048]{1,0:T(1,128)S(1)}, s32[1,2048]{1,0:T(1,128)}, u32[]{:S(2)}) copy-start(s32[1,2048]{1,0:T(1,128)} %param.18) | copy-start | bytes 24580
  14.5 18.9 %copy-start.94 = (bf16[2,96,192]{2,1,0:T(8,128)(2,1)S(1)}, bf16[2,96,192]{2,1,0:T(8,128)(2,1)}, u32[]{:S(2)}) copy-start(bf16[2,96,192]{2,1,0:T(8,128)(2,1)} %param.22) | copy-start | bytes 221188
  32.0 47.9 %copy-start.67 = (bf16[1,3,768,192]{2,3,1,0:T(8,128)(2,1)S(1)}, bf16[1,3,768,192]{2,3,1,0:T(8,128)(2,1)}, u32[]{:S(2)}) copy-start(bf16[1,3,768,192]{2,3,1,0:T(8,128)(2,1)} %copy.76) | copy-start | bytes 2654212
  46.1 46.6 %copy-start.44 = (f32[2048,64]{0,1:T(8,128)}, f32[2048,64]{0,1:T(8,128)S(1)}, u32[]{:S(2)}) copy-start(f32[2048,64]{0,1:T(8,128)S(1)} %get-tuple-element.527) | copy-start | bytes 1572868
  46.1 46.6 %copy-start.46 = (f32[2048,64]{0,1:T(8,128)}, f32[2048,64]{0,1:T(8,128)S(1)}, u32[]{:S(2)}) copy-start(f32[2048,64]{0,1:T(8,128)S(1)} %get-tuple-element.554) | copy-start | bytes 1572868
  112.3 23.8 %copy-start.90 = (bf16[2,384,192]{1,2,0:T(8,128)(2,1)S(1)}, bf16[2,384,192]{1,2,0:T(8,128)(2,1)}, u32[]{:S(2)}) copy-start(bf16[2,384,192]{1,2,0:T(8,128)(2,1)} %param.24) | copy-start | bytes 884740
  112.3 77.7 %all-gather.29.cloned.1.call-start = ((), (), s32[]{:S(2)}) async-start(), calls=%async_computation.28 | async-start | bytes 5308416 | tf_op jit(solution)/shard_map/all_gather | solution.py:256
  136.0 81.1 %all-gather.31.cloned.1.call-start = ((), (), s32[]{:S(2)}) async-start(), calls=%async_computation.29 | async-start | bytes 5308416 | tf_op jit(solution)/shard_map/all_gather | solution.py:257
  161.3 127.0 %all-gather.23.cloned.1.call-start = ((), (), s32[]{:S(2)}) async-start(), calls=%async_computation.18 | async-start | bytes 3932160 | tf_op jit(solution)/shard_map/all_gather | solution.py:185
  189.6 19.9 %copy-start.108 = (f32[512]{0:T(512)}, f32[512]{0:T(512)S(1)}, u32[]{:S(2)}) copy-start(f32[512]{0:T(512)S(1)} %broadcast_multiply_fusion.24) | copy-start | bytes 6148
  190.0 19.5 %copy-start.114 = (f32[512]{0:T(512)}, f32[512]{0:T(512)S(1)}, u32[]{:S(2)}) copy-start(f32[512]{0:T(512)S(1)} %add_rsqrt_fusion.2) | copy-start | bytes 6148
  223.2 180.3 %copy-start.2 = (f32[512,768]{1,0:T(8,128)}, f32[512,768]{1,0:T(8,128)S(1)}, u32[]{:S(2)}) copy-start(f32[512,768]{1,0:T(8,128)S(1)} %get-tuple-element.543) | copy-start | bytes 4718596
  224.7 178.7 %reduce-scatter.23.cloned.1.call-start = ((), (), s32[]{:S(2)}) async-start(), calls=%async_computation.19 | async-start | bytes 3932160 | tf_op jit(solution)/shard_map/reduce_scatter | solution.py:189
  241.7 50.6 %copy-start.69 = (bf16[1,3,768,192]{2,3,1,0:T(8,128)(2,1)}, bf16[1,3,768,192]{2,3,1,0:T(8,128)(2,1)S(1)}, u32[]{:S(2)}) copy-start(bf16[1,3,768,192]{2,3,1,0:T(8,128)(2,1)S(1)} %copy.86) | copy-start | bytes 2654212
  328.3 22.0 %copy-start.87 = (bf16[1,384,192]{1,2,0:T(8,128)(2,1)S(1)}, bf16[1,384,192]{1,2,0:T(8,128)(2,1)}, u32[]{:S(2)}) copy-start(bf16[1,384,192]{1,2,0:T(8,128)(2,1)} %get-tuple-element.518) | copy-start | bytes 442372
  328.3 78.0 %all-gather.33.cloned.1.call-start = ((), (), s32[]{:S(2)}) async-start(), calls=%async_computation.30 | async-start | bytes 5308416 | tf_op jit(solution)/shard_map/all_gather | solution.py:256
  350.2 81.9 %all-gather.35.cloned.1.call-start = ((), (), s32[]{:S(2)}) async-start(), calls=%async_computation.31 | async-start | bytes 5308416 | tf_op jit(solution)/shard_map/all_gather | solution.py:257
  374.9 31.3 %copy-start.113 = (f32[768]{0:T(1024)S(1)}, f32[768]{0:T(1024)}, u32[]{:S(2)}) copy-start(f32[768]{0:T(1024)} %get-tuple-element.372) | copy-start | bytes 9220
  374.9 133.3 %all-gather.25.cloned.1.call-start = ((), (), s32[]{:S(2)}) async-start(), calls=%async_computation.20 | async-start | bytes 3932160 | tf_op jit(solution)/shard_map/all_gather | solution.py:185
  406.3 25.9 %copy-start.80 = (bf16[512,768]{1,0:T(8,128)(2,1)S(1)}, bf16[512,768]{1,0:T(8,128)(2,1)}, u32[]{:S(2)}) copy-start(bf16[512,768]{1,0:T(8,128)(2,1)} %param.25) | copy-start | bytes 2359300
  444.6 285.8 %reduce-scatter.25.cloned.1.call-start = ((), (), s32[]{:S(2)}) async-start(), calls=%async_computation.21 | async-start | bytes 3932160 | tf_op jit(solution)/shard_map/reduce_scatter | solution.py:189
  671.4 139.1 %reduce-scatter.31.cloned.1.call-start = ((), (), s32[]{:S(2)}) async-start(), calls=%async_computation.25 | async-start | bytes 10616832 | tf_op jit(solution)/shard_map/reduce_scatter | solution.py:333
  679.8 210.7 %reduce-scatter.35.cloned.1.call-start = ((), (), s32[]{:S(2)}) async-start(), calls=%async_computation.27 | async-start | bytes 10616832 | tf_op jit(solution)/shard_map/reduce_scatter | solution.py:334
  689.1 41.4 %copy-start.3 = (f32[512,768]{1,0:T(8,128)S(1)}, f32[512,768]{1,0:T(8,128)}, u32[]{:S(2)}) copy-start(f32[512,768]{1,0:T(8,128)} %copy-done.2) | copy-start | bytes 4718596
  689.1 41.4 %copy-start.96 = (f32[768]{0:T(1024)S(1)}, f32[768]{0:T(1024)}, u32[]{:S(2)}) copy-start(f32[768]{0:T(1024)} %copy-done.95) | copy-start | bytes 9220
  689.1 41.4 %copy-start.102 = (f32[512]{0:T(512)S(1)}, f32[512]{0:T(512)}, u32[]{:S(2)}) copy-start(f32[512]{0:T(512)} %copy-done.101) | copy-start | bytes 6148
  689.1 41.4 %copy-start.106 = (f32[512]{0:T(512)S(1)}, f32[512]{0:T(512)}, u32[]{:S(2)}) copy-start(f32[512]{0:T(512)} %copy-done.105) | copy-start | bytes 6148
  689.1 44.0 %copy-start.37 = (f32[512,768]{1,0:T(8,128)S(1)}, f32[512,768]{1,0:T(8,128)}, u32[]{:S(2)}) copy-start(f32[512,768]{1,0:T(8,128)} %get-tuple-element.455) | copy-start | bytes 4718596
  689.1 267.1 %all-gather.27.cloned.1.call-start = ((), (), s32[]{:S(2)}) async-start(), calls=%async_computation.22 | async-start | bytes 3932160 | tf_op jit(solution)/shard_map/all_gather | solution.py:185
  746.5 455.6 %reduce-scatter.29.cloned.1.call-start = ((), (), s32[]{:S(2)}) async-start(), calls=%async_computation.24 | async-start | bytes 10616832 | tf_op jit(solution)/shard_map/reduce_scatter | solution.py:333
  755.5 452.8 %reduce-scatter.39.cloned.1.call-start = ((), (), s32[]{:S(2)}) async-start(), calls=%async_computation.33 | async-start | bytes 737280
  812.9 143.3 %copy-start.55 = (bf16[1,768,192]{2,1,0:T(8,128)(2,1)S(1)}, bf16[1,768,192]{2,1,0:T(8,128)(2,1)}, u32[]{:S(2)}) copy-start(bf16[1,768,192]{2,1,0:T(8,128)(2,1)} %all-gather.1) | copy-start | bytes 884740
  812.9 397.1 %reduce-scatter.43.cloned.1.call-start = ((), (), s32[]{:S(2)}) async-start(), calls=%async_computation.35 | async-start | bytes 737280
  892.9 322.1 %reduce-scatter.27.cloned.1.call-start = ((), (), s32[]{:S(2)}) async-start(), calls=%async_computation.23 | async-start | bytes 3932160 | tf_op jit(solution)/shard_map/reduce_scatter | solution.py:189
  1125.2 140.0 %reduce-scatter.33.cloned.1.call-start = ((), (), s32[]{:S(2)}) async-start(), calls=%async_computation.26 | async-start | bytes 10616832 | tf_op jit(solution)/shard_map/reduce_scatter | solution.py:334
  1139.8 12.7 all-to-all-start.3
  1152.5 21.0 %all-to-all-start.1 = ((bf16[8,3,96,192]{2,3,1,0:T(8,128)(2,1)}), bf16[8,3,96,192]{2,3,1,0:T(8,128)(2,1)S(1)}, u32[]{:S(2)}, u32[]{:S(2)}) async-start(bf16[8,3,96,192]{2,3,1,0:T(8,128)(2,1)} %bitcast.503), calls=%async_computation.5 | async-start | bytes 2359296 | tf_op jit(solution)/shard_map/all_to_all | solution.py:22
  1173.5 15.1 %all-to-all-start.2 = ((bf16[8,96,192]{1,2,0:T(8,128)(2,1)}), bf16[8,96,192]{1,2,0:T(8,128)(2,1)S(1)}, u32[]{:S(2)}, u32[]{:S(2)}) async-start(bf16[8,96,192]{1,2,0:T(8,128)(2,1)} %copy.109), calls=%async_computation.6 | async-start | bytes 786432 | tf_op jit(solution)/shard_map/all_to_all | solution.py:22
  1189.3 24.2 %all-to-all-start = ((bf16[8,3,96,192]{2,3,1,0:T(8,128)(2,1)}), bf16[8,3,96,192]{2,3,1,0:T(8,128)(2,1)S(1)}, u32[]{:S(2)}, u32[]{:S(2)}) async-start(bf16[8,3,96,192]{2,3,1,0:T(8,128)(2,1)} %bitcast.412), calls=%async_computation.4 | async-start | bytes 2359296 | tf_op jit(solution)/shard_map/all_to_all | solution.py:22
  1193.5 118.3 %reduce-scatter.37.cloned.1.call-start = ((), (), s32[]{:S(2)}) async-start(), calls=%async_computation.32 | async-start | bytes 737280
  1206.7 107.4 %reduce-scatter.41.cloned.1.call-start = ((), (), s32[]{:S(2)}) async-start(), calls=%async_computation.34 | async-start | bytes 737280
  1217.0 52.6 %copy-start.107 = (f32[1,2,768]{2,0,1:T(1,128)S(1)}, f32[1,2,768]{2,0,1:T(1,128)}, u32[]{:S(2)}) copy-start(f32[1,2,768]{2,0,1:T(1,128)} %stack.106) | copy-start | bytes 18436
  1217.0 93.1 %copy-start.38 = (f32[512,768]{1,0:T(8,128)S(1)}, f32[512,768]{1,0:T(8,128)}, u32[]{:S(2)}) copy-start(f32[512,768]{1,0:T(8,128)} %get-tuple-element.453) | copy-start | bytes 4718596
  1217.0 93.1 %copy-start.58 = (bf16[512,768]{1,0:T(8,128)(2,1)S(1)}, bf16[512,768]{1,0:T(8,128)(2,1)}, u32[]{:S(2)}) copy-start(bf16[512,768]{1,0:T(8,128)(2,1)} %reduce-scatter.27.cloned.1.call-done) | copy-start | bytes 2359300
  (104 other events, 400.3 us)
Sparse Core Ops, SparseCore 0:
  13.7 66.1 all-gather.20
  112.5 75.5 reduce-scatter.20
  224.8 63.4 all-gather.22
  328.4 74.9 reduce-scatter.22
  444.8 63.4 all-gather.24
  671.5 58.8 reduce-scatter.24
  734.0 76.4 reduce-scatter.30
  814.0 76.4 reduce-scatter.34
  892.7 63.4 all-gather.26
  959.5 75.1 reduce-scatter.28
  1037.6 21.8 reduce-scatter.38
  1062.2 20.3 reduce-scatter.42
  1125.3 59.9 reduce-scatter.26
  1188.7 76.4 reduce-scatter.32
  1267.3 22.0 reduce-scatter.36
  1291.6 20.3 reduce-scatter.40
Sparse Core Ops, SparseCore 1:
  136.1 39.6 all-gather.28
  177.5 39.5 all-gather.30
  350.3 40.3 all-gather.32
  392.6 39.6 all-gather.34
where the time goes:
time: 1330 us; the launch traced here: 1320 us
  waiting for transfers between devices  500 us (38%)
  matrix products  393 us (30%)
  blocking collectives  181 us (14%)
  local copies, waits for them, and re-layouts  155 us (12%)
  other arithmetic  59.2 us (4%)
  between operations  17.6 us (1%)
  starting transfers between devices  17.3 us (1%)
    all_gather x4, waiting for transfers between devices, gather_rows(): return lax.all_gather(values, 'head', axis=0, tiled=True)  197 us
    reduce_scatter x2, waiting for transfers between devices, body(): lax.psum_scatter(grad_down, 'dp', scatter_dimension=0, tiled=True)  126 us
    reduce_scatter x4, waiting for transfers between devices, sum_rows(): lax.psum_scatter(values.astype(jnp.bfloat16), 'head', scatter_dimension=0...  96.3 us
    dot_general x8, matrix products, block_backward(): jnp.einsum('hqk,qhm->khm', grad_scores, phi_query, preferred_element_type...  65.4 us
    reduce_scatter x2, waiting for transfers between devices, body(): lax.psum_scatter(grad_up, 'dp', scatter_dimension=0, tiled=True)  54.5 us
    all_gather x2, blocking collectives, body(): lax.all_gather(down_weight[layer_index], 'head', axis=1, tiled=True)  49.1 us
    dot_general x8, matrix products, block_backward(): jnp.einsum('hqk,khm->qhm', grad_scores, phi_key, preferred_element_type=j...  48.5 us
    all_gather x2, blocking collectives, body(): lax.all_gather(up_weight[layer_index], 'head', axis=1, tiled=True)  43.1 us
  transfers between devices with their start and end apart: 24, of which 13 were waited for; matrix products, arithmetic and copies ran while one was open for 25% of the time, Pallas kernels for 0%

commit v1 on v0

v1 whole, which is shorter than its diff:
```python
import functools
import math

import jax
import jax.numpy as jnp
from jax import lax
from jax.experimental import pallas as pl
from jax.experimental.pallas import tpu as pltpu
from jax.sharding import PartitionSpec as P

MOST = 64
EPSILON = 1e-05
QUERY_ROWS = 128
KEY_ROWS = QUERY_ROWS + 2 * MOST
GROUP = 4
VMEM_BYTES = 60 * 2**20

BF16 = jnp.bfloat16
F32 = jnp.float32
CONTRACT_LAST = (((1,), (1,)), ((), ()))
CONTRACT_FIRST = (((0,), (0,)), ((), ()))
CONTRACT_MIDDLE = (((1,), (0,)), ((), ()))

ERF_TOP = (
    0.00022905065861350646,
    0.0034082910107109506,
    0.050955695062380861,
    0.18520832239976145,
    1.128379143519084,
)
ERF_BOTTOM = (
    -1.1791602954361697e-7,
    0.000023547966471313185,
    0.0010179625278914885,
    0.014070470171167667,
    0.11098505178285362,
    0.49746925110067538,
    1.0,
)


def dot(left, right, dims=CONTRACT_MIDDLE):
    return lax.dot_general(left, right, dims, preferred_element_type=F32)


def polynomial(terms, at):
    total = jnp.full_like(at, terms[0])
    for term in terms[1:]:
        total = total * at + term
    return total


def erf(values):
    values = jnp.clip(values, -3.832506856900711, 3.832506856900711)
    square = values * values
    return values * polynomial(ERF_TOP, square) / polynomial(ERF_BOTTOM, square)


def gelu_and_slope(hidden):
    cumulative = 0.5 * (1.0 + erf(hidden * (1.0 / math.sqrt(2.0))))
    density = jnp.exp(-0.5 * hidden * hidden) * (1.0 / math.sqrt(2.0 * math.pi))
    return hidden * cumulative, cumulative + hidden * density


def normalised(values):
    centred = values - jnp.mean(values, axis=-1, keepdims=True)
    inverse = lax.rsqrt(jnp.mean(centred * centred, axis=-1, keepdims=True) + EPSILON)
    return centred * inverse, inverse


def norm_back(grad_out, gain, hat, inverse):
    scaled = grad_out * gain
    first_mean = jnp.mean(scaled, axis=-1, keepdims=True)
    second_mean = jnp.mean(scaled * hat, axis=-1, keepdims=True)
    return inverse * (scaled - first_mean - hat * second_mean)


def each_block(count, size, step):
    def run(index, carry):
        step(pl.ds(pl.multiple_of(index * size, size), size), index)
        return carry

    lax.fori_loop(0, count, run, 0)


def swap_halves(values, half):
    width = values.shape[-1]
    lane = lax.broadcasted_iota(jnp.int32, values.shape, len(values.shape) - 1)
    ahead = pltpu.roll(values, width - half, 1)
    behind = pltpu.roll(values, half, 1)
    return jnp.where(lane % (2 * half) < half, ahead, behind)


def two_parts(values):
    high = values.astype(BF16)
    return high, (values - high.astype(F32)).astype(BF16)


def phi_of(rows, table, ones):
    high, low = two_parts(rows)
    square_high, square_low = two_parts(rows * rows)
    logits = dot(high, table) + dot(low, table)
    squares = dot(square_high, ones) + dot(square_low, ones)
    return jnp.exp(logits - 0.5 * squares) * (1.0 / math.sqrt(table.shape[1] // GROUP))


def head_masks(width, dtype):
    lane = lax.broadcasted_iota(jnp.int32, (1, width), 1) // (width // GROUP)
    return [jnp.where(lane == head, 1.0, 0.0).astype(dtype) for head in range(GROUP)]


def spread_heads(values):
    return jnp.concatenate([values * mask for mask in head_masks(values.shape[1], BF16)], axis=0)


def gather_heads(values):
    masks = head_masks(values.shape[-1], F32)
    total = values[0] * masks[0]
    for head in range(1, GROUP):
        total = total + values[head] * masks[head]
    return total


def block_scores(phi_q, phi_k, ids_column, ids_row):
    scores = dot(phi_q, phi_k, CONTRACT_LAST)
    same = (ids_column == ids_row).astype(F32)
    scores = scores.reshape(GROUP, QUERY_ROWS, KEY_ROWS) * same[None]
    totals = jnp.sum(scores, axis=-1, keepdims=True)
    inverse = jnp.where(totals > 0.0, 1.0 / totals, 0.0)
    return scores * inverse, inverse, same


def key_start(index, rows):
    start = jnp.clip(index * QUERY_ROWS - MOST, 0, rows - KEY_ROWS)
    return pl.multiple_of(start, MOST)


def attention_forward(
    scale,
    state,
    gain_1,
    gain_2,
    qkv,
    out_weight,
    table,
    ones,
    cosine,
    sine,
    ids_column,
    ids_row,
    normed_a,
    query,
    key,
    value,
    mixed,
    middle,
    normed_c,
    total,
    phi_q,
    phi_k,
):
    group = pl.program_id(0)
    rows = state.shape[0]
    half = cosine.shape[1] // GROUP // 2

    @pl.when(group == 0)
    def _():
        def step(block, index):
            hat, _ = normalised(state[block, :])
            normed_a[block, :] = (hat * gain_1[...]).astype(BF16)
            total[block, :] = state[block, :]

        each_block(rows // 64, 64, step)

    for part, (held, phi) in enumerate(((query, phi_q), (key, phi_k))):
        projected = dot(normed_a[...], qkv[part])
        turned = (projected * cosine[...] + swap_halves(projected, half) * sine[...]) * scale
        held[...] = turned
        phi[...] = phi_of(turned, table[0], ones[...]).astype(BF16)
    value[...] = dot(normed_a[...], qkv[2]).astype(BF16)

    def step(block, index):
        keys = pl.ds(key_start(index, rows), KEY_ROWS)
        weights, _, _ = block_scores(
            spread_heads(phi_q[block, :]), phi_k[keys, :], ids_column[block, :], ids_row[index]
        )
        weights = weights.reshape(GROUP * QUERY_ROWS, KEY_ROWS).astype(BF16)
        found = dot(weights, value[keys, :])
        mixed[block, :] = gather_heads(found.reshape(GROUP, QUERY_ROWS, -1)).astype(BF16)

    each_block(rows // QUERY_ROWS, QUERY_ROWS, step)
    total[...] += dot(mixed[...], out_weight[...], CONTRACT_LAST)

    @pl.when(group == pl.num_programs(0) - 1)
    def _():
        def step(block, index):
            middle[block, :] = total[block, :]
            hat, _ = normalised(total[block, :])
            normed_c[block, :] = (hat * gain_2[...]).astype(BF16)

        each_block(rows // 64, 64, step)


def attention_backward(
    scale,
    grad_middle,
    state,
    gain_1,
    qkv,
    out_weight,
    table,
    ones,
    cosine,
    sine,
    ids_column,
    ids_row,
    normed_a,
    query,
    key,
    value,
    mixed,
    grad_state,
    grad_gain,
    grad_qkv,
    grad_out,
    total,
    branch,
    grad_mixed,
    phi_q,
    phi_k,
    grad_phi_q,
    grad_phi_k,
    grad_value,
):
    group = pl.program_id(0)
    rows = state.shape[0]
    half = cosine.shape[1] // GROUP // 2
    own = pl.ds(MOST, rows - 2 * MOST)

    @pl.when(group == 0)
    def _():
        branch[...] = grad_middle[...].astype(BF16)
        total[...] = jnp.zeros_like(total)

    grad_mixed[...] = dot(branch[...], out_weight[...]).astype(BF16)
    grad_out[...] = dot(branch[own, :], mixed[own, :], CONTRACT_FIRST).astype(BF16)
    phi_q[...] = phi_of(query[...], table[0], ones[...])
    phi_k[...] = phi_of(key[...], table[0], ones[...])
    grad_phi_k[...] = jnp.zeros_like(grad_phi_k)
    grad_value[...] = jnp.zeros_like(grad_value)

    def step(block, index):
        keys = pl.ds(key_start(index, rows), KEY_ROWS)
        spread_q = spread_heads(phi_q[block, :].astype(BF16))
        spread_grad = spread_heads(grad_mixed[block, :])
        keys_phi = phi_k[keys, :].astype(BF16)
        weights, inverse, same = block_scores(
            spread_q, keys_phi, ids_column[block, :], ids_row[index]
        )
        flat = (GROUP * QUERY_ROWS, KEY_ROWS)
        grad_weights = dot(spread_grad, value[keys, :], CONTRACT_LAST)
        grad_value[keys, :] += dot(
            weights.reshape(flat).astype(BF16), spread_grad, CONTRACT_FIRST
        )
        grad_weights = grad_weights.reshape(weights.shape)
        inner = jnp.sum(grad_weights * weights, axis=-1, keepdims=True)
        grad_scores = ((grad_weights - inner) * inverse * same[None]).astype(BF16).reshape(flat)
        found = dot(grad_scores, keys_phi)
        grad_phi_q[block, :] = gather_heads(found.reshape(GROUP, QUERY_ROWS, -1))
        grad_phi_k[keys, :] += dot(grad_scores, spread_q, CONTRACT_FIRST)

    each_block(rows // QUERY_ROWS, QUERY_ROWS, step)

    def through_map(grad_phi, phi, held):
        high, low = two_parts(grad_phi[...] * phi[...])
        along = dot(high, table[0], CONTRACT_LAST) + dot(low, table[0], CONTRACT_LAST)
        summed = dot(high, ones[...], CONTRACT_LAST) + dot(low, ones[...], CONTRACT_LAST)
        grad_rows = (along - held[...] * summed) * scale
        turned = grad_rows * cosine[...] + swap_halves(grad_rows * sine[...], half)
        return turned.astype(BF16)

    for part in range(3):
        if part == 0:
            gradient = through_map(grad_phi_q, phi_q, query)
        elif part == 1:
            gradient = through_map(grad_phi_k, phi_k, key)
        else:
            gradient = grad_value[...].astype(BF16)
        grad_mixed[...] = gradient
        grad_qkv[part] = dot(normed_a[own, :], grad_mixed[own, :], CONTRACT_FIRST).astype(BF16)
        total[...] += dot(grad_mixed[...], qkv[part], CONTRACT_LAST)

    @pl.when(group == pl.num_programs(0) - 1)
    def _():
        grad_gain[...] = jnp.zeros_like(grad_gain)

        def step(block, index):
            hat, inverse = normalised(state[block, :])
            back = norm_back(total[block, :], gain_1[...], hat, inverse)
            grad_state[block, :] = grad_middle[block, :] + back

            @pl.when((index > 0) & (index < rows // 64 - 1))
            def _():
                grad_gain[...] += jnp.sum(total[block, :] * hat, axis=0, keepdims=True)

        each_block(rows // 64, 64, step)


def feed_forward(middle, normed_c, up, down, activated, slope, state, total, hidden):
    chunk = pl.program_id(0)
    rows = middle.shape[0]

    @pl.when(chunk == 0)
    def _():
        total[...] = middle[...]

    hidden[...] = dot(normed_c[...], up[...], CONTRACT_LAST)

    def step(block, index):
        value, back = gelu_and_slope(hidden[block, :])
        activated[block, :] = value.astype(BF16)
        slope[block, :] = back.astype(BF16)

    each_block(rows // 32, 32, step)
    total[...] += dot(activated[...], down[...])

    @pl.when(chunk == pl.num_programs(0) - 1)
    def _():
        state[...] = total[...]


def feed_back(
    gradient,
    middle,
    gain_2,
    normed_c,
    activated,
    slope,
    up,
    down,
    grad_middle,
    grad_gain,
    grad_up,
    grad_down,
    total,
    branch,
    grad_hidden,
    grad_act,
):
    chunk = pl.program_id(0)
    rows = middle.shape[0]
    own = pl.ds(MOST, rows - 2 * MOST)

    @pl.when(chunk == 0)
    def _():
        branch[...] = gradient[...].astype(BF16)
        total[...] = jnp.zeros_like(total)

    grad_act[...] = dot(branch[...], down[...], CONTRACT_LAST)

    def step(block, index):
        grad_hidden[block, :] = (grad_act[block, :] * slope[block, :].astype(F32)).astype(BF16)

    each_block(rows // 32, 32, step)
    grad_down[...] = dot(activated[own, :], branch[own, :], CONTRACT_FIRST).astype(BF16)
    grad_up[...] = dot(grad_hidden[own, :], normed_c[own, :], CONTRACT_FIRST).astype(BF16)
    total[...] += dot(grad_hidden[...], up[...])

    @pl.when(chunk == pl.num_programs(0) - 1)
    def _():
        grad_gain[...] = jnp.zeros_like(grad_gain)

        def step(block, index):
            hat, inverse = normalised(middle[block, :])
            back = norm_back(total[block, :], gain_2[...], hat, inverse)
            grad_middle[block, :] = gradient[block, :] + back

            @pl.when((index > 0) & (index < rows // 64 - 1))
            def _():
                grad_gain[...] += jnp.sum(total[block, :] * hat, axis=0, keepdims=True)

        each_block(rows // 64, 64, step)


def whole(shape):
    return pl.BlockSpec(shape, lambda step: (0,) * len(shape))


def columns(rows, width):
    return pl.BlockSpec((rows, width), lambda step: (0, step))


def leading(shape):
    return pl.BlockSpec(shape, lambda step: (step,) + (0,) * (len(shape) - 1))


def parts_columns(parts, rows, width):
    return pl.BlockSpec((parts, rows, width), lambda step: (0, 0, step))


def struct(shape, dtype):
    return jax.ShapeDtypeStruct(shape, dtype)


def kernel_call(kernel, steps, in_specs, out_specs, out_shape, scratch, flops):
    return pl.pallas_call(
        kernel,
        grid=(steps,),
        in_specs=in_specs,
        out_specs=out_specs,
        out_shape=out_shape,
        scratch_shapes=scratch,
        compiler_params=pltpu.CompilerParams(vmem_limit_bytes=VMEM_BYTES),
        cost_estimate=pl.CostEstimate(flops=flops, bytes_accessed=flops // 600, transcendentals=0),
    )


def run_attention_forward(state, gains, qkv, out_weight, table, ones, tables, ids, scale):
    rows, width = state.shape
    wide = table.shape[1]
    small = table.shape[2]
    blocks = rows // QUERY_ROWS
    return kernel_call(
        functools.partial(attention_forward, scale),
        width // wide,
        [
            whole((rows, width)),
            whole((1, width)),
            whole((1, width)),
            parts_columns(3, width, wide),
            columns(width, wide),
            leading((1, wide, small)),
            whole((wide, small)),
            whole((rows, wide)),
            whole((rows, wide)),
            whole((rows, 1)),
            whole((blocks, 1, KEY_ROWS)),
        ],
        [
            whole((rows, width)),
            columns(rows, wide),
            columns(rows, wide),
            columns(rows, wide),
            columns(rows, wide),
            whole((rows, width)),
            whole((rows, width)),
        ],
        [
            struct((rows, width), BF16),
            struct((rows, width), F32),
            struct((rows, width), F32),
            struct((rows, width), BF16),
            struct((rows, width), BF16),
            struct((rows, width), F32),
            struct((rows, width), BF16),
        ],
        [
            pltpu.VMEM((rows, width), F32),
            pltpu.VMEM((rows, small), BF16),
            pltpu.VMEM((rows, small), BF16),
        ],
        2 * rows * width * width * 5,
    )(state, gains[0][None], gains[1][None], qkv, out_weight, table, ones, *tables, *ids)


def run_attention_backward(
    grad_middle, state, gain, qkv, out_weight, table, ones, tables, ids, kept, scale
):
    rows, width = state.shape
    wide = table.shape[1]
    small = table.shape[2]
    blocks = rows // QUERY_ROWS
    return kernel_call(
        functools.partial(attention_backward, scale),
        width // wide,
        [
            whole((rows, width)),
            whole((rows, width)),
            whole((1, width)),
            parts_columns(3, width, wide),
            columns(width, wide),
            leading((1, wide, small)),
            whole((wide, small)),
            whole((rows, wide)),
            whole((rows, wide)),
            whole((rows, 1)),
            whole((blocks, 1, KEY_ROWS)),
            whole((rows, width)),
            columns(rows, wide),
            columns(rows, wide),
            columns(rows, wide),
            columns(rows, wide),
        ],
        [
            whole((rows, width)),
            whole((1, width)),
            parts_columns(3, width, wide),
            columns(width, wide),
        ],
        [
            struct((rows, width), F32),
            struct((1, width), F32),
            struct((3, width, width), BF16),
            struct((width, width), BF16),
        ],
        [
            pltpu.VMEM((rows, width), F32),
            pltpu.VMEM((rows, width), BF16),
            pltpu.VMEM((rows, wide), BF16),
            pltpu.VMEM((rows, small), F32),
            pltpu.VMEM((rows, small), F32),
            pltpu.VMEM((rows, small), F32),
            pltpu.VMEM((rows, small), F32),
            pltpu.VMEM((rows, wide), F32),
        ],
        2 * rows * width * width * 10,
    )(grad_middle, state, gain[None], qkv, out_weight, table, ones, *tables, *ids, *kept)


def hidden_chunk(count):
    return 512 if count % 512 == 0 else count


def run_feed_forward(middle, normed_c, up, down):
    rows, width = middle.shape
    count = up.shape[0]
    chunk = hidden_chunk(count)
    return kernel_call(
        feed_forward,
        count // chunk,
        [
            whole((rows, width)),
            whole((rows, width)),
            leading((chunk, width)),
            leading((chunk, width)),
        ],
        [columns(rows, chunk), columns(rows, chunk), whole((rows, width))],
        [
            struct((rows, count), BF16),
            struct((rows, count), BF16),
            struct((rows, width), F32),
        ],
        [pltpu.VMEM((rows, width), F32), pltpu.VMEM((rows, chunk), F32)],
        4 * rows * width * count,
    )(middle, normed_c, up, down)


def run_feed_back(gradient, middle, gain, normed_c, activated, slope, up, down):
    rows, width = middle.shape
    count = up.shape[0]
    chunk = hidden_chunk(count)
    return kernel_call(
        feed_back,
        count // chunk,
        [
            whole((rows, width)),
            whole((rows, width)),
            whole((1, width)),
            whole((rows, width)),
            columns(rows, chunk),
            columns(rows, chunk),
            leading((chunk, width)),
            leading((chunk, width)),
        ],
        [
            whole((rows, width)),
            whole((1, width)),
            leading((chunk, width)),
            leading((chunk, width)),
        ],
        [
            struct((rows, width), F32),
            struct((1, width), F32),
            struct((count, width), BF16),
            struct((count, width), BF16),
        ],
        [
            pltpu.VMEM((rows, width), F32),
            pltpu.VMEM((rows, width), BF16),
            pltpu.VMEM((rows, chunk), BF16),
            pltpu.VMEM((rows, chunk), F32),
        ],
        8 * rows * width * count,
    )(gradient, middle, gain[None], normed_c, activated, slope, up, down)


def gather_weight(weight, dim):
    wide = lax.all_gather(weight, "head", axis=dim + 1, tiled=True)
    return lax.all_gather(wide, "dp", axis=dim, tiled=True)


def scatter_grad(gradient, dim):
    part = lax.psum_scatter(gradient, "dp", scatter_dimension=dim, tiled=True)
    return lax.psum_scatter(part, "head", scatter_dimension=dim + 1, tiled=True).astype(F32)


def with_halo(inputs, cotangent):
    count = lax.axis_size("head")
    both = jnp.concatenate([inputs, cotangent], axis=1)
    before = lax.ppermute(both[-MOST:], "head", [(i, i + 1) for i in range(count - 1)])
    after = lax.ppermute(both[:MOST], "head", [(i + 1, i) for i in range(count - 1)])
    joined = jnp.concatenate([before, both, after], axis=0).astype(F32)
    return joined[:, : inputs.shape[1]], joined[:, inputs.shape[1] :]


def window_ids(segment_ids, own_rows):
    padded = jnp.pad(segment_ids[0], (MOST, MOST), constant_values=-1)
    begin = lax.axis_index("head") * own_rows
    ids = lax.dynamic_slice(padded, (begin,), (own_rows + 2 * MOST,))
    place = jnp.arange(ids.shape[0])
    earlier = (ids[:, None] == ids[None, :]) & (place[None, :] < place[:, None])
    position = jnp.sum(earlier.astype(F32), axis=1)
    used = (ids >= ids[MOST]) & (ids <= ids[MOST + own_rows - 1])
    column = jnp.where(used, ids, -1)[:, None]
    row = jnp.where(used, ids, -2)
    starts = [
        min(max(b * QUERY_ROWS - MOST, 0), ids.shape[0] - KEY_ROWS)
        for b in range(ids.shape[0] // QUERY_ROWS)
    ]
    rows = jnp.stack([row[start : start + KEY_ROWS] for start in starts])[:, None, :]
    return position, (column, rows)


def rotary_tables(position, head_width):
    halves = head_width // 2
    frequency = jnp.exp(jnp.arange(halves, dtype=F32) * (-2.0 * math.log(10000.0) / head_width))
    angles = position[:, None] * frequency[None, :]
    cosine, sine = jnp.cos(angles), jnp.sin(angles)
    return (
        jnp.tile(jnp.concatenate([cosine, cosine], axis=1), (1, GROUP)),
        jnp.tile(jnp.concatenate([-sine, sine], axis=1), (1, GROUP)),
    )


def body(
    inputs,
    segment_ids,
    features,
    norm_gain,
    query_key_value,
    output_weight,
    up_weight,
    down_weight,
    cotangent,
):
    layer_count = norm_gain.shape[0]
    own_rows = inputs.shape[0]
    head_width = features.shape[3]
    feature_count = features.shape[2]
    scale = head_width ** (-0.25)
    own = slice(MOST, MOST + own_rows)

    state, gradient = with_halo(inputs, cotangent)
    position, ids = window_ids(segment_ids, own_rows)
    tables = rotary_tables(position, head_width)
    all_features = lax.all_gather(features, "head", axis=1, tiled=True)
    shaped = all_features.reshape(layer_count, -1, GROUP, feature_count, head_width)
    eye = jnp.eye(GROUP, dtype=BF16)
    blocks = jnp.einsum("lghmw,hk->lghwkm", shaped, eye).reshape(
        layer_count, -1, GROUP * head_width, GROUP * feature_count
    )
    ones = jnp.kron(eye, jnp.ones((head_width, feature_count), BF16))

    weights = [
        (
            gather_weight(query_key_value[layer], 1),
            gather_weight(output_weight[layer], 0),
            gather_weight(up_weight[layer], 0),
            gather_weight(down_weight[layer], 0),
        )
        for layer in range(layer_count)
    ]
    stored = []
    for layer in range(layer_count):
        qkv, out_weight, up, down = weights[layer]
        normed_a, query, key, value, mixed, middle, normed_c = run_attention_forward(
            state, norm_gain[layer], qkv, out_weight, blocks[layer], ones, tables, ids, scale
        )
        activated, slope, after = run_feed_forward(middle, normed_c, up, down)
        stored.append((state, (normed_a, query, key, value, mixed), middle, normed_c, activated, slope))
        state = after
    outputs = state[own].astype(BF16)
    gains = [None] * layer_count
    shares = [None] * layer_count
    for layer in reversed(range(layer_count)):
        qkv, out_weight, up, down = weights[layer]
        before, kept, middle, normed_c, activated, slope = stored[layer]
        grad_middle, gain_c, grad_up, grad_down = run_feed_back(
            gradient, middle, norm_gain[layer, 1], normed_c, activated, slope, up, down
        )
        gradient, gain_a, grad_qkv, grad_out = run_attention_backward(
            grad_middle,
            before,
            norm_gain[layer, 0],
            qkv,
            out_weight,
            blocks[layer],
            ones,
            tables,
            ids,
            kept,
            scale,
        )
        gains[layer] = jnp.concatenate([gain_a, gain_c])
        shares[layer] = (
            scatter_grad(grad_qkv, 1),
            scatter_grad(grad_out, 0),
            scatter_grad(grad_up, 0),
            scatter_grad(grad_down, 0),
        )
    gain_total = lax.psum(jnp.stack(gains), ("dp", "head"))
    return (
        outputs,
        gradient[own],
        gain_total[:, 0],
        gain_total[:, 1],
        *(jnp.stack(list(kind)) for kind in zip(*shares)),
    )


def solution(mesh):
    in_specs = (
        P(("dp", "head"), None),
        P("dp", None),
        P(None, "head", None, None),
        P(),
        P(None, None, "dp", "head"),
        P(None, "dp", "head"),
        P(None, "dp", "head"),
        P(None, "dp", "head"),
        P(("dp", "head"), None),
    )
    out_specs = (
        P(("dp", "head"), None),
        P(("dp", "head"), None),
        P(),
        P(),
        P(None, None, "dp", "head"),
        P(None, "dp", "head"),
        P(None, "dp", "head"),
        P(None, "dp", "head"),
    )
    return jax.shard_map(body, mesh=mesh, in_specs=in_specs, out_specs=out_specs, check_vma=False)
```

time: 1330 us -> 1030 us (0.77)
  matrix products: 393 us -> 0 us
  Pallas kernels: 0 us -> 224 us
  local copies, waits for them, and re-layouts: 155 us -> 55.4 us
  other arithmetic: 59.2 us -> 4.79 us
  waiting for transfers between devices: 500 us -> 527 us
    dot_general x86 -> x0, matrix products: 385 us -> none  [the longest x8 65.4 us: block_backward(): jnp.einsum('hqk,qhm->khm', grad_scores, phi_query, preferred_element_type...]
    pallas_call x0 -> x8, Pallas kernels: none -> 224 us  [the longest x2 69.9 us: run_attention_backward(): kernel_call(functools.partial(attention_backward, scale), width // wide,...]
    all_gather x8, waiting for transfers between devices: 210 us -> 51.5 us  [gather_weight(): return lax.all_gather(wide, 'dp', axis=dim, tiled=True)]
    unnamed x24 -> x32, waiting for transfers between devices: 0.34 us -> 126 us
    reduce_scatter x8, waiting for transfers between devices: 277 us -> 350 us  [scatter_grad(): part = lax.psum_scatter(gradient, 'dp', scatter_dimension=dim, tiled=True)]
    dynamic_update_slice x24 -> x0, local copies, waits for them, and re-layouts: 41.1 us -> none  [the longest x16 41 us: body(): lax.map(block_backward, (phi_query, phi_key, value_windows, id_blocks, id...]
    reshape x20 -> x1, local copies, waits for them, and re-layouts: 26.3 us -> 0.1 us  [body(): all_features.reshape(layer_count, -1, GROUP, feature_count, head_width)]
    convert_element_type x29 -> x1, other arithmetic: 22.5 us -> 0.52 us  [with_halo(): joined = jnp.concatenate([before, both, after], axis=0).astype(F32)]
  transfers between devices with their start and end apart: 24 -> 26, of which waited for: 13 -> 15; matrix products, arithmetic and copies ran while one was open for 25% -> 6% of each run, Pallas kernels for 0% -> 14%
where the time goes in v1:
time: 1030 us; the launch traced here: 1020 us
  waiting for transfers between devices  527 us (51%)
  Pallas kernels  224 us (22%)
  blocking collectives  186 us (18%)
  local copies, waits for them, and re-layouts  55.4 us (5%)
  between operations  15.3 us (1%)
    reduce_scatter x8, waiting for transfers between devices, scatter_grad(): part = lax.psum_scatter(gradient, 'dp', scatter_dimension=dim, tiled=True)  350 us
    all_gather x8, blocking collectives, gather_weight(): wide = lax.all_gather(weight, 'head', axis=dim + 1, tiled=True)  132 us
    unnamed x32, waiting for transfers between devices  126 us
    pallas_call x2, Pallas kernels, run_attention_backward(): kernel_call(functools.partial(attention_backward, scale), width // wide,...  69.9 us
    pallas_call x2, Pallas kernels, run_attention_forward(): kernel_call(functools.partial(attention_forward, scale), width // wide, [...  52.2 us
    all_gather x8, waiting for transfers between devices, gather_weight(): return lax.all_gather(wide, 'dp', axis=dim, tiled=True)  51.5 us
    pallas_call x2, Pallas kernels, run_feed_back(): kernel_call(feed_back, count // chunk, [whole((rows, width)), whole((rows...  51.2 us
    pallas_call x2, Pallas kernels, run_feed_forward(): kernel_call(feed_forward, count // chunk, [whole((rows, width)), whole((r...  50.6 us
  transfers between devices with their start and end apart: 26, of which 15 were waited for; matrix products, arithmetic and copies ran while one was open for 6% of the time, Pallas kernels for 14%

profile of v1, /device:TPU:0, one launch (start us, length us, event | category | flops | bytes accessed | tf_op | source)
XLA Modules:
  0.0 1019.3 jit_solution(6111690551395360565)
XLA Ops:
  8.2 16.2 %all-gather.2 = bf16[1,96,768]{1,0,2:T(2,128)(2,1)S(1)} all-gather(bf16[1,96,192]{1,0,2:T(2,128)(2,1)S(1)} %copy.140), channel_id=4, replica_groups=mesh['dp'=8,'head'=4] {'head'}, dimensions={2}, use_global_device_ids=true | all-gather | bytes 184320 | tf_op jit(solution)/shard_map/all_gather | solution.py:588
  26.6 18.3 %all-gather = bf16[1,3,96,768]{2,1,0,3:T(4,128)(2,1)S(1)} all-gather(bf16[1,3,96,192]{2,1,0,3:T(4,128)(2,1)S(1)} %copy.139), channel_id=2, replica_groups=mesh['dp'=8,'head'=4] {'head'}, dimensions={3}, use_global_device_ids=true | all-gather | bytes 552960 | tf_op jit(solution)/shard_map/all_gather | solution.py:588
  46.2 16.6 %all-gather.4 = bf16[1,384,768]{1,2,0:T(8,128)(2,1)S(1)} all-gather(bf16[1,384,192]{1,2,0:T(8,128)(2,1)S(1)} %get-tuple-element.121), channel_id=6, replica_groups=mesh['dp'=8,'head'=4] {'head'}, dimensions={2}, use_global_device_ids=true | all-gather | bytes 737280 | tf_op jit(solution)/shard_map/all_gather | solution.py:588
  64.0 15.0 %all-gather.6 = bf16[1,384,768]{1,2,0:T(8,128)(2,1)S(1)} all-gather(bf16[1,384,192]{1,2,0:T(8,128)(2,1)S(1)} %get-tuple-element.119), channel_id=8, replica_groups=mesh['dp'=8,'head'=4] {'head'}, dimensions={2}, use_global_device_ids=true | all-gather | bytes 737280 | tf_op jit(solution)/shard_map/all_gather | solution.py:588
  80.3 15.4 %all-gather.10 = bf16[1,96,768]{1,0,2:T(2,128)(2,1)S(1)} all-gather(bf16[1,96,192]{1,0,2:T(2,128)(2,1)S(1)} %copy.142), channel_id=12, replica_groups=mesh['dp'=8,'head'=4] {'head'}, dimensions={2}, use_global_device_ids=true | all-gather | bytes 184320 | tf_op jit(solution)/shard_map/all_gather | solution.py:588
  96.9 18.8 %all-gather.8 = bf16[1,3,96,768]{2,1,0,3:T(4,128)(2,1)S(1)} all-gather(bf16[1,3,96,192]{2,1,0,3:T(4,128)(2,1)S(1)} %copy.141), channel_id=10, replica_groups=mesh['dp'=8,'head'=4] {'head'}, dimensions={3}, use_global_device_ids=true | all-gather | bytes 552960 | tf_op jit(solution)/shard_map/all_gather | solution.py:588
  116.9 15.6 %all-gather.12 = bf16[1,384,768]{1,2,0:T(8,128)(2,1)S(1)} all-gather(bf16[1,384,192]{1,2,0:T(8,128)(2,1)S(1)} %get-tuple-element.120), channel_id=14, replica_groups=mesh['dp'=8,'head'=4] {'head'}, dimensions={2}, use_global_device_ids=true | all-gather | bytes 737280 | tf_op jit(solution)/shard_map/all_gather | solution.py:588
  133.7 16.2 %all-gather.14 = bf16[1,384,768]{1,2,0:T(8,128)(2,1)S(1)} all-gather(bf16[1,384,192]{1,2,0:T(8,128)(2,1)S(1)} %get-tuple-element.118), channel_id=16, replica_groups=mesh['dp'=8,'head'=4] {'head'}, dimensions={2}, use_global_device_ids=true | all-gather | bytes 737280 | tf_op jit(solution)/shard_map/all_gather | solution.py:588
  151.9 1.3 collective-permute-start.1
  153.2 4.6 collective-permute-start
  157.8 13.6 %all_gather.55 = bf16[2,12,32,64]{3,2,1,0:T(8,128)(2,1)S(1)} all-gather(bf16[2,3,32,64]{3,2,1,0:T(8,128)(2,1)S(1)} %copy-done.5), channel_id=1, replica_groups=mesh['dp'=8,'head'=4] {'head'}, dimensions={1}, use_global_device_ids=true | all-gather | bytes 122880 | tf_op jit(solution)/shard_map/all_gather | solution.py:656
  178.0 1.4 fusion.2
  183.2 2.1 fusion.5
  185.3 26.2 %shard_map.152 = (bf16[640,768]{1,0:T(8,128)(2,1)}, f32[640,768]{1,0:T(8,128)}, f32[640,768]{1,0:T(8,128)}, bf16[640,768]{1,0:T(8,128)(2,1)}, bf16[640,768]{1,0:...) custom-call(f32[640,768]{1,0:T(8,128)} %get-tuple-element.113.state, f32[1,768]{1,0:T(1,128)} %get-tuple-element.130.gain_1, ...), custom_call_target="tpu_custom_call" | custom-call | flops 3774873600 | bytes 6291456 | tf_op jit(solution)/shard_map/pallas_call | solution.py:423
  211.6 25.3 %shard_map.153 = (bf16[640,3072]{1,0:T(8,128)(2,1)}, bf16[640,3072]{1,0:T(8,128)(2,1)}, f32[640,768]{1,0:T(8,128)}) custom-call(f32[640,768]{1,0:T(8,128)} %get-tuple-element.44.middle, bf16[640,768]{1,0:T(8,128)(2,1)} %get-tuple-element.45.normed_c, bf16[3072,768]{1,0:T(8,128)(2,1)} %bitcast.107, bf16[3072,768]{1,0:T(8,128)(2,1)} %bitcast.109), custom_call_target="tpu_custom_call" | custom-call | flops 6039797760 | bytes 10066329 | tf_op jit(solution)/shard_map/pallas_call | solution.py:528
  237.0 26.0 %shard_map.154 = (bf16[640,768]{1,0:T(8,128)(2,1)}, f32[640,768]{1,0:T(8,128)}, f32[640,768]{1,0:T(8,128)}, bf16[640,768]{1,0:T(8,128)(2,1)}, bf16[640,768]{1,0:...) custom-call(f32[640,768]{1,0:T(8,128)} %get-tuple-element.46.state, f32[1,768]{1,0:T(1,128)} %get-tuple-element.131.gain_1, ...), custom_call_target="tpu_custom_call" | custom-call | flops 3774873600 | bytes 6291456 | tf_op jit(solution)/shard_map/pallas_call | solution.py:423
  263.0 10.6 %all-gather.37.cloned.1.call-done = bf16[1,3072,768]{2,1,0:T(8,128)(2,1)} async-done(((bf16[1,384,768]{2,1,0:T(8,128)(2,1)}), bf16[1,3072,768]{2,1,0:T(8,128)(2,1)}) %all-gather.37.cloned.1.call-update) | async-done | bytes 4718608 | tf_op jit(solution)/shard_map/all_gather | solution.py:589
  273.5 40.8 %all-gather.39.cloned.1.call-done = bf16[1,3072,768]{2,1,0:T(8,128)(2,1)} async-done(((bf16[1,384,768]{2,1,0:T(8,128)(2,1)}), bf16[1,3072,768]{2,1,0:T(8,128)(2,1)}) %all-gather.39.cloned.1.call-update) | async-done | bytes 4718608 | tf_op jit(solution)/shard_map/all_gather | solution.py:589
  314.4 25.3 %shard_map.155 = (bf16[640,3072]{1,0:T(8,128)(2,1)}, bf16[640,3072]{1,0:T(8,128)(2,1)}, f32[640,768]{1,0:T(8,128)}) custom-call(f32[640,768]{1,0:T(8,128)} %get-tuple-element.47.middle, bf16[640,768]{1,0:T(8,128)(2,1)} %get-tuple-element.48.normed_c, bf16[3072,768]{1,0:T(8,128)(2,1)} %bitcast.111, bf16[3072,768]{1,0:T(8,128)(2,1)} %bitcast.113), custom_call_target="tpu_custom_call" | custom-call | flops 6039797760 | bytes 10066329 | tf_op jit(solution)/shard_map/pallas_call | solution.py:528
  339.6 25.6 %shard_map.156 = (f32[640,768]{1,0:T(8,128)}, f32[1,768]{1,0:T(1,128)}, bf16[3072,768]{1,0:T(8,128)(2,1)}, bf16[3072,768]{1,0:T(8,128)(2,1)}) custom-call(f32[640,768]{1,0:T(8,128)} %get-tuple-element.112.gradient, f32[640,768]{1,0:T(8,128)} %get-tuple-element.47.middle, f32[1,768]{1,0:T(1,128)} %get-tuple-element.128.gain_2, ...), custom_call_target="tpu_custom_call" | custom-call | flops 12079595520 | bytes 20132660 | tf_op jit(solution)/shard_map/pallas_call | solution.py:552
  365.3 35.0 %shard_map.157 = (f32[640,768]{1,0:T(8,128)}, f32[1,768]{1,0:T(1,128)}, bf16[3,768,768]{2,1,0:T(8,128)(2,1)}, bf16[768,768]{1,0:T(8,128)(2,1)}) custom-call(f32[640,768]{1,0:T(8,128)} %get-tuple-element.52.grad_middle, f32[640,768]{1,0:T(8,128)} %get-tuple-element.46.state, f32[1,768]{1,0:T(1,128)} %get-tuple-element.131.gain_1, ...), custom_call_target="tpu_custom_call" | custom-call | flops 7549747200 | bytes 12582912 | tf_op jit(solution)/shard_map/pallas_call | solution.py:473
  400.3 25.6 %shard_map.158 = (f32[640,768]{1,0:T(8,128)}, f32[1,768]{1,0:T(1,128)}, bf16[3072,768]{1,0:T(8,128)(2,1)}, bf16[3072,768]{1,0:T(8,128)(2,1)}) custom-call(f32[640,768]{1,0:T(8,128)} %get-tuple-element.58.gradient, f32[640,768]{1,0:T(8,128)} %get-tuple-element.44.middle, f32[1,768]{1,0:T(1,128)} %get-tuple-element.129.gain_2, ...), custom_call_target="tpu_custom_call" | custom-call | flops 12079595520 | bytes 20132660 | tf_op jit(solution)/shard_map/pallas_call | solution.py:552
  425.9 34.9 %shard_map.159 = (f32[640,768]{1,0:T(8,128)}, f32[1,768]{1,0:T(1,128)}, bf16[3,768,768]{2,1,0:T(8,128)(2,1)}, bf16[768,768]{1,0:T(8,128)(2,1)}) custom-call(f32[640,768]{1,0:T(8,128)} %get-tuple-element.61.grad_middle, f32[640,768]{1,0:T(8,128)} %get-tuple-element.113.state, f32[1,768]{1,0:T(1,128)} %get-tuple-element.130.gain_1, ...), custom_call_target="tpu_custom_call" | custom-call | flops 7549747200 | bytes 12582912 | tf_op jit(solution)/shard_map/pallas_call | solution.py:473
  464.8 1.7 copy.127
  466.6 31.3 %reduce-scatter.37.cloned.1.call-done = bf16[96,768]{1,0:T(8,128)(2,1)} async-done(((bf16[768,768]{1,0:T(8,128)(2,1)}), bf16[96,768]{1,0:T(8,128)(2,1)}) %reduce-scatter.37.cloned.1.call-update) | async-done | bytes 147472 | tf_op jit(solution)/shard_map/reduce_scatter | solution.py:593
  497.8 1.7 copy.125
  499.6 49.8 %reduce-scatter.35.cloned.1.call-done = bf16[3,96,768]{2,1,0:T(8,128)(2,1)} async-done(((bf16[3,768,768]{2,1,0:T(8,128)(2,1)}), bf16[3,96,768]{2,1,0:T(8,128)(2,1)}) %reduce-scatter.35.cloned.1.call-update) | async-done | bytes 442384 | tf_op jit(solution)/shard_map/reduce_scatter | solution.py:593
  549.4 1.4 copy.123
  550.9 1.2 reshape.78
  552.2 48.7 %reduce-scatter.33.cloned.1.call-done = bf16[3,96,768]{2,1,0:T(8,128)(2,1)} async-done(((bf16[3,768,768]{2,1,0:T(8,128)(2,1)}), bf16[3,96,768]{2,1,0:T(8,128)(2,1)}) %reduce-scatter.33.cloned.1.call-update) | async-done | bytes 442384 | tf_op jit(solution)/shard_map/reduce_scatter | solution.py:593
  600.9 1.4 copy.121
  602.3 1.2 reshape.76
  603.6 54.6 %reduce-scatter.43.cloned.1.call-done = bf16[384,768]{1,0:T(8,128)(2,1)} async-done(((bf16[3072,768]{1,0:T(8,128)(2,1)}), bf16[384,768]{1,0:T(8,128)(2,1)}) %reduce-scatter.43.cloned.1.call-update) | async-done | bytes 589840 | tf_op jit(solution)/shard_map/reduce_scatter | solution.py:593
  658.2 2.1 copy.131
  660.4 55.4 %reduce-scatter.41.cloned.1.call-done = bf16[384,768]{1,0:T(8,128)(2,1)} async-done(((bf16[3072,768]{1,0:T(8,128)(2,1)}), bf16[384,768]{1,0:T(8,128)(2,1)}) %reduce-scatter.41.cloned.1.call-update) | async-done | bytes 589840 | tf_op jit(solution)/shard_map/reduce_scatter | solution.py:593
  715.8 2.2 copy.129
  718.0 55.0 %reduce-scatter.47.cloned.1.call-done = bf16[384,768]{1,0:T(8,128)(2,1)} async-done(((bf16[3072,768]{1,0:T(8,128)(2,1)}), bf16[384,768]{1,0:T(8,128)(2,1)}) %reduce-scatter.47.cloned.1.call-update) | async-done | bytes 589840 | tf_op jit(solution)/shard_map/reduce_scatter | solution.py:593
  773.0 2.1 copy.135
  775.2 55.4 %reduce-scatter.45.cloned.1.call-done = bf16[384,768]{1,0:T(8,128)(2,1)} async-done(((bf16[3072,768]{1,0:T(8,128)(2,1)}), bf16[384,768]{1,0:T(8,128)(2,1)}) %reduce-scatter.45.cloned.1.call-update) | async-done | bytes 589840 | tf_op jit(solution)/shard_map/reduce_scatter | solution.py:593
  830.6 2.1 copy.133
  832.8 2.4 slice.161
  836.5 39.9 %psum.7 = f32[2,2,768]{2,1,0:T(2,128)S(1)} all-reduce(f32[2,2,768]{2,1,0:T(2,128)S(1)} %pad_maximum_fusion.2), channel_id=1, replica_groups=mesh['dp'=8,'head'=4] {'dp','head'}, use_global_device_ids=true, to_apply=%region_1.2 | all-reduce | flops 3072 | bytes 24576 | tf_op jit(solution)/shard_map/psum | solution.py:711
  880.1 16.2 %reduce-scatter.51.cloned.1.call-done = bf16[192,288]{1,0:T(8,128)(2,1)} async-done(((bf16[768,288]{1,0:T(8,128)(2,1)}), bf16[192,288]{1,0:T(8,128)(2,1)}) %reduce-scatter.51.cloned.1.call-update) | async-done | bytes 110608
  897.5 21.8 %reduce-scatter.49.cloned.1.call-done = bf16[192,288]{1,0:T(8,128)(2,1)} async-done(((bf16[768,288]{1,0:T(8,128)(2,1)}), bf16[192,288]{1,0:T(8,128)(2,1)}) %reduce-scatter.49.cloned.1.call-update) | async-done | bytes 110608
  921.4 20.6 %reduce-scatter.59.cloned.1.call-done = bf16[192,384]{1,0:T(8,128)(2,1)} async-done(((bf16[768,384]{1,0:T(8,128)(2,1)}), bf16[192,384]{1,0:T(8,128)(2,1)}) %reduce-scatter.59.cloned.1.call-update) | async-done | bytes 147472
  943.0 21.5 %reduce-scatter.57.cloned.1.call-done = bf16[192,384]{1,0:T(8,128)(2,1)} async-done(((bf16[768,384]{1,0:T(8,128)(2,1)}), bf16[192,384]{1,0:T(8,128)(2,1)}) %reduce-scatter.57.cloned.1.call-update) | async-done | bytes 147472
  966.8 20.5 %reduce-scatter.63.cloned.1.call-done = bf16[192,384]{1,0:T(8,128)(2,1)} async-done(((bf16[768,384]{1,0:T(8,128)(2,1)}), bf16[192,384]{1,0:T(8,128)(2,1)}) %reduce-scatter.63.cloned.1.call-update) | async-done | bytes 147472
  988.3 21.4 %reduce-scatter.61.cloned.1.call-done = bf16[192,384]{1,0:T(8,128)(2,1)} async-done(((bf16[768,384]{1,0:T(8,128)(2,1)}), bf16[192,384]{1,0:T(8,128)(2,1)}) %reduce-scatter.61.cloned.1.call-update) | async-done | bytes 147472
  (152 shorter events, 41.8 us)
Async XLA Ops:
  7.2 178.2 %all-gather.27.cloned.1.call-start = ((), (), s32[]{:S(2)}) async-start(), calls=%async_computation.25 | async-start | bytes 1327104 | tf_op jit(solution)/shard_map/all_gather | solution.py:589
  25.3 20.8 %copy-start.3 = (bf16[2,384,192]{1,2,0:T(8,128)(2,1)S(1)}, bf16[2,384,192]{1,2,0:T(8,128)(2,1)}, u32[]{:S(2)}) copy-start(bf16[2,384,192]{1,2,0:T(8,128)(2,1)} %param.15) | copy-start | bytes 884740
  25.3 160.0 %all-gather.25.cloned.1.call-start = ((), (), s32[]{:S(2)}) async-start(), calls=%async_computation.24 | async-start | bytes 3981312 | tf_op jit(solution)/shard_map/all_gather | solution.py:589
  46.1 17.9 %copy-start.4 = (bf16[2,384,192]{1,2,0:T(8,128)(2,1)S(1)}, bf16[2,384,192]{1,2,0:T(8,128)(2,1)}, u32[]{:S(2)}) copy-start(bf16[2,384,192]{1,2,0:T(8,128)(2,1)} %param.16) | copy-start | bytes 884740
  46.1 165.5 %all-gather.29.cloned.1.call-start = ((), (), s32[]{:S(2)}) async-start(), calls=%async_computation.26 | async-start | bytes 5308416 | tf_op jit(solution)/shard_map/all_gather | solution.py:589
  63.9 147.7 %all-gather.31.cloned.1.call-start = ((), (), s32[]{:S(2)}) async-start(), calls=%async_computation.27 | async-start | bytes 5308416 | tf_op jit(solution)/shard_map/all_gather | solution.py:589
  80.1 156.8 %all-gather.35.cloned.1.call-start = ((), (), s32[]{:S(2)}) async-start(), calls=%async_computation.29 | async-start | bytes 1327104 | tf_op jit(solution)/shard_map/all_gather | solution.py:589
  96.7 140.3 %all-gather.33.cloned.1.call-start = ((), (), s32[]{:S(2)}) async-start(), calls=%async_computation.28 | async-start | bytes 3981312 | tf_op jit(solution)/shard_map/all_gather | solution.py:589
  116.8 156.7 %all-gather.37.cloned.1.call-start = ((), (), s32[]{:S(2)}) async-start(), calls=%async_computation.30 | async-start | bytes 5308416 | tf_op jit(solution)/shard_map/all_gather | solution.py:589
  132.5 18.6 %copy-start.1 = (bf16[512,768]{1,0:T(8,128)(2,1)S(1)}, bf16[512,768]{1,0:T(8,128)(2,1)}, u32[]{:S(2)}) copy-start(bf16[512,768]{1,0:T(8,128)(2,1)} %param.9) | copy-start | bytes 2359300
  133.6 180.8 %all-gather.39.cloned.1.call-start = ((), (), s32[]{:S(2)}) async-start(), calls=%async_computation.31 | async-start | bytes 5308416 | tf_op jit(solution)/shard_map/all_gather | solution.py:589
  133.7 17.5 %copy-start.2 = (bf16[512,768]{1,0:T(8,128)(2,1)S(1)}, bf16[512,768]{1,0:T(8,128)(2,1)}, u32[]{:S(2)}) copy-start(bf16[512,768]{1,0:T(8,128)(2,1)} %param.17) | copy-start | bytes 2359300
  151.0 6.8 copy-start.5
  151.0 313.7 %reduce-scatter.39.cloned.1.call-start = ((), (), s32[]{:S(2)}) async-start(), calls=%async_computation.19 | async-start | bytes 1327104 | tf_op jit(solution)/shard_map/reduce_scatter | solution.py:593
  151.9 30.8 %collective-permute-start.1 = (bf16[64,1536]{1,0:T(8,128)(2,1)}, bf16[64,1536]{1,0:T(8,128)(2,1)S(1)}, u32[]{:S(2)}, u32[]{:S(2)}) collective-permute-start(bf16[64,1536]{1,0:T(8,128)(2,1)} %get-tuple-element.115), channel_id=1, source_target_pairs={{1,0},{2,1},{3,2},{5,4},{6,5},{7,6},{9,8},{10,9},{11,10},{13,12},{... | collective-permute-start | bytes 589832 | tf_op jit(solution)/shard_map/ppermute | solution.py:601
  153.2 29.5 %collective-permute-start = (bf16[64,1536]{1,0:T(8,128)(2,1)S(1)}, bf16[64,1536]{1,0:T(8,128)(2,1)S(1)}, u32[]{:S(2)}, u32[]{:S(2)}) collective-permute-start(bf16[64,1536]{1,0:T(8,128)(2,1)S(1)} %get-tuple-element.114), channel_id=1, source_target_pairs={{0,1},{1,2},{2,3},{4,5},{5,6},{6,7},{8,9},{9,10},{10,11},{12,13},{... | collective-permute-start | bytes 589832 | tf_op jit(solution)/shard_map/ppermute | solution.py:600
  171.5 2.9 copy-start.6
  176.3 5.8 copy-start.7
  400.3 97.6 %reduce-scatter.37.cloned.1.call-start = ((), (), s32[]{:S(2)}) async-start(), calls=%async_computation.18 | async-start | bytes 1327104 | tf_op jit(solution)/shard_map/reduce_scatter | solution.py:593
  460.9 88.5 %reduce-scatter.35.cloned.1.call-start = ((), (), s32[]{:S(2)}) async-start(), calls=%async_computation.17 | async-start | bytes 3981312 | tf_op jit(solution)/shard_map/reduce_scatter | solution.py:593
  461.6 139.2 %reduce-scatter.33.cloned.1.call-start = ((), (), s32[]{:S(2)}) async-start(), calls=%async_computation.16 | async-start | bytes 3981312 | tf_op jit(solution)/shard_map/reduce_scatter | solution.py:593
  462.2 196.0 %reduce-scatter.43.cloned.1.call-start = ((), (), s32[]{:S(2)}) async-start(), calls=%async_computation.21 | async-start | bytes 5308416 | tf_op jit(solution)/shard_map/reduce_scatter | solution.py:593
  462.9 252.9 %reduce-scatter.41.cloned.1.call-start = ((), (), s32[]{:S(2)}) async-start(), calls=%async_computation.20 | async-start | bytes 5308416 | tf_op jit(solution)/shard_map/reduce_scatter | solution.py:593
  463.5 309.5 %reduce-scatter.47.cloned.1.call-start = ((), (), s32[]{:S(2)}) async-start(), calls=%async_computation.23 | async-start | bytes 5308416 | tf_op jit(solution)/shard_map/reduce_scatter | solution.py:593
  464.1 366.5 %reduce-scatter.45.cloned.1.call-start = ((), (), s32[]{:S(2)}) async-start(), calls=%async_computation.22 | async-start | bytes 5308416 | tf_op jit(solution)/shard_map/reduce_scatter | solution.py:593
  464.7 412.9 %reduce-scatter.55.cloned.1.call-start = ((), (), s32[]{:S(2)}) async-start(), calls=%async_computation.35 | async-start | bytes 245760
  466.5 412.0 %reduce-scatter.53.cloned.1.call-start = ((), (), s32[]{:S(2)}) async-start(), calls=%async_computation.34 | async-start | bytes 245760
  499.6 396.7 %reduce-scatter.51.cloned.1.call-start = ((), (), s32[]{:S(2)}) async-start(), calls=%async_computation.33 | async-start | bytes 737280
  552.1 367.1 %reduce-scatter.49.cloned.1.call-start = ((), (), s32[]{:S(2)}) async-start(), calls=%async_computation.32 | async-start | bytes 737280
  603.6 338.4 %reduce-scatter.59.cloned.1.call-start = ((), (), s32[]{:S(2)}) async-start(), calls=%async_computation.37 | async-start | bytes 737280
  660.4 304.2 %reduce-scatter.57.cloned.1.call-start = ((), (), s32[]{:S(2)}) async-start(), calls=%async_computation.36 | async-start | bytes 737280
  718.0 269.3 %reduce-scatter.63.cloned.1.call-start = ((), (), s32[]{:S(2)}) async-start(), calls=%async_computation.39 | async-start | bytes 737280
  775.2 60.0 %copy-start = (f32[640,768]{1,0:T(8,128)S(1)}, f32[640,768]{1,0:T(8,128)}, u32[]{:S(2)}) copy-start(f32[640,768]{1,0:T(8,128)} %get-tuple-element.67) | copy-start | bytes 5898244
  775.2 234.6 %reduce-scatter.61.cloned.1.call-start = ((), (), s32[]{:S(2)}) async-start(), calls=%async_computation.38 | async-start | bytes 737280
  835.1 1.3 copy-start.8
  835.1 1.3 copy-start.9
  835.1 1.3 copy-start.10
  835.1 1.3 copy-start.11
Sparse Core Ops, SparseCore 0:
  25.5 25.8 all-gather.26
  53.8 33.9 all-gather.24
  90.2 38.9 all-gather.28
  131.5 38.9 all-gather.30
  172.2 24.1 all-gather.34
  198.2 33.9 all-gather.32
  234.6 38.9 all-gather.36
  275.4 38.9 all-gather.38
  400.4 36.7 reduce-scatter.38
  461.0 36.7 reduce-scatter.36
  501.3 48.0 reduce-scatter.34
  552.7 48.0 reduce-scatter.32
  604.3 53.8 reduce-scatter.42
  661.9 53.8 reduce-scatter.40
  719.1 53.8 reduce-scatter.46
  776.7 53.8 reduce-scatter.44
  833.3 19.3 reduce-scatter.54
  855.5 17.6 reduce-scatter.52
  876.0 20.1 reduce-scatter.50
  899.0 20.2 reduce-scatter.48
  921.5 20.4 reduce-scatter.58
  944.3 20.2 reduce-scatter.56
  966.8 20.4 reduce-scatter.62
  989.4 20.2 reduce-scatter.60

commit v2 on v1

v2 whole, which is shorter than its diff:
```python
import functools
import math

import jax
import jax.numpy as jnp
from jax import lax
from jax.experimental import pallas as pl
from jax.experimental.pallas import tpu as pltpu
from jax.sharding import PartitionSpec as P

MOST = 64
EPSILON = 1e-05
QUERY_ROWS = 128
KEY_ROWS = QUERY_ROWS + 2 * MOST
GROUP = 4
VMEM_BYTES = 60 * 2**20

BF16 = jnp.bfloat16
F32 = jnp.float32
CONTRACT_LAST = (((1,), (1,)), ((), ()))
CONTRACT_FIRST = (((0,), (0,)), ((), ()))
CONTRACT_MIDDLE = (((1,), (0,)), ((), ()))

TAIL_SCALE = 0.3275911 / math.sqrt(2.0)
TAIL_TERMS = (1.061405429, -1.453152027, 1.421413741, -0.284496736, 0.254829592)


def dot(left, right, dims=CONTRACT_MIDDLE):
    return lax.dot_general(left, right, dims, preferred_element_type=F32)


def gelu_and_slope(hidden):
    bell = jnp.exp(hidden * hidden * -0.5)
    below = 1.0 + jnp.abs(hidden) * TAIL_SCALE
    guess = pl.reciprocal(below, approx=True)
    inverse = guess * (2.0 - below * guess)
    tail = 0.5 * TAIL_TERMS[0]
    for term in TAIL_TERMS[1:]:
        tail = tail * inverse + 0.5 * term
    tail = tail * inverse * bell
    cumulative = jnp.where(hidden > 0.0, 1.0 - tail, tail)
    return hidden * cumulative, cumulative + hidden * (bell * (1.0 / math.sqrt(2.0 * math.pi)))


def normalised(values):
    centred = values - jnp.mean(values, axis=-1, keepdims=True)
    inverse = lax.rsqrt(jnp.mean(centred * centred, axis=-1, keepdims=True) + EPSILON)
    return centred * inverse, inverse


def norm_back(grad_out, gain, hat, inverse):
    scaled = grad_out * gain
    first_mean = jnp.mean(scaled, axis=-1, keepdims=True)
    second_mean = jnp.mean(scaled * hat, axis=-1, keepdims=True)
    return inverse * (scaled - first_mean - hat * second_mean)


def each_block(count, size, step):
    def run(index, carry):
        step(pl.ds(pl.multiple_of(index * size, size), size), index)
        return carry

    lax.fori_loop(0, count, run, 0)


def swap_halves(values, half):
    width = values.shape[-1]
    lane = lax.broadcasted_iota(jnp.int32, values.shape, len(values.shape) - 1)
    ahead = pltpu.roll(values, width - half, 1)
    behind = pltpu.roll(values, half, 1)
    return jnp.where(lane % (2 * half) < half, ahead, behind)


def two_parts(values):
    high = values.astype(BF16)
    return high, (values - high.astype(F32)).astype(BF16)


def phi_of(rows, table, ones):
    high, low = two_parts(rows)
    square_high, square_low = two_parts(rows * rows)
    logits = dot(high, table) + dot(low, table)
    squares = dot(square_high, ones) + dot(square_low, ones)
    return jnp.exp(logits - 0.5 * squares) * (1.0 / math.sqrt(table.shape[1] // GROUP))


def head_masks(width, dtype):
    lane = lax.broadcasted_iota(jnp.int32, (1, width), 1) // (width // GROUP)
    return [jnp.where(lane == head, 1.0, 0.0).astype(dtype) for head in range(GROUP)]


def spread_heads(values):
    return jnp.concatenate([values * mask for mask in head_masks(values.shape[1], BF16)], axis=0)


def gather_heads(values):
    masks = head_masks(values.shape[-1], F32)
    total = values[0] * masks[0]
    for head in range(1, GROUP):
        total = total + values[head] * masks[head]
    return total


def block_scores(phi_q, phi_k, ids_column, ids_row):
    scores = dot(phi_q, phi_k, CONTRACT_LAST)
    same = (ids_column == ids_row).astype(F32)
    scores = scores.reshape(GROUP, QUERY_ROWS, KEY_ROWS) * same[None]
    totals = jnp.sum(scores, axis=-1, keepdims=True)
    inverse = jnp.where(totals > 0.0, 1.0 / totals, 0.0)
    return scores * inverse, inverse, same


def key_start(index, rows):
    start = jnp.clip(index * QUERY_ROWS - MOST, 0, rows - KEY_ROWS)
    return pl.multiple_of(start, MOST)


def attention_forward(
    scale,
    piece_count,
    places,
    state,
    gain_1,
    gain_2,
    table,
    ones,
    cosine,
    sine,
    ids_column,
    ids_row,
    *others,
):
    pieces = others[:piece_count]
    (weights, normed_a, query, key, value, mixed, middle, normed_c, total, phi_q, phi_k, arrived) = (
        others[piece_count:]
    )
    group = pl.program_id(0)
    rows = state.shape[0]
    width = state.shape[1]
    wide = query.shape[1]
    half = cosine.shape[1] // GROUP // 2

    def copies():
        for index, piece in enumerate(pieces):
            place = pl.ds(pl.multiple_of(places[index], 16), piece.shape[0])
            yield pltpu.make_async_copy(piece, weights.at[place, :], arrived.at[index])

    def part_of(part):
        return weights[:, pl.ds(pl.multiple_of(part * width + group * wide, wide), wide)]

    @pl.when(group == 0)
    def _():
        for copy in copies():
            copy.start()

        def step(block, index):
            hat, _ = normalised(state[block, :])
            normed_a[block, :] = (hat * gain_1[...]).astype(BF16)
            total[block, :] = state[block, :]

        each_block(rows // 64, 64, step)
        for copy in copies():
            copy.wait()

    for part, (held, phi) in enumerate(((query, phi_q), (key, phi_k))):
        projected = dot(normed_a[...], part_of(part))
        turned = (projected * cosine[...] + swap_halves(projected, half) * sine[...]) * scale
        held[...] = turned
        phi[...] = phi_of(turned, table[0], ones[...]).astype(BF16)
    value[...] = dot(normed_a[...], part_of(2)).astype(BF16)

    def step(block, index):
        keys = pl.ds(key_start(index, rows), KEY_ROWS)
        weights, _, _ = block_scores(
            spread_heads(phi_q[block, :]), phi_k[keys, :], ids_column[block, :], ids_row[index]
        )
        weights = weights.reshape(GROUP * QUERY_ROWS, KEY_ROWS).astype(BF16)
        found = dot(weights, value[keys, :])
        mixed[block, :] = gather_heads(found.reshape(GROUP, QUERY_ROWS, -1)).astype(BF16)

    each_block(rows // QUERY_ROWS, QUERY_ROWS, step)
    total[...] += dot(mixed[...], part_of(3), CONTRACT_LAST)

    @pl.when(group == pl.num_programs(0) - 1)
    def _():
        def step(block, index):
            middle[block, :] = total[block, :]
            hat, _ = normalised(total[block, :])
            normed_c[block, :] = (hat * gain_2[...]).astype(BF16)

        each_block(rows // 64, 64, step)


def attention_backward(
    scale,
    places,
    grad_middle,
    state,
    gain_1,
    weight_q,
    weight_k,
    weight_v,
    out_weight,
    table,
    ones,
    cosine,
    sine,
    ids_column,
    ids_row,
    normed_a,
    query,
    key,
    value,
    mixed,
    grad_state,
    grad_gain,
    grad_far,
    grad_near,
    grad_weight,
    leaving,
    total,
    branch,
    grad_mixed,
    phi_q,
    phi_k,
    grad_phi_q,
    grad_phi_k,
    grad_value,
):
    group = pl.program_id(0)
    rows = state.shape[0]
    half = cosine.shape[1] // GROUP // 2
    own = pl.ds(MOST, rows - 2 * MOST)
    width = state.shape[1]
    wide = query.shape[1]

    def part_of(part):
        return pl.ds(pl.multiple_of(part * width + group * wide, wide), wide)

    @pl.when(group == 0)
    def _():
        branch[...] = grad_middle[...].astype(BF16)
        total[...] = jnp.zeros_like(total)

    grad_mixed[...] = dot(branch[...], out_weight[...]).astype(BF16)
    grad_weight[:, part_of(3)] = dot(branch[own, :], mixed[own, :], CONTRACT_FIRST).astype(BF16)
    phi_q[...] = phi_of(query[...], table[0], ones[...])
    phi_k[...] = phi_of(key[...], table[0], ones[...])
    grad_phi_k[...] = jnp.zeros_like(grad_phi_k)
    grad_value[...] = jnp.zeros_like(grad_value)

    def step(block, index):
        keys = pl.ds(key_start(index, rows), KEY_ROWS)
        spread_q = spread_heads(phi_q[block, :].astype(BF16))
        spread_grad = spread_heads(grad_mixed[block, :])
        keys_phi = phi_k[keys, :].astype(BF16)
        weights, inverse, same = block_scores(
            spread_q, keys_phi, ids_column[block, :], ids_row[index]
        )
        flat = (GROUP * QUERY_ROWS, KEY_ROWS)
        grad_weights = dot(spread_grad, value[keys, :], CONTRACT_LAST)
        grad_value[keys, :] += dot(
            weights.reshape(flat).astype(BF16), spread_grad, CONTRACT_FIRST
        )
        grad_weights = grad_weights.reshape(weights.shape)
        inner = jnp.sum(grad_weights * weights, axis=-1, keepdims=True)
        grad_scores = ((grad_weights - inner) * inverse * same[None]).astype(BF16).reshape(flat)
        found = dot(grad_scores, keys_phi)
        grad_phi_q[block, :] = gather_heads(found.reshape(GROUP, QUERY_ROWS, -1))
        grad_phi_k[keys, :] += dot(grad_scores, spread_q, CONTRACT_FIRST)

    each_block(rows // QUERY_ROWS, QUERY_ROWS, step)

    def through_map(grad_phi, phi, held):
        high, low = two_parts(grad_phi[...] * phi[...])
        along = dot(high, table[0], CONTRACT_LAST) + dot(low, table[0], CONTRACT_LAST)
        summed = dot(high, ones[...], CONTRACT_LAST) + dot(low, ones[...], CONTRACT_LAST)
        grad_rows = (along - held[...] * summed) * scale
        turned = grad_rows * cosine[...] + swap_halves(grad_rows * sine[...], half)
        return turned.astype(BF16)

    for part in range(3):
        if part == 0:
            gradient = through_map(grad_phi_q, phi_q, query)
        elif part == 1:
            gradient = through_map(grad_phi_k, phi_k, key)
        else:
            gradient = grad_value[...].astype(BF16)
        grad_mixed[...] = gradient
        found = dot(normed_a[own, :], grad_mixed[own, :], CONTRACT_FIRST)
        grad_weight[:, part_of(part)] = found.astype(BF16)
        weight = (weight_q, weight_k, weight_v)[part]
        total[...] += dot(grad_mixed[...], weight[...], CONTRACT_LAST)

    def copies():
        count = leaving.shape[0]
        size = width // count
        for index in range(count):
            place = pl.ds(pl.multiple_of(places[index], 16), size)
            target = grad_far if index < count // 2 else grad_near
            to = pl.ds(index % (count // 2) * size, size)
            yield pltpu.make_async_copy(grad_weight.at[place, :], target.at[to, :], leaving.at[index])

    @pl.when(group == pl.num_programs(0) - 1)
    def _():
        for copy in copies():
            copy.start()
        grad_gain[...] = jnp.zeros_like(grad_gain)

        def step(block, index):
            hat, inverse = normalised(state[block, :])
            back = norm_back(total[block, :], gain_1[...], hat, inverse)
            grad_state[block, :] = grad_middle[block, :] + back

            @pl.when((index > 0) & (index < rows // 64 - 1))
            def _():
                grad_gain[...] += jnp.sum(total[block, :] * hat, axis=0, keepdims=True)

        each_block(rows // 64, 64, step)
        for copy in copies():
            copy.wait()


def arriving(pieces, held, arrived, step, chunk):
    begin = 0
    begins = []
    for piece in pieces:
        begins.append(begin)
        begin += piece.shape[0]

    def copy(index):
        place = pl.ds(begins[index], pieces[index].shape[0])
        return pltpu.make_async_copy(pieces[index], held.at[place, :], arrived.at[index])

    @pl.when(step == 0)
    def _():
        for index in range(len(pieces)):
            copy(index).start()

    for at in range(held.shape[0] // chunk):
        fresh = [
            index
            for index in range(len(pieces))
            if at * chunk <= begins[index] < (at + 1) * chunk
        ]
        if fresh:

            @pl.when(step == at)
            def _(fresh=fresh):
                for index in fresh:
                    copy(index).wait()


def feed_forward(chunk, piece_count, carried, normed_c, *others):
    pieces = others[:piece_count]
    activated, slope, state, held, total, hidden, arrived = others[piece_count:]
    step_at = pl.program_id(0)
    rows, width = carried.shape
    arriving(pieces, held, arrived, step_at, chunk)
    place = pl.ds(pl.multiple_of(step_at * chunk, chunk), chunk)

    @pl.when(step_at == 0)
    def _():
        total[...] = carried[...]

    hidden[...] = dot(normed_c[...], held[place, :width], CONTRACT_LAST)

    def step(block, index):
        value, back = gelu_and_slope(hidden[block, :])
        activated[block, :] = value.astype(BF16)
        slope[block, :] = back.astype(BF16)

    each_block(rows // 32, 32, step)
    total[...] += dot(activated[...], held[place, width:])

    @pl.when(step_at == pl.num_programs(0) - 1)
    def _():
        state[...] = total[...]


def feed_back(
    first,
    last,
    chunk,
    side_steps,
    piece_count,
    gradient,
    middle,
    gain_2,
    normed_c,
    side_activated,
    side_slope,
    corner_activated,
    corner_slope,
    *others,
):
    if not first:
        carried, *others = others
    pieces = others[:piece_count]
    grad_weight, grad_middle, *others = others[piece_count:]
    if last:
        grad_gain, *others = others
    held, total, branch, grad_hidden, grad_act, arrived = others
    step_at = pl.program_id(0)
    rows, width = middle.shape
    own = pl.ds(MOST, rows - 2 * MOST)
    arriving(pieces, held, arrived, step_at, chunk)
    place = pl.ds(pl.multiple_of(step_at * chunk, chunk), chunk)

    @pl.when(step_at == 0)
    def _():
        branch[...] = gradient[...].astype(BF16)
        total[...] = jnp.zeros_like(total) if first else carried[...]

    def work(activated, slope):
        grad_act[...] = dot(branch[...], held[place, width:], CONTRACT_LAST)

        def step(block, index):
            grad_hidden[block, :] = (grad_act[block, :] * slope[block, :].astype(F32)).astype(BF16)

        each_block(rows // 32, 32, step)
        grad_up = dot(grad_hidden[own, :], normed_c[own, :], CONTRACT_FIRST)
        grad_down = dot(activated[own, :], branch[own, :], CONTRACT_FIRST)
        grad_weight[:, :width] = grad_up.astype(BF16)
        grad_weight[:, width:] = grad_down.astype(BF16)
        total[...] += dot(grad_hidden[...], held[place, :width])

    @pl.when(step_at < side_steps)
    def _():
        work(side_activated, side_slope)

    @pl.when(step_at >= side_steps)
    def _():
        work(corner_activated, corner_slope)

    @pl.when(step_at == pl.num_programs(0) - 1)
    def _():
        if not last:
            grad_middle[...] = total[...]
            return
        grad_gain[...] = jnp.zeros_like(grad_gain)

        def step(block, index):
            hat, inverse = normalised(middle[block, :])
            back = norm_back(total[block, :], gain_2[...], hat, inverse)
            grad_middle[block, :] = gradient[block, :] + back

            @pl.when((index > 0) & (index < rows // 64 - 1))
            def _():
                grad_gain[...] += jnp.sum(total[block, :] * hat, axis=0, keepdims=True)

        each_block(rows // 64, 64, step)


def joining(parts, rows, source, joined):
    count, _, width = source.shape
    for part in range(parts):
        side = [source[at, part * rows : (part + 1) * rows, :] for at in range(count)]
        joined[:, part * count * width : (part + 1) * count * width] = jnp.concatenate(side, axis=1)


def tabulating(begin, source, tables):
    layers, groups, wide, small = tables.shape
    deep, feats = wide // GROUP, small // GROUP
    own_heads = groups * GROUP // source.shape[0]
    tables[...] = jnp.zeros_like(tables)
    for layer in range(layers):
        for index in range(groups * GROUP):
            group, place = index // GROUP, index % GROUP
            column = (layer * own_heads + index % own_heads) * feats
            tables[
                layer,
                group,
                place * deep : (place + 1) * deep,
                place * feats : (place + 1) * feats,
            ] = source[index // own_heads, begin : begin + deep, column : column + feats]


def parting(parts, *others):
    *sources, target = others
    count, rows, width = target.shape
    rows = rows // parts
    for part in range(parts):
        for at in range(count):
            begin = (part * count + at) * width
            total = sources[0][:, begin : begin + width].astype(F32)
            for source in sources[1:]:
                total = total + source[:, begin : begin + width].astype(F32)
            target[at, part * rows : (part + 1) * rows, :] = total.astype(target.dtype)


def adding_corner(near, far, to_x, to_y):
    half = to_x.shape[0]
    for target, place in ((to_x, slice(0, half)), (to_y, slice(half, 2 * half))):
        target[...] = (near[place, :].astype(F32) + far[place, :].astype(F32)).astype(BF16)


def adding_sides(near_x, far_x, near_y, far_y, from_x, from_y, to_x, to_y):
    half = from_x.shape[0]
    top, bottom = slice(0, half), slice(half, 2 * half)
    for near, far, place, more, target in (
        (near_x, far_x, top, None, to_x),
        (near_x, far_x, bottom, from_y, to_x),
        (near_y, far_y, top, from_x, to_y),
        (near_y, far_y, bottom, None, to_y),
    ):
        total = near[place, :].astype(F32) + far[place, :].astype(F32)
        if more is not None:
            total = total + more[...].astype(F32)
        target[place, :] = total.astype(BF16)


def whole(shape):
    return pl.BlockSpec(shape, lambda step, *_: (0,) * len(shape))


def columns(rows, width):
    return pl.BlockSpec((rows, width), lambda step, *_: (0, step))


def leading(shape):
    return pl.BlockSpec(shape, lambda step, *_: (step,) + (0,) * (len(shape) - 1))


def struct(shape, dtype):
    return jax.ShapeDtypeStruct(shape, dtype)


ANYWHERE = pl.BlockSpec(memory_space=pl.ANY)


def kernel_call(kernel, steps, in_specs, out_specs, out_shape, scratch, flops, prefetch=0):
    return pl.pallas_call(
        kernel,
        grid_spec=pltpu.PrefetchScalarGridSpec(
            num_scalar_prefetch=prefetch,
            grid=(steps,),
            in_specs=in_specs,
            out_specs=out_specs,
            scratch_shapes=scratch,
        ),
        out_shape=out_shape,
        compiler_params=pltpu.CompilerParams(vmem_limit_bytes=VMEM_BYTES),
        cost_estimate=pl.CostEstimate(flops=flops, bytes_accessed=flops // 600, transcendentals=0),
    )


def run_attention_forward(state, gains, pieces, places, table, ones, *, tables, ids, scale):
    rows, width = state.shape
    wide = table.shape[1]
    small = table.shape[2]
    blocks = rows // QUERY_ROWS
    return kernel_call(
        functools.partial(attention_forward, scale, len(pieces)),
        width // wide,
        [
            whole((rows, width)),
            whole((1, width)),
            whole((1, width)),
            leading((1, wide, small)),
            whole((wide, small)),
            whole((rows, wide)),
            whole((rows, wide)),
            whole((rows, 1)),
            whole((blocks, 1, KEY_ROWS)),
            *[ANYWHERE for _ in pieces],
        ],
        [
            whole((width, 4 * width)),
            whole((rows, width)),
            columns(rows, wide),
            columns(rows, wide),
            columns(rows, wide),
            columns(rows, wide),
            whole((rows, width)),
            whole((rows, width)),
        ],
        [
            struct((width, 4 * width), BF16),
            struct((rows, width), BF16),
            struct((rows, width), F32),
            struct((rows, width), F32),
            struct((rows, width), BF16),
            struct((rows, width), BF16),
            struct((rows, width), F32),
            struct((rows, width), BF16),
        ],
        [
            pltpu.VMEM((rows, width), F32),
            pltpu.VMEM((rows, small), BF16),
            pltpu.VMEM((rows, small), BF16),
            pltpu.SemaphoreType.DMA((len(pieces),)),
        ],
        FORWARD_COST,
        1,
    )(places, state, gains[0][None], gains[1][None], table, ones, *tables, *ids, *pieces)


def run_attention_backward(
    grad_middle, *, state, gain, weights, places, table, ones, tables, ids, kept, scale
):
    rows, width = state.shape
    wide = table.shape[1]
    small = table.shape[2]
    blocks = rows // QUERY_ROWS
    per_part = width // wide

    def weight_part(part):
        return pl.BlockSpec((width, wide), lambda step, _: (0, part * per_part + step))

    return kernel_call(
        functools.partial(attention_backward, scale),
        per_part,
        [
            whole((rows, width)),
            whole((rows, width)),
            whole((1, width)),
            *[weight_part(part) for part in range(4)],
            leading((1, wide, small)),
            whole((wide, small)),
            whole((rows, wide)),
            whole((rows, wide)),
            whole((rows, 1)),
            whole((blocks, 1, KEY_ROWS)),
            whole((rows, width)),
            columns(rows, wide),
            columns(rows, wide),
            columns(rows, wide),
            columns(rows, wide),
        ],
        [whole((rows, width)), whole((1, width)), ANYWHERE, ANYWHERE],
        [
            struct((rows, width), F32),
            struct((1, width), F32),
            struct((width // 2, 4 * width), BF16),
            struct((width // 2, 4 * width), BF16),
        ],
        [
            pltpu.VMEM((width, 4 * width), BF16),
            pltpu.SemaphoreType.DMA(places.shape),
            pltpu.VMEM((rows, width), F32),
            pltpu.VMEM((rows, width), BF16),
            pltpu.VMEM((rows, wide), BF16),
            pltpu.VMEM((rows, small), F32),
            pltpu.VMEM((rows, small), F32),
            pltpu.VMEM((rows, small), F32),
            pltpu.VMEM((rows, small), F32),
            pltpu.VMEM((rows, wide), F32),
        ],
        BACKWARD_COST,
        1,
    )(places, grad_middle, state, gain[None], *[weights] * 4, table, ones, *tables, *ids, *kept)


def run_feed_forward(carried, normed_c, pieces):
    rows, width = carried.shape
    count = sum(piece.shape[0] for piece in pieces)
    return kernel_call(
        functools.partial(feed_forward, CHUNK, len(pieces)),
        count // CHUNK,
        [whole((rows, width)), whole((rows, width)), *[ANYWHERE for _ in pieces]],
        [columns(rows, CHUNK), columns(rows, CHUNK), whole((rows, width))],
        [
            struct((rows, count), BF16),
            struct((rows, count), BF16),
            struct((rows, width), F32),
        ],
        [
            pltpu.VMEM((count, 2 * width), BF16),
            pltpu.VMEM((rows, width), F32),
            pltpu.VMEM((rows, CHUNK), F32),
            pltpu.SemaphoreType.DMA((len(pieces),)),
        ],
        FORWARD_COST // 3,
    )(carried, normed_c, *pieces)


def run_feed_back(gradient, middle, gain, normed_c, kept, pieces, side, carried):
    rows, width = middle.shape
    count = sum(piece.shape[0] for piece in pieces)
    chunk = CHUNK
    steps = count // chunk
    first, last = carried is None, carried is not None
    sides, corners = kept
    side_steps = sides[side][0].shape[1] // chunk
    corner_begin = side * (steps - side_steps)
    side_columns = pl.BlockSpec((rows, chunk), lambda step: (0, jnp.minimum(step, side_steps - 1)))
    corner_columns = pl.BlockSpec(
        (rows, chunk), lambda step: (0, corner_begin + jnp.maximum(step - side_steps, 0))
    )
    return kernel_call(
        functools.partial(feed_back, first, last, chunk, side_steps, len(pieces)),
        steps,
        [
            whole((rows, width)),
            whole((rows, width)),
            whole((1, width)),
            whole((rows, width)),
            side_columns,
            side_columns,
            corner_columns,
            corner_columns,
            *([] if first else [whole((rows, width))]),
            *[ANYWHERE for _ in pieces],
        ],
        [
            leading((chunk, 2 * width)),
            whole((rows, width)),
            *([whole((1, width))] if last else []),
        ],
        [
            struct((count, 2 * width), BF16),
            struct((rows, width), F32),
            *([struct((1, width), F32)] if last else []),
        ],
        [
            pltpu.VMEM((count, 2 * width), BF16),
            pltpu.VMEM((rows, width), F32),
            pltpu.VMEM((rows, width), BF16),
            pltpu.VMEM((rows, chunk), BF16),
            pltpu.VMEM((rows, chunk), F32),
            pltpu.SemaphoreType.DMA((len(pieces),)),
        ],
        FORWARD_COST // 2,
    )(
        gradient,
        middle,
        gain[None],
        normed_c,
        *sides[side],
        *corners,
        *([] if first else [carried]),
        *pieces,
    )


HEAD_DEVICES = 4
CHUNK = 384
X, Y, CORE = 2, 4, 1
FORWARD_COST = 29_000_000_000
BACKWARD_COST = 40_000_000_000


def hop(values, bit):
    count = lax.axis_size("dp")
    return lax.ppermute(values, "dp", [(i, i ^ bit) for i in range(count)])


def exchange(values):
    return lax.all_to_all(values, "head", split_axis=0, concat_axis=0, tiled=True)


def together(*values):
    return lax.optimization_barrier(values)


def by_permutes():
    return lax.axis_size("dp") == 8 and lax.axis_size("head") == HEAD_DEVICES


def join_columns(source, parts, rows):
    count, _, width = source.shape
    return kernel_call(
        functools.partial(joining, parts, rows),
        1,
        [whole(source.shape)],
        whole((rows, parts * count * width)),
        struct((rows, parts * count * width), BF16),
        [],
        1_000_000,
    )(source)


def feature_tables(source, begin, shape):
    return kernel_call(
        functools.partial(tabulating, begin),
        1,
        [whole(source.shape)],
        whole(shape),
        struct(shape, BF16),
        [],
        1_000_000,
    )(source)


def block_of(rows, columns_all, index):
    return pl.BlockSpec((rows, columns_all), lambda *_: (index, 0))


def part_columns(near, far, from_x, from_y, parts):
    rows, columns_all = from_x.shape
    shape = (HEAD_DEVICES, parts * rows, columns_all // parts // HEAD_DEVICES)
    return kernel_call(
        functools.partial(parting, parts),
        1,
        [block_of(rows, columns_all, 0) for _ in range(4)],
        whole(shape),
        struct(shape, BF16),
        [],
        1_000_000,
    )(near, far, from_x, from_y)


def next_chips(own):
    return hop(own, X), hop(own, Y), hop(own, CORE)


def halves_to_pass(over_x, over_y):
    half = over_x.shape[0] // 2
    return over_x[:half], over_y[half:]


def chip_across(passed):
    to_y, to_x = passed
    return hop(to_y, Y), hop(to_x, X)


def other_core(pieces):
    return tuple(hop(piece, CORE) for piece in pieces)


def piece_places(rows):
    own = lax.axis_index("dp")
    bits = [(0, 0), (X, 0), (Y, 0), (X | Y, 0), (X | Y, rows // 2)]
    return jnp.stack(
        [(own ^ (bit | core)) * rows + begin for core in (0, CORE) for bit, begin in bits]
    ).astype(jnp.int32)


def block_places(rows):
    own = lax.axis_index("dp")
    return jnp.stack(
        [(own ^ (bit | core)) * rows for core in (CORE, 0) for bit in (0, X, Y, X | Y)]
    ).astype(jnp.int32)


class Reduction:
    def __init__(self, far, near, parts):
        self.near, self.parts = near, parts
        self.rows, self.width = near.shape[0] // 4, near.shape[1]
        self.came = hop(far, CORE)

    def corner(self):
        self.far = self.came
        shape = (self.rows // 2, self.width)
        self.sent = kernel_call(
            adding_corner,
            1,
            [block_of(self.rows, self.width, 3)] * 2,
            [whole(shape)] * 2,
            [struct(shape, BF16)] * 2,
            [],
            1_000_000,
        )(self.near, self.far)

    def sides(self):
        half, shape = (self.rows // 2, self.width), (self.rows, self.width)
        self.sent = kernel_call(
            adding_sides,
            1,
            [block_of(self.rows, self.width, index) for index in (1, 1, 2, 2)] + [whole(half)] * 2,
            [whole(shape)] * 2,
            [struct(shape, BF16)] * 2,
            [],
            1_000_000,
        )(self.near, self.far, self.near, self.far, *self.came)

    def heads(self):
        self.sent = part_columns(self.near, self.far, *self.came, self.parts)

    def send(self):
        to_x, to_y = self.sent
        self.came = hop(to_x, X), hop(to_y, Y)

    def send_heads(self):
        self.came = exchange(self.sent)

    def result(self):
        total = jnp.sum(self.came.astype(F32), axis=0)
        return total.reshape(self.parts, -1, total.shape[1])


def summed_share(far, near, parts):
    joined = jnp.concatenate([near, far])
    joined = joined.reshape(joined.shape[0], parts, -1)
    part = lax.psum_scatter(joined, "dp", scatter_dimension=0, tiled=True)
    part = lax.psum_scatter(part, "head", scatter_dimension=2, tiled=True)
    return part.swapaxes(0, 1).astype(F32)


def sum_over_all(values):
    if not by_permutes():
        return lax.psum(values, ("dp", "head"))
    for bit in (CORE, X, Y):
        values = values + hop(values, bit)
    for bit in (1, 2):
        values = values + lax.ppermute(values, "head", [(i, i ^ bit) for i in range(HEAD_DEVICES)])
    return values


def with_halo(inputs, cotangent):
    count = lax.axis_size("head")
    both = jnp.concatenate([inputs, cotangent], axis=1)
    before = lax.ppermute(both[-MOST:], "head", [(i, i + 1) for i in range(count - 1)])
    after = lax.ppermute(both[:MOST], "head", [(i + 1, i) for i in range(count - 1)])
    joined = jnp.concatenate([before, both, after], axis=0).astype(F32)
    return joined[:, : inputs.shape[1]], joined[:, inputs.shape[1] :]


def window_ids(segment_ids, own_rows):
    padded = jnp.pad(segment_ids[0], (MOST, MOST), constant_values=-1)
    begin = lax.axis_index("head") * own_rows
    ids = lax.dynamic_slice(padded, (begin,), (own_rows + 2 * MOST,))
    place = jnp.arange(ids.shape[0])
    earlier = (ids[:, None] == ids[None, :]) & (place[None, :] < place[:, None])
    position = jnp.sum(earlier.astype(F32), axis=1)
    used = (ids >= ids[MOST]) & (ids <= ids[MOST + own_rows - 1])
    column = jnp.where(used, ids, -1)[:, None]
    row = jnp.where(used, ids, -2)
    starts = [
        min(max(b * QUERY_ROWS - MOST, 0), ids.shape[0] - KEY_ROWS)
        for b in range(ids.shape[0] // QUERY_ROWS)
    ]
    rows = jnp.stack([row[start : start + KEY_ROWS] for start in starts])[:, None, :]
    return position, (column, rows)


def rotary_tables(position, head_width):
    halves = head_width // 2
    frequency = jnp.exp(jnp.arange(halves, dtype=F32) * (-2.0 * math.log(10000.0) / head_width))
    angles = position[:, None] * frequency[None, :]
    cosine, sine = jnp.cos(angles), jnp.sin(angles)
    return (
        jnp.tile(jnp.concatenate([cosine, cosine], axis=1), (1, GROUP)),
        jnp.tile(jnp.concatenate([-sine, sine], axis=1), (1, GROUP)),
    )


def body(
    inputs,
    segment_ids,
    features,
    norm_gain,
    query_key_value,
    output_weight,
    up_weight,
    down_weight,
    cotangent,
):
    layer_count = norm_gain.shape[0]
    own_rows = inputs.shape[0]
    head_width = features.shape[3]
    feature_count = features.shape[2]
    scale = head_width ** (-0.25)
    own_place = slice(MOST, MOST + own_rows)

    state, gradient = with_halo(inputs, cotangent)
    position, ids = window_ids(segment_ids, own_rows)
    tables = rotary_tables(position, head_width)
    in_rows, part_width = output_weight.shape[1:]
    groups = state.shape[1] // (GROUP * head_width)
    table_shape = (layer_count, groups, GROUP * head_width, GROUP * feature_count)
    chunks = []
    for layer in range(layer_count):
        chunks.append((4, query_key_value[layer].reshape(-1, part_width), output_weight[layer]))
        chunks.append((2, up_weight[layer], down_weight[layer]))
    attend = functools.partial(
        run_attention_forward, tables=tables, ids=ids, scale=scale
    )
    ones = jnp.kron(
        jnp.eye(GROUP, dtype=BF16), jnp.ones((head_width, feature_count), BF16)
    )
    stored = []
    if by_permutes():
        attention_places = piece_places(in_rows)
        grad_places = block_places(in_rows)
        feature_rows = jnp.moveaxis(features, 3, 0).reshape(head_width, -1)

        def to_send(index):
            _, *weights = chunks[index]
            sent = jnp.concatenate(weights + [feature_rows] if index == 0 else weights)
            return jnp.broadcast_to(sent[None], (HEAD_DEVICES,) + sent.shape)

        def join(index, came):
            parts, *weights = chunks[index]
            return join_columns(came, parts, weights[-1].shape[0])

        came = exchange(to_send(0))
        own = join(0, came)
        blocks = feature_tables(came, 4 * in_rows, table_shape)
        own, sent = together(own, to_send(1))
        came = exchange(sent)
        over_x, over_y, over_core = next_chips(own)
        passed = halves_to_pass(over_x, over_y)
        across = chip_across(passed)
        own_feed = join(1, came)
        for layer in range(layer_count):
            more = layer + 1 < layer_count
            near = (own, over_x, over_y) + tuple(across)
            far = (over_core,) + other_core(near[1:])
            attention_pieces = near + far
            own = own_feed
            state, own = together(state, own)
            over_x, over_y, over_core = next_chips(own)
            weights, *kept, middle, normed_c = attend(
                state,
                norm_gain[layer],
                attention_pieces,
                attention_places,
                blocks[layer],
                ones,
            )

            middle, over_x, over_y, over_core = together(middle, over_x, over_y, over_core)
            sides = own, over_x, over_y
            passed = halves_to_pass(over_x, over_y)
            carried, passed, sent = together(middle, passed, to_send(2 * layer + 2) if more else ())
            across = chip_across(passed)
            far_sides = (over_core,) + other_core(sides[1:])
            came = exchange(sent) if more else ()
            near_kept = run_feed_forward(carried, normed_c, sides)

            carried, across, far_sides, came = together(near_kept[2], across, far_sides, came)
            far_across = other_core(across)
            if more:
                own = join(2 * layer + 2, came)
                carried, own, sent = together(carried, own, to_send(2 * layer + 3))
                over_x, over_y, over_core = next_chips(own)
                came = exchange(sent)
            near_pieces, last_pieces = sides + across, across + far_across
            far_pieces = far_sides + far_across
            far_kept = run_feed_forward(carried, normed_c, far_sides)

            carried = far_kept[2]
            if more:
                carried, over_x, over_y, over_core = together(carried, over_x, over_y, over_core)
                passed = halves_to_pass(over_x, over_y)
                carried, passed = together(carried, passed)
                across = chip_across(passed)
            last_kept = run_feed_forward(carried, normed_c, last_pieces)
            hidden_kept = (near_kept[:2], far_kept[:2]), last_kept[:2]
            stored.append(
                (state, weights, kept, middle, normed_c, hidden_kept, near_pieces, far_pieces)
            )
            state = last_kept[2]
            if more:
                state, across, came = together(state, across, came)
                own_feed = join(2 * layer + 3, came)
    else:
        all_features = lax.all_gather(features, "head", axis=1, tiled=True)
        shaped = all_features.reshape(layer_count, -1, GROUP, feature_count, head_width)
        blocks = jnp.einsum("lghmw,hk->lghwkm", shaped, jnp.eye(GROUP, dtype=BF16)).reshape(
            table_shape
        )
        owned = []
        for parts, *weights in chunks:
            rows = weights[-1].shape[0]
            joined = jnp.concatenate(weights).reshape(parts, rows, part_width)
            joined = lax.all_gather(joined, "head", axis=2, tiled=True)
            joined = lax.all_gather(joined, "dp", axis=1, tiled=True)
            owned.append(joined.swapaxes(0, 1).reshape(joined.shape[1], -1))
        middle_row = inputs.shape[1] // 2
        attention_places = jnp.array([0, middle_row], jnp.int32)
        grad_places = jnp.array([middle_row, 0], jnp.int32)
        for layer in range(layer_count):
            own_attention, own_feed = owned[2 * layer], owned[2 * layer + 1]
            weights, *kept, middle, normed_c = attend(
                state,
                norm_gain[layer],
                (own_attention[:middle_row], own_attention[middle_row:]),
                attention_places,
                blocks[layer],
                ones,
            )
            size = own_feed.shape[0] // 8
            near_pieces, far_pieces = (own_feed[: 4 * size],), (own_feed[4 * size :],)
            near_kept = run_feed_forward(middle, normed_c, (own_feed[: 3 * size],))
            far_kept = run_feed_forward(near_kept[2], normed_c, (own_feed[4 * size : 7 * size],))
            last = (own_feed[3 * size : 4 * size], own_feed[7 * size :])
            last_kept = run_feed_forward(far_kept[2], normed_c, last)
            hidden_kept = (near_kept[:2], far_kept[:2]), last_kept[:2]
            stored.append(
                (state, weights, kept, middle, normed_c, hidden_kept, near_pieces, far_pieces)
            )
            state = last_kept[2]
    outputs = state[own_place].astype(BF16)

    gains = [None] * layer_count
    sums = [None] * layer_count
    for layer in reversed(range(layer_count)):
        before, weights, kept, middle, normed_c, hidden_kept, near_pieces, far_pieces = stored[layer]
        feed = (middle, norm_gain[layer, 1], normed_c, hidden_kept)
        attention_back = functools.partial(
            run_attention_backward,
            state=before,
            gain=norm_gain[layer, 0],
            weights=weights,
            places=grad_places,
            table=blocks[layer],
            ones=ones,
            tables=tables,
            ids=ids,
            kept=kept,
            scale=scale,
        )
        if not by_permutes():
            feed_far, carried = run_feed_back(gradient, *feed, far_pieces, 1, None)
            feed_near, grad_middle, gain_c = run_feed_back(gradient, *feed, near_pieces, 0, carried)
            gradient, gain_a, far, near = attention_back(grad_middle)
            gains[layer] = jnp.concatenate([gain_a, gain_c])
            sums[layer] = summed_share(feed_far, feed_near, 2), summed_share(far, near, 4)
            continue
        later = sums[layer + 1] if layer + 1 < layer_count else None
        if later:
            later_feed, later_attention = later
            later_feed.sides()
            gradient, later_feed.sent = together(gradient, later_feed.sent)
            later_feed.send()
        feed_far, carried = run_feed_back(gradient, *feed, far_pieces, 1, None)

        feed_came = None
        if later:
            carried, feed_far, later_attention.came = together(carried, feed_far, later_attention.came)
            later_attention.corner()
            carried, later_attention.sent = together(carried, later_attention.sent)
            later_attention.send()
        far_hop = hop(feed_far, CORE)
        feed_near, grad_middle, gain_c = run_feed_back(gradient, *feed, near_pieces, 0, carried)

        feed_sum = Reduction(feed_far, feed_near, 2)
        grad_middle, feed_near, feed_sum.came = together(grad_middle, feed_near, far_hop)
        feed_sum.near = feed_near
        feed_sum.corner()
        grad_middle, feed_sum.sent = together(grad_middle, feed_sum.sent)
        if later:
            grad_middle, later_attention.came, later_feed.came = together(
                grad_middle, later_attention.came, later_feed.came
            )
            later_attention.sides()
            later_feed.heads()
            grad_middle, later_attention.sent, later_feed.sent = together(
                grad_middle, later_attention.sent, later_feed.sent
            )
            later_attention.send()
            later_feed.send_heads()
        feed_sum.send()
        gradient, gain_a, far, near = attention_back(grad_middle)

        gains[layer] = jnp.concatenate([gain_a, gain_c])
        gradient, far, near, gains[layer], feed_sum.came = together(
            gradient, far, near, gains[layer], feed_sum.came
        )
        if later:
            gradient, far, near, later_attention.came, later_feed.came = together(
                gradient, far, near, later_attention.came, later_feed.came
            )
            later_attention.heads()
        sums[layer] = feed_sum, Reduction(far, near, 4)
    if by_permutes():
        feed_sum, attention_sum = sums[0]
        feed_sum.sides()
        feed_sum.send()
        gain_all, attention_sum.came, feed_sent = together(
            jnp.stack(gains), attention_sum.came, feed_sum.sent
        )
        attention_sum.corner()
        attention_sum.send()
        for layer in range(1, layer_count):
            later_attention = sums[layer][1]
            later_attention.sent, attention_sent = together(
                later_attention.sent, attention_sum.sent
            )
            later_attention.send_heads()
        gain_all, attention_sum.came = together(gain_all, attention_sum.came)
        attention_sum.sides()
        attention_sum.send()
        feed_sum.came, attention_sent = together(feed_sum.came, attention_sum.sent)
        feed_sum.heads()
        feed_sum.send_heads()
        gain_all, attention_sum.came, feed_sent = together(
            gain_all, attention_sum.came, feed_sum.sent
        )
        attention_sum.heads()
        attention_sum.send_heads()
        gain_total = sum_over_all(gain_all)
        sums = [(feed_sum.result(), attention_sum.result()) for feed_sum, attention_sum in sums]
    else:
        gain_total = sum_over_all(jnp.stack(gains))
    results = [
        (attention_share[:3], attention_share[3], feed_share[0], feed_share[1])
        for feed_share, attention_share in sums
    ]
    return (
        outputs,
        gradient[own_place],
        gain_total[:, 0],
        gain_total[:, 1],
        *(jnp.stack(list(kind)) for kind in zip(*results)),
    )


def solution(mesh):
    in_specs = (
        P(("dp", "head"), None),
        P("dp", None),
        P(None, "head", None, None),
        P(),
        P(None, None, "dp", "head"),
        P(None, "dp", "head"),
        P(None, "dp", "head"),
        P(None, "dp", "head"),
        P(("dp", "head"), None),
    )
    out_specs = (
        P(("dp", "head"), None),
        P(("dp", "head"), None),
        P(),
        P(),
        P(None, None, "dp", "head"),
        P(None, "dp", "head"),
        P(None, "dp", "head"),
        P(None, "dp", "head"),
    )
    return jax.shard_map(body, mesh=mesh, in_specs=in_specs, out_specs=out_specs, check_vma=False)
```

time: 1030 us -> 581 us (0.56)
  waiting for transfers between devices: 527 us -> 81.6 us
  blocking collectives: 186 us -> 0 us
  Pallas kernels: 224 us -> 321 us
  starting transfers between devices: 6.82 us -> 90.7 us
  between operations: 15.3 us -> 2.05 us
    reduce_scatter x8 -> x0, waiting for transfers between devices: 350 us -> none  [scatter_grad(): part = lax.psum_scatter(gradient, 'dp', scatter_dimension=dim, tiled=True)]
    all_gather x9 -> x0, blocking collectives: 146 us -> none  [the longest x8 132 us: gather_weight(): wide = lax.all_gather(weight, 'head', axis=dim + 1, tiled=True)]
    unnamed x32 -> x0, waiting for transfers between devices: 126 us -> none
    pallas_call x8 -> x31, Pallas kernels: 224 us -> 321 us  [the longest x6 71.3 us: run_feed_forward(): kernel_call(functools.partial(feed_forward, CHUNK, len(pieces)), count //...]
    ppermute x0 -> x61, waiting for transfers between devices: none -> 52.3 us  [the longest x59 40.9 us: hop(): return lax.ppermute(values, 'dp', [(i, i ^ bit) for i in range(count)])]
    all_gather x8 -> x0, waiting for transfers between devices: 51.5 us -> none  [gather_weight(): return lax.all_gather(wide, 'dp', axis=dim, tiled=True)]
    ppermute x0 -> x61, starting transfers between devices: none -> 48.1 us  [the longest x59 41.3 us: hop(): return lax.ppermute(values, 'dp', [(i, i ^ bit) for i in range(count)])]
    psum x1 -> x0, blocking collectives: 39.9 us -> none  [body(): gain_total = lax.psum(jnp.stack(gains), ('dp', 'head'))]
  transfers between devices with their start and end apart: 26 -> 71, of which waited for: 15 -> 20; matrix products, arithmetic and copies ran while one was open for 6% -> 9% of each run, Pallas kernels for 14% -> 49%
where the time goes in v2:
time: 581 us; the launch traced here: 570 us
  Pallas kernels  321 us (55%)
  starting transfers between devices  90.7 us (16%)
  waiting for transfers between devices  81.6 us (14%)
  local copies, waits for them, and re-layouts  63 us (11%)
  other arithmetic  12 us (2%)
    pallas_call x6, Pallas kernels, run_feed_forward(): kernel_call(functools.partial(feed_forward, CHUNK, len(pieces)), count //...  71.3 us
    pallas_call x4, Pallas kernels, run_feed_back(): kernel_call(functools.partial(feed_back, first, last, chunk, side_steps,...  71.3 us
    pallas_call x2, Pallas kernels, run_attention_backward(): kernel_call(functools.partial(attention_backward, scale), per_part, [whol...  70.8 us
    pallas_call x2, Pallas kernels, run_attention_forward(): kernel_call(functools.partial(attention_forward, scale, len(pieces)), wid...  56.4 us
    ppermute x59, starting transfers between devices, hop(): return lax.ppermute(values, 'dp', [(i, i ^ bit) for i in range(count)])  41.3 us
    ppermute x59, waiting for transfers between devices, hop(): return lax.ppermute(values, 'dp', [(i, i ^ bit) for i in range(count)])  40.9 us
    all_to_all x8, starting transfers between devices, exchange(): lax.all_to_all(values, 'head', split_axis=0, concat_axis=0, tiled=True)  36.1 us
    all_to_all x8, waiting for transfers between devices, exchange(): lax.all_to_all(values, 'head', split_axis=0, concat_axis=0, tiled=True)  29.3 us
  transfers between devices with their start and end apart: 71, of which 20 were waited for; matrix products, arithmetic and copies ran while one was open for 9% of the time, Pallas kernels for 49%

profile of v2, /device:TPU:0, one launch (start us, length us, event | category | flops | bytes accessed | tf_op | source)
XLA Modules:
  0.0 570.5 jit_solution(5129653758173112368)
XLA Ops:
  5.9 6.3 %all-to-all-start = ((bf16[4,448,192]{1,2,0:T(8,128)(2,1)}), bf16[4,448,192]{1,2,0:T(8,128)(2,1)S(1)}, u32[]{:S(2)}, u32[]{:S(2)}) async-start(bf16[4,448,192]{1,2,0:T(8,128)(2,1)} %broadcast_in_dim.23), calls=%async_computation | async-start | bytes 1572864 | tf_op jit(solution)/shard_map/all_to_all | solution.py:750
  15.5 5.3 collective-permute-start
  22.3 11.1 %all-to-all-done = bf16[4,448,192]{1,2,0:T(8,128)(2,1)S(1)} async-done(((bf16[4,448,192]{1,2,0:T(8,128)(2,1)}), bf16[4,448,192]{1,2,0:T(8,128)(2,1)S(1)}, u32[]{:S(2)}, u32[]{:S(2)}) %all-to-all-start) | async-done | bytes 688160 | tf_op jit(solution)/shard_map/all_to_all | solution.py:750
  37.9 3.5 all-to-all-start.1
  74.5 2.7 shard_map.153.others_0_.others_1_
  79.7 28.2 %shard_map.155 = (bf16[768,3072]{1,0:T(8,128)(2,1)}, bf16[640,768]{1,0:T(8,128)(2,1)}, f32[640,768]{1,0:T(8,128)}, f32[640,768]{1,0:T(8,128)}, bf16[640,768]{1,0...) custom-call(s32[10]{0:T(128)} %stack.99.places, ...), custom_call_target="tpu_custom_call" | custom-call | flops 28999999488 | bytes 48333332 | tf_op jit(solution)/shard_map/pallas_call | solution.py:553
  113.2 4.8 all-to-all-start.2
  117.9 12.8 %shard_map.156 = (bf16[640,1152]{1,0:T(8,128)(2,1)}, bf16[640,1152]{1,0:T(8,128)(2,1)}, f32[640,768]{1,0:T(8,128)}) custom-call(f32[640,768]{1,0:T(8,128)} %get-tuple-element.191.carried.middle, bf16[640,768]{1,0:T(8,128)(2,1)} %get-tuple-element.192.normed_c, bf16[384,1536]{1,0:T(8,128)(2,1)} %shard_map.153.others_0_.others_1_, ...), custom_call_target="tpu_custom_call" | custom-call | flops 9666666496 | bytes 16111111 | tf_op jit(solution)/shard_map/pallas_call | solution.py:658
  130.7 3.1 all-to-all-done.2
  140.8 3.7 all-to-all-start.3
  144.6 12.8 %shard_map.158 = (bf16[640,1152]{1,0:T(8,128)(2,1)}, bf16[640,1152]{1,0:T(8,128)(2,1)}, f32[640,768]{1,0:T(8,128)}) custom-call(f32[640,768]{1,0:T(8,128)} %get-tuple-element.200.carried, bf16[640,768]{1,0:T(8,128)(2,1)} %get-tuple-element.192.normed_c, bf16[384,1536]{1,0:T(8,128)(2,1)} %copy-done.32, bf16[384,1536]{1,0:T(8,128)(2,1)} %collective-permute-done.16.others_1_, ...), custom_call_target="tpu_custom_call" | custom-call | flops 9666666496 | bytes 16111111 | tf_op jit(solution)/shard_map/pallas_call | solution.py:658
  162.2 10.1 %shard_map.159 = (bf16[640,768]{1,0:T(8,128)(2,1)}, bf16[640,768]{1,0:T(8,128)(2,1)}, f32[640,768]{1,0:T(8,128)}) custom-call(f32[640,768]{1,0:T(8,128)} %get-tuple-element.209.carried, bf16[640,768]{1,0:T(8,128)(2,1)} %get-tuple-element.192.normed_c, bf16[192,1536]{1,0:T(8,128)(2,1)} %collective-permute-done.14.others_0_.others_4_, ...), custom_call_target="tpu_custom_call" | custom-call | flops 9666666496 | bytes 16111111 | tf_op jit(solution)/shard_map/pallas_call | solution.py:658
  176.0 2.7 shard_map.160.others_0_.others_1_
  180.7 28.2 %shard_map.161 = (bf16[768,3072]{1,0:T(8,128)(2,1)}, bf16[640,768]{1,0:T(8,128)(2,1)}, f32[640,768]{1,0:T(8,128)}, f32[640,768]{1,0:T(8,128)}, bf16[640,768]{1,0...) custom-call(s32[10]{0:T(128)} %stack.99.places, ...), custom_call_target="tpu_custom_call" | custom-call | flops 28999999488 | bytes 48333332 | tf_op jit(solution)/shard_map/pallas_call | solution.py:553
  212.8 12.8 %shard_map.162 = (bf16[640,1152]{1,0:T(8,128)(2,1)}, bf16[640,1152]{1,0:T(8,128)(2,1)}, f32[640,768]{1,0:T(8,128)}) custom-call(f32[640,768]{1,0:T(8,128)} %get-tuple-element.227.carried.middle, bf16[640,768]{1,0:T(8,128)(2,1)} %get-tuple-element.228.normed_c, bf16[384,1536]{1,0:T(8,128)(2,1)} %shard_map.160.others_0_.others_1_, ...), custom_call_target="tpu_custom_call" | custom-call | flops 9666666496 | bytes 16111111 | tf_op jit(solution)/shard_map/pallas_call | solution.py:658
  227.4 12.8 %shard_map.163 = (bf16[640,1152]{1,0:T(8,128)(2,1)}, bf16[640,1152]{1,0:T(8,128)(2,1)}, f32[640,768]{1,0:T(8,128)}) custom-call(f32[640,768]{1,0:T(8,128)} %get-tuple-element.233.carried, bf16[640,768]{1,0:T(8,128)(2,1)} %get-tuple-element.228.normed_c, bf16[384,1536]{1,0:T(8,128)(2,1)} %copy-done.33, bf16[384,1536]{1,0:T(8,128)(2,1)} %collective-permute-done.34.others_1_, ...), custom_call_target="tpu_custom_call" | custom-call | flops 9666666496 | bytes 16111111 | tf_op jit(solution)/shard_map/pallas_call | solution.py:658
  241.2 10.1 %shard_map.164 = (bf16[640,768]{1,0:T(8,128)(2,1)}, bf16[640,768]{1,0:T(8,128)(2,1)}, f32[640,768]{1,0:T(8,128)}) custom-call(f32[640,768]{1,0:T(8,128)} %get-tuple-element.237.carried, bf16[640,768]{1,0:T(8,128)(2,1)} %get-tuple-element.228.normed_c, bf16[192,1536]{1,0:T(8,128)(2,1)} %copy-done.37, ...), custom_call_target="tpu_custom_call" | custom-call | flops 9666666496 | bytes 16111111 | tf_op jit(solution)/shard_map/pallas_call | solution.py:658
  251.3 16.3 %shard_map.165 = (bf16[1536,1536]{1,0:T(8,128)(2,1)}, f32[640,768]{1,0:T(8,128)}) custom-call(f32[640,768]{1,0:T(8,128)} %get-tuple-element.390.gradient, f32[640,768]{1,0:T(8,128)} %get-tuple-element.227.carried.middle, f32[1,768]{1,0:T(1,128)} %get-tuple-element.410.gain_2, bf16[640,768]{1,0:T(8,128)(2,1)} %get-tuple-element.228.normed_c, ...), custom_call_target="tpu_custom_call" | custom-call | flops 14499999744 | bytes 24166666 | tf_op jit(solution)/shard_map/pallas_call | solution.py:691
  268.4 19.4 %shard_map.166 = (bf16[1536,1536]{1,0:T(8,128)(2,1)}, f32[640,768]{1,0:T(8,128)}, f32[1,768]{1,0:T(1,128)}) custom-call(f32[640,768]{1,0:T(8,128)} %get-tuple-element.390.gradient, f32[640,768]{1,0:T(8,128)} %get-tuple-element.227.carried.middle, f32[1,768]{1,0:T(1,128)} %get-tuple-element.410.gain_2, bf16[640,768]{1,0:T(8,128)(2,1)} %get-tuple-element.228.normed_c, ...), custom_call_target="tpu_custom_call" | custom-call | flops 14499999744 | bytes 24166666 | tf_op jit(solution)/shard_map/pallas_call | solution.py:691
  287.8 2.8 shard_map.167
  293.1 35.4 %shard_map.168 = (f32[640,768]{1,0:T(8,128)}, f32[1,768]{1,0:T(1,128)}, bf16[384,3072]{1,0:T(8,128)(2,1)}, bf16[384,3072]{1,0:T(8,128)(2,1)}) custom-call(s32[8]{0:T(128)} %stack.106.places, f32[640,768]{1,0:T(8,128)} %get-tuple-element.256.grad_middle, f32[640,768]{1,0:T(8,128)} %get-tuple-element.218.state, f32[1,768]{1,0:T(1,128)} %get-tuple-element.413.gain_1, ...), custom_call_target="tpu_custom_call" | custom-call | flops 40000000000 | bytes 66666664 | tf_op jit(solution)/shard_map/pallas_call | solution.py:611
  330.8 4.4 shard_map.169
  335.2 15.9 %shard_map.170 = (bf16[1536,1536]{1,0:T(8,128)(2,1)}, f32[640,768]{1,0:T(8,128)}) custom-call(f32[640,768]{1,0:T(8,128)} %get-tuple-element.275.gradient, f32[640,768]{1,0:T(8,128)} %get-tuple-element.191.carried.middle, f32[1,768]{1,0:T(1,128)} %get-tuple-element.411.gain_2, bf16[640,768]{1,0:T(8,128)(2,1)} %get-tuple-element.192.normed_c, ...), custom_call_target="tpu_custom_call" | custom-call | flops 14499999744 | bytes 24166666 | tf_op jit(solution)/shard_map/pallas_call | solution.py:691
  357.5 19.6 %shard_map.172 = (bf16[1536,1536]{1,0:T(8,128)(2,1)}, f32[640,768]{1,0:T(8,128)}, f32[1,768]{1,0:T(1,128)}) custom-call(f32[640,768]{1,0:T(8,128)} %get-tuple-element.275.gradient, f32[640,768]{1,0:T(8,128)} %get-tuple-element.191.carried.middle, f32[1,768]{1,0:T(1,128)} %get-tuple-element.411.gain_2, bf16[640,768]{1,0:T(8,128)(2,1)} %get-tuple-element.192.normed_c, ...), custom_call_target="tpu_custom_call" | custom-call | flops 14499999744 | bytes 24166666 | tf_op jit(solution)/shard_map/pallas_call | solution.py:691
  377.1 2.8 shard_map.173
  381.0 5.2 collective-permute-done.43.from_x
  387.6 2.9 shard_map.174
  390.5 4.5 shard_map.175
  399.1 2.5 copy.169
  401.6 3.8 all-to-all-start.4
  405.4 35.4 %shard_map.176 = (f32[640,768]{1,0:T(8,128)}, f32[1,768]{1,0:T(1,128)}, bf16[384,3072]{1,0:T(8,128)(2,1)}, bf16[384,3072]{1,0:T(8,128)(2,1)}) custom-call(s32[8]{0:T(128)} %stack.106.places, f32[640,768]{1,0:T(8,128)} %get-tuple-element.311.grad_middle, f32[640,768]{1,0:T(8,128)} %get-tuple-element.184.state, f32[1,768]{1,0:T(1,128)} %get-tuple-element.412.gain_1, ...), custom_call_target="tpu_custom_call" | custom-call | flops 40000000000 | bytes 66666664 | tf_op jit(solution)/shard_map/pallas_call | solution.py:611
  444.1 4.5 shard_map.177
  456.9 2.9 shard_map.182
  462.0 5.1 all-to-all-start.6
  467.0 16.4 %collective-permute-done.52.from_x = bf16[48,3072]{1,0:T(8,128)(2,1)S(1)} collective-permute-done((bf16[48,3072]{1,0:T(8,128)(2,1)}, bf16[48,3072]{1,0:T(8,128)(2,1)S(1)}, u32[]{:S(2)}, u32[]{:S(2)}) %collective-permute-start.52) | collective-permute-done | bytes 294944 | tf_op jit(solution)/shard_map/ppermute | solution.py:746
  484.9 2.9 shard_map.179
  489.6 4.5 shard_map.180
  494.1 8.9 %collective-permute-done.54.others_2_ = bf16[96,3072]{1,0:T(8,128)(2,1)S(1)} collective-permute-done((bf16[96,3072]{1,0:T(8,128)(2,1)}, bf16[96,3072]{1,0:T(8,128)(2,1)S(1)}, u32[]{:S(2)}, u32[]{:S(2)}) %collective-permute-start.54) | collective-permute-done | bytes 589856 | tf_op jit(solution)/shard_map/ppermute | solution.py:746
  504.7 2.9 shard_map.181
  507.5 2.3 copy.170
  509.9 5.1 all-to-all-start.5
  516.4 13.5 %all-to-all-done.5 = bf16[4,384,192]{1,2,0:T(8,128)(2,1)} async-done(((bf16[4,384,192]{1,2,0:T(8,128)(2,1)}), bf16[4,384,192]{1,2,0:T(8,128)(2,1)}, u32[]{:S(2)}, u32[]{:S(2)}) %all-to-all-start.5) | async-done | bytes 589856 | tf_op jit(solution)/shard_map/all_to_all | solution.py:750
  529.9 3.8 all-to-all-start.7
  533.8 2.4 slice.269
  537.5 2.5 collective-permute-done.59
  545.9 6.8 %collective-permute-done.61 = f32[2,2,768]{2,1,0:T(2,128)S(1)} collective-permute-done((f32[2,2,768]{2,1,0:T(2,128)S(1)}, f32[2,2,768]{2,1,0:T(2,128)S(1)}, u32[]{:S(2)}, u32[]{:S(2)}) %collective-permute-start.61) | collective-permute-done | bytes 12320 | tf_op jit(solution)/shard_map/ppermute | solution.py:897
  552.6 4.7 collective-permute-start.62
  557.6 4.7 collective-permute-done.62
  (300 shorter events, 132.7 us)
Async XLA Ops:
  5.9 27.5 %all-to-all-start = ((bf16[4,448,192]{1,2,0:T(8,128)(2,1)}), bf16[4,448,192]{1,2,0:T(8,128)(2,1)S(1)}, u32[]{:S(2)}, u32[]{:S(2)}) async-start(bf16[4,448,192]{1,2,0:T(8,128)(2,1)} %broadcast_in_dim.23), calls=%async_computation | async-start | bytes 1572864 | tf_op jit(solution)/shard_map/all_to_all | solution.py:750
  14.2 47.3 %collective-permute-start.1 = (bf16[64,1536]{1,0:T(8,128)(2,1)}, bf16[64,1536]{1,0:T(8,128)(2,1)}, u32[]{:S(2)}, u32[]{:S(2)}) collective-permute-start(bf16[64,1536]{1,0:T(8,128)(2,1)} %get-tuple-element.393), channel_id=1, source_target_pairs={{1,0},{2,1},{3,2},{5,4},{6,5},{7,6},{9,8},{10,9},{11,10},{13,12},{... | collective-permute-start | bytes 589832 | tf_op jit(solution)/shard_map/ppermute | solution.py:905
  15.5 46.0 %collective-permute-start = (bf16[64,1536]{1,0:T(8,128)(2,1)}, bf16[64,1536]{1,0:T(8,128)(2,1)}, u32[]{:S(2)}, u32[]{:S(2)}) collective-permute-start(bf16[64,1536]{1,0:T(8,128)(2,1)} %get-tuple-element.392), channel_id=1, source_target_pairs={{0,1},{1,2},{2,3},{4,5},{5,6},{6,7},{8,9},{9,10},{10,11},{12,13},{... | collective-permute-start | bytes 589832 | tf_op jit(solution)/shard_map/ppermute | solution.py:904
  37.9 35.0 %all-to-all-start.1 = ((bf16[4,768,192]{1,2,0:T(8,128)(2,1)}), bf16[4,768,192]{1,2,0:T(8,128)(2,1)S(1)}, u32[]{:S(2)}, u32[]{:S(2)}) async-start(bf16[4,768,192]{1,2,0:T(8,128)(2,1)} %broadcast_in_dim.24), calls=%async_computation.1 | async-start | bytes 2359296 | tf_op jit(solution)/shard_map/all_to_all | solution.py:750
  63.1 16.5 %collective-permute-start.7 = (bf16[96,3072]{1,0:T(8,128)(2,1)}, bf16[96,3072]{1,0:T(8,128)(2,1)}, u32[]{:S(2)}, u32[]{:S(2)}) collective-permute-start(bf16[96,3072]{1,0:T(8,128)(2,1)} %collective-permute-done.2.others_1_), channel_id=1, source_target_pairs={{0,4},{4,0},{8,12},{12,8},{16,20},{20,16},{24,28},{28,24},{1,5},{5... | collective-permute-start | bytes 1769480 | tf_op jit(solution)/shard_map/ppermute | solution.py:746
  63.6 16.0 %collective-permute-start.8 = (bf16[96,3072]{1,0:T(8,128)(2,1)}, bf16[96,3072]{1,0:T(8,128)(2,1)}, u32[]{:S(2)}, u32[]{:S(2)}) collective-permute-start(bf16[96,3072]{1,0:T(8,128)(2,1)} %collective-permute-done.3.others_2_), channel_id=1, source_target_pairs={{0,4},{4,0},{8,12},{12,8},{16,20},{20,16},{24,28},{28,24},{1,5},{5... | collective-permute-start | bytes 1769480 | tf_op jit(solution)/shard_map/ppermute | solution.py:746
  77.2 30.7 %collective-permute-start.11 = (bf16[384,1536]{1,0:T(8,128)(2,1)}, bf16[384,1536]{1,0:T(8,128)(2,1)S(1)}, u32[]{:S(2)}, u32[]{:S(2)}) collective-permute-start(bf16[384,1536]{1,0:T(8,128)(2,1)} %shard_map.153.others_0_.others_1_), channel_id=1, source_target_pairs={{0,8},{4,12},{8,0},{12,4},{16,24},{20,28},{24,16},{28,20},{1,9},{5... | collective-permute-start | bytes 3538952 | tf_op jit(solution)/shard_map/ppermute | solution.py:746
  78.7 29.2 %collective-permute-start.12 = (bf16[384,1536]{1,0:T(8,128)(2,1)}, bf16[384,1536]{1,0:T(8,128)(2,1)}, u32[]{:S(2)}, u32[]{:S(2)}) collective-permute-start(bf16[384,1536]{1,0:T(8,128)(2,1)} %shard_map.153.others_0_.others_1_), channel_id=1, source_target_pairs={{0,16},{4,20},{8,24},{12,28},{16,0},{20,4},{24,8},{28,12},{1,17},{... | collective-permute-start | bytes 3538952 | tf_op jit(solution)/shard_map/ppermute | solution.py:746
  79.4 28.5 %collective-permute-start.13 = (bf16[384,1536]{1,0:T(8,128)(2,1)}, bf16[384,1536]{1,0:T(8,128)(2,1)S(1)}, u32[]{:S(2)}, u32[]{:S(2)}) collective-permute-start(bf16[384,1536]{1,0:T(8,128)(2,1)} %shard_map.153.others_0_.others_1_), channel_id=1, source_target_pairs={{0,4},{4,0},{8,12},{12,8},{16,20},{20,16},{24,28},{28,24},{1,5},{5... | collective-permute-start | bytes 3538952 | tf_op jit(solution)/shard_map/ppermute | solution.py:746
  107.9 25.9 %collective-permute-start.16 = (bf16[384,1536]{1,0:T(8,128)(2,1)S(1)}, bf16[384,1536]{1,0:T(8,128)(2,1)}, u32[]{:S(2)}, u32[]{:S(2)}) collective-permute-start(bf16[384,1536]{1,0:T(8,128)(2,1)S(1)} %collective-permute-done.11.others_1_.others_2_), channel_id=1, source_target_pairs={{0,4},{4,0},{8,12},{12,8},{16,20},{20,16},{24,28},{28,24},{1,5},{5... | collective-permute-start | bytes 3538952 | tf_op jit(solution)/shard_map/ppermute | solution.py:746
  108.3 25.5 %collective-permute-start.17 = (bf16[384,1536]{1,0:T(8,128)(2,1)}, bf16[384,1536]{1,0:T(8,128)(2,1)}, u32[]{:S(2)}, u32[]{:S(2)}) collective-permute-start(bf16[384,1536]{1,0:T(8,128)(2,1)} %collective-permute-done.12.others_2_.others_3_), channel_id=1, source_target_pairs={{0,4},{4,0},{8,12},{12,8},{16,20},{20,16},{24,28},{28,24},{1,5},{5... | collective-permute-start | bytes 3538952 | tf_op jit(solution)/shard_map/ppermute | solution.py:746
  111.3 19.4 %collective-permute-start.14 = (bf16[192,1536]{1,0:T(8,128)(2,1)S(1)}, bf16[192,1536]{1,0:T(8,128)(2,1)}, u32[]{:S(2)}, u32[]{:S(2)}) collective-permute-start(bf16[192,1536]{1,0:T(8,128)(2,1)S(1)} %slice.201), channel_id=1, source_target_pairs={{0,16},{4,20},{8,24},{12,28},{16,0},{20,4},{24,8},{28,12},{1,17},{... | collective-permute-start | bytes 1769480 | tf_op jit(solution)/shard_map/ppermute | solution.py:746
  112.6 18.1 %collective-permute-start.15 = (bf16[192,1536]{1,0:T(8,128)(2,1)S(1)}, bf16[192,1536]{1,0:T(8,128)(2,1)}, u32[]{:S(2)}, u32[]{:S(2)}) collective-permute-start(bf16[192,1536]{1,0:T(8,128)(2,1)S(1)} %slice.202), channel_id=1, source_target_pairs={{0,8},{4,12},{8,0},{12,4},{16,24},{20,28},{24,16},{28,20},{1,9},{5... | collective-permute-start | bytes 1769480 | tf_op jit(solution)/shard_map/ppermute | solution.py:746
  113.2 20.6 %all-to-all-start.2 = ((bf16[4,384,192]{1,2,0:T(8,128)(2,1)}), bf16[4,384,192]{1,2,0:T(8,128)(2,1)S(1)}, u32[]{:S(2)}, u32[]{:S(2)}) async-start(bf16[4,384,192]{1,2,0:T(8,128)(2,1)} %broadcast_in_dim.29), calls=%async_computation.2 | async-start | bytes 1179648 | tf_op jit(solution)/shard_map/all_to_all | solution.py:750
  138.2 19.2 %collective-permute-start.18 = (bf16[96,3072]{1,0:T(8,128)(2,1)}, bf16[96,3072]{1,0:T(8,128)(2,1)S(1)}, u32[]{:S(2)}, u32[]{:S(2)}) collective-permute-start(bf16[96,3072]{1,0:T(8,128)(2,1)} %shard_map.157.others_0_), channel_id=1, source_target_pairs={{0,8},{4,12},{8,0},{12,4},{16,24},{20,28},{24,16},{28,20},{1,9},{5... | collective-permute-start | bytes 1769480 | tf_op jit(solution)/shard_map/ppermute | solution.py:746
  139.7 17.7 %collective-permute-start.19 = (bf16[96,3072]{1,0:T(8,128)(2,1)}, bf16[96,3072]{1,0:T(8,128)(2,1)}, u32[]{:S(2)}, u32[]{:S(2)}) collective-permute-start(bf16[96,3072]{1,0:T(8,128)(2,1)} %shard_map.157.others_0_), channel_id=1, source_target_pairs={{0,16},{4,20},{8,24},{12,28},{16,0},{20,4},{24,8},{28,12},{1,17},{... | collective-permute-start | bytes 1769480 | tf_op jit(solution)/shard_map/ppermute | solution.py:746
  140.3 17.1 %collective-permute-start.20 = (bf16[96,3072]{1,0:T(8,128)(2,1)}, bf16[96,3072]{1,0:T(8,128)(2,1)}, u32[]{:S(2)}, u32[]{:S(2)}) collective-permute-start(bf16[96,3072]{1,0:T(8,128)(2,1)} %shard_map.157.others_0_), channel_id=1, source_target_pairs={{0,4},{4,0},{8,12},{12,8},{16,20},{20,16},{24,28},{28,24},{1,5},{5... | collective-permute-start | bytes 1769480 | tf_op jit(solution)/shard_map/ppermute | solution.py:746
  140.3 20.2 %collective-permute-start.21 = (bf16[192,1536]{1,0:T(8,128)(2,1)}, bf16[192,1536]{1,0:T(8,128)(2,1)S(1)}, u32[]{:S(2)}, u32[]{:S(2)}) collective-permute-start(bf16[192,1536]{1,0:T(8,128)(2,1)} %collective-permute-done.14.others_0_.others_4_), channel_id=1, source_target_pairs={{0,4},{4,0},{8,12},{12,8},{16,20},{20,16},{24,28},{28,24},{1,5},{5... | collective-permute-start | bytes 1769480 | tf_op jit(solution)/shard_map/ppermute | solution.py:746
  140.8 20.3 %collective-permute-start.22 = (bf16[192,1536]{1,0:T(8,128)(2,1)}, bf16[192,1536]{1,0:T(8,128)(2,1)S(1)}, u32[]{:S(2)}, u32[]{:S(2)}) collective-permute-start(bf16[192,1536]{1,0:T(8,128)(2,1)} %collective-permute-done.15.others_1_.others_5_), channel_id=1, source_target_pairs={{0,4},{4,0},{8,12},{12,8},{16,20},{20,16},{24,28},{28,24},{1,5},{5... | collective-permute-start | bytes 1769480 | tf_op jit(solution)/shard_map/ppermute | solution.py:746
  140.8 33.2 %all-to-all-start.3 = ((bf16[4,768,192]{1,2,0:T(8,128)(2,1)}), bf16[4,768,192]{1,2,0:T(8,128)(2,1)S(1)}, u32[]{:S(2)}, u32[]{:S(2)}) async-start(bf16[4,768,192]{1,2,0:T(8,128)(2,1)} %broadcast_in_dim.30), calls=%async_computation.3 | async-start | bytes 2359296 | tf_op jit(solution)/shard_map/all_to_all | solution.py:750
  157.4 22.3 %collective-permute-start.25 = (bf16[96,3072]{1,0:T(8,128)(2,1)S(1)}, bf16[96,3072]{1,0:T(8,128)(2,1)}, u32[]{:S(2)}, u32[]{:S(2)}) collective-permute-start(bf16[96,3072]{1,0:T(8,128)(2,1)S(1)} %collective-permute-done.18.others_1_), channel_id=1, source_target_pairs={{0,4},{4,0},{8,12},{12,8},{16,20},{20,16},{24,28},{28,24},{1,5},{5... | collective-permute-start | bytes 1769480 | tf_op jit(solution)/shard_map/ppermute | solution.py:746
  159.0 21.7 %collective-permute-start.26 = (bf16[96,3072]{1,0:T(8,128)(2,1)}, bf16[96,3072]{1,0:T(8,128)(2,1)}, u32[]{:S(2)}, u32[]{:S(2)}) collective-permute-start(bf16[96,3072]{1,0:T(8,128)(2,1)} %collective-permute-done.19.others_2_), channel_id=1, source_target_pairs={{0,4},{4,0},{8,12},{12,8},{16,20},{20,16},{24,28},{28,24},{1,5},{5... | collective-permute-start | bytes 1769480 | tf_op jit(solution)/shard_map/ppermute | solution.py:746
  178.8 30.2 %collective-permute-start.29 = (bf16[384,1536]{1,0:T(8,128)(2,1)}, bf16[384,1536]{1,0:T(8,128)(2,1)S(1)}, u32[]{:S(2)}, u32[]{:S(2)}) collective-permute-start(bf16[384,1536]{1,0:T(8,128)(2,1)} %shard_map.160.others_0_.others_1_), channel_id=1, source_target_pairs={{0,8},{4,12},{8,0},{12,4},{16,24},{20,28},{24,16},{28,20},{1,9},{5... | collective-permute-start | bytes 3538952 | tf_op jit(solution)/shard_map/ppermute | solution.py:746
  179.7 29.3 %collective-permute-start.30 = (bf16[384,1536]{1,0:T(8,128)(2,1)}, bf16[384,1536]{1,0:T(8,128)(2,1)S(1)}, u32[]{:S(2)}, u32[]{:S(2)}) collective-permute-start(bf16[384,1536]{1,0:T(8,128)(2,1)} %shard_map.160.others_0_.others_1_), channel_id=1, source_target_pairs={{0,16},{4,20},{8,24},{12,28},{16,0},{20,4},{24,8},{28,12},{1,17},{... | collective-permute-start | bytes 3538952 | tf_op jit(solution)/shard_map/ppermute | solution.py:746
  180.7 28.3 %collective-permute-start.31 = (bf16[384,1536]{1,0:T(8,128)(2,1)}, bf16[384,1536]{1,0:T(8,128)(2,1)S(1)}, u32[]{:S(2)}, u32[]{:S(2)}) collective-permute-start(bf16[384,1536]{1,0:T(8,128)(2,1)} %shard_map.160.others_0_.others_1_), channel_id=1, source_target_pairs={{0,4},{4,0},{8,12},{12,8},{16,20},{20,16},{24,28},{28,24},{1,5},{5... | collective-permute-start | bytes 3538952 | tf_op jit(solution)/shard_map/ppermute | solution.py:746
  209.0 17.8 %collective-permute-start.34 = (bf16[384,1536]{1,0:T(8,128)(2,1)S(1)}, bf16[384,1536]{1,0:T(8,128)(2,1)}, u32[]{:S(2)}, u32[]{:S(2)}) collective-permute-start(bf16[384,1536]{1,0:T(8,128)(2,1)S(1)} %collective-permute-done.29.others_1_.others_2_), channel_id=1, source_target_pairs={{0,4},{4,0},{8,12},{12,8},{16,20},{20,16},{24,28},{28,24},{1,5},{5... | collective-permute-start | bytes 3538952 | tf_op jit(solution)/shard_map/ppermute | solution.py:746
  210.1 16.8 %collective-permute-start.35 = (bf16[384,1536]{1,0:T(8,128)(2,1)S(1)}, bf16[384,1536]{1,0:T(8,128)(2,1)}, u32[]{:S(2)}, u32[]{:S(2)}) collective-permute-start(bf16[384,1536]{1,0:T(8,128)(2,1)S(1)} %collective-permute-done.30.others_2_.others_3_), channel_id=1, source_target_pairs={{0,4},{4,0},{8,12},{12,8},{16,20},{20,16},{24,28},{28,24},{1,5},{5... | collective-permute-start | bytes 3538952 | tf_op jit(solution)/shard_map/ppermute | solution.py:746
  267.6 20.2 %collective-permute-start.38 = (bf16[1536,1536]{1,0:T(8,128)(2,1)}, bf16[1536,1536]{1,0:T(8,128)(2,1)}, u32[]{:S(2)}, u32[]{:S(2)}) collective-permute-start(bf16[1536,1536]{1,0:T(8,128)(2,1)} %get-tuple-element.250), channel_id=1, source_target_pairs={{0,4},{4,0},{8,12},{12,8},{16,20},{20,16},{24,28},{28,24},{1,5},{5... | collective-permute-start | bytes 14155784 | tf_op jit(solution)/shard_map/ppermute | solution.py:746
  290.6 39.2 %collective-permute-start.39 = (bf16[192,1536]{1,0:T(8,128)(2,1)}, bf16[192,1536]{1,0:T(8,128)(2,1)S(1)}, u32[]{:S(2)}, u32[]{:S(2)}) collective-permute-start(bf16[192,1536]{1,0:T(8,128)(2,1)} %get-tuple-element.268), channel_id=1, source_target_pairs={{0,8},{4,12},{8,0},{12,4},{16,24},{20,28},{24,16},{28,20},{1,9},{5... | collective-permute-start | bytes 1769480 | tf_op jit(solution)/shard_map/ppermute | solution.py:746
  291.7 38.1 %collective-permute-start.40 = (bf16[192,1536]{1,0:T(8,128)(2,1)}, bf16[192,1536]{1,0:T(8,128)(2,1)S(1)}, u32[]{:S(2)}, u32[]{:S(2)}) collective-permute-start(bf16[192,1536]{1,0:T(8,128)(2,1)} %get-tuple-element.269), channel_id=1, source_target_pairs={{0,16},{4,20},{8,24},{12,28},{16,0},{20,4},{24,8},{28,12},{1,17},{... | collective-permute-start | bytes 1769480 | tf_op jit(solution)/shard_map/ppermute | solution.py:746
  329.8 21.3 %collective-permute-start.41 = (bf16[384,3072]{1,0:T(8,128)(2,1)}, bf16[384,3072]{1,0:T(8,128)(2,1)S(1)}, u32[]{:S(2)}, u32[]{:S(2)}) collective-permute-start(bf16[384,3072]{1,0:T(8,128)(2,1)} %get-tuple-element.284), channel_id=1, source_target_pairs={{0,4},{4,0},{8,12},{12,8},{16,20},{20,16},{24,28},{28,24},{1,5},{5... | collective-permute-start | bytes 7077896 | tf_op jit(solution)/shard_map/ppermute | solution.py:746
  351.1 26.0 %collective-permute-start.42 = (bf16[1536,1536]{1,0:T(8,128)(2,1)}, bf16[1536,1536]{1,0:T(8,128)(2,1)}, u32[]{:S(2)}, u32[]{:S(2)}) collective-permute-start(bf16[1536,1536]{1,0:T(8,128)(2,1)} %get-tuple-element.293), channel_id=1, source_target_pairs={{0,4},{4,0},{8,12},{12,8},{16,20},{20,16},{24,28},{28,24},{1,5},{5... | collective-permute-start | bytes 14155784 | tf_op jit(solution)/shard_map/ppermute | solution.py:746
  351.2 29.0 %collective-permute-start.45 = (bf16[384,1536]{1,0:T(8,128)(2,1)}, bf16[384,1536]{1,0:T(8,128)(2,1)S(1)}, u32[]{:S(2)}, u32[]{:S(2)}) collective-permute-start(bf16[384,1536]{1,0:T(8,128)(2,1)} %get-tuple-element.302), channel_id=1, source_target_pairs={{0,8},{4,12},{8,0},{12,4},{16,24},{20,28},{24,16},{28,20},{1,9},{5... | collective-permute-start | bytes 3538952 | tf_op jit(solution)/shard_map/ppermute | solution.py:746
  351.8 29.1 %collective-permute-start.46 = (bf16[384,1536]{1,0:T(8,128)(2,1)}, bf16[384,1536]{1,0:T(8,128)(2,1)}, u32[]{:S(2)}, u32[]{:S(2)}) collective-permute-start(bf16[384,1536]{1,0:T(8,128)(2,1)} %get-tuple-element.303), channel_id=1, source_target_pairs={{0,16},{4,20},{8,24},{12,28},{16,0},{20,4},{24,8},{28,12},{1,17},{... | collective-permute-start | bytes 3538952 | tf_op jit(solution)/shard_map/ppermute | solution.py:746
  354.9 31.2 %collective-permute-start.43 = (bf16[48,3072]{1,0:T(8,128)(2,1)}, bf16[48,3072]{1,0:T(8,128)(2,1)S(1)}, u32[]{:S(2)}, u32[]{:S(2)}) collective-permute-start(bf16[48,3072]{1,0:T(8,128)(2,1)} %get-tuple-element.300), channel_id=1, source_target_pairs={{0,8},{4,12},{8,0},{12,4},{16,24},{20,28},{24,16},{28,20},{1,9},{5... | collective-permute-start | bytes 884744 | tf_op jit(solution)/shard_map/ppermute | solution.py:746
  356.0 30.3 %collective-permute-start.44 = (bf16[48,3072]{1,0:T(8,128)(2,1)}, bf16[48,3072]{1,0:T(8,128)(2,1)S(1)}, u32[]{:S(2)}, u32[]{:S(2)}) collective-permute-start(bf16[48,3072]{1,0:T(8,128)(2,1)} %get-tuple-element.301), channel_id=1, source_target_pairs={{0,16},{4,20},{8,24},{12,28},{16,0},{20,4},{24,8},{28,12},{1,17},{... | collective-permute-start | bytes 884744 | tf_op jit(solution)/shard_map/ppermute | solution.py:746
  395.0 47.1 %collective-permute-start.47 = (bf16[192,1536]{1,0:T(8,128)(2,1)}, bf16[192,1536]{1,0:T(8,128)(2,1)S(1)}, u32[]{:S(2)}, u32[]{:S(2)}) collective-permute-start(bf16[192,1536]{1,0:T(8,128)(2,1)} %get-tuple-element.323), channel_id=1, source_target_pairs={{0,8},{4,12},{8,0},{12,4},{16,24},{20,28},{24,16},{28,20},{1,9},{5... | collective-permute-start | bytes 1769480 | tf_op jit(solution)/shard_map/ppermute | solution.py:746
  396.1 46.0 %collective-permute-start.48 = (bf16[192,1536]{1,0:T(8,128)(2,1)}, bf16[192,1536]{1,0:T(8,128)(2,1)S(1)}, u32[]{:S(2)}, u32[]{:S(2)}) collective-permute-start(bf16[192,1536]{1,0:T(8,128)(2,1)} %get-tuple-element.324), channel_id=1, source_target_pairs={{0,16},{4,20},{8,24},{12,28},{16,0},{20,4},{24,8},{28,12},{1,17},{... | collective-permute-start | bytes 1769480 | tf_op jit(solution)/shard_map/ppermute | solution.py:746
  396.7 45.5 %collective-permute-start.49 = (bf16[96,3072]{1,0:T(8,128)(2,1)}, bf16[96,3072]{1,0:T(8,128)(2,1)S(1)}, u32[]{:S(2)}, u32[]{:S(2)}) collective-permute-start(bf16[96,3072]{1,0:T(8,128)(2,1)} %get-tuple-element.328), channel_id=1, source_target_pairs={{0,8},{4,12},{8,0},{12,4},{16,24},{20,28},{24,16},{28,20},{1,9},{5... | collective-permute-start | bytes 1769480 | tf_op jit(solution)/shard_map/ppermute | solution.py:746
  397.7 44.5 %collective-permute-start.50 = (bf16[96,3072]{1,0:T(8,128)(2,1)}, bf16[96,3072]{1,0:T(8,128)(2,1)S(1)}, u32[]{:S(2)}, u32[]{:S(2)}) collective-permute-start(bf16[96,3072]{1,0:T(8,128)(2,1)} %get-tuple-element.329), channel_id=1, source_target_pairs={{0,16},{4,20},{8,24},{12,28},{16,0},{20,4},{24,8},{28,12},{1,17},{... | collective-permute-start | bytes 1769480 | tf_op jit(solution)/shard_map/ppermute | solution.py:746
  401.6 42.5 %all-to-all-start.4 = ((bf16[4,768,192]{1,2,0:T(8,128)(2,1)}), bf16[4,768,192]{1,2,0:T(8,128)(2,1)S(1)}, u32[]{:S(2)}, u32[]{:S(2)}) async-start(bf16[4,768,192]{1,2,0:T(8,128)(2,1)} %copy.169), calls=%async_computation.4 | async-start | bytes 2359296 | tf_op jit(solution)/shard_map/all_to_all | solution.py:750
  448.6 41.0 %collective-permute-start.56 = (bf16[384,1536]{1,0:T(8,128)(2,1)}, bf16[384,1536]{1,0:T(8,128)(2,1)}, u32[]{:S(2)}, u32[]{:S(2)}) collective-permute-start(bf16[384,1536]{1,0:T(8,128)(2,1)} %get-tuple-element.337), channel_id=1, source_target_pairs={{0,8},{4,12},{8,0},{12,4},{16,24},{20,28},{24,16},{28,20},{1,9},{5... | collective-permute-start | bytes 3538952 | tf_op jit(solution)/shard_map/ppermute | solution.py:746
  449.6 40.0 %collective-permute-start.57 = (bf16[384,1536]{1,0:T(8,128)(2,1)}, bf16[384,1536]{1,0:T(8,128)(2,1)}, u32[]{:S(2)}, u32[]{:S(2)}) collective-permute-start(bf16[384,1536]{1,0:T(8,128)(2,1)} %get-tuple-element.338), channel_id=1, source_target_pairs={{0,16},{4,20},{8,24},{12,28},{16,0},{20,4},{24,8},{28,12},{1,17},{... | collective-permute-start | bytes 3538952 | tf_op jit(solution)/shard_map/ppermute | solution.py:746
  454.5 29.0 %collective-permute-start.52 = (bf16[48,3072]{1,0:T(8,128)(2,1)}, bf16[48,3072]{1,0:T(8,128)(2,1)S(1)}, u32[]{:S(2)}, u32[]{:S(2)}) collective-permute-start(bf16[48,3072]{1,0:T(8,128)(2,1)} %get-tuple-element.342), channel_id=1, source_target_pairs={{0,8},{4,12},{8,0},{12,4},{16,24},{20,28},{24,16},{28,20},{1,9},{5... | collective-permute-start | bytes 884744 | tf_op jit(solution)/shard_map/ppermute | solution.py:746
  455.5 28.7 %collective-permute-start.53 = (bf16[48,3072]{1,0:T(8,128)(2,1)}, bf16[48,3072]{1,0:T(8,128)(2,1)S(1)}, u32[]{:S(2)}, u32[]{:S(2)}) collective-permute-start(bf16[48,3072]{1,0:T(8,128)(2,1)} %get-tuple-element.343), channel_id=1, source_target_pairs={{0,16},{4,20},{8,24},{12,28},{16,0},{20,4},{24,8},{28,12},{1,17},{... | collective-permute-start | bytes 884744 | tf_op jit(solution)/shard_map/ppermute | solution.py:746
  462.0 47.9 %all-to-all-start.6 = ((bf16[4,384,192]{1,2,0:T(8,128)(2,1)}), bf16[4,384,192]{1,2,0:T(8,128)(2,1)S(1)}, u32[]{:S(2)}, u32[]{:S(2)}) async-start(bf16[4,384,192]{1,2,0:T(8,128)(2,1)} %copy.172), calls=%async_computation.6 | async-start | bytes 1179648 | tf_op jit(solution)/shard_map/all_to_all | solution.py:750
  509.9 20.0 %all-to-all-start.5 = ((bf16[4,384,192]{1,2,0:T(8,128)(2,1)}), bf16[4,384,192]{1,2,0:T(8,128)(2,1)}, u32[]{:S(2)}, u32[]{:S(2)}) async-start(bf16[4,384,192]{1,2,0:T(8,128)(2,1)} %copy.170), calls=%async_computation.5 | async-start | bytes 1179648 | tf_op jit(solution)/shard_map/all_to_all | solution.py:750
  529.9 36.7 %all-to-all-start.7 = ((bf16[4,768,192]{1,2,0:T(8,128)(2,1)}), bf16[4,768,192]{1,2,0:T(8,128)(2,1)S(1)}, u32[]{:S(2)}, u32[]{:S(2)}) async-start(bf16[4,768,192]{1,2,0:T(8,128)(2,1)} %copy.174), calls=%async_computation.7 | async-start | bytes 2359296 | tf_op jit(solution)/shard_map/all_to_all | solution.py:750
  (64 other events, 519.6 us)

commit v3 on v2

v3 whole, which is shorter than its diff:
```python
import functools
import math

import jax
import jax.numpy as jnp
from jax import lax
from jax.experimental import pallas as pl
from jax.experimental.pallas import tpu as pltpu
from jax.sharding import PartitionSpec as P

MOST = 64
EPSILON = 1e-05
QUERY_ROWS = 128
KEY_ROWS = QUERY_ROWS + 2 * MOST
GROUP = 4
VMEM_BYTES = 60 * 2**20

BF16 = jnp.bfloat16
F32 = jnp.float32
CONTRACT_LAST = (((1,), (1,)), ((), ()))
CONTRACT_FIRST = (((0,), (0,)), ((), ()))
CONTRACT_MIDDLE = (((1,), (0,)), ((), ()))

TAIL_SCALE = 0.3275911 / math.sqrt(2.0)
TAIL_TERMS = (1.061405429, -1.453152027, 1.421413741, -0.284496736, 0.254829592)


def dot(left, right, dims=CONTRACT_MIDDLE):
    return lax.dot_general(left, right, dims, preferred_element_type=F32)


def gelu_and_slope(hidden):
    bell = jnp.exp(hidden * hidden * -0.5)
    below = 1.0 + jnp.abs(hidden) * TAIL_SCALE
    guess = pl.reciprocal(below, approx=True)
    inverse = guess * (2.0 - below * guess)
    tail = 0.5 * TAIL_TERMS[0]
    for term in TAIL_TERMS[1:]:
        tail = tail * inverse + 0.5 * term
    tail = tail * inverse * bell
    cumulative = jnp.where(hidden > 0.0, 1.0 - tail, tail)
    return hidden * cumulative, cumulative + hidden * (bell * (1.0 / math.sqrt(2.0 * math.pi)))


def normalised(values):
    centred = values - jnp.mean(values, axis=-1, keepdims=True)
    inverse = lax.rsqrt(jnp.mean(centred * centred, axis=-1, keepdims=True) + EPSILON)
    return centred * inverse, inverse


def norm_back(grad_out, gain, hat, inverse):
    scaled = grad_out * gain
    first_mean = jnp.mean(scaled, axis=-1, keepdims=True)
    second_mean = jnp.mean(scaled * hat, axis=-1, keepdims=True)
    return inverse * (scaled - first_mean - hat * second_mean)


def each_block(rows, size, step):
    for block in row_blocks(rows, size):
        step(block)


def own_block(block, rows):
    return MOST <= block.start and block.stop <= rows - MOST


def swap_halves(values, half):
    width = values.shape[-1]
    lane = lax.broadcasted_iota(jnp.int32, values.shape, len(values.shape) - 1)
    ahead = pltpu.roll(values, width - half, 1)
    behind = pltpu.roll(values, half, 1)
    return jnp.where(lane % (2 * half) < half, ahead, behind)


def two_parts(values):
    high = values.astype(BF16)
    return high, (values - high.astype(F32)).astype(BF16)


def row_blocks(rows, size):
    return [slice(begin, begin + size) for begin in range(0, rows, size)]


def spread_parts(rows, target, place):
    width = rows.shape[1]
    for index, part in enumerate((*two_parts(rows), *two_parts(rows * rows))):
        target[place, index * width : (index + 1) * width] = part


def phi_of(parts, table):
    return jnp.exp(dot(parts, table)) * (1.0 / math.sqrt(table.shape[1] // GROUP))


def head_masks(width, dtype):
    lane = lax.broadcasted_iota(jnp.int32, (1, width), 1) // (width // GROUP)
    return [jnp.where(lane == head, 1.0, 0.0).astype(dtype) for head in range(GROUP)]


def spread_heads(values):
    return jnp.concatenate([values * mask for mask in head_masks(values.shape[1], BF16)], axis=0)


def gather_heads(values):
    masks = head_masks(values.shape[-1], F32)
    total = values[0] * masks[0]
    for head in range(1, GROUP):
        total = total + values[head] * masks[head]
    return total


def block_scores(phi_q, phi_k, ids_column, ids_row):
    scores = dot(phi_q, phi_k, CONTRACT_LAST)
    same = (ids_column == ids_row).astype(F32)
    scores = scores.reshape(GROUP, QUERY_ROWS, KEY_ROWS) * same[None]
    totals = jnp.sum(scores, axis=-1, keepdims=True)
    inverse = jnp.where(totals > 0.0, 1.0 / totals, 0.0)
    return scores * inverse, inverse, same


def query_blocks(rows):
    for index, block in enumerate(row_blocks(rows, QUERY_ROWS)):
        begin = min(max(block.start - MOST, 0), rows - KEY_ROWS)
        yield index, block, slice(begin, begin + KEY_ROWS)


def attention_forward(
    scale,
    piece_count,
    places,
    state,
    gain_1,
    gain_2,
    table,
    cosine,
    sine,
    ids_column,
    ids_row,
    *others,
):
    pieces = others[:piece_count]
    weights_out, normed_a, query, key, value, mixed, middle, normed_c, *others = others[piece_count:]
    weights, total, projected, parts, phi, arrived, leaving = others
    group = pl.program_id(0)
    groups = weights.shape[0]
    rows = state.shape[0]
    wide = query.shape[1]
    deep = weights.shape[2]
    half = cosine.shape[1] // GROUP // 2

    def columns_of(at):
        return pl.ds(at * deep, deep)

    def arriving_at(at):
        for index, piece in enumerate(pieces):
            place = pl.ds(pl.multiple_of(places[index], 16), piece.shape[0])
            yield pltpu.make_async_copy(
                piece.at[:, columns_of(at)], weights.at[at, place, :], arrived.at[at, index]
            )

    def leaving_at(at):
        return pltpu.make_async_copy(
            weights.at[at], weights_out.at[:, columns_of(at)], leaving.at[at]
        )

    @pl.when(group == 0)
    def _():
        for at in range(groups):
            for copy in arriving_at(at):
                copy.start()

        def step(block):
            hat, _ = normalised(state[block, :])
            normed_a[block, :] = (hat * gain_1[...]).astype(BF16)
            total[block, :] = state[block, :]

        each_block(rows, 64, step)

    for at in range(groups):

        @pl.when(group == at)
        def _(at=at):
            for copy in arriving_at(at):
                copy.wait()
            leaving_at(at).start()

    projected[...] = dot(normed_a[...], weights[group, :, : 3 * wide])
    for block in row_blocks(rows, 64):
        for part, held in enumerate((query, key)):
            values = projected[block, part * wide : (part + 1) * wide]
            turned = values * cosine[block, :] + swap_halves(values, half) * sine[block, :]
            turned = turned * scale
            held[block, :] = turned
            spread_parts(turned, parts, slice(part * rows + block.start, part * rows + block.stop))
        value[block, :] = projected[block, 2 * wide :].astype(BF16)
    phi[...] = phi_of(parts[...], table[0]).astype(BF16)

    for index, block, keys in query_blocks(rows):
        scores, _, _ = block_scores(
            spread_heads(phi[block, :]),
            phi[rows + keys.start : rows + keys.stop, :],
            ids_column[block, :],
            ids_row[index],
        )
        scores = scores.reshape(GROUP * QUERY_ROWS, KEY_ROWS).astype(BF16)
        found = dot(scores, value[keys, :])
        mixed[block, :] = gather_heads(found.reshape(GROUP, QUERY_ROWS, -1)).astype(BF16)

    total[...] += dot(mixed[...], weights[group, :, 3 * wide :], CONTRACT_LAST)

    @pl.when(group == groups - 1)
    def _():
        def step(block):
            middle[block, :] = total[block, :]
            hat, _ = normalised(total[block, :])
            normed_c[block, :] = (hat * gain_2[...]).astype(BF16)

        each_block(rows, 64, step)
        for at in range(groups):
            leaving_at(at).wait()


class Arrivals:
    def __init__(self, semaphores):
        self.semaphores, self.copies = semaphores, []

    def start(self, source, target):
        copy = pltpu.make_async_copy(source, target, self.semaphores.at[len(self.copies)])
        copy.start()
        self.copies.append(copy)
        return copy


def attention_backward(first, last, scale, groups, split, places, branch_in, weights_in, mixed_in, query_in, key_in, value_in, *others):
    normed_in, cosine_in, sine_in, *others = others
    if not first:
        total_in, *others = others
    if last:
        grad_middle, state, gain_1, *others = others
    table, back_table, ids_column, ids_row, *others = others
    if last:
        grad_state, grad_gain, *others = others
    else:
        total_out, *others = others
    grad_targets, others = others[: 1 + split], others[1 + split :]
    (
        branch,
        weights,
        mixed,
        query,
        key,
        value,
        normed_a,
        cosine,
        sine,
        total,
        grad_weight,
        grad_mixed,
        parts,
        phi,
        grad_phi,
        grad_value,
        grad_parts,
        grad_projected,
        arrived,
        leaving,
    ) = others
    _, rows, wide = query.shape
    half = wide // GROUP // 2
    own_rows = rows - 2 * MOST
    own = pl.ds(MOST, own_rows)
    small = phi.shape[1]
    deep = weights.shape[2]
    arrivals = Arrivals(arrived)
    got_branch = arrivals.start(branch_in, branch)
    got = []
    for at, group in enumerate(groups):
        columns_in = pl.ds(group * wide, wide)
        got.append(
            (
                arrivals.start(
                    weights_in.at[:, pl.ds(group * deep + 3 * wide, wide)],
                    weights.at[at, :, pl.ds(3 * wide, wide)],
                ),
                arrivals.start(query_in.at[:, columns_in], query.at[at]),
                arrivals.start(key_in.at[:, columns_in], key.at[at]),
                arrivals.start(mixed_in.at[own, columns_in], mixed.at[at]),
                arrivals.start(value_in.at[:, columns_in], value.at[at]),
                arrivals.start(
                    weights_in.at[:, pl.ds(group * deep, 3 * wide)],
                    weights.at[at, :, pl.ds(0, 3 * wide)],
                ),
            )
        )
        if at == 0:
            got_shared = [
                arrivals.start(cosine_in, cosine),
                arrivals.start(sine_in, sine),
                arrivals.start(normed_in.at[own, :], normed_a),
            ]
    if not first:
        got_total = arrivals.start(total_in, total)
    got_branch.wait()
    count = leaving.shape[1]
    size = grad_weight.shape[1] // count
    copies = []
    for at in range(len(groups)):
        got_last, *got_rows, got_first = got[at]
        got_last.wait()
        for copy in got_rows:
            copy.wait()
        grad_mixed[...] = dot(branch[...], weights[at, :, 3 * wide :]).astype(BF16)
        for block in row_blocks(rows, 64):
            for part, held in enumerate((query, key)):
                place = slice(part * rows + block.start, part * rows + block.stop)
                spread_parts(held[at, block, :], parts, place)
        phi[...] = phi_of(parts[...], table[at])
        grad_phi[rows:, :] = jnp.zeros((rows, small), F32)
        grad_value[...] = jnp.zeros_like(grad_value)
        found = dot(branch[own, :], mixed[at], CONTRACT_FIRST)
        grad_weight[at, :, 3 * wide :] = found.astype(BF16)

        for index, block, keys in query_blocks(rows):
            far_keys = slice(rows + keys.start, rows + keys.stop)
            spread_q = spread_heads(phi[block, :].astype(BF16))
            spread_grad = spread_heads(grad_mixed[block, :])
            keys_phi = phi[far_keys, :].astype(BF16)
            scores, inverse, same = block_scores(
                spread_q, keys_phi, ids_column[block, :], ids_row[index]
            )
            flat = (GROUP * QUERY_ROWS, KEY_ROWS)
            grad_scores = dot(spread_grad, value[at, keys, :], CONTRACT_LAST)
            grad_value[keys, :] += dot(
                scores.reshape(flat).astype(BF16), spread_grad, CONTRACT_FIRST
            )
            grad_scores = grad_scores.reshape(scores.shape)
            inner = jnp.sum(grad_scores * scores, axis=-1, keepdims=True)
            grad_scores = ((grad_scores - inner) * inverse * same[None]).astype(BF16).reshape(flat)
            found = dot(grad_scores, keys_phi)
            grad_phi[block, :] = gather_heads(found.reshape(GROUP, QUERY_ROWS, -1))
            grad_phi[far_keys, :] += dot(grad_scores, spread_q, CONTRACT_FIRST)

        if at == 0:
            for copy in got_shared:
                copy.wait()
        got_first.wait()
        for block in row_blocks(2 * rows, 128):
            high, low = two_parts(grad_phi[block, :] * phi[block, :])
            grad_parts[block, :small] = high
            grad_parts[block, small:] = low
        for part, held in enumerate((query, key)):
            for block in row_blocks(rows, 128):
                there = slice(part * rows + block.start, part * rows + block.stop)
                both = dot(grad_parts[there, :], back_table[at], CONTRACT_LAST)
                grad_rows = (both[:, :wide] - held[at, block, :] * both[:, wide:]) * scale
                turned = grad_rows * cosine[block, :]
                turned = turned + swap_halves(grad_rows * sine[block, :], half)
                grad_projected[block, part * wide : (part + 1) * wide] = turned.astype(BF16)
        grad_projected[:, 2 * wide :] = grad_value[...].astype(BF16)
        found = dot(normed_a[...], grad_projected[own, :], CONTRACT_FIRST)
        grad_weight[at, :, : 3 * wide] = found.astype(BF16)
        for index in range(count):
            place = pl.ds(pl.multiple_of(places[index], 16), size) if split else pl.ds(0, size)
            each = count // len(grad_targets)
            target = grad_targets[index // each]
            to = pl.ds(index % each * size, size)
            copies.append(
                pltpu.make_async_copy(
                    grad_weight.at[at, place, :],
                    target.at[to, pl.ds(at * deep, deep)],
                    leaving.at[at, index],
                )
            )
            copies[-1].start()
        back = dot(grad_projected[...], weights[at, :, : 3 * wide], CONTRACT_LAST)
        ending = at == len(groups) - 1
        if at == 0 and not first:
            got_total.wait()
        if at > 0 or not first:
            back = total[...] + back
        if ending and not last:
            total_out[...] = back
        else:
            total[...] = back
    if last:
        grad_gain[...] = jnp.zeros_like(grad_gain)

        def step(block):
            hat, inverse = normalised(state[block, :])
            back = norm_back(total[block, :], gain_1[...], hat, inverse)
            grad_state[block, :] = grad_middle[block, :] + back
            if own_block(block, rows):
                grad_gain[...] += jnp.sum(total[block, :] * hat, axis=0, keepdims=True)

        each_block(rows, 64, step)
    for copy in copies:
        copy.wait()


def begins_of(pieces):
    begins = [0]
    for piece in pieces:
        begins.append(begins[-1] + piece.shape[0])
    return begins


def hidden_chunks(count):
    return [slice(begin, min(begin + CHUNK, count)) for begin in range(0, count, CHUNK)]


def feed_forward(piece_count, carried_in, normed_in, *others):
    pieces = others[:piece_count]
    activated_out, slope_out, state_out, *others = others[piece_count:]
    held, carried, normed_c, hidden, activated, slope, arrived, leaving = others
    rows, width = carried.shape
    count = held.shape[0]
    begins = begins_of(pieces)
    copies = [
        pltpu.make_async_copy(
            piece, held.at[pl.ds(begins[index], piece.shape[0]), :], arrived.at[index]
        )
        for index, piece in enumerate(pieces)
    ]
    norm_copy = pltpu.make_async_copy(normed_in, normed_c, arrived.at[piece_count])
    carried_copy = pltpu.make_async_copy(carried_in, carried, arrived.at[piece_count + 1])
    norm_copy.start()
    for copy in copies:
        copy.start()
    carried_copy.start()
    norm_copy.wait()
    chunks = hidden_chunks(count)
    waited = 0
    outgoing = []

    def project(chunk):
        hidden[:, chunk] = dot(normed_c[...], held[chunk, :width], CONTRACT_LAST)

    def wait_until(row):
        nonlocal waited
        while waited < piece_count and begins[waited] < row:
            copies[waited].wait()
            waited += 1

    wait_until(chunks[0].stop)
    project(chunks[0])
    wait_until(count)
    for index, chunk in enumerate(chunks):
        if index + 1 < len(chunks):
            project(chunks[index + 1])
        for block in row_blocks(rows, 32):
            value, back = gelu_and_slope(hidden[block, chunk])
            activated[block, chunk] = value.astype(BF16)
            slope[block, chunk] = back.astype(BF16)
        for target, source in ((activated_out, activated), (slope_out, slope)):
            outgoing.append(
                pltpu.make_async_copy(
                    source.at[:, chunk], target.at[:, chunk], leaving.at[len(outgoing)]
                )
            )
            outgoing[-1].start()
    carried_copy.wait()
    carried[...] += dot(activated[...], held[:, width:])
    outgoing.append(pltpu.make_async_copy(carried, state_out, leaving.at[len(outgoing)]))
    outgoing[-1].start()
    for copy in outgoing:
        copy.wait()


def feed_back(first, last, segments, piece_count, places, gradient_in, middle, gain_2, normed_in, *others):
    kept, others = others[: 2 * len(segments)], others[2 * len(segments) :]
    if not first:
        total_in, *others = others
    pieces = others[:piece_count]
    grad_out, grad_middle, *others = others[piece_count:]
    if last:
        grad_gain, grad_attn, *others = others
    (
        held,
        gradient,
        normed_c,
        activated,
        slope,
        total,
        branch,
        grad_hidden,
        grad_weight,
        arrived,
        leaving,
    ) = others
    rows, width = gradient.shape
    own_rows = rows - 2 * MOST
    own = pl.ds(MOST, own_rows)
    count = held.shape[0]
    begins = begins_of(pieces)
    arrivals = Arrivals(arrived)
    left, right = pl.ds(0, width), pl.ds(width, width)

    def weight_half(half):
        return [
            arrivals.start(
                piece.at[:, half], held.at[pl.ds(begins[index], piece.shape[0]), half]
            )
            for index, piece in enumerate(pieces)
        ]

    def leave(half, offset):
        copies = []
        for index, piece in enumerate(pieces):
            size = piece.shape[0]
            copies.append(
                pltpu.make_async_copy(
                    grad_weight.at[pl.ds(begins[index], size), half],
                    grad_out.at[pl.ds(pl.multiple_of(places[index], 16), size), half],
                    leaving.at[offset + index],
                )
            )
            copies[-1].start()
        return copies

    got_gradient = arrivals.start(gradient_in, gradient)
    got_down = weight_half(right)
    got_act, got_slope, begin = [], [], 0
    for index, (column, size) in enumerate(segments):
        place = pl.ds(begin, size)
        act, back = kept[2 * index : 2 * index + 2]
        source = pl.ds(column, size)
        got_act.append(arrivals.start(act.at[own, source], activated.at[:, place]))
        got_slope.append(arrivals.start(back.at[:, source], slope.at[:, place]))
        begin += size
    got_norm = arrivals.start(normed_in.at[own, :], normed_c)
    got_up = weight_half(left)
    if not first:
        got_total = arrivals.start(total_in, total)
    got_gradient.wait()
    for block in row_blocks(rows, 64):
        branch[block, :] = gradient[block, :].astype(BF16)
    for copy in got_down + got_act:
        copy.wait()
    for chunk in row_blocks(count, count // 2):
        found = dot(activated[:, chunk], branch[own, :], CONTRACT_FIRST)
        grad_weight[chunk, width:] = found.astype(BF16)
    down_leaves = leave(right, 0)
    for copy in got_slope + [got_norm] + got_up:
        copy.wait()
    for chunk in hidden_chunks(count):
        grad_act = dot(branch[...], held[chunk, width:], CONTRACT_LAST)
        grad_hidden[:, chunk] = (grad_act * slope[:, chunk].astype(F32)).astype(BF16)
    for chunk in row_blocks(count, count // 2):
        found = dot(grad_hidden[MOST : MOST + own_rows, chunk], normed_c[...], CONTRACT_FIRST)
        grad_weight[chunk, :width] = found.astype(BF16)
    up_leaves = leave(left, piece_count)
    back = dot(grad_hidden[...], held[:, :width])
    if not first:
        got_total.wait()
        back = total[...] + back
    if not last:
        grad_middle[...] = back
    else:
        total[...] = back
        grad_gain[...] = jnp.zeros_like(grad_gain)

        def step(block):
            hat, inverse = normalised(middle[block, :])
            back = gradient[block, :] + norm_back(total[block, :], gain_2[...], hat, inverse)
            grad_middle[block, :] = back
            grad_attn[block, :] = back.astype(BF16)
            if own_block(block, rows):
                grad_gain[...] += jnp.sum(total[block, :] * hat, axis=0, keepdims=True)

        each_block(rows, 64, step)
    for copy in down_leaves + up_leaves:
        copy.wait()


def column_runs(parts, part, begin, width, group_width):
    stop = begin + width
    while begin < stop:
        group = begin // group_width
        end = min(stop, (group + 1) * group_width)
        place = group * parts * group_width + part * group_width + begin % group_width
        yield begin, end, place
        begin = end


def joining(parts, begin, group_width, source, joined):
    rows = joined.shape[0]
    count = source.shape[0]
    width = joined.shape[1] // parts // count
    across = source.shape[2] // width
    for part in range(parts):
        top = begin + part // across * rows
        left = part % across * width
        side = [source[at, top : top + rows, left : left + width] for at in range(count)]
        side = jnp.concatenate(side, axis=1)
        for first, end, place in column_runs(parts, part, 0, count * width, group_width):
            joined[:, place : place + end - first] = side[:, first:end]


def tabulating(begin, source, *others):
    layers = len(others) // 2
    groups, _, small = others[0].shape
    feats = small // GROUP
    own_heads = groups * GROUP // source.shape[0]
    wide = others[layers].shape[1] // 2
    deep = wide // GROUP
    thin = source.shape[1] - begin
    runs = deep // thin
    run_width = layers * own_heads * feats
    for target in others:
        target[...] = jnp.zeros_like(target)
    for layer in range(layers):
        tables, back_tables = others[layer], others[layers + layer]
        for index in range(groups * GROUP):
            group, place = index // GROUP, index % GROUP
            column = (layer * own_heads + index % own_heads) * feats
            across = slice(place * feats, (place + 1) * feats)
            again = slice(small + place * feats, small + (place + 1) * feats)
            for part in range(4):
                for run in range(runs):
                    top = part * wide + place * deep + run * thin
                    down = slice(top, top + thin)
                    if part < 2:
                        at = run * run_width + column
                        value = source[index // own_heads, begin : begin + thin, at : at + feats]
                    else:
                        value = jnp.full((thin, feats), -0.5, BF16)
                    tables[group, down, across] = value
                    if part < 2:
                        value = value if part < 1 else jnp.ones((thin, feats), BF16)
                        back_tables[group, down, across] = value
                        back_tables[group, down, again] = value


def parting(parts, group_width, pieces, *others):
    *sources, target = others
    count, rows, all_width = target.shape
    width = all_width // parts
    each = len(sources) // pieces
    starts = [0]
    for piece in range(pieces - 1):
        starts.append(starts[-1] + sources[piece * each].shape[1])
    for part in range(parts):
        for at in range(count):
            runs = []
            for begin, end, place in column_runs(parts, part, at * width, width, group_width):
                piece = max(at for at in range(pieces) if starts[at] <= place)
                run = slice(place - starts[piece], place - starts[piece] + end - begin)
                mine = sources[piece * each : (piece + 1) * each]
                total = mine[0][:, run].astype(F32)
                for source in mine[1:]:
                    total = total + source[:, run].astype(F32)
                runs.append(total)
            total = runs[0] if len(runs) == 1 else jnp.concatenate(runs, axis=1)
            target[at, :, part * width : (part + 1) * width] = total.astype(target.dtype)


def finishing(parts, *others):
    sources, targets = others[: -len(parts)], others[-len(parts) :]
    for layer, source in enumerate(sources):
        begin = 0
        for target, count in zip(targets, parts):
            for part in range(count):
                width = target.shape[-1]
                run = slice(begin, begin + width)
                total = source[0, :, run].astype(F32)
                for at in range(1, source.shape[0]):
                    total = total + source[at, :, run].astype(F32)
                if count > 1:
                    target[layer, part] = total
                else:
                    target[layer] = total
                begin += width


def adding_corner(near, far, to_x, to_y):
    half = to_x.shape[0]
    for target, place in ((to_x, slice(0, half)), (to_y, slice(half, 2 * half))):
        target[...] = (near[place, :].astype(F32) + far[place, :].astype(F32)).astype(BF16)


def adding_sides(near_x, far_x, near_y, far_y, from_x, from_y, to_x, to_y):
    half = from_x.shape[0]
    top, bottom = slice(0, half), slice(half, 2 * half)
    for near, far, place, more, target in (
        (near_x, far_x, top, None, to_x),
        (near_x, far_x, bottom, from_y, to_x),
        (near_y, far_y, top, from_x, to_y),
        (near_y, far_y, bottom, None, to_y),
    ):
        total = near[place, :].astype(F32) + far[place, :].astype(F32)
        if more is not None:
            total = total + more[...].astype(F32)
        target[place, :] = total.astype(BF16)


def whole(shape):
    return pl.BlockSpec(
        shape, lambda step, *_: (0,) * len(shape), pipeline_mode=pl.Buffered(buffer_count=1)
    )


def columns(rows, width):
    return pl.BlockSpec((rows, width), lambda step, *_: (0, step))


def leading(shape):
    return pl.BlockSpec(shape, lambda step, *_: (step,) + (0,) * (len(shape) - 1))


def struct(shape, dtype):
    return jax.ShapeDtypeStruct(shape, dtype)


ANYWHERE = pl.BlockSpec(memory_space=pltpu.HBM)


def kernel_call(kernel, steps, in_specs, out_specs, out_shape, scratch, flops, prefetch=0):
    return pl.pallas_call(
        kernel,
        grid_spec=pltpu.PrefetchScalarGridSpec(
            num_scalar_prefetch=prefetch,
            grid=(steps,),
            in_specs=in_specs,
            out_specs=out_specs,
            scratch_shapes=scratch,
        ),
        out_shape=out_shape,
        compiler_params=pltpu.CompilerParams(vmem_limit_bytes=VMEM_BYTES),
        cost_estimate=pl.CostEstimate(flops=flops, bytes_accessed=flops // 600, transcendentals=0),
    )


def run_attention_forward(state, gains, pieces, places, table, *, tables, ids, scale):
    rows, width = state.shape
    wide = tables[0].shape[1]
    groups, deep, small = table.shape
    blocks = rows // QUERY_ROWS
    return kernel_call(
        functools.partial(attention_forward, scale, len(pieces)),
        groups,
        [
            whole((rows, width)),
            whole((1, width)),
            whole((1, width)),
            leading((1, deep, small)),
            whole((rows, wide)),
            whole((rows, wide)),
            whole((rows, 1)),
            whole((blocks, 1, KEY_ROWS)),
            *[ANYWHERE for _ in pieces],
        ],
        [
            ANYWHERE,
            whole((rows, width)),
            columns(rows, wide),
            columns(rows, wide),
            columns(rows, wide),
            columns(rows, wide),
            whole((rows, width)),
            whole((rows, width)),
        ],
        [
            struct((width, 4 * width), BF16),
            struct((rows, width), BF16),
            struct((rows, width), F32),
            struct((rows, width), F32),
            struct((rows, width), BF16),
            struct((rows, width), BF16),
            struct((rows, width), F32),
            struct((rows, width), BF16),
        ],
        [
            pltpu.VMEM((groups, width, 4 * wide), BF16),
            pltpu.VMEM((rows, width), F32),
            pltpu.VMEM((rows, 3 * wide), F32),
            pltpu.VMEM((2 * rows, deep), BF16),
            pltpu.VMEM((2 * rows, small), BF16),
            pltpu.SemaphoreType.DMA((groups, len(pieces))),
            pltpu.SemaphoreType.DMA((groups,)),
        ],
        FORWARD_COST,
        1,
    )(places, state, gains[0][None], gains[1][None], table, *tables, *ids, *pieces)


def run_attention_backward(
    groups,
    carried,
    *,
    grad_middle,
    branch,
    state,
    gain,
    weights,
    places,
    table,
    back_table,
    tables,
    ids,
    kept,
    scale,
):
    rows, width = state.shape
    wide = tables[0].shape[1]
    all_groups, deep, small = table.shape
    first, last = groups[0] == 0, groups[-1] == all_groups - 1
    count = len(groups)
    normed_a, query, key, value, mixed = kept
    own_rows = rows - 2 * MOST
    blocks = rows // QUERY_ROWS
    copied = [branch, weights, mixed, query, key, value, normed_a, *tables]
    ending = [grad_middle, state, gain[None]] if last else []
    split = places.shape[0] > 1
    halves = 1 + split
    return kernel_call(
        functools.partial(attention_backward, first, last, scale, groups, split),
        1,
        [
            *[ANYWHERE] * (len(copied) + (not first)),
            *([whole((rows, width)), whole((rows, width)), whole((1, width))] if last else []),
            whole((count, deep, small)),
            whole((count,) + back_table.shape[1:]),
            whole((rows, 1)),
            whole((blocks, 1, KEY_ROWS)),
        ],
        [
            *([whole((rows, width)), whole((1, width))] if last else [whole((rows, width))]),
            *[ANYWHERE] * halves,
        ],
        [
            struct((rows, width), F32),
            *([struct((1, width), F32)] if last else []),
            *[struct((width // halves, count * 4 * wide), BF16)] * halves,
        ],
        [
            pltpu.VMEM((rows, width), BF16),
            pltpu.VMEM((count, width, 4 * wide), BF16),
            pltpu.VMEM((count, own_rows, wide), BF16),
            pltpu.VMEM((count, rows, wide), F32),
            pltpu.VMEM((count, rows, wide), F32),
            pltpu.VMEM((count, rows, wide), BF16),
            pltpu.VMEM((own_rows, width), BF16),
            pltpu.VMEM((rows, wide), F32),
            pltpu.VMEM((rows, wide), F32),
            pltpu.VMEM((rows, width), F32),
            pltpu.VMEM((count, width, 4 * wide), BF16),
            pltpu.VMEM((rows, wide), BF16),
            pltpu.VMEM((2 * rows, deep), BF16),
            pltpu.VMEM((2 * rows, small), F32),
            pltpu.VMEM((2 * rows, small), F32),
            pltpu.VMEM((rows, wide), F32),
            pltpu.VMEM((2 * rows, 2 * small), BF16),
            pltpu.VMEM((rows, 3 * wide), BF16),
            pltpu.SemaphoreType.DMA((5 + 6 * count,)),
            pltpu.SemaphoreType.DMA((count,) + places.shape),
        ],
        BACKWARD_COST // 3 * count,
        1,
    )(
        places,
        *copied,
        *([] if first else [carried]),
        *ending,
        table[groups[0] : groups[-1] + 1],
        back_table[groups[0] : groups[-1] + 1],
        *ids,
    )


def run_feed_forward(carried, normed_c, pieces):
    rows, width = carried.shape
    count = sum(piece.shape[0] for piece in pieces)
    return kernel_call(
        functools.partial(feed_forward, len(pieces)),
        1,
        [ANYWHERE] * (2 + len(pieces)),
        [ANYWHERE] * 3,
        [
            struct((rows, count), BF16),
            struct((rows, count), BF16),
            struct((rows, width), F32),
        ],
        [
            pltpu.VMEM((count, 2 * width), BF16),
            pltpu.VMEM((rows, width), F32),
            pltpu.VMEM((rows, width), BF16),
            pltpu.VMEM((rows, count), F32),
            pltpu.VMEM((rows, count), BF16),
            pltpu.VMEM((rows, count), BF16),
            pltpu.SemaphoreType.DMA((len(pieces) + 2,)),
            pltpu.SemaphoreType.DMA((2 * len(hidden_chunks(count)) + 1,)),
        ],
        FORWARD_COST // 3,
    )(carried, normed_c, *pieces)


def run_feed_back(gradient, middle, gain, normed_c, stretches, pieces, places, carried, last):
    rows, width = middle.shape
    count = sum(piece.shape[0] for piece in pieces)
    first = carried is None
    kept = [array for arrays, _, _ in stretches for array in arrays]
    segments = [(column, size) for _, column, size in stretches]
    arrivals = 2 + not_first(first) + 2 * len(pieces) + len(kept)
    return kernel_call(
        functools.partial(feed_back, first, last, segments, len(pieces)),
        1,
        [
            ANYWHERE,
            whole((rows, width)),
            whole((1, width)),
            *[ANYWHERE] * (1 + len(kept) + not_first(first) + len(pieces)),
        ],
        [
            ANYWHERE,
            whole((rows, width)),
            *([whole((1, width)), whole((rows, width))] if last else []),
        ],
        [
            struct((count, 2 * width), BF16),
            struct((rows, width), F32),
            *([struct((1, width), F32), struct((rows, width), BF16)] if last else []),
        ],
        [
            pltpu.VMEM((count, 2 * width), BF16),
            pltpu.VMEM((rows, width), F32),
            pltpu.VMEM((rows - 2 * MOST, width), BF16),
            pltpu.VMEM((rows - 2 * MOST, count), BF16),
            pltpu.VMEM((rows, count), BF16),
            pltpu.VMEM((rows, width), F32),
            pltpu.VMEM((rows, width), BF16),
            pltpu.VMEM((rows, count), BF16),
            pltpu.VMEM((count, 2 * width), BF16),
            pltpu.SemaphoreType.DMA((arrivals,)),
            pltpu.SemaphoreType.DMA((2 * len(pieces),)),
        ],
        FORWARD_COST // 2,
        1,
    )(
        places,
        gradient,
        middle,
        gain[None],
        normed_c,
        *kept,
        *([] if first else [carried]),
        *pieces,
    )


def not_first(first):
    return 0 if first else 1


HEAD_DEVICES = 4
CHUNK = 512
X, Y, CORE = 2, 4, 1
FORWARD_COST = 29_000_000_000
BACKWARD_COST = 40_000_000_000


def hop(values, bit):
    count = lax.axis_size("dp")
    return lax.ppermute(values, "dp", [(i, i ^ bit) for i in range(count)])


def exchange(values):
    return lax.all_to_all(values, "head", split_axis=0, concat_axis=0, tiled=True)


def together(*values):
    return lax.optimization_barrier(values)


def by_permutes():
    return lax.axis_size("dp") == 8 and lax.axis_size("head") == HEAD_DEVICES


def group_width(parts, width, wide):
    return wide if parts == 4 else width


def join_columns(source, parts, begin, rows, width, wide):
    count = source.shape[0]
    return kernel_call(
        functools.partial(joining, parts, begin, group_width(parts, count * width, wide)),
        1,
        [whole(source.shape)],
        whole((rows, parts * count * width)),
        struct((rows, parts * count * width), BF16),
        [],
        1_000_000,
    )(source)


def feature_tables(source, begin, shapes):
    return kernel_call(
        functools.partial(tabulating, begin),
        1,
        [whole(source.shape)],
        [whole(shape) for shape in shapes],
        [struct(shape, BF16) for shape in shapes],
        [],
        1_000_000,
    )(source)


def block_of(rows, columns_all, index):
    return pl.BlockSpec((rows, columns_all), lambda *_: (index, 0))


def part_columns(pieces, parts, wide):
    rows = pieces[0][-1].shape[0]
    columns_all = sum(piece[0].shape[1] for piece in pieces)
    shape = (HEAD_DEVICES, rows, columns_all // HEAD_DEVICES)
    return kernel_call(
        functools.partial(
            parting, parts, group_width(parts, columns_all // parts, wide), len(pieces)
        ),
        1,
        [block_of(rows, source.shape[1], 0) for piece in pieces for source in piece],
        whole(shape),
        struct(shape, BF16),
        [],
        1_000_000,
    )(*[source for piece in pieces for source in piece])


def finish(sources, parts):
    _, rows, width = sources[0].shape
    width = width // sum(parts)
    shapes = [
        (len(sources), count, rows, width) if count > 1 else (len(sources), rows, width)
        for count in parts
    ]
    return kernel_call(
        functools.partial(finishing, parts),
        1,
        [whole(source.shape) for source in sources],
        [whole(shape) for shape in shapes],
        [struct(shape, F32) for shape in shapes],
        [],
        1_000_000,
    )(*sources)


def next_chips(own):
    return hop(own, X), hop(own, Y), hop(own, CORE)


def halves_to_pass(over_x, over_y):
    half = over_x.shape[0] // 2
    return over_x[:half], over_y[half:]


def chip_across(passed):
    to_y, to_x = passed
    return hop(to_y, Y), hop(to_x, X)


def other_core(pieces):
    return tuple(hop(piece, CORE) for piece in pieces)


def piece_places(rows):
    own = lax.axis_index("dp")
    bits = [(0, 0), (X, 0), (Y, 0), (X | Y, 0), (X | Y, rows // 2)]
    return jnp.stack(
        [(own ^ (bit | core)) * rows + begin for core in (0, CORE) for bit, begin in bits]
    ).astype(jnp.int32)


def block_places(rows):
    own = lax.axis_index("dp")
    return jnp.stack(
        [(own ^ (bit | core)) * rows for core in (CORE, 0) for bit in (0, X, Y, X | Y)]
    ).astype(jnp.int32)


class Reduction:
    def __init__(self, far, slow):
        self.slow, self.stage, self.left = slow, 0, 1
        self.came = hop(far, CORE)

    def prepare(self):
        rows, width = self.near.shape[0] // 4, self.near.shape[1]
        half, shape = (rows // 2, width), (rows, width)
        if self.stage == 0:
            self.far = self.came
            kernel, operands = adding_corner, (self.near, self.far)
            specs, out = [block_of(rows, width, 3)] * 2, half
        else:
            kernel, operands = adding_sides, (self.near, self.far, self.near, self.far, *self.came)
            specs, out = [block_of(rows, width, at) for at in (1, 1, 2, 2)] + [whole(half)] * 2, shape
        self.sent = kernel_call(
            kernel, 1, specs, [whole(out)] * 2, [struct(out, BF16)] * 2, [], 1_000_000
        )(*operands)

    def send(self):
        to_x, to_y = self.sent
        self.came = hop(to_x, X), hop(to_y, Y)
        self.stage += 1
        self.left = self.slow[self.stage - 1]

    def arrays(self):
        return [self.near, self.far, *self.came]


class Sharing:
    def __init__(self, reductions, parts, wide, slow):
        self.reductions, self.parts, self.wide, self.slow = reductions, parts, wide, slow
        self.stage, self.left, self.came = 0, 0, ()

    def prepare(self):
        pieces = [reduction.arrays() for reduction in self.reductions]
        self.sent = part_columns(pieces, self.parts, self.wide)

    def send(self):
        self.came = exchange(self.sent)
        self.stage, self.left = 1, self.slow


class Traffic:
    def __init__(self):
        self.moving = []

    def slot(self, values):
        ready = []
        for item in self.moving:
            item.left -= 1
            if item.left <= 0:
                ready.append(item)
        values, came = together(values, [item.came for item in ready])
        for item, arrived in zip(ready, came):
            item.came = arrived
        sending = []
        for item in ready:
            if isinstance(item, Sharing):
                if item.stage == 0 and all(r.stage == 3 for r in item.reductions):
                    sending.append(item)
            elif item.stage < 2:
                sending.append(item)
            else:
                item.stage = 3
        for item in ready:
            if isinstance(item, Sharing) and item.stage == 0 and item not in sending:
                if all(r.stage == 3 for r in item.reductions):
                    sending.append(item)
        for item in sending:
            item.prepare()
        values, sent = together(values, [item.sent for item in sending])
        for item, prepared in zip(sending, sent):
            item.sent = prepared
            item.send()
        self.moving = [
            item
            for item in self.moving
            if item.stage < (1 if isinstance(item, Sharing) else 3) or item.left > 0
        ]
        return values


def grouped_columns(values, parts, wide):
    rows = values.shape[0]
    return values.reshape(rows, parts, -1, wide).swapaxes(1, 2).reshape(rows, -1)


def over_heads(part, parts, wide):
    rows = part.shape[0]
    if parts == 4:
        part = part.reshape(rows, -1, parts, wide).swapaxes(1, 2)
    part = part.reshape(rows, parts, -1)
    part = lax.psum_scatter(part, "head", scatter_dimension=2, tiled=True)
    return part.swapaxes(0, 1).astype(F32)


def shared_gain(values, stage):
    if stage < 3:
        return values + hop(values, (CORE, X, Y)[stage])
    bit = 1 << (stage - 3)
    return values + lax.ppermute(values, "head", [(i, i ^ bit) for i in range(HEAD_DEVICES)])


def with_halo(inputs, cotangent):
    count = lax.axis_size("head")
    both = jnp.concatenate([inputs, cotangent], axis=1)
    before = lax.ppermute(both[-MOST:], "head", [(i, i + 1) for i in range(count - 1)])
    after = lax.ppermute(both[:MOST], "head", [(i + 1, i) for i in range(count - 1)])
    joined = jnp.concatenate([before, both, after], axis=0).astype(F32)
    return joined[:, : inputs.shape[1]], joined[:, inputs.shape[1] :]


def window_ids(segment_ids, own_rows):
    padded = jnp.pad(segment_ids[0], (MOST, MOST), constant_values=-1)
    begin = lax.axis_index("head") * own_rows
    ids = lax.dynamic_slice(padded, (begin,), (own_rows + 2 * MOST,))
    place = jnp.arange(ids.shape[0])
    earlier = (ids[:, None] == ids[None, :]) & (place[None, :] < place[:, None])
    position = jnp.sum(earlier.astype(F32), axis=1)
    used = (ids >= ids[MOST]) & (ids <= ids[MOST + own_rows - 1])
    column = jnp.where(used, ids, -1)[:, None]
    row = jnp.where(used, ids, -2)
    starts = [
        min(max(b * QUERY_ROWS - MOST, 0), ids.shape[0] - KEY_ROWS)
        for b in range(ids.shape[0] // QUERY_ROWS)
    ]
    rows = jnp.stack([row[start : start + KEY_ROWS] for start in starts])[:, None, :]
    return position, (column, rows)


def rotary_tables(position, head_width):
    halves = head_width // 2
    frequency = jnp.exp(jnp.arange(halves, dtype=F32) * (-2.0 * math.log(10000.0) / head_width))
    angles = position[:, None] * frequency[None, :]
    cosine, sine = jnp.cos(angles), jnp.sin(angles)
    return (
        jnp.tile(jnp.concatenate([cosine, cosine], axis=1), (1, GROUP)),
        jnp.tile(jnp.concatenate([-sine, sine], axis=1), (1, GROUP)),
    )


def body(
    inputs,
    segment_ids,
    features,
    norm_gain,
    query_key_value,
    output_weight,
    up_weight,
    down_weight,
    cotangent,
):
    layer_count = norm_gain.shape[0]
    own_rows = inputs.shape[0]
    head_width = features.shape[3]
    feature_count = features.shape[2]
    scale = head_width ** (-0.25)
    own_place = slice(MOST, MOST + own_rows)

    in_rows, part_width = output_weight.shape[1:]
    groups = inputs.shape[1] // (GROUP * head_width)
    wide, small = GROUP * head_width, GROUP * feature_count
    table_shapes = [(groups, 4 * wide, small)] * layer_count + [
        (groups, 2 * wide, 2 * small)
    ] * layer_count
    chunks = []
    for layer in range(layer_count):
        chunks.append((4, *query_key_value[layer], output_weight[layer]))
        chunks.append((2, up_weight[layer], down_weight[layer]))
    stored = []
    if by_permutes():
        attention_places = piece_places(in_rows)
        grad_places = block_places(in_rows)
        feed_places = piece_places(up_weight.shape[1])[jnp.array([0, 1, 2, 5, 6, 7, 3, 4, 8, 9])]
        feature_rows = jnp.moveaxis(features, 3, 0).reshape(4, head_width // 4, -1)
        feature_rows = jnp.concatenate(list(feature_rows), axis=1)

        def join(index, came, begin=0):
            parts, *weights = chunks[index]
            return join_columns(came, parts, begin, *weights[-1].shape, wide)

        def gathered_columns(sent):
            return lax.all_gather(sent, "head", axis=0, tiled=False)

        sent = jnp.concatenate([jnp.concatenate(chunks[0][1:], axis=1), feature_rows])
        sent = jnp.broadcast_to(sent[None], (HEAD_DEVICES,) + sent.shape)
        sent, inputs, cotangent = together(sent, inputs, cotangent)
        came = exchange(sent)
        state, gradient = with_halo(inputs, cotangent)
        position, ids = window_ids(segment_ids, own_rows)
        tables = rotary_tables(position, head_width)
        both = []
        for layer in range(1, layer_count):
            q, k, v, o = chunks[2 * layer][1:]
            both.append(
                jnp.concatenate(
                    [
                        jnp.concatenate(pair, axis=1)
                        for pair in ((q, k), (v, o), chunks[2 * layer + 1][1:])
                    ]
                )
            )
        first_feed = jnp.concatenate(chunks[1][1:], axis=1)
        came, state, gradient, tables, ids, first_feed = together(
            came, state, gradient, tables, ids, first_feed
        )
        attend = functools.partial(run_attention_forward, tables=tables, ids=ids, scale=scale)
        own = join(0, came)
        came_feed = gathered_columns(first_feed)
        over_x, over_y, over_core = next_chips(own)
        made = feature_tables(came, in_rows, table_shapes)
        over_x, over_y, over_core, made, both = together(over_x, over_y, over_core, made, both)
        blocks, back_blocks = made[:layer_count], made[layer_count:]
        passed = halves_to_pass(over_x, over_y)
        across = chip_across(passed)
        own_feed = join(1, came_feed)
        for layer in range(layer_count):
            more = layer + 1 < layer_count
            near = (own, over_x, over_y) + tuple(across)
            far = (over_core,) + other_core(near[1:])
            attention_pieces = near + far
            own = own_feed
            state, own, sent = together(state, own, both[layer] if more else ())
            over_x, over_y, over_core = next_chips(own)
            came = gathered_columns(sent) if more else ()
            weights, *kept, middle, normed_c = attend(
                state,
                norm_gain[layer],
                attention_pieces,
                attention_places,
                blocks[layer],
            )

            middle, over_x, over_y, over_core = together(middle, over_x, over_y, over_core)
            sides = own, over_x, over_y
            passed = halves_to_pass(over_x, over_y)
            carried, passed = together(middle, passed)
            across = chip_across(passed)
            far_sides = (over_core,) + other_core(sides[1:])
            near_kept = run_feed_forward(carried, normed_c, sides)

            carried, across, far_sides = together(near_kept[2], across, far_sides)
            far_across = other_core(across)
            if more:
                carried, came = together(carried, came)
                carried, own = together(carried, join(2 * layer + 2, came))
                over_x, over_y, over_core = next_chips(own)
            last_pieces = across + far_across
            feed_pieces = sides, far_sides, across, far_across
            far_kept = run_feed_forward(carried, normed_c, far_sides)

            carried = far_kept[2]
            if more:
                carried, over_x, over_y, over_core = together(carried, over_x, over_y, over_core)
                passed = halves_to_pass(over_x, over_y)
                carried, passed = together(carried, passed)
                across = chip_across(passed)
            last_kept = run_feed_forward(carried, normed_c, last_pieces)
            hidden_kept = near_kept[:2], far_kept[:2], last_kept[:2]
            stored.append(
                (state, weights, kept, middle, normed_c, hidden_kept, feed_pieces)
            )
            state = last_kept[2]
            if more:
                state, across, came = together(state, across, came)
                own_feed = join(2 * layer + 3, came, 2 * in_rows)
    else:
        state, gradient = with_halo(inputs, cotangent)
        position, ids = window_ids(segment_ids, own_rows)
        tables = rotary_tables(position, head_width)
        attend = functools.partial(run_attention_forward, tables=tables, ids=ids, scale=scale)
        all_features = lax.all_gather(features, "head", axis=1, tiled=True)
        shaped = all_features.reshape(layer_count, -1, GROUP, feature_count, head_width)
        eye = jnp.eye(GROUP, dtype=BF16)
        block = jnp.einsum("lghmw,hk->lghwkm", shaped, eye).reshape(layer_count, groups, wide, small)
        ones = jnp.kron(eye, jnp.ones((head_width, feature_count), BF16))
        ones = jnp.broadcast_to(ones, block.shape)
        blocks = jnp.concatenate([block, block, ones * -0.5, ones * -0.5], axis=2)
        back_blocks = jnp.concatenate([block, ones], axis=2)
        back_blocks = jnp.concatenate([back_blocks, back_blocks], axis=3)
        owned = []
        for parts, *weights in chunks:
            rows = weights[-1].shape[0]
            joined = jnp.stack(weights)
            joined = lax.all_gather(joined, "head", axis=2, tiled=True)
            joined = lax.all_gather(joined, "dp", axis=1, tiled=True)
            joined = joined.swapaxes(0, 1).reshape(joined.shape[1], -1)
            owned.append(grouped_columns(joined, parts, wide) if parts == 4 else joined)
        middle_row = inputs.shape[1] // 2
        attention_places = jnp.array([0, middle_row], jnp.int32)
        size = up_weight.shape[1] * lax.axis_size("dp") // 8
        feed_places = jnp.array([0, 4 * size, 3 * size, 7 * size], jnp.int32)
        for layer in range(layer_count):
            own_attention, own_feed = owned[2 * layer], owned[2 * layer + 1]
            weights, *kept, middle, normed_c = attend(
                state,
                norm_gain[layer],
                (own_attention[:middle_row], own_attention[middle_row:]),
                attention_places,
                blocks[layer],
            )
            size = own_feed.shape[0] // 8
            feed_pieces = [
                (own_feed[begin * size : end * size],) for begin, end in ((0, 3), (4, 7), (3, 4), (7, 8))
            ]
            near_kept = run_feed_forward(middle, normed_c, feed_pieces[0])
            far_kept = run_feed_forward(near_kept[2], normed_c, feed_pieces[1])
            last_kept = run_feed_forward(far_kept[2], normed_c, feed_pieces[2] + feed_pieces[3])
            hidden_kept = near_kept[:2], far_kept[:2], last_kept[:2]
            stored.append(
                (state, weights, kept, middle, normed_c, hidden_kept, feed_pieces)
            )
            state = last_kept[2]
    outputs = state[own_place].astype(BF16)

    gains = [None] * layer_count
    shares = [None] * layer_count
    traffic = Traffic()
    summing = []
    for layer in reversed(range(layer_count)):
        before, weights, kept, middle, normed_c, hidden_kept, feed_pieces = stored[layer]
        near_kept, far_kept, corner_kept = hidden_kept
        side, corner = near_kept[0].shape[1], corner_kept[0].shape[1] // 2
        stretches = [
            (near_kept, 0, side),
            (far_kept, 0, side),
            (corner_kept, 0, corner),
            (corner_kept, corner, corner),
        ]
        feed = (middle, norm_gain[layer, 1], normed_c)
        attend_back = functools.partial(
            run_attention_backward,
            state=before,
            gain=norm_gain[layer, 0],
            weights=weights,
            table=blocks[layer],
            back_table=back_blocks[layer],
            tables=tables,
            ids=ids,
            kept=kept,
            scale=scale,
        )
        if layer > 0 or not by_permutes():
            pieces = [piece for part in feed_pieces for piece in part]
            feed_grad, grad_middle, gain_c, branch = run_feed_back(
                gradient, *feed, stretches, pieces, feed_places, None, True
            )
            feed_part = lax.psum_scatter(feed_grad, "dp", scatter_dimension=0, tiled=True)
            gradient, gain_a, *grad = attend_back(
                tuple(range(groups)),
                None,
                grad_middle=grad_middle,
                branch=branch,
                places=grad_places if by_permutes() else jnp.zeros((1,), jnp.int32),
            )
            if by_permutes():
                gains[layer] = jnp.concatenate([gain_a, gain_c])
                attention_sum = Reduction(grad[0], (1, 1))
                attention_sum.near, attention_sum.left = grad[1], 2
                traffic.moving.append(attention_sum)
                summing.append((layer, feed_part, attention_sum))
                continue
            [grad] = grad
            attention_part = lax.psum_scatter(grad, "dp", scatter_dimension=0, tiled=True)
            gains[layer] = jnp.concatenate([gain_a, gain_c])
            shares[layer] = over_heads(feed_part, 2, wide), over_heads(attention_part, 4, wide)
            continue
        relative = [
            jnp.array(begins_of(feed_pieces[at] + feed_pieces[2 + at])[:-1], jnp.int32) for at in (0, 1)
        ]
        gradient = traffic.slot(gradient)
        feed_far, carried = run_feed_back(
            gradient,
            *feed,
            [stretches[1], stretches[3]],
            feed_pieces[1] + feed_pieces[3],
            relative[1],
            None,
            False,
        )
        carried, feed_far = traffic.slot((carried, feed_far))
        feed_sum = Reduction(feed_far, (1, 1))
        traffic.moving.append(feed_sum)
        feed_near, grad_middle, gain_c, branch = run_feed_back(
            gradient,
            *feed,
            [stretches[0], stretches[2]],
            feed_pieces[0] + feed_pieces[2],
            relative[0],
            carried,
            True,
        )
        feed_sum.near = feed_near
        feed_share = Sharing([feed_sum], 2, wide, 2)
        traffic.moving.append(feed_share)
        carried, attention_sums = None, []
        for call_groups in (tuple(range(groups - 1)), (groups - 1,)):
            branch, grad_middle, carried = traffic.slot((branch, grad_middle, carried))
            if attention_sums:
                traffic.moving.append(attention_sums[-1])
                for later, feed_part, attention_sum in summing:
                    carried, feed_part = together(carried, feed_part)
                    share = Sharing([], 2, wide, 1)
                    share.sent = part_columns([[feed_part]], 2, wide)
                    parted = part_columns([attention_sum.arrays()], 4, wide)
                    carried, share.sent, parted = together(carried, share.sent, parted)
                    share.send()
                    traffic.moving.append(share)
                    parted = lax.psum_scatter(parted, "head", scatter_dimension=0, tiled=True)
                    shares[later] = share, parted
            carried, *gain_a, far, near = attend_back(
                call_groups, carried, grad_middle=grad_middle, branch=branch, places=grad_places
            )
            carried, far, near = together(carried, far, near)
            attention_sums.append(Reduction(far, (1, 1)))
            attention_sums[-1].near = near
        gradient = carried
        gains[layer] = jnp.concatenate([*gain_a, gain_c])
        traffic.moving.append(attention_sums[-1])
        attention_share = Sharing(attention_sums, 4, wide, 1)
        traffic.moving.append(attention_share)
        shares[layer] = feed_share, attention_share
    if by_permutes():
        gain_all = jnp.stack(gains)
        input_grad = gradient[own_place]
        gain_all = traffic.slot(gain_all)
        gain_all = shared_gain(gain_all, 0)
        gain_all = traffic.slot(gain_all)
        gain_all, outputs, input_grad = together(gain_all, outputs, input_grad)
        gain_all, parted = together(gain_all, [share[1] for share in shares[1:]])
        gain_all = shared_gain(shared_gain(gain_all, 1), 2)
        gain_all = traffic.slot(gain_all)
        up_grad, down_grad = finish([share[0].came for share in shares], (1, 1))
        gain_all = shared_gain(shared_gain(gain_all, 3), 4)
        gain_all, up_grad, down_grad = together(gain_all, up_grad, down_grad)
        while traffic.moving:
            gain_all = traffic.slot(gain_all)
        gain_total = gain_all
        qkv_grad, out_grad = finish([shares[0][1].came] + parted, (3, 1))
    else:
        gain_total = lax.psum(jnp.stack(gains), ("dp", "head"))
        input_grad = gradient[own_place]
        results = [(a[:3], a[3], f[0], f[1]) for f, a in shares]
        qkv_grad, out_grad, up_grad, down_grad = (
            jnp.stack(list(kind)) for kind in zip(*results)
        )
    return (
        outputs,
        input_grad,
        gain_total[:, 0],
        gain_total[:, 1],
        qkv_grad,
        out_grad,
        up_grad,
        down_grad,
    )


def solution(mesh):
    in_specs = (
        P(("dp", "head"), None),
        P("dp", None),
        P(None, "head", None, None),
        P(),
        P(None, None, "dp", "head"),
        P(None, "dp", "head"),
        P(None, "dp", "head"),
        P(None, "dp", "head"),
        P(("dp", "head"), None),
    )
    out_specs = (
        P(("dp", "head"), None),
        P(("dp", "head"), None),
        P(),
        P(),
        P(None, None, "dp", "head"),
        P(None, "dp", "head"),
        P(None, "dp", "head"),
        P(None, "dp", "head"),
    )
    return jax.shard_map(body, mesh=mesh, in_specs=in_specs, out_specs=out_specs, check_vma=False)
```

time: 581 us -> 504 us (0.87)
  Pallas kernels: 321 us -> 268 us
  local copies, waits for them, and re-layouts: 63 us -> 42.6 us
  starting transfers between devices: 90.7 us -> 75 us
  between operations: 2.05 us -> 15.1 us
    pallas_call x30 -> x32, Pallas kernels: 319 us -> 265 us  [the longest x3 66.7 us: run_attention_backward(): kernel_call(functools.partial(attention_backward, first, last, scale, gro...]
    all_to_all x8 -> x4, waiting for transfers between devices: 29.3 us -> 8.96 us  [exchange(): lax.all_to_all(values, 'head', split_axis=0, concat_axis=0, tiled=True)]
    ppermute x59, waiting for transfers between devices: 40.9 us -> 56.6 us  [hop(): return lax.ppermute(values, 'dp', [(i, i ^ bit) for i in range(count)])]
    all_to_all x8 -> x4, starting transfers between devices: 36.1 us -> 21.1 us  [exchange(): lax.all_to_all(values, 'head', split_axis=0, concat_axis=0, tiled=True)]
    reduce_scatter x0 -> x2, waiting for transfers between devices: none -> 12.1 us  [the longest x1 12.1 us: body(): parted = lax.psum_scatter(parted, 'head', scatter_dimension=0, tiled=True)]
    ppermute x2, waiting for transfers between devices: 11.4 us -> 5.61 us  [shared_gain(): lax.ppermute(values, 'head', [(i, i ^ bit) for i in range(HEAD_DEVICES)])]
    unnamed x92 -> x121, local copies, waits for them, and re-layouts: 17.6 us -> 13 us
  transfers between devices with their start and end apart: 71 -> 71, of which waited for: 20 -> 27; matrix products, arithmetic and copies ran while one was open for 9% -> 7% of each run, Pallas kernels for 49% -> 45%
where the time goes in v3:
time: 504 us; the launch traced here: 495 us
  Pallas kernels  268 us (53%)
  waiting for transfers between devices  86.9 us (17%)
  starting transfers between devices  75 us (15%)
  local copies, waits for them, and re-layouts  42.6 us (8%)
  between operations  15.1 us (3%)
  other arithmetic  6.77 us (1%)
    pallas_call x3, Pallas kernels, run_attention_backward(): kernel_call(functools.partial(attention_backward, first, last, scale, gro...  66.7 us
    ppermute x59, waiting for transfers between devices, hop(): return lax.ppermute(values, 'dp', [(i, i ^ bit) for i in range(count)])  56.6 us
    pallas_call x6, Pallas kernels, run_feed_forward(): kernel_call(functools.partial(feed_forward, len(pieces)), 1, [ANYWHERE] *...  53.6 us
    pallas_call x3, Pallas kernels, run_feed_back(): kernel_call(functools.partial(feed_back, first, last, segments, len(piece...  53.1 us
    pallas_call x2, Pallas kernels, run_attention_forward(): kernel_call(functools.partial(attention_forward, scale, len(pieces)), gro...  42.2 us
    ppermute x59, starting transfers between devices, hop(): return lax.ppermute(values, 'dp', [(i, i ^ bit) for i in range(count)])  40.8 us
    all_to_all x4, starting transfers between devices, exchange(): lax.all_to_all(values, 'head', split_axis=0, concat_axis=0, tiled=True)  21.1 us
    pallas_call x8, Pallas kernels, prepare(): kernel_call(kernel, 1, specs, [whole(out)] * 2, [struct(out, BF16)] * 2,...  20.8 us
  transfers between devices with their start and end apart: 71, of which 27 were waited for; matrix products, arithmetic and copies ran while one was open for 7% of the time, Pallas kernels for 45%

profile of v3, /device:TPU:0, one launch (start us, length us, event | category | flops | bytes accessed | tf_op | source)
XLA Modules:
  0.0 494.7 jit_solution(2817796416704584880)
XLA Ops:
  12.6 6.3 %all-to-all-start = ((bf16[4,112,768]{2,1,0:T(8,128)(2,1)}), bf16[4,112,768]{2,1,0:T(8,128)(2,1)S(1)}, u32[]{:S(2)}, u32[]{:S(2)}) async-start(bf16[4,112,768]{2,1,0:T(8,128)(2,1)} %broadcast_in_dim.29), calls=%async_computation | async-start | bytes 1376256 | tf_op jit(solution)/shard_map/all_to_all | solution.py:966
  21.0 4.6 collective-permute-start
  32.2 2.3 collective-permute-done
  46.5 3.4 shard_map.181
  50.0 8.3 %collective-permute-done.3.others_2_ = bf16[96,3072]{1,0:T(8,128)(2,1)} collective-permute-done((bf16[96,3072]{1,0:T(8,128)(2,1)}, bf16[96,3072]{1,0:T(8,128)(2,1)}, u32[]{:S(2)}, u32[]{:S(2)}) %collective-permute-start.3) | collective-permute-done | bytes 589856 | tf_op jit(solution)/shard_map/ppermute | solution.py:962
  64.2 4.8 collective-permute-done.6.others_4_
  75.6 2.4 copy.87
  77.9 2.6 shard_map.179.others_0_.others_5_
  82.4 21.2 %shard_map.182 = (bf16[768,3072]{1,0:T(8,128)(2,1)}, bf16[640,768]{1,0:T(8,128)(2,1)}, f32[640,768]{1,0:T(8,128)}, f32[640,768]{1,0:T(8,128)}, bf16[640,768]{1,0...) custom-call(s32[10]{0:T(128)} %stack.132.places, ...), custom_call_target="tpu_custom_call" | custom-call | flops 28999999488 | bytes 48333332 | tf_op jit(solution)/shard_map/pallas_call | solution.py:737
  103.6 5.7 %collective-permute-done.12.others_2_.others_7_ = bf16[384,1536]{1,0:T(8,128)(2,1)S(1)} collective-permute-done((bf16[384,1536]{1,0:T(8,128)(2,1)}, bf16[384,1536]{1,0:T(8,128)(2,1)S(1)}, u32[]{:S(2)}, u32[]{:S(2)}) %collective-permute-start.12) | collective-permute-done | bytes 1179680 | tf_op jit(solution)/shard_map/ppermute | solution.py:962
  112.3 9.6 %shard_map.183 = (bf16[640,1152]{1,0:T(8,128)(2,1)}, bf16[640,1152]{1,0:T(8,128)(2,1)}, f32[640,768]{1,0:T(8,128)}) custom-call(f32[640,768]{1,0:T(8,128)} %get-tuple-element.256.carried_in.middle, bf16[640,768]{1,0:T(8,128)(2,1)} %get-tuple-element.257.normed_in, bf16[384,1536]{1,0:T(8,128)(2,1)} %shard_map.179.others_0_.others_5_, ...), custom_call_target="tpu_custom_call" | custom-call | flops 9666666496 | bytes 16111111 | tf_op jit(solution)/shard_map/pallas_call | solution.py:872
  121.9 4.2 collective-permute-done.14.others_0_.others_8_
  127.4 2.5 shard_map.184.others_0_
  131.4 9.5 %shard_map.185 = (bf16[640,1152]{1,0:T(8,128)(2,1)}, bf16[640,1152]{1,0:T(8,128)(2,1)}, f32[640,768]{1,0:T(8,128)}) custom-call(f32[640,768]{1,0:T(8,128)} %get-tuple-element.266.carried_in, bf16[640,768]{1,0:T(8,128)(2,1)} %get-tuple-element.257.normed_in, bf16[384,1536]{1,0:T(8,128)(2,1)} %copy-done.38, ...), custom_call_target="tpu_custom_call" | custom-call | flops 9666666496 | bytes 16111111 | tf_op jit(solution)/shard_map/pallas_call | solution.py:872
  141.0 4.9 collective-permute-done.19.others_2_
  149.9 7.6 %shard_map.186 = (bf16[640,768]{1,0:T(8,128)(2,1)}, bf16[640,768]{1,0:T(8,128)(2,1)}, f32[640,768]{1,0:T(8,128)}) custom-call(f32[640,768]{1,0:T(8,128)} %get-tuple-element.275.carried_in, bf16[640,768]{1,0:T(8,128)(2,1)} %get-tuple-element.257.normed_in, bf16[192,1536]{1,0:T(8,128)(2,1)} %collective-permute-done.14.others_0_.others_8_, ...), custom_call_target="tpu_custom_call" | custom-call | flops 9666666496 | bytes 16111111 | tf_op jit(solution)/shard_map/pallas_call | solution.py:872
  158.1 2.8 shard_map.187.others_0_.others_8_
  164.0 21.1 %shard_map.188 = (bf16[768,3072]{1,0:T(8,128)(2,1)}, bf16[640,768]{1,0:T(8,128)(2,1)}, f32[640,768]{1,0:T(8,128)}, f32[640,768]{1,0:T(8,128)}, bf16[640,768]{1,0...) custom-call(s32[10]{0:T(128)} %stack.132.places, ...), custom_call_target="tpu_custom_call" | custom-call | flops 28999999488 | bytes 48333332 | tf_op jit(solution)/shard_map/pallas_call | solution.py:737
  185.1 4.5 collective-permute-done.30.others_2_.others_10_
  194.5 9.5 %shard_map.189 = (bf16[640,1152]{1,0:T(8,128)(2,1)}, bf16[640,1152]{1,0:T(8,128)(2,1)}, f32[640,768]{1,0:T(8,128)}) custom-call(f32[640,768]{1,0:T(8,128)} %get-tuple-element.294.carried_in.middle, bf16[640,768]{1,0:T(8,128)(2,1)} %get-tuple-element.291.normed_in, bf16[384,1536]{1,0:T(8,128)(2,1)} %shard_map.187.others_0_.others_8_, ...), custom_call_target="tpu_custom_call" | custom-call | flops 9666666496 | bytes 16111111 | tf_op jit(solution)/shard_map/pallas_call | solution.py:872
  204.0 3.5 collective-permute-done.32.others_0_.others_14_
  208.8 9.6 %shard_map.190 = (bf16[640,1152]{1,0:T(8,128)(2,1)}, bf16[640,1152]{1,0:T(8,128)(2,1)}, f32[640,768]{1,0:T(8,128)}) custom-call(f32[640,768]{1,0:T(8,128)} %get-tuple-element.301.carried_in, bf16[640,768]{1,0:T(8,128)(2,1)} %get-tuple-element.291.normed_in, bf16[384,1536]{1,0:T(8,128)(2,1)} %collective-permute-done.31.others_0_.others_11_, ...), custom_call_target="tpu_custom_call" | custom-call | flops 9666666496 | bytes 16111111 | tf_op jit(solution)/shard_map/pallas_call | solution.py:872
  219.5 7.8 %shard_map.191 = (bf16[640,768]{1,0:T(8,128)(2,1)}, bf16[640,768]{1,0:T(8,128)(2,1)}, f32[640,768]{1,0:T(8,128)}) custom-call(f32[640,768]{1,0:T(8,128)} %get-tuple-element.307.carried_in, bf16[640,768]{1,0:T(8,128)(2,1)} %get-tuple-element.291.normed_in, bf16[192,1536]{1,0:T(8,128)(2,1)} %copy-done.43, ...), custom_call_target="tpu_custom_call" | custom-call | flops 9666666496 | bytes 16111111 | tf_op jit(solution)/shard_map/pallas_call | solution.py:872
  227.3 23.3 %shard_map.192 = (bf16[3072,1536]{1,0:T(8,128)(2,1)}, f32[640,768]{1,0:T(8,128)}, f32[1,768]{1,0:T(1,128)}, bf16[640,768]{1,0:T(8,128)(2,1)}) custom-call(s32[10]{0:T(128)} %gather_fusion, f32[640,768]{1,0:T(8,128)} %get-tuple-element.233.gradient_in, f32[640,768]{1,0:T(8,128)} %get-tuple-element.294.carried_in.middle, f32[1,768]{1,0:T(1,128)} %get-tuple-element.506.gain_2, ...), custom_call_target="tpu_custom_call" | custom-call | flops 14499999744 | bytes 24166666 | tf_op jit(solution)/shard_map/pallas_call | solution.py:903
  251.3 30.2 %shard_map.193 = (f32[640,768]{1,0:T(8,128)}, f32[1,768]{1,0:T(1,128)}, bf16[384,3072]{1,0:T(8,128)(2,1)}, bf16[384,3072]{1,0:T(8,128)(2,1)}) custom-call(s32[8]{0:T(128)} %stack.112.places, bf16[640,768]{1,0:T(8,128)(2,1)} %get-tuple-element.312.branch_in, bf16[768,3072]{1,0:T(8,128)(2,1)} %get-tuple-element.313.weights_in, ...), custom_call_target="tpu_custom_call" | custom-call | flops 40000000000 | bytes 66666664 | tf_op jit(solution)/shard_map/pallas_call | solution.py:814
  281.6 14.2 %shard_map.194 = (bf16[1536,1536]{1,0:T(8,128)(2,1)}, f32[640,768]{1,0:T(8,128)}) custom-call(s32[5]{0:T(128)} %constant.53.clone.places, f32[640,768]{1,0:T(8,128)} %get-tuple-element.321.gradient_in, f32[640,768]{1,0:T(8,128)} %get-tuple-element.256.carried_in.middle, f32[1,768]{1,0:T(1,128)} %get-tuple-element.507.gain_2, ...), custom_call_target="tpu_custom_call" | custom-call | flops 14499999744 | bytes 24166666 | tf_op jit(solution)/shard_map/pallas_call | solution.py:903
  305.7 15.7 %shard_map.196 = (bf16[1536,1536]{1,0:T(8,128)(2,1)}, f32[640,768]{1,0:T(8,128)}, f32[1,768]{1,0:T(1,128)}, bf16[640,768]{1,0:T(8,128)(2,1)}) custom-call(s32[5]{0:T(128)} %constant.53.clone.places, f32[640,768]{1,0:T(8,128)} %get-tuple-element.321.gradient_in, f32[640,768]{1,0:T(8,128)} %get-tuple-element.256.carried_in.middle, ...), custom_call_target="tpu_custom_call" | custom-call | flops 14499999744 | bytes 24166666 | tf_op jit(solution)/shard_map/pallas_call | solution.py:903
  322.2 3.0 shard_map.197
  325.2 2.8 shard_map.198
  332.1 21.3 %shard_map.199 = (f32[640,768]{1,0:T(8,128)}, bf16[384,2048]{1,0:T(8,128)(2,1)}, bf16[384,2048]{1,0:T(8,128)(2,1)}) custom-call(s32[8]{0:T(128)} %stack.112.places, bf16[640,768]{1,0:T(8,128)(2,1)} %get-tuple-element.374.branch_in, bf16[768,3072]{1,0:T(8,128)(2,1)} %get-tuple-element.355.weights_in, bf16[640,768]{1,0:T(8,128)(2,1)} %get-tuple-element.356.mixed_in, ...), custom_call_target="tpu_custom_call" | custom-call | flops 26666665984 | bytes 44444444 | tf_op jit(solution)/shard_map/pallas_call | solution.py:814
  353.5 3.0 collective-permute-done.44.from_x
  357.4 4.4 shard_map.200
  363.9 2.9 shard_map.202
  366.7 2.5 shard_map.201
  369.3 7.1 %all-to-all-start.1 = ((bf16[4,384,384]{2,1,0:T(8,128)(2,1)}), bf16[4,384,384]{2,1,0:T(8,128)(2,1)S(1)}, u32[]{:S(2)}, u32[]{:S(2)}) async-start(bf16[4,384,384]{2,1,0:T(8,128)(2,1)} %shard_map.201), calls=%async_computation.2 | async-start | bytes 2359296 | tf_op jit(solution)/shard_map/all_to_all | solution.py:966
  376.4 15.2 %shard_map.203 = (f32[640,768]{1,0:T(8,128)}, f32[1,768]{1,0:T(1,128)}, bf16[384,1024]{1,0:T(8,128)(2,1)}, bf16[384,1024]{1,0:T(8,128)(2,1)}) custom-call(s32[8]{0:T(128)} %stack.112.places, bf16[640,768]{1,0:T(8,128)(2,1)} %get-tuple-element.374.branch_in, bf16[768,3072]{1,0:T(8,128)(2,1)} %get-tuple-element.355.weights_in, ...), custom_call_target="tpu_custom_call" | custom-call | flops 13333332992 | bytes 22222222 | tf_op jit(solution)/shard_map/pallas_call | solution.py:814
  394.1 8.9 %all-to-all-done.1.others_1_ = bf16[4,384,384]{2,1,0:T(8,128)(2,1)S(1)} async-done(((bf16[4,384,384]{2,1,0:T(8,128)(2,1)}), bf16[4,384,384]{2,1,0:T(8,128)(2,1)S(1)}, u32[]{:S(2)}, u32[]{:S(2)}) %all-to-all-start.1) | async-done | bytes 1179680 | tf_op jit(solution)/shard_map/all_to_all | solution.py:966
  403.0 4.6 shard_map.204
  411.3 3.7 all-to-all-start.2
  427.5 2.6 shard_map.207
  434.1 2.4 slice.211
  437.8 12.1 %reduce-scatter.5.cloned.1.call-done.others_1_ = bf16[1,96,768]{2,1,0:T(8,128)(2,1)} async-done(((bf16[4,96,768]{2,1,0:T(8,128)(2,1)}), bf16[1,96,768]{2,1,0:T(8,128)(2,1)}) %reduce-scatter.5.cloned.1.call-update) | async-done | bytes 147472 | tf_op jit(solution)/shard_map/reduce_scatter | solution.py:1487
  458.1 3.3 shard_map.209
  461.4 4.1 all-to-all-start.3
  467.5 5.6 %collective-permute-done.61 = f32[2,2,768]{2,1,0:T(2,128)S(1)} collective-permute-done((f32[2,2,768]{2,1,0:T(2,128)S(1)}, f32[2,2,768]{2,1,0:T(2,128)S(1)}, u32[]{:S(2)}, u32[]{:S(2)}) %collective-permute-start.61) | collective-permute-done | bytes 12320 | tf_op jit(solution)/shard_map/ppermute | solution.py:1179
  473.1 4.8 collective-permute-start.62
  477.9 3.1 shard_map.210
  481.0 2.3 copy.105
  (314 shorter events, 118.0 us)
Async XLA Ops:
  12.6 26.7 %all-to-all-start = ((bf16[4,112,768]{2,1,0:T(8,128)(2,1)}), bf16[4,112,768]{2,1,0:T(8,128)(2,1)S(1)}, u32[]{:S(2)}, u32[]{:S(2)}) async-start(bf16[4,112,768]{2,1,0:T(8,128)(2,1)} %broadcast_in_dim.29), calls=%async_computation | async-start | bytes 1376256 | tf_op jit(solution)/shard_map/all_to_all | solution.py:966
  18.9 56.6 %all-gather.5.cloned.1.call-start = ((), (), s32[]{:S(2)}) async-start(), calls=%async_computation.8 | async-start | bytes 1474560 | tf_op jit(solution)/shard_map/all_gather | solution.py:1261
  21.0 13.5 %collective-permute-start = (bf16[64,1536]{1,0:T(8,128)(2,1)}, bf16[64,1536]{1,0:T(8,128)(2,1)}, u32[]{:S(2)}, u32[]{:S(2)}) collective-permute-start(bf16[64,1536]{1,0:T(8,128)(2,1)} %get-tuple-element.486), channel_id=1, source_target_pairs={{0,1},{1,2},{2,3},{4,5},{5,6},{6,7},{8,9},{9,10},{10,11},{12,13},{... | collective-permute-start | bytes 589832 | tf_op jit(solution)/shard_map/ppermute | solution.py:1185
  39.5 88.0 %all-gather.7.cloned.1.call-start = ((), (), s32[]{:S(2)}) async-start(), calls=%async_computation.9 | async-start | bytes 2211840 | tf_op jit(solution)/shard_map/all_gather | solution.py:1261
  42.2 16.1 %collective-permute-start.3 = (bf16[96,3072]{1,0:T(8,128)(2,1)}, bf16[96,3072]{1,0:T(8,128)(2,1)}, u32[]{:S(2)}, u32[]{:S(2)}) collective-permute-start(bf16[96,3072]{1,0:T(8,128)(2,1)} %shard_map.180.others_0_), channel_id=1, source_target_pairs={{0,16},{4,20},{8,24},{12,28},{16,0},{20,4},{24,8},{28,12},{1,17},{... | collective-permute-start | bytes 1769480 | tf_op jit(solution)/shard_map/ppermute | solution.py:962
  43.8 15.8 %collective-permute-start.2 = (bf16[96,3072]{1,0:T(8,128)(2,1)}, bf16[96,3072]{1,0:T(8,128)(2,1)}, u32[]{:S(2)}, u32[]{:S(2)}) collective-permute-start(bf16[96,3072]{1,0:T(8,128)(2,1)} %shard_map.180.others_0_), channel_id=1, source_target_pairs={{0,8},{4,12},{8,0},{12,4},{16,24},{20,28},{24,16},{28,20},{1,9},{5... | collective-permute-start | bytes 1769480 | tf_op jit(solution)/shard_map/ppermute | solution.py:962
  63.6 18.8 %collective-permute-start.7 = (bf16[96,3072]{1,0:T(8,128)(2,1)}, bf16[96,3072]{1,0:T(8,128)(2,1)}, u32[]{:S(2)}, u32[]{:S(2)}) collective-permute-start(bf16[96,3072]{1,0:T(8,128)(2,1)} %collective-permute-done.2.others_1_), channel_id=1, source_target_pairs={{0,4},{4,0},{8,12},{12,8},{16,20},{20,16},{24,28},{28,24},{1,5},{5... | collective-permute-start | bytes 1769480 | tf_op jit(solution)/shard_map/ppermute | solution.py:962
  63.6 18.8 %collective-permute-start.8 = (bf16[96,3072]{1,0:T(8,128)(2,1)}, bf16[96,3072]{1,0:T(8,128)(2,1)}, u32[]{:S(2)}, u32[]{:S(2)}) collective-permute-start(bf16[96,3072]{1,0:T(8,128)(2,1)} %collective-permute-done.3.others_2_), channel_id=1, source_target_pairs={{0,4},{4,0},{8,12},{12,8},{16,20},{20,16},{24,28},{28,24},{1,5},{5... | collective-permute-start | bytes 1769480 | tf_op jit(solution)/shard_map/ppermute | solution.py:962
  80.6 286.2 %reduce-scatter.3.cloned.1.call-start = ((), (), s32[]{:S(2)}) async-start(), calls=%async_computation.6 | async-start | bytes 10616832 | tf_op jit(solution)/shard_map/reduce_scatter | solution.py:1426
  80.6 23.0 %collective-permute-start.13 = (bf16[384,1536]{1,0:T(8,128)(2,1)}, bf16[384,1536]{1,0:T(8,128)(2,1)S(1)}, u32[]{:S(2)}, u32[]{:S(2)}) collective-permute-start(bf16[384,1536]{1,0:T(8,128)(2,1)} %shard_map.179.others_0_.others_5_), channel_id=1, source_target_pairs={{0,4},{4,0},{8,12},{12,8},{16,20},{20,16},{24,28},{28,24},{1,5},{5... | collective-permute-start | bytes 3538952 | tf_op jit(solution)/shard_map/ppermute | solution.py:962
  81.2 28.2 %collective-permute-start.12 = (bf16[384,1536]{1,0:T(8,128)(2,1)}, bf16[384,1536]{1,0:T(8,128)(2,1)S(1)}, u32[]{:S(2)}, u32[]{:S(2)}) collective-permute-start(bf16[384,1536]{1,0:T(8,128)(2,1)} %shard_map.179.others_0_.others_5_), channel_id=1, source_target_pairs={{0,16},{4,20},{8,24},{12,28},{16,0},{20,4},{24,8},{28,12},{1,17},{... | collective-permute-start | bytes 3538952 | tf_op jit(solution)/shard_map/ppermute | solution.py:962
  81.9 28.1 %collective-permute-start.11 = (bf16[384,1536]{1,0:T(8,128)(2,1)}, bf16[384,1536]{1,0:T(8,128)(2,1)S(1)}, u32[]{:S(2)}, u32[]{:S(2)}) collective-permute-start(bf16[384,1536]{1,0:T(8,128)(2,1)} %shard_map.179.others_0_.others_5_), channel_id=1, source_target_pairs={{0,8},{4,12},{8,0},{12,4},{16,24},{20,28},{24,16},{28,20},{1,9},{5... | collective-permute-start | bytes 3538952 | tf_op jit(solution)/shard_map/ppermute | solution.py:962
  110.0 16.9 %collective-permute-start.16 = (bf16[384,1536]{1,0:T(8,128)(2,1)S(1)}, bf16[384,1536]{1,0:T(8,128)(2,1)}, u32[]{:S(2)}, u32[]{:S(2)}) collective-permute-start(bf16[384,1536]{1,0:T(8,128)(2,1)S(1)} %collective-permute-done.11.others_1_.others_6_), channel_id=1, source_target_pairs={{0,4},{4,0},{8,12},{12,8},{16,20},{20,16},{24,28},{28,24},{1,5},{5... | collective-permute-start | bytes 3538952 | tf_op jit(solution)/shard_map/ppermute | solution.py:962
  110.0 16.9 %collective-permute-start.17 = (bf16[384,1536]{1,0:T(8,128)(2,1)S(1)}, bf16[384,1536]{1,0:T(8,128)(2,1)}, u32[]{:S(2)}, u32[]{:S(2)}) collective-permute-start(bf16[384,1536]{1,0:T(8,128)(2,1)S(1)} %collective-permute-done.12.others_2_.others_7_), channel_id=1, source_target_pairs={{0,4},{4,0},{8,12},{12,8},{16,20},{20,16},{24,28},{28,24},{1,5},{5... | collective-permute-start | bytes 3538952 | tf_op jit(solution)/shard_map/ppermute | solution.py:962
  110.6 15.5 %collective-permute-start.14 = (bf16[192,1536]{1,0:T(8,128)(2,1)S(1)}, bf16[192,1536]{1,0:T(8,128)(2,1)}, u32[]{:S(2)}, u32[]{:S(2)}) collective-permute-start(bf16[192,1536]{1,0:T(8,128)(2,1)S(1)} %slice.175), channel_id=1, source_target_pairs={{0,16},{4,20},{8,24},{12,28},{16,0},{20,4},{24,8},{28,12},{1,17},{... | collective-permute-start | bytes 1769480 | tf_op jit(solution)/shard_map/ppermute | solution.py:962
  111.8 15.1 %collective-permute-start.15 = (bf16[192,1536]{1,0:T(8,128)(2,1)S(1)}, bf16[192,1536]{1,0:T(8,128)(2,1)}, u32[]{:S(2)}, u32[]{:S(2)}) collective-permute-start(bf16[192,1536]{1,0:T(8,128)(2,1)S(1)} %slice.176), channel_id=1, source_target_pairs={{0,8},{4,12},{8,0},{12,4},{16,24},{20,28},{24,16},{28,20},{1,9},{5... | collective-permute-start | bytes 1769480 | tf_op jit(solution)/shard_map/ppermute | solution.py:962
  126.9 21.4 %collective-permute-start.21 = (bf16[192,1536]{1,0:T(8,128)(2,1)}, bf16[192,1536]{1,0:T(8,128)(2,1)S(1)}, u32[]{:S(2)}, u32[]{:S(2)}) collective-permute-start(bf16[192,1536]{1,0:T(8,128)(2,1)} %collective-permute-done.14.others_0_.others_8_), channel_id=1, source_target_pairs={{0,4},{4,0},{8,12},{12,8},{16,20},{20,16},{24,28},{28,24},{1,5},{5... | collective-permute-start | bytes 1769480 | tf_op jit(solution)/shard_map/ppermute | solution.py:962
  126.9 21.9 %collective-permute-start.22 = (bf16[192,1536]{1,0:T(8,128)(2,1)}, bf16[192,1536]{1,0:T(8,128)(2,1)S(1)}, u32[]{:S(2)}, u32[]{:S(2)}) collective-permute-start(bf16[192,1536]{1,0:T(8,128)(2,1)} %collective-permute-done.15.others_1_.others_9_), channel_id=1, source_target_pairs={{0,4},{4,0},{8,12},{12,8},{16,20},{20,16},{24,28},{28,24},{1,5},{5... | collective-permute-start | bytes 1769480 | tf_op jit(solution)/shard_map/ppermute | solution.py:962
  130.0 15.9 %collective-permute-start.19 = (bf16[96,3072]{1,0:T(8,128)(2,1)}, bf16[96,3072]{1,0:T(8,128)(2,1)S(1)}, u32[]{:S(2)}, u32[]{:S(2)}) collective-permute-start(bf16[96,3072]{1,0:T(8,128)(2,1)} %shard_map.184.others_0_), channel_id=1, source_target_pairs={{0,16},{4,20},{8,24},{12,28},{16,0},{20,4},{24,8},{28,12},{1,17},{... | collective-permute-start | bytes 1769480 | tf_op jit(solution)/shard_map/ppermute | solution.py:962
  130.9 15.6 %collective-permute-start.18 = (bf16[96,3072]{1,0:T(8,128)(2,1)}, bf16[96,3072]{1,0:T(8,128)(2,1)S(1)}, u32[]{:S(2)}, u32[]{:S(2)}) collective-permute-start(bf16[96,3072]{1,0:T(8,128)(2,1)} %shard_map.184.others_0_), channel_id=1, source_target_pairs={{0,8},{4,12},{8,0},{12,4},{16,24},{20,28},{24,16},{28,20},{1,9},{5... | collective-permute-start | bytes 1769480 | tf_op jit(solution)/shard_map/ppermute | solution.py:962
  146.5 14.5 %collective-permute-start.25 = (bf16[96,3072]{1,0:T(8,128)(2,1)S(1)}, bf16[96,3072]{1,0:T(8,128)(2,1)S(1)}, u32[]{:S(2)}, u32[]{:S(2)}) collective-permute-start(bf16[96,3072]{1,0:T(8,128)(2,1)S(1)} %collective-permute-done.18.others_1_), channel_id=1, source_target_pairs={{0,4},{4,0},{8,12},{12,8},{16,20},{20,16},{24,28},{28,24},{1,5},{5... | collective-permute-start | bytes 1769480 | tf_op jit(solution)/shard_map/ppermute | solution.py:962
  146.6 15.3 %collective-permute-start.26 = (bf16[96,3072]{1,0:T(8,128)(2,1)S(1)}, bf16[96,3072]{1,0:T(8,128)(2,1)}, u32[]{:S(2)}, u32[]{:S(2)}) collective-permute-start(bf16[96,3072]{1,0:T(8,128)(2,1)S(1)} %collective-permute-done.19.others_2_), channel_id=1, source_target_pairs={{0,4},{4,0},{8,12},{12,8},{16,20},{20,16},{24,28},{28,24},{1,5},{5... | collective-permute-start | bytes 1769480 | tf_op jit(solution)/shard_map/ppermute | solution.py:962
  160.9 24.1 %collective-permute-start.31 = (bf16[384,1536]{1,0:T(8,128)(2,1)}, bf16[384,1536]{1,0:T(8,128)(2,1)}, u32[]{:S(2)}, u32[]{:S(2)}) collective-permute-start(bf16[384,1536]{1,0:T(8,128)(2,1)} %shard_map.187.others_0_.others_8_), channel_id=1, source_target_pairs={{0,4},{4,0},{8,12},{12,8},{16,20},{20,16},{24,28},{28,24},{1,5},{5... | collective-permute-start | bytes 3538952 | tf_op jit(solution)/shard_map/ppermute | solution.py:962
  161.0 28.5 %collective-permute-start.30 = (bf16[384,1536]{1,0:T(8,128)(2,1)}, bf16[384,1536]{1,0:T(8,128)(2,1)S(1)}, u32[]{:S(2)}, u32[]{:S(2)}) collective-permute-start(bf16[384,1536]{1,0:T(8,128)(2,1)} %shard_map.187.others_0_.others_8_), channel_id=1, source_target_pairs={{0,16},{4,20},{8,24},{12,28},{16,0},{20,4},{24,8},{28,12},{1,17},{... | collective-permute-start | bytes 3538952 | tf_op jit(solution)/shard_map/ppermute | solution.py:962
  161.9 28.4 %collective-permute-start.29 = (bf16[384,1536]{1,0:T(8,128)(2,1)}, bf16[384,1536]{1,0:T(8,128)(2,1)S(1)}, u32[]{:S(2)}, u32[]{:S(2)}) collective-permute-start(bf16[384,1536]{1,0:T(8,128)(2,1)} %shard_map.187.others_0_.others_8_), channel_id=1, source_target_pairs={{0,8},{4,12},{8,0},{12,4},{16,24},{20,28},{24,16},{28,20},{1,9},{5... | collective-permute-start | bytes 3538952 | tf_op jit(solution)/shard_map/ppermute | solution.py:962
  190.3 18.0 %collective-permute-start.34 = (bf16[384,1536]{1,0:T(8,128)(2,1)S(1)}, bf16[384,1536]{1,0:T(8,128)(2,1)}, u32[]{:S(2)}, u32[]{:S(2)}) collective-permute-start(bf16[384,1536]{1,0:T(8,128)(2,1)S(1)} %collective-permute-done.29.others_1_.others_9_), channel_id=1, source_target_pairs={{0,4},{4,0},{8,12},{12,8},{16,20},{20,16},{24,28},{28,24},{1,5},{5... | collective-permute-start | bytes 3538952 | tf_op jit(solution)/shard_map/ppermute | solution.py:962
  190.3 18.0 %collective-permute-start.35 = (bf16[384,1536]{1,0:T(8,128)(2,1)S(1)}, bf16[384,1536]{1,0:T(8,128)(2,1)}, u32[]{:S(2)}, u32[]{:S(2)}) collective-permute-start(bf16[384,1536]{1,0:T(8,128)(2,1)S(1)} %collective-permute-done.30.others_2_.others_10_), channel_id=1, source_target_pairs={{0,4},{4,0},{8,12},{12,8},{16,20},{20,16},{24,28},{28,24},{1,5},{5... | collective-permute-start | bytes 3538952 | tf_op jit(solution)/shard_map/ppermute | solution.py:962
  192.2 15.3 %collective-permute-start.32 = (bf16[192,1536]{1,0:T(8,128)(2,1)S(1)}, bf16[192,1536]{1,0:T(8,128)(2,1)S(1)}, u32[]{:S(2)}, u32[]{:S(2)}) collective-permute-start(bf16[192,1536]{1,0:T(8,128)(2,1)S(1)} %slice.183), channel_id=1, source_target_pairs={{0,16},{4,20},{8,24},{12,28},{16,0},{20,4},{24,8},{28,12},{1,17},{... | collective-permute-start | bytes 1769480 | tf_op jit(solution)/shard_map/ppermute | solution.py:962
  193.3 15.1 %collective-permute-start.33 = (bf16[192,1536]{1,0:T(8,128)(2,1)S(1)}, bf16[192,1536]{1,0:T(8,128)(2,1)}, u32[]{:S(2)}, u32[]{:S(2)}) collective-permute-start(bf16[192,1536]{1,0:T(8,128)(2,1)S(1)} %slice.184), channel_id=1, source_target_pairs={{0,8},{4,12},{8,0},{12,4},{16,24},{20,28},{24,16},{28,20},{1,9},{5... | collective-permute-start | bytes 1769480 | tf_op jit(solution)/shard_map/ppermute | solution.py:962
  281.5 14.3 %collective-permute-start.38 = (bf16[384,3072]{1,0:T(8,128)(2,1)}, bf16[384,3072]{1,0:T(8,128)(2,1)S(1)}, u32[]{:S(2)}, u32[]{:S(2)}) collective-permute-start(bf16[384,3072]{1,0:T(8,128)(2,1)} %get-tuple-element.330), channel_id=1, source_target_pairs={{0,4},{4,0},{8,12},{12,8},{16,20},{20,16},{24,28},{28,24},{1,5},{5... | collective-permute-start | bytes 7077896 | tf_op jit(solution)/shard_map/ppermute | solution.py:962
  299.5 21.9 %collective-permute-start.41 = (bf16[1536,1536]{1,0:T(8,128)(2,1)}, bf16[1536,1536]{1,0:T(8,128)(2,1)}, u32[]{:S(2)}, u32[]{:S(2)}) collective-permute-start(bf16[1536,1536]{1,0:T(8,128)(2,1)} %get-tuple-element.342), channel_id=1, source_target_pairs={{0,4},{4,0},{8,12},{12,8},{16,20},{20,16},{24,28},{28,24},{1,5},{5... | collective-permute-start | bytes 14155784 | tf_op jit(solution)/shard_map/ppermute | solution.py:962
  303.4 18.0 %collective-permute-start.39 = (bf16[48,3072]{1,0:T(8,128)(2,1)S(1)}, bf16[48,3072]{1,0:T(8,128)(2,1)S(1)}, u32[]{:S(2)}, u32[]{:S(2)}) collective-permute-start(bf16[48,3072]{1,0:T(8,128)(2,1)S(1)} %copy-done.52), channel_id=1, source_target_pairs={{0,8},{4,12},{8,0},{12,4},{16,24},{20,28},{24,16},{28,20},{1,9},{5... | collective-permute-start | bytes 884744 | tf_op jit(solution)/shard_map/ppermute | solution.py:962
  304.6 16.8 %collective-permute-start.40 = (bf16[48,3072]{1,0:T(8,128)(2,1)S(1)}, bf16[48,3072]{1,0:T(8,128)(2,1)S(1)}, u32[]{:S(2)}, u32[]{:S(2)}) collective-permute-start(bf16[48,3072]{1,0:T(8,128)(2,1)S(1)} %copy-done.51), channel_id=1, source_target_pairs={{0,16},{4,20},{8,24},{12,28},{16,0},{20,4},{24,8},{28,12},{1,17},{... | collective-permute-start | bytes 884744 | tf_op jit(solution)/shard_map/ppermute | solution.py:962
  328.0 25.5 %collective-permute-start.42 = (bf16[96,3072]{1,0:T(8,128)(2,1)}, bf16[96,3072]{1,0:T(8,128)(2,1)S(1)}, u32[]{:S(2)}, u32[]{:S(2)}) collective-permute-start(bf16[96,3072]{1,0:T(8,128)(2,1)} %get-tuple-element.363), channel_id=1, source_target_pairs={{0,8},{4,12},{8,0},{12,4},{16,24},{20,28},{24,16},{28,20},{1,9},{5... | collective-permute-start | bytes 1769480 | tf_op jit(solution)/shard_map/ppermute | solution.py:962
  328.7 24.8 %collective-permute-start.43 = (bf16[96,3072]{1,0:T(8,128)(2,1)}, bf16[96,3072]{1,0:T(8,128)(2,1)S(1)}, u32[]{:S(2)}, u32[]{:S(2)}) collective-permute-start(bf16[96,3072]{1,0:T(8,128)(2,1)} %get-tuple-element.364), channel_id=1, source_target_pairs={{0,16},{4,20},{8,24},{12,28},{16,0},{20,4},{24,8},{28,12},{1,17},{... | collective-permute-start | bytes 1769480 | tf_op jit(solution)/shard_map/ppermute | solution.py:962
  329.7 26.9 %collective-permute-start.44 = (bf16[192,1536]{1,0:T(8,128)(2,1)}, bf16[192,1536]{1,0:T(8,128)(2,1)S(1)}, u32[]{:S(2)}, u32[]{:S(2)}) collective-permute-start(bf16[192,1536]{1,0:T(8,128)(2,1)} %get-tuple-element.365), channel_id=1, source_target_pairs={{0,8},{4,12},{8,0},{12,4},{16,24},{20,28},{24,16},{28,20},{1,9},{5... | collective-permute-start | bytes 1769480 | tf_op jit(solution)/shard_map/ppermute | solution.py:962
  330.8 25.9 %collective-permute-start.45 = (bf16[192,1536]{1,0:T(8,128)(2,1)}, bf16[192,1536]{1,0:T(8,128)(2,1)}, u32[]{:S(2)}, u32[]{:S(2)}) collective-permute-start(bf16[192,1536]{1,0:T(8,128)(2,1)} %get-tuple-element.366), channel_id=1, source_target_pairs={{0,16},{4,20},{8,24},{12,28},{16,0},{20,4},{24,8},{28,12},{1,17},{... | collective-permute-start | bytes 1769480 | tf_op jit(solution)/shard_map/ppermute | solution.py:962
  353.4 39.0 %collective-permute-start.48 = (bf16[384,2048]{1,0:T(8,128)(2,1)}, bf16[384,2048]{1,0:T(8,128)(2,1)S(1)}, u32[]{:S(2)}, u32[]{:S(2)}) collective-permute-start(bf16[384,2048]{1,0:T(8,128)(2,1)} %get-tuple-element.389), channel_id=1, source_target_pairs={{0,4},{4,0},{8,12},{12,8},{16,20},{20,16},{24,28},{28,24},{1,5},{5... | collective-permute-start | bytes 4718600 | tf_op jit(solution)/shard_map/ppermute | solution.py:962
  361.8 30.6 %collective-permute-start.46 = (bf16[384,1536]{1,0:T(8,128)(2,1)}, bf16[384,1536]{1,0:T(8,128)(2,1)}, u32[]{:S(2)}, u32[]{:S(2)}) collective-permute-start(bf16[384,1536]{1,0:T(8,128)(2,1)} %get-tuple-element.387), channel_id=1, source_target_pairs={{0,8},{4,12},{8,0},{12,4},{16,24},{20,28},{24,16},{28,20},{1,9},{5... | collective-permute-start | bytes 3538952 | tf_op jit(solution)/shard_map/ppermute | solution.py:962
  362.6 29.8 %collective-permute-start.47 = (bf16[384,1536]{1,0:T(8,128)(2,1)}, bf16[384,1536]{1,0:T(8,128)(2,1)}, u32[]{:S(2)}, u32[]{:S(2)}) collective-permute-start(bf16[384,1536]{1,0:T(8,128)(2,1)} %get-tuple-element.388), channel_id=1, source_target_pairs={{0,16},{4,20},{8,24},{12,28},{16,0},{20,4},{24,8},{28,12},{1,17},{... | collective-permute-start | bytes 3538952 | tf_op jit(solution)/shard_map/ppermute | solution.py:962
  369.3 33.8 %all-to-all-start.1 = ((bf16[4,384,384]{2,1,0:T(8,128)(2,1)}), bf16[4,384,384]{2,1,0:T(8,128)(2,1)S(1)}, u32[]{:S(2)}, u32[]{:S(2)}) async-start(bf16[4,384,384]{2,1,0:T(8,128)(2,1)} %shard_map.201), calls=%async_computation.2 | async-start | bytes 2359296 | tf_op jit(solution)/shard_map/all_to_all | solution.py:966
  411.3 46.0 %all-to-all-start.2 = ((bf16[4,384,384]{2,1,0:T(8,128)(2,1)}), bf16[4,384,384]{2,1,0:T(8,128)(2,1)S(1)}, u32[]{:S(2)}, u32[]{:S(2)}) async-start(bf16[4,384,384]{2,1,0:T(8,128)(2,1)} %shard_map.204), calls=%async_computation.4 | async-start | bytes 2359296 | tf_op jit(solution)/shard_map/all_to_all | solution.py:966
  415.0 34.8 %reduce-scatter.5.cloned.1.call-start = ((), (), s32[]{:S(2)}) async-start(), calls=%async_computation.7 | async-start | bytes 737280 | tf_op jit(solution)/shard_map/reduce_scatter | solution.py:1487
  430.1 27.3 %collective-permute-start.57 = (bf16[96,2048]{1,0:T(8,128)(2,1)}, bf16[96,2048]{1,0:T(8,128)(2,1)S(1)}, u32[]{:S(2)}, u32[]{:S(2)}) collective-permute-start(bf16[96,2048]{1,0:T(8,128)(2,1)} %get-tuple-element.429), channel_id=1, source_target_pairs={{0,8},{4,12},{8,0},{12,4},{16,24},{20,28},{24,16},{28,20},{1,9},{5... | collective-permute-start | bytes 1179656 | tf_op jit(solution)/shard_map/ppermute | solution.py:962
  430.9 26.5 %collective-permute-start.58 = (bf16[96,2048]{1,0:T(8,128)(2,1)}, bf16[96,2048]{1,0:T(8,128)(2,1)}, u32[]{:S(2)}, u32[]{:S(2)}) collective-permute-start(bf16[96,2048]{1,0:T(8,128)(2,1)} %get-tuple-element.430), channel_id=1, source_target_pairs={{0,16},{4,20},{8,24},{12,28},{16,0},{20,4},{24,8},{28,12},{1,17},{... | collective-permute-start | bytes 1179656 | tf_op jit(solution)/shard_map/ppermute | solution.py:962
  432.1 25.2 %collective-permute-start.59 = (bf16[96,1024]{1,0:T(8,128)(2,1)}, bf16[96,1024]{1,0:T(8,128)(2,1)}, u32[]{:S(2)}, u32[]{:S(2)}) collective-permute-start(bf16[96,1024]{1,0:T(8,128)(2,1)} %get-tuple-element.431), channel_id=1, source_target_pairs={{0,8},{4,12},{8,0},{12,4},{16,24},{20,28},{24,16},{28,20},{1,9},{5... | collective-permute-start | bytes 589832 | tf_op jit(solution)/shard_map/ppermute | solution.py:962
  433.0 24.3 %collective-permute-start.60 = (bf16[96,1024]{1,0:T(8,128)(2,1)}, bf16[96,1024]{1,0:T(8,128)(2,1)}, u32[]{:S(2)}, u32[]{:S(2)}) collective-permute-start(bf16[96,1024]{1,0:T(8,128)(2,1)} %get-tuple-element.432), channel_id=1, source_target_pairs={{0,16},{4,20},{8,24},{12,28},{16,0},{20,4},{24,8},{28,12},{1,17},{... | collective-permute-start | bytes 589832 | tf_op jit(solution)/shard_map/ppermute | solution.py:962
  461.4 23.0 %all-to-all-start.3 = ((bf16[4,96,768]{2,1,0:T(8,128)(2,1)}), bf16[4,96,768]{2,1,0:T(8,128)(2,1)S(1)}, u32[]{:S(2)}, u32[]{:S(2)}) async-start(bf16[4,96,768]{2,1,0:T(8,128)(2,1)} %shard_map.209), calls=%async_computation.5 | async-start | bytes 1179648 | tf_op jit(solution)/shard_map/all_to_all | solution.py:966
  (80 other events, 525.8 us)
Sparse Core Ops, SparseCore 0:
  39.6 33.9 all-gather.4
  80.7 42.4 all-gather.6
  250.7 82.7 reduce-scatter.2
  418.4 31.3 reduce-scatter.4

commit v4 on v3

--- a/solution.py
+++ b/solution.py
@@ -396,6 +396,16 @@
         copy.wait()
 
 
+def adding(stages, *others):
+    takes = [2 if stage == 0 else 6 for stage in stages]
+    targets = others[sum(takes) :]
+    begin = 0
+    for index, (stage, count) in enumerate(zip(stages, takes)):
+        kernel = adding_corner if stage == 0 else adding_sides
+        kernel(*others[begin : begin + count], *targets[2 * index : 2 * index + 2])
+        begin += count
+
+
 def begins_of(pieces):
     begins = [0]
     for piece in pieces:
@@ -516,16 +526,18 @@
             copies[-1].start()
         return copies
 
+    def stretch(which, rows_taken, target):
+        copies, begin = [], 0
+        for index, (column, size) in enumerate(segments):
+            source = kept[2 * index + which].at[rows_taken, pl.ds(column, size)]
+            copies.append(arrivals.start(source, target.at[:, pl.ds(begin, size)]))
+            begin += size
+        return copies
+
     got_gradient = arrivals.start(gradient_in, gradient)
+    got_act = stretch(0, own, activated)
     got_down = weight_half(right)
-    got_act, got_slope, begin = [], [], 0
-    for index, (column, size) in enumerate(segments):
-        place = pl.ds(begin, size)
-        act, back = kept[2 * index : 2 * index + 2]
-        source = pl.ds(column, size)
-        got_act.append(arrivals.start(act.at[own, source], activated.at[:, place]))
-        got_slope.append(arrivals.start(back.at[:, source], slope.at[:, place]))
-        begin += size
+    got_slope = stretch(1, pl.ds(0, rows), slope)
     got_norm = arrivals.start(normed_in.at[own, :], normed_c)
     got_up = weight_half(left)
     if not first:
@@ -533,17 +545,19 @@
     got_gradient.wait()
     for block in row_blocks(rows, 64):
         branch[block, :] = gradient[block, :].astype(BF16)
-    for copy in got_down + got_act:
+    for copy in got_act:
         copy.wait()
     for chunk in row_blocks(count, count // 2):
         found = dot(activated[:, chunk], branch[own, :], CONTRACT_FIRST)
         grad_weight[chunk, width:] = found.astype(BF16)
     down_leaves = leave(right, 0)
-    for copy in got_slope + [got_norm] + got_up:
+    for copy in got_down + got_slope:
         copy.wait()
     for chunk in hidden_chunks(count):
         grad_act = dot(branch[...], held[chunk, width:], CONTRACT_LAST)
         grad_hidden[:, chunk] = (grad_act * slope[:, chunk].astype(F32)).astype(BF16)
+    for copy in [got_norm] + got_up:
+        copy.wait()
     for chunk in row_blocks(count, count // 2):
         found = dot(grad_hidden[MOST : MOST + own_rows, chunk], normed_c[...], CONTRACT_FIRST)
         grad_weight[chunk, :width] = found.astype(BF16)
@@ -630,9 +644,21 @@
                         back_tables[group, down, again] = value
 
 
-def parting(parts, group_width, pieces, *others):
+def parting(parts, group_width, pieces, gains, *others):
+    if gains:
+        gain, *others = others
     *sources, target = others
     count, rows, all_width = target.shape
+    if gains:
+        rows -= GAIN_ROWS
+        left, done = gain[...], 0
+        for _ in range(3):
+            part = left.astype(BF16)
+            left = left - part.astype(F32)
+            for at in range(count):
+                target[at, rows + done : rows + done + gains, :] = part
+            done += gains
+        target[:, rows + done :, :] = jnp.zeros((count, GAIN_ROWS - done, all_width), BF16)
     width = all_width // parts
     each = len(sources) // pieces
     starts = [0]
@@ -650,25 +676,50 @@
                     total = total + source[:, run].astype(F32)
                 runs.append(total)
             total = runs[0] if len(runs) == 1 else jnp.concatenate(runs, axis=1)
-            target[at, :, part * width : (part + 1) * width] = total.astype(target.dtype)
-
-
-def finishing(parts, *others):
+            target[at, :rows, part * width : (part + 1) * width] = total.astype(target.dtype)
+
+
+def finishing(parts, gains, turned, *others):
+    if gains:
+        *others, gain_out = others
+        total = 0.0
+        first = others[0]
+        rows = first.shape[1] - GAIN_ROWS
+        for at in range(first.shape[0]):
+            for part in range(3):
+                begin = rows + part * gains
+                total = total + first[at, begin : begin + gains, :].astype(F32)
+        gain_out[...] = total
     sources, targets = others[: -len(parts)], others[-len(parts) :]
+    rows = targets[0].shape[-1 if turned else -2]
     for layer, source in enumerate(sources):
         begin = 0
         for target, count in zip(targets, parts):
             for part in range(count):
-                width = target.shape[-1]
+                width = target.shape[-2 if turned else -1]
                 run = slice(begin, begin + width)
-                total = source[0, :, run].astype(F32)
+                total = source[0, :rows, run].astype(F32)
                 for at in range(1, source.shape[0]):
-                    total = total + source[at, :, run].astype(F32)
-                if count > 1:
+                    total = total + source[at, :rows, run].astype(F32)
+                if turned:
+                    target[layer] = total.T
+                elif count > 1:
                     target[layer, part] = total
                 else:
                     target[layer] = total
                 begin += width
+
+
+def turning(cosine_in, sine_in, ids_in, cosine, sine, ids_column):
+    half = cosine_in.shape[0]
+    down = cosine_in[...].T
+    across = sine_in[...].T
+    for head in range(cosine.shape[1] // (2 * half)):
+        for part in range(2):
+            place = slice((2 * head + part) * half, (2 * head + part + 1) * half)
+            cosine[:, place] = down
+            sine[:, place] = across if part else -across
+    ids_column[...] = ids_in[...].T[:, :1].astype(jnp.int32)
 
 
 def adding_corner(near, far, to_x, to_y):
@@ -779,7 +830,7 @@
         ],
         FORWARD_COST,
         1,
-    )(places, state, gains[0][None], gains[1][None], table, *tables, *ids, *pieces)
+    )(places, state, gains[0], gains[1], table, *tables, *ids, *pieces)
 
 
 def run_attention_backward(
@@ -808,7 +859,7 @@
     own_rows = rows - 2 * MOST
     blocks = rows // QUERY_ROWS
     copied = [branch, weights, mixed, query, key, value, normed_a, *tables]
-    ending = [grad_middle, state, gain[None]] if last else []
+    ending = [grad_middle, state, gain] if last else []
     split = places.shape[0] > 1
     halves = 1 + split
     return kernel_call(
@@ -817,8 +868,8 @@
         [
             *[ANYWHERE] * (len(copied) + (not first)),
             *([whole((rows, width)), whole((rows, width)), whole((1, width))] if last else []),
-            whole((count, deep, small)),
-            whole((count,) + back_table.shape[1:]),
+            pl.BlockSpec((count, deep, small), lambda *_: (groups[0] // count, 0, 0)),
+            pl.BlockSpec((count,) + back_table.shape[1:], lambda *_: (groups[0] // count, 0, 0)),
             whole((rows, 1)),
             whole((blocks, 1, KEY_ROWS)),
         ],
@@ -860,8 +911,8 @@
         *copied,
         *([] if first else [carried]),
         *ending,
-        table[groups[0] : groups[-1] + 1],
-        back_table[groups[0] : groups[-1] + 1],
+        table,
+        back_table,
         *ids,
     )
 
@@ -891,6 +942,16 @@
         ],
         FORWARD_COST // 3,
     )(carried, normed_c, *pieces)
+
+
+def kept_stretches(near_kept, far_kept, corner_kept):
+    side, corner = near_kept[0].shape[1], corner_kept[0].shape[1] // 2
+    return [
+        (near_kept[:2], 0, side),
+        (far_kept[:2], 0, side),
+        (corner_kept[:2], 0, corner),
+        (corner_kept[:2], corner, corner),
+    ]
 
 
 def run_feed_back(gradient, middle, gain, normed_c, stretches, pieces, places, carried, last):
@@ -938,7 +999,7 @@
         places,
         gradient,
         middle,
-        gain[None],
+        gain,
         normed_c,
         *kept,
         *([] if first else [carried]),
@@ -952,6 +1013,7 @@
 
 HEAD_DEVICES = 4
 CHUNK = 512
+GAIN_ROWS = 16
 X, Y, CORE = 2, 4, 1
 FORWARD_COST = 29_000_000_000
 BACKWARD_COST = 40_000_000_000
@@ -1007,32 +1069,44 @@
     return pl.BlockSpec((rows, columns_all), lambda *_: (index, 0))
 
 
-def part_columns(pieces, parts, wide):
+def part_columns(pieces, parts, wide, gain=None):
     rows = pieces[0][-1].shape[0]
     columns_all = sum(piece[0].shape[1] for piece in pieces)
-    shape = (HEAD_DEVICES, rows, columns_all // HEAD_DEVICES)
+    gains = 0 if gain is None else gain.shape[0]
+    shape = (
+        HEAD_DEVICES,
+        rows + (GAIN_ROWS if gains else 0),
+        columns_all // HEAD_DEVICES,
+    )
     return kernel_call(
         functools.partial(
-            parting, parts, group_width(parts, columns_all // parts, wide), len(pieces)
+            parting, parts, group_width(parts, columns_all // parts, wide), len(pieces), gains
         ),
         1,
-        [block_of(rows, source.shape[1], 0) for piece in pieces for source in piece],
+        [
+            *([whole(gain.shape)] if gains else []),
+            *[block_of(rows, source.shape[1], 0) for piece in pieces for source in piece],
+        ],
         whole(shape),
         struct(shape, BF16),
         [],
         1_000_000,
-    )(*[source for piece in pieces for source in piece])
-
-
-def finish(sources, parts):
-    _, rows, width = sources[0].shape
-    width = width // sum(parts)
+    )(*([gain] if gains else []), *[source for piece in pieces for source in piece])
+
+
+def finish(sources, parts, rows, gains=0, turned=False):
+    all_width = sources[0].shape[2]
+    width = all_width // sum(parts)
     shapes = [
         (len(sources), count, rows, width) if count > 1 else (len(sources), rows, width)
         for count in parts
     ]
+    if turned:
+        shapes = [(len(sources), width, rows) for _ in parts]
+    if gains:
+        shapes.append((gains, all_width))
     return kernel_call(
-        functools.partial(finishing, parts),
+        functools.partial(finishing, parts, gains, turned),
         1,
         [whole(source.shape) for source in sources],
         [whole(shape) for shape in shapes],
@@ -1060,12 +1134,11 @@
     return tuple(hop(piece, CORE) for piece in pieces)
 
 
-def piece_places(rows):
+def piece_places(rows, order=range(10)):
     own = lax.axis_index("dp")
     bits = [(0, 0), (X, 0), (Y, 0), (X | Y, 0), (X | Y, rows // 2)]
-    return jnp.stack(
-        [(own ^ (bit | core)) * rows + begin for core in (0, CORE) for bit, begin in bits]
-    ).astype(jnp.int32)
+    places = [(own ^ (bit | core)) * rows + begin for core in (0, CORE) for bit, begin in bits]
+    return jnp.stack([places[at] for at in order]).astype(jnp.int32)
 
 
 def block_places(rows):
@@ -1080,19 +1153,14 @@
         self.slow, self.stage, self.left = slow, 0, 1
         self.came = hop(far, CORE)
 
-    def prepare(self):
-        rows, width = self.near.shape[0] // 4, self.near.shape[1]
-        half, shape = (rows // 2, width), (rows, width)
+    def operands(self):
+        rows = self.near.shape[0] // 4
+        half = rows // 2
         if self.stage == 0:
             self.far = self.came
-            kernel, operands = adding_corner, (self.near, self.far)
-            specs, out = [block_of(rows, width, 3)] * 2, half
-        else:
-            kernel, operands = adding_sides, (self.near, self.far, self.near, self.far, *self.came)
-            specs, out = [block_of(rows, width, at) for at in (1, 1, 2, 2)] + [whole(half)] * 2, shape
-        self.sent = kernel_call(
-            kernel, 1, specs, [whole(out)] * 2, [struct(out, BF16)] * 2, [], 1_000_000
-        )(*operands)
+            return [(self.near, rows, 3), (self.far, rows, 3)], half
+        sides = [(array, rows, at) for at in (1, 2) for array in (self.near, self.far)]
+        return sides + [(array, half, 0) for array in self.came], rows
 
     def send(self):
         to_x, to_y = self.sent
@@ -1104,14 +1172,37 @@
         return [self.near, self.far, *self.came]
 
 
+def prepare(reductions):
+    arrays, in_specs, out_specs, shapes = [], [], [], []
+    for reduction in reductions:
+        operands, out_rows = reduction.operands()
+        width = reduction.near.shape[1]
+        for array, rows, at in operands:
+            arrays.append(array)
+            in_specs.append(block_of(rows, width, at))
+        out_specs += [whole((out_rows, width))] * 2
+        shapes += [struct((out_rows, width), BF16)] * 2
+    sent = kernel_call(
+        functools.partial(adding, [reduction.stage for reduction in reductions]),
+        1,
+        in_specs,
+        out_specs,
+        shapes,
+        [],
+        1_000_000,
+    )(*arrays)
+    for index, reduction in enumerate(reductions):
+        reduction.sent = sent[2 * index : 2 * index + 2]
+
+
 class Sharing:
     def __init__(self, reductions, parts, wide, slow):
         self.reductions, self.parts, self.wide, self.slow = reductions, parts, wide, slow
-        self.stage, self.left, self.came = 0, 0, ()
+        self.stage, self.left, self.came, self.gain = 0, 0, (), None
 
     def prepare(self):
         pieces = [reduction.arrays() for reduction in self.reductions]
-        self.sent = part_columns(pieces, self.parts, self.wide)
+        self.sent = part_columns(pieces, self.parts, self.wide, self.gain)
 
     def send(self):
         self.came = exchange(self.sent)
@@ -1144,8 +1235,12 @@
             if isinstance(item, Sharing) and item.stage == 0 and item not in sending:
                 if all(r.stage == 3 for r in item.reductions):
                     sending.append(item)
+        reductions = [item for item in sending if isinstance(item, Reduction)]
+        if reductions:
+            prepare(reductions)
         for item in sending:
-            item.prepare()
+            if isinstance(item, Sharing):
+                item.prepare()
         values, sent = together(values, [item.sent for item in sending])
         for item, prepared in zip(sending, sent):
             item.sent = prepared
@@ -1172,11 +1267,8 @@
     return part.swapaxes(0, 1).astype(F32)
 
 
-def shared_gain(values, stage):
-    if stage < 3:
-        return values + hop(values, (CORE, X, Y)[stage])
-    bit = 1 << (stage - 3)
-    return values + lax.ppermute(values, "head", [(i, i ^ bit) for i in range(HEAD_DEVICES)])
+def shared_gain(values, bit):
+    return values + hop(values, bit)
 
 
 def with_halo(inputs, cotangent):
@@ -1196,7 +1288,7 @@
     earlier = (ids[:, None] == ids[None, :]) & (place[None, :] < place[:, None])
     position = jnp.sum(earlier.astype(F32), axis=1)
     used = (ids >= ids[MOST]) & (ids <= ids[MOST + own_rows - 1])
-    column = jnp.where(used, ids, -1)[:, None]
+    column = jnp.where(used, ids, -1)
     row = jnp.where(used, ids, -2)
     starts = [
         min(max(b * QUERY_ROWS - MOST, 0), ids.shape[0] - KEY_ROWS)
@@ -1206,15 +1298,24 @@
     return position, (column, rows)
 
 
-def rotary_tables(position, head_width):
+def rotary_tables(position, ids, head_width):
     halves = head_width // 2
     frequency = jnp.exp(jnp.arange(halves, dtype=F32) * (-2.0 * math.log(10000.0) / head_width))
-    angles = position[:, None] * frequency[None, :]
-    cosine, sine = jnp.cos(angles), jnp.sin(angles)
-    return (
-        jnp.tile(jnp.concatenate([cosine, cosine], axis=1), (1, GROUP)),
-        jnp.tile(jnp.concatenate([-sine, sine], axis=1), (1, GROUP)),
-    )
+    angles = frequency[:, None] * position[None, :]
+    column, rows = ids
+    count = position.shape[0]
+    wide = (count, GROUP * head_width)
+    spread = jnp.broadcast_to(column.astype(F32)[None], (8, count))
+    cosine, sine, column = kernel_call(
+        turning,
+        1,
+        [whole(angles.shape)] * 2 + [whole(spread.shape)],
+        [whole(wide), whole(wide), whole((count, 1))],
+        [struct(wide, F32), struct(wide, F32), struct((count, 1), jnp.int32)],
+        [],
+        1_000_000,
+    )(jnp.cos(angles), jnp.sin(angles), spread)
+    return (cosine, sine), (column, rows)
 
 
 def body(
@@ -1249,7 +1350,8 @@
     if by_permutes():
         attention_places = piece_places(in_rows)
         grad_places = block_places(in_rows)
-        feed_places = piece_places(up_weight.shape[1])[jnp.array([0, 1, 2, 5, 6, 7, 3, 4, 8, 9])]
+        gain_rows = [[norm_gain[layer, at][None] for at in range(2)] for layer in range(layer_count)]
+        feed_places = piece_places(up_weight.shape[1], (0, 1, 2, 5, 6, 7, 3, 4, 8, 9))
         feature_rows = jnp.moveaxis(features, 3, 0).reshape(4, head_width // 4, -1)
         feature_rows = jnp.concatenate(list(feature_rows), axis=1)
 
@@ -1266,7 +1368,7 @@
         came = exchange(sent)
         state, gradient = with_halo(inputs, cotangent)
         position, ids = window_ids(segment_ids, own_rows)
-        tables = rotary_tables(position, head_width)
+        tables, ids = rotary_tables(position, ids, head_width)
         both = []
         for layer in range(1, layer_count):
             q, k, v, o = chunks[2 * layer][1:]
@@ -1279,8 +1381,8 @@
                 )
             )
         first_feed = jnp.concatenate(chunks[1][1:], axis=1)
-        came, state, gradient, tables, ids, first_feed = together(
-            came, state, gradient, tables, ids, first_feed
+        came, state, gradient, tables, ids, first_feed, gain_rows, attention_places = together(
+            came, state, gradient, tables, ids, first_feed, gain_rows, attention_places
         )
         attend = functools.partial(run_attention_forward, tables=tables, ids=ids, scale=scale)
         own = join(0, came)
@@ -1303,7 +1405,7 @@
             came = gathered_columns(sent) if more else ()
             weights, *kept, middle, normed_c = attend(
                 state,
-                norm_gain[layer],
+                gain_rows[layer],
                 attention_pieces,
                 attention_places,
                 blocks[layer],
@@ -1325,6 +1427,13 @@
                 over_x, over_y, over_core = next_chips(own)
             last_pieces = across + far_across
             feed_pieces = sides, far_sides, across, far_across
+            if not more:
+                rest = run_feed_forward(carried, normed_c, far_sides + last_pieces)
+                side = near_kept[0].shape[1]
+                stretches = [(near_kept[:2], 0, side), (rest[:2], 0, rest[0].shape[1])]
+                stored.append((state, weights, kept, middle, normed_c, stretches, feed_pieces))
+                state = rest[2]
+                break
             far_kept = run_feed_forward(carried, normed_c, far_sides)
 
             carried = far_kept[2]
@@ -1334,18 +1443,17 @@
                 carried, passed = together(carried, passed)
                 across = chip_across(passed)
             last_kept = run_feed_forward(carried, normed_c, last_pieces)
-            hidden_kept = near_kept[:2], far_kept[:2], last_kept[:2]
-            stored.append(
-                (state, weights, kept, middle, normed_c, hidden_kept, feed_pieces)
-            )
+            stretches = kept_stretches(near_kept, far_kept, last_kept)
+            stored.append((state, weights, kept, middle, normed_c, stretches, feed_pieces))
             state = last_kept[2]
             if more:
                 state, across, came = together(state, across, came)
                 own_feed = join(2 * layer + 3, came, 2 * in_rows)
     else:
+        gain_rows = [[norm_gain[layer, at][None] for at in range(2)] for layer in range(layer_count)]
         state, gradient = with_halo(inputs, cotangent)
         position, ids = window_ids(segment_ids, own_rows)
-        tables = rotary_tables(position, head_width)
+        tables, ids = rotary_tables(position, ids, head_width)
         attend = functools.partial(run_attention_forward, tables=tables, ids=ids, scale=scale)
         all_features = lax.all_gather(features, "head", axis=1, tiled=True)
         shaped = all_features.reshape(layer_count, -1, GROUP, feature_count, head_width)
@@ -1372,7 +1480,7 @@
             own_attention, own_feed = owned[2 * layer], owned[2 * layer + 1]
             weights, *kept, middle, normed_c = attend(
                 state,
-                norm_gain[layer],
+                gain_rows[layer],
                 (own_attention[:middle_row], own_attention[middle_row:]),
                 attention_places,
                 blocks[layer],
@@ -1384,10 +1492,8 @@
             near_kept = run_feed_forward(middle, normed_c, feed_pieces[0])
             far_kept = run_feed_forward(near_kept[2], normed_c, feed_pieces[1])
             last_kept = run_feed_forward(far_kept[2], normed_c, feed_pieces[2] + feed_pieces[3])
-            hidden_kept = near_kept[:2], far_kept[:2], last_kept[:2]
-            stored.append(
-                (state, weights, kept, middle, normed_c, hidden_kept, feed_pieces)
-            )
+            stretches = kept_stretches(near_kept, far_kept, last_kept)
+            stored.append((state, weights, kept, middle, normed_c, stretches, feed_pieces))
             state = last_kept[2]
     outputs = state[own_place].astype(BF16)
 
@@ -1396,20 +1502,12 @@
     traffic = Traffic()
     summing = []
     for layer in reversed(range(layer_count)):
-        before, weights, kept, middle, normed_c, hidden_kept, feed_pieces = stored[layer]
-        near_kept, far_kept, corner_kept = hidden_kept
-        side, corner = near_kept[0].shape[1], corner_kept[0].shape[1] // 2
-        stretches = [
-            (near_kept, 0, side),
-            (far_kept, 0, side),
-            (corner_kept, 0, corner),
-            (corner_kept, corner, corner),
-        ]
-        feed = (middle, norm_gain[layer, 1], normed_c)
+        before, weights, kept, middle, normed_c, stretches, feed_pieces = stored[layer]
+        feed = (middle, gain_rows[layer][1], normed_c)
         attend_back = functools.partial(
             run_attention_backward,
             state=before,
-            gain=norm_gain[layer, 0],
+            gain=gain_rows[layer][0],
             weights=weights,
             table=blocks[layer],
             back_table=back_blocks[layer],
@@ -1473,19 +1571,20 @@
         traffic.moving.append(feed_share)
         carried, attention_sums = None, []
         for call_groups in (tuple(range(groups - 1)), (groups - 1,)):
+            if attention_sums:
+                for index, (later, feed_part, attention_sum) in enumerate(summing):
+                    carried, feed_part = together(carried, feed_part)
+                    parted = part_columns([[feed_part]], 2, wide)
+                    carried, parted = together(carried, parted)
+                    parted = lax.psum_scatter(parted, "head", scatter_dimension=0, tiled=True)
+                    summing[index] = later, parted, attention_sum
             branch, grad_middle, carried = traffic.slot((branch, grad_middle, carried))
             if attention_sums:
                 traffic.moving.append(attention_sums[-1])
-                for later, feed_part, attention_sum in summing:
-                    carried, feed_part = together(carried, feed_part)
-                    share = Sharing([], 2, wide, 1)
-                    share.sent = part_columns([[feed_part]], 2, wide)
-                    parted = part_columns([attention_sum.arrays()], 4, wide)
-                    carried, share.sent, parted = together(carried, share.sent, parted)
-                    share.send()
-                    traffic.moving.append(share)
-                    parted = lax.psum_scatter(parted, "head", scatter_dimension=0, tiled=True)
-                    shares[later] = share, parted
+                for later, parted, attention_sum in summing:
+                    attention_part = part_columns([attention_sum.arrays()], 4, wide)
+                    carried, attention_part = together(carried, attention_part)
+                    shares[later] = parted, attention_part
             carried, *gain_a, far, near = attend_back(
                 call_groups, carried, grad_middle=grad_middle, branch=branch, places=grad_places
             )
@@ -1499,22 +1598,30 @@
         traffic.moving.append(attention_share)
         shares[layer] = feed_share, attention_share
     if by_permutes():
-        gain_all = jnp.stack(gains)
+        gain_all = jnp.concatenate(gains)
         input_grad = gradient[own_place]
         gain_all = traffic.slot(gain_all)
-        gain_all = shared_gain(gain_all, 0)
+        gain_all = shared_gain(shared_gain(gain_all, CORE), X)
         gain_all = traffic.slot(gain_all)
         gain_all, outputs, input_grad = together(gain_all, outputs, input_grad)
-        gain_all, parted = together(gain_all, [share[1] for share in shares[1:]])
-        gain_all = shared_gain(shared_gain(gain_all, 1), 2)
-        gain_all = traffic.slot(gain_all)
-        up_grad, down_grad = finish([share[0].came for share in shares], (1, 1))
-        gain_all = shared_gain(shared_gain(gain_all, 3), 4)
-        gain_all, up_grad, down_grad = together(gain_all, up_grad, down_grad)
-        while traffic.moving:
-            gain_all = traffic.slot(gain_all)
-        gain_total = gain_all
-        qkv_grad, out_grad = finish([shares[0][1].came] + parted, (3, 1))
+        gain_all = shared_gain(gain_all, Y)
+        gain_all, parted, attention_parts = together(
+            gain_all, [share[0] for share in shares[1:]], [share[1] for share in shares[1:]]
+        )
+        attention_parts = [
+            lax.psum_scatter(part, "head", scatter_dimension=0, tiled=True)
+            for part in attention_parts
+        ]
+        attention_share.gain = gain_all
+        parted = traffic.slot(parted)
+        turned = finish([shares[0][0].came] + parted, (1, 1), up_weight.shape[1], turned=True)
+        up_grad, down_grad = traffic.slot(turned)
+        up_grad, down_grad = up_grad.swapaxes(1, 2), down_grad.swapaxes(1, 2)
+        assert not traffic.moving
+        qkv_grad, out_grad, gain_total = finish(
+            [shares[0][1].came] + attention_parts, (3, 1), in_rows, 2 * layer_count
+        )
+        gain_total = gain_total.reshape(layer_count, 2, -1)
     else:
         gain_total = lax.psum(jnp.stack(gains), ("dp", "head"))
         input_grad = gradient[own_place]

time: 504 us -> 481 us (0.954)
  starting transfers between devices: 75 us -> 63.9 us
  Pallas kernels: 268 us -> 258 us
  local copies, waits for them, and re-layouts: 42.6 us -> 35 us
  waiting for transfers between devices: 86.9 us -> 92.4 us
    all_to_all x4 -> x3, waiting for transfers between devices: 8.96 us -> 22.8 us  [exchange(): lax.all_to_all(values, 'head', split_axis=0, concat_axis=0, tiled=True)]
    ppermute x59, waiting for transfers between devices: 56.6 us -> 68.8 us  [hop(): return lax.ppermute(values, 'dp', [(i, i ^ bit) for i in range(count)])]
    reduce_scatter x1, waiting for transfers between devices: 12.1 us -> 0.01 us  [body(): parted = lax.psum_scatter(parted, 'head', scatter_dimension=0, tiled=True)]
    ppermute x2 -> x0, starting transfers between devices: 6.83 us -> none  [shared_gain(): lax.ppermute(values, 'head', [(i, i ^ bit) for i in range(HEAD_DEVICES)])]
    ppermute x2 -> x0, waiting for transfers between devices: 5.61 us -> none  [shared_gain(): lax.ppermute(values, 'head', [(i, i ^ bit) for i in range(HEAD_DEVICES)])]
    all_to_all x4 -> x3, starting transfers between devices: 21.1 us -> 16 us  [exchange(): lax.all_to_all(values, 'head', split_axis=0, concat_axis=0, tiled=True)]
    pallas_call x6 -> x5, Pallas kernels: 53.6 us -> 49.4 us  [run_feed_forward(): kernel_call(functools.partial(feed_forward, len(pieces)), 1, [ANYWHERE] *...]
    pallas_call x10 -> x8, Pallas kernels: 26 us -> 23.8 us  [the longest x5 16.1 us: prepare(): kernel_call(functools.partial(adding, [reduction.stage for reduction in r...]
  transfers between devices with their start and end apart: 71 -> 69, of which waited for: 27 -> 27; matrix products, arithmetic and copies ran while one was open for 7% -> 5% of each run, Pallas kernels for 45% -> 47%
where the time goes in v4:
time: 481 us; the launch traced here: 471 us
  Pallas kernels  258 us (54%)
  waiting for transfers between devices  92.4 us (19%)
  starting transfers between devices  63.9 us (13%)
  local copies, waits for them, and re-layouts  35 us (7%)
  between operations  14.7 us (3%)
  other arithmetic  7.39 us (2%)
    ppermute x59, waiting for transfers between devices, hop(): return lax.ppermute(values, 'dp', [(i, i ^ bit) for i in range(count)])  68.8 us
    pallas_call x3, Pallas kernels, run_attention_backward(): kernel_call(functools.partial(attention_backward, first, last, scale, gro...  67.2 us
    pallas_call x5, Pallas kernels, run_feed_forward(): kernel_call(functools.partial(feed_forward, len(pieces)), 1, [ANYWHERE] *...  49.4 us
    pallas_call x3, Pallas kernels, run_feed_back(): kernel_call(functools.partial(feed_back, first, last, segments, len(piece...  49.2 us
    pallas_call x2, Pallas kernels, run_attention_forward(): kernel_call(functools.partial(attention_forward, scale, len(pieces)), gro...  42.1 us
    ppermute x59, starting transfers between devices, hop(): return lax.ppermute(values, 'dp', [(i, i ^ bit) for i in range(count)])  41.6 us
    all_to_all x3, waiting for transfers between devices, exchange(): lax.all_to_all(values, 'head', split_axis=0, concat_axis=0, tiled=True)  22.8 us
    pallas_call x5, Pallas kernels, prepare(): kernel_call(functools.partial(adding, [reduction.stage for reduction in r...  16.1 us
  transfers between devices with their start and end apart: 69, of which 27 were waited for; matrix products, arithmetic and copies ran while one was open for 5% of the time, Pallas kernels for 47%

profile of v4, /device:TPU:0, one launch (start us, length us, event | category | flops | bytes accessed | tf_op | source)
XLA Modules:
  0.0 471.4 jit_solution(7272361964830617045)
XLA Ops:
  12.6 6.3 %all-to-all-start = ((bf16[4,112,768]{2,1,0:T(8,128)(2,1)}), bf16[4,112,768]{2,1,0:T(8,128)(2,1)S(1)}, u32[]{:S(2)}, u32[]{:S(2)}) async-start(bf16[4,112,768]{2,1,0:T(8,128)(2,1)} %broadcast_in_dim.13), calls=%async_computation | async-start | bytes 1376256 | tf_op jit(solution)/shard_map/all_to_all | solution.py:1028
  21.1 4.6 collective-permute-start
  31.8 2.8 shard_map.170
  38.9 2.2 fusion.2
  48.2 3.4 shard_map.173
  51.6 8.4 %collective-permute-done.3.others_2_ = bf16[96,3072]{1,0:T(8,128)(2,1)} collective-permute-done((bf16[96,3072]{1,0:T(8,128)(2,1)}, bf16[96,3072]{1,0:T(8,128)(2,1)}, u32[]{:S(2)}, u32[]{:S(2)}) %collective-permute-start.3) | collective-permute-done | bytes 589856 | tf_op jit(solution)/shard_map/ppermute | solution.py:1024
  65.9 4.8 %collective-permute-done.6.others_4_ = bf16[48,3072]{1,0:T(8,128)(2,1)S(1)} collective-permute-done((bf16[48,3072]{1,0:T(8,128)(2,1)S(1)}, bf16[48,3072]{1,0:T(8,128)(2,1)S(1)}, u32[]{:S(2)}, u32[]{:S(2)}) %collective-permute-start.6) | collective-permute-done | bytes 294944 | tf_op jit(solution)/shard_map/ppermute | solution.py:1024
  70.6 2.3 collective-permute-done.5.others_3_
  73.5 2.4 copy.56
  75.9 2.6 shard_map.171.others_0_.others_5_
  81.6 21.2 %shard_map.174 = (bf16[768,3072]{1,0:T(8,128)(2,1)}, bf16[640,768]{1,0:T(8,128)(2,1)}, f32[640,768]{1,0:T(8,128)}, f32[640,768]{1,0:T(8,128)}, bf16[640,768]{1,0...) custom-call(s32[10]{0:T(128)} %stack.123.places, ...), custom_call_target="tpu_custom_call" | custom-call | flops 28999999488 | bytes 48333332 | tf_op jit(solution)/shard_map/pallas_call | solution.py:788
  102.9 4.3 collective-permute-done.12.others_2_.others_7_
  111.5 9.5 %shard_map.175 = (bf16[640,1152]{1,0:T(8,128)(2,1)}, bf16[640,1152]{1,0:T(8,128)(2,1)}, f32[640,768]{1,0:T(8,128)}) custom-call(f32[640,768]{1,0:T(8,128)} %get-tuple-element.269.carried_in.middle, bf16[640,768]{1,0:T(8,128)(2,1)} %get-tuple-element.270.normed_in, bf16[384,1536]{1,0:T(8,128)(2,1)} %shard_map.171.others_0_.others_5_, ...), custom_call_target="tpu_custom_call" | custom-call | flops 9666666496 | bytes 16111111 | tf_op jit(solution)/shard_map/pallas_call | solution.py:923
  121.0 3.4 collective-permute-done.14.others_0_.others_8_
  125.7 2.5 shard_map.176.others_0_
  130.7 9.5 %shard_map.177 = (bf16[640,1152]{1,0:T(8,128)(2,1)}, bf16[640,1152]{1,0:T(8,128)(2,1)}, f32[640,768]{1,0:T(8,128)}) custom-call(f32[640,768]{1,0:T(8,128)} %get-tuple-element.279.carried_in, bf16[640,768]{1,0:T(8,128)(2,1)} %get-tuple-element.270.normed_in, bf16[384,1536]{1,0:T(8,128)(2,1)} %copy-done.31, ...), custom_call_target="tpu_custom_call" | custom-call | flops 9666666496 | bytes 16111111 | tf_op jit(solution)/shard_map/pallas_call | solution.py:923
  140.2 3.9 collective-permute-done.19.others_2_
  148.8 7.6 %shard_map.178 = (bf16[640,768]{1,0:T(8,128)(2,1)}, bf16[640,768]{1,0:T(8,128)(2,1)}, f32[640,768]{1,0:T(8,128)}) custom-call(f32[640,768]{1,0:T(8,128)} %get-tuple-element.288.carried_in, bf16[640,768]{1,0:T(8,128)(2,1)} %get-tuple-element.270.normed_in, bf16[192,1536]{1,0:T(8,128)(2,1)} %collective-permute-done.14.others_0_.others_8_, ...), custom_call_target="tpu_custom_call" | custom-call | flops 9666666496 | bytes 16111111 | tf_op jit(solution)/shard_map/pallas_call | solution.py:923
  157.0 2.8 shard_map.179.others_0_.others_4_
  163.2 20.9 %shard_map.180 = (bf16[768,3072]{1,0:T(8,128)(2,1)}, bf16[640,768]{1,0:T(8,128)(2,1)}, f32[640,768]{1,0:T(8,128)}, f32[640,768]{1,0:T(8,128)}, bf16[640,768]{1,0...) custom-call(s32[10]{0:T(128)} %stack.123.places, ...), custom_call_target="tpu_custom_call" | custom-call | flops 28999999488 | bytes 48333332 | tf_op jit(solution)/shard_map/pallas_call | solution.py:788
  184.1 4.3 collective-permute-done.30.others_2_.others_6_
  191.8 9.5 %shard_map.181 = (bf16[640,1152]{1,0:T(8,128)(2,1)}, bf16[640,1152]{1,0:T(8,128)(2,1)}, f32[640,768]{1,0:T(8,128)}) custom-call(f32[640,768]{1,0:T(8,128)} %get-tuple-element.309.carried_in.middle, bf16[640,768]{1,0:T(8,128)(2,1)} %get-tuple-element.306.normed_in, bf16[384,1536]{1,0:T(8,128)(2,1)} %shard_map.179.others_0_.others_4_, ...), custom_call_target="tpu_custom_call" | custom-call | flops 9666666496 | bytes 16111111 | tf_op jit(solution)/shard_map/pallas_call | solution.py:923
  201.4 3.8 collective-permute-done.32.others_3_.others_10_
  209.9 13.3 %shard_map.182 = (bf16[640,1920]{1,0:T(8,128)(2,1)}, bf16[640,1920]{1,0:T(8,128)(2,1)}, f32[640,768]{1,0:T(8,128)}) custom-call(f32[640,768]{1,0:T(8,128)} %get-tuple-element.316.carried_in, bf16[640,768]{1,0:T(8,128)(2,1)} %get-tuple-element.306.normed_in, bf16[384,1536]{1,0:T(8,128)(2,1)} %collective-permute-done.31.others_0_.others_7_, ...), custom_call_target="tpu_custom_call" | custom-call | flops 9666666496 | bytes 16111111 | tf_op jit(solution)/shard_map/pallas_call | solution.py:923
  223.2 21.3 %shard_map.183 = (bf16[3072,1536]{1,0:T(8,128)(2,1)}, f32[640,768]{1,0:T(8,128)}, f32[1,768]{1,0:T(1,128)}, bf16[640,768]{1,0:T(8,128)(2,1)}) custom-call(s32[10]{0:T(128)} %stack.114.places, f32[640,768]{1,0:T(8,128)} %get-tuple-element.243.gradient_in, f32[640,768]{1,0:T(8,128)} %get-tuple-element.309.carried_in.middle, ...), custom_call_target="tpu_custom_call" | custom-call | flops 14499999744 | bytes 24166666 | tf_op jit(solution)/shard_map/pallas_call | solution.py:964
  245.2 31.1 %shard_map.184 = (f32[640,768]{1,0:T(8,128)}, f32[1,768]{1,0:T(1,128)}, bf16[384,3072]{1,0:T(8,128)(2,1)}, bf16[384,3072]{1,0:T(8,128)(2,1)}) custom-call(s32[8]{0:T(128)} %stack.103.places, bf16[640,768]{1,0:T(8,128)(2,1)} %get-tuple-element.324.branch_in, bf16[768,3072]{1,0:T(8,128)(2,1)} %get-tuple-element.325.weights_in, ...), custom_call_target="tpu_custom_call" | custom-call | flops 40000000000 | bytes 66666664 | tf_op jit(solution)/shard_map/pallas_call | solution.py:865
  276.4 13.2 %shard_map.185 = (bf16[1536,1536]{1,0:T(8,128)(2,1)}, f32[640,768]{1,0:T(8,128)}) custom-call(s32[5]{0:T(128)} %constant.47.clone.places, f32[640,768]{1,0:T(8,128)} %get-tuple-element.333.gradient_in, f32[640,768]{1,0:T(8,128)} %get-tuple-element.269.carried_in.middle, f32[1,768]{1,0:T(1,128)} %get-tuple-element.255.gain_2, ...), custom_call_target="tpu_custom_call" | custom-call | flops 14499999744 | bytes 24166666 | tf_op jit(solution)/shard_map/pallas_call | solution.py:964
  291.0 2.1 shard_map.186
  294.7 14.8 %shard_map.187 = (bf16[1536,1536]{1,0:T(8,128)(2,1)}, f32[640,768]{1,0:T(8,128)}, f32[1,768]{1,0:T(1,128)}, bf16[640,768]{1,0:T(8,128)(2,1)}) custom-call(s32[5]{0:T(128)} %constant.47.clone.places, f32[640,768]{1,0:T(8,128)} %get-tuple-element.333.gradient_in, f32[640,768]{1,0:T(8,128)} %get-tuple-element.269.carried_in.middle, ...), custom_call_target="tpu_custom_call" | custom-call | flops 14499999744 | bytes 24166666 | tf_op jit(solution)/shard_map/pallas_call | solution.py:964
  310.4 4.1 shard_map.188
  318.5 21.0 %shard_map.189 = (f32[640,768]{1,0:T(8,128)}, bf16[384,2048]{1,0:T(8,128)(2,1)}, bf16[384,2048]{1,0:T(8,128)(2,1)}) custom-call(s32[8]{0:T(128)} %stack.103.places, bf16[640,768]{1,0:T(8,128)(2,1)} %get-tuple-element.390.branch_in, bf16[768,3072]{1,0:T(8,128)(2,1)} %get-tuple-element.367.weights_in, bf16[640,768]{1,0:T(8,128)(2,1)} %get-tuple-element.368.mixed_in, ...), custom_call_target="tpu_custom_call" | custom-call | flops 26666665984 | bytes 44444444 | tf_op jit(solution)/shard_map/pallas_call | solution.py:865
  339.6 2.6 shard_map.190
  342.2 4.9 %collective-permute-done.44.others_4_ = bf16[192,1536]{1,0:T(8,128)(2,1)S(1)} collective-permute-done((bf16[192,1536]{1,0:T(8,128)(2,1)}, bf16[192,1536]{1,0:T(8,128)(2,1)S(1)}, u32[]{:S(2)}, u32[]{:S(2)}) %collective-permute-start.44) | collective-permute-done | bytes 589856 | tf_op jit(solution)/shard_map/ppermute | solution.py:1024
  348.0 4.8 %shard_map.191 = (bf16[384,1536]{1,0:T(8,128)(2,1)}, bf16[384,1536]{1,0:T(8,128)(2,1)}) custom-call(bf16[1536,1536]{1,0:T(8,128)(2,1)} %get-tuple-element.359.others_6_.others_0_.others_2_, bf16[1536,1536]{1,0:T(8,128)(2,1)} %collective-permute-done.41.others_7_.others_1_.others_3_, bf16[1536,1536]{1,0:T(8,128)(2,1)} %get-tuple-element.359.others_6_.others_0_.others_2_, ...), custom_call_target="tpu_custom_call" | custom-call | flops 1000000 | bytes 1666 | tf_op jit(solution)/shard_map/pallas_call | solution.py:1185
  352.8 2.9 shard_map.192
  357.7 15.0 %shard_map.193 = (f32[640,768]{1,0:T(8,128)}, f32[1,768]{1,0:T(1,128)}, bf16[384,1024]{1,0:T(8,128)(2,1)}, bf16[384,1024]{1,0:T(8,128)(2,1)}) custom-call(s32[8]{0:T(128)} %stack.103.places, bf16[640,768]{1,0:T(8,128)(2,1)} %get-tuple-element.390.branch_in, bf16[768,3072]{1,0:T(8,128)(2,1)} %get-tuple-element.367.weights_in, ...), custom_call_target="tpu_custom_call" | custom-call | flops 13333332992 | bytes 22222222 | tf_op jit(solution)/shard_map/pallas_call | solution.py:865
  375.3 8.2 %collective-permute-done.46.others_2_ = bf16[384,1536]{1,0:T(8,128)(2,1)S(1)} collective-permute-done((bf16[384,1536]{1,0:T(8,128)(2,1)}, bf16[384,1536]{1,0:T(8,128)(2,1)S(1)}, u32[]{:S(2)}, u32[]{:S(2)}) %collective-permute-start.46) | collective-permute-done | bytes 1179680 | tf_op jit(solution)/shard_map/ppermute | solution.py:1024
  384.5 4.3 shard_map.194
  390.9 4.7 %all-to-all-start.1 = ((bf16[4,384,384]{2,1,0:T(8,128)(2,1)}), bf16[4,384,384]{2,1,0:T(8,128)(2,1)S(1)}, u32[]{:S(2)}, u32[]{:S(2)}) async-start(bf16[4,384,384]{2,1,0:T(8,128)(2,1)} %shard_map.194), calls=%async_computation.3 | async-start | bytes 2359296 | tf_op jit(solution)/shard_map/all_to_all | solution.py:1028
  402.0 2.9 collective-permute-done.51
  406.3 3.0 shard_map.196
  413.3 2.4 slice.167
  418.3 6.7 %collective-permute-done.56 = f32[4,768]{1,0:T(4,128)S(1)} collective-permute-done((f32[4,768]{1,0:T(4,128)S(1)}, f32[4,768]{1,0:T(4,128)S(1)}, u32[]{:S(2)}, u32[]{:S(2)}) %collective-permute-start.56) | collective-permute-done | bytes 12320 | tf_op jit(solution)/shard_map/ppermute | solution.py:1024
  426.4 3.3 shard_map.197
  429.7 5.0 %all-to-all-start.2 = ((bf16[4,112,768]{2,1,0:T(8,128)(2,1)}), bf16[4,112,768]{2,1,0:T(8,128)(2,1)S(1)}, u32[]{:S(2)}, u32[]{:S(2)}) async-start(bf16[4,112,768]{2,1,0:T(8,128)(2,1)} %shard_map.197), calls=%async_computation.4 | async-start | bytes 1376256 | tf_op jit(solution)/shard_map/all_to_all | solution.py:1028
  434.7 2.8 shard_map.198
  437.5 22.2 %all-to-all-done.2.others_0_ = bf16[4,112,768]{2,1,0:T(8,128)(2,1)S(1)} async-done(((bf16[4,112,768]{2,1,0:T(8,128)(2,1)}), bf16[4,112,768]{2,1,0:T(8,128)(2,1)S(1)}, u32[]{:S(2)}, u32[]{:S(2)}) %all-to-all-start.2) | async-done | bytes 688160 | tf_op jit(solution)/shard_map/all_to_all | solution.py:1028
  460.6 2.1 shard_map.199
  (275 shorter events, 95.2 us)
Async XLA Ops:
  12.6 28.4 %all-to-all-start = ((bf16[4,112,768]{2,1,0:T(8,128)(2,1)}), bf16[4,112,768]{2,1,0:T(8,128)(2,1)S(1)}, u32[]{:S(2)}, u32[]{:S(2)}) async-start(bf16[4,112,768]{2,1,0:T(8,128)(2,1)} %broadcast_in_dim.13), calls=%async_computation | async-start | bytes 1376256 | tf_op jit(solution)/shard_map/all_to_all | solution.py:1028
  18.9 54.5 %all-gather.5.cloned.1.call-start = ((), (), s32[]{:S(2)}) async-start(), calls=%async_computation.9 | async-start | bytes 1474560 | tf_op jit(solution)/shard_map/all_gather | solution.py:1363
  21.1 16.3 %collective-permute-start = (bf16[64,1536]{1,0:T(8,128)(2,1)}, bf16[64,1536]{1,0:T(8,128)(2,1)}, u32[]{:S(2)}, u32[]{:S(2)}) collective-permute-start(bf16[64,1536]{1,0:T(8,128)(2,1)} %get-tuple-element.468), channel_id=1, source_target_pairs={{0,1},{1,2},{2,3},{4,5},{5,6},{6,7},{8,9},{9,10},{10,11},{12,13},{... | collective-permute-start | bytes 589832 | tf_op jit(solution)/shard_map/ppermute | solution.py:1277
  41.1 84.6 %all-gather.7.cloned.1.call-start = ((), (), s32[]{:S(2)}) async-start(), calls=%async_computation.10 | async-start | bytes 2211840 | tf_op jit(solution)/shard_map/all_gather | solution.py:1363
  44.0 16.1 %collective-permute-start.3 = (bf16[96,3072]{1,0:T(8,128)(2,1)}, bf16[96,3072]{1,0:T(8,128)(2,1)}, u32[]{:S(2)}, u32[]{:S(2)}) collective-permute-start(bf16[96,3072]{1,0:T(8,128)(2,1)} %shard_map.172.others_0_), channel_id=1, source_target_pairs={{0,16},{4,20},{8,24},{12,28},{16,0},{20,4},{24,8},{28,12},{1,17},{... | collective-permute-start | bytes 1769480 | tf_op jit(solution)/shard_map/ppermute | solution.py:1024
  45.5 15.8 %collective-permute-start.2 = (bf16[96,3072]{1,0:T(8,128)(2,1)}, bf16[96,3072]{1,0:T(8,128)(2,1)}, u32[]{:S(2)}, u32[]{:S(2)}) collective-permute-start(bf16[96,3072]{1,0:T(8,128)(2,1)} %shard_map.172.others_0_), channel_id=1, source_target_pairs={{0,8},{4,12},{8,0},{12,4},{16,24},{20,28},{24,16},{28,20},{1,9},{5... | collective-permute-start | bytes 1769480 | tf_op jit(solution)/shard_map/ppermute | solution.py:1024
  65.4 16.3 %collective-permute-start.7 = (bf16[96,3072]{1,0:T(8,128)(2,1)}, bf16[96,3072]{1,0:T(8,128)(2,1)}, u32[]{:S(2)}, u32[]{:S(2)}) collective-permute-start(bf16[96,3072]{1,0:T(8,128)(2,1)} %collective-permute-done.2.others_1_), channel_id=1, source_target_pairs={{0,4},{4,0},{8,12},{12,8},{16,20},{20,16},{24,28},{28,24},{1,5},{5... | collective-permute-start | bytes 1769480 | tf_op jit(solution)/shard_map/ppermute | solution.py:1024
  65.4 16.3 %collective-permute-start.8 = (bf16[96,3072]{1,0:T(8,128)(2,1)}, bf16[96,3072]{1,0:T(8,128)(2,1)}, u32[]{:S(2)}, u32[]{:S(2)}) collective-permute-start(bf16[96,3072]{1,0:T(8,128)(2,1)} %collective-permute-done.3.others_2_), channel_id=1, source_target_pairs={{0,4},{4,0},{8,12},{12,8},{16,20},{20,16},{24,28},{28,24},{1,5},{5... | collective-permute-start | bytes 1769480 | tf_op jit(solution)/shard_map/ppermute | solution.py:1024
  78.5 261.2 %reduce-scatter.4.cloned.1.call-start = ((), (), s32[]{:S(2)}) async-start(), calls=%async_computation.6 | async-start | bytes 10616832 | tf_op jit(solution)/shard_map/reduce_scatter | solution.py:1524
  78.5 24.4 %collective-permute-start.13 = (bf16[384,1536]{1,0:T(8,128)(2,1)}, bf16[384,1536]{1,0:T(8,128)(2,1)S(1)}, u32[]{:S(2)}, u32[]{:S(2)}) collective-permute-start(bf16[384,1536]{1,0:T(8,128)(2,1)} %shard_map.171.others_0_.others_5_), channel_id=1, source_target_pairs={{0,4},{4,0},{8,12},{12,8},{16,20},{20,16},{24,28},{28,24},{1,5},{5... | collective-permute-start | bytes 3538952 | tf_op jit(solution)/shard_map/ppermute | solution.py:1024
  78.6 28.6 %collective-permute-start.12 = (bf16[384,1536]{1,0:T(8,128)(2,1)}, bf16[384,1536]{1,0:T(8,128)(2,1)S(1)}, u32[]{:S(2)}, u32[]{:S(2)}) collective-permute-start(bf16[384,1536]{1,0:T(8,128)(2,1)} %shard_map.171.others_0_.others_5_), channel_id=1, source_target_pairs={{0,16},{4,20},{8,24},{12,28},{16,0},{20,4},{24,8},{28,12},{1,17},{... | collective-permute-start | bytes 3538952 | tf_op jit(solution)/shard_map/ppermute | solution.py:1024
  80.2 28.2 %collective-permute-start.11 = (bf16[384,1536]{1,0:T(8,128)(2,1)}, bf16[384,1536]{1,0:T(8,128)(2,1)S(1)}, u32[]{:S(2)}, u32[]{:S(2)}) collective-permute-start(bf16[384,1536]{1,0:T(8,128)(2,1)} %shard_map.171.others_0_.others_5_), channel_id=1, source_target_pairs={{0,8},{4,12},{8,0},{12,4},{16,24},{20,28},{24,16},{28,20},{1,9},{5... | collective-permute-start | bytes 3538952 | tf_op jit(solution)/shard_map/ppermute | solution.py:1024
  108.4 16.8 %collective-permute-start.16 = (bf16[384,1536]{1,0:T(8,128)(2,1)S(1)}, bf16[384,1536]{1,0:T(8,128)(2,1)}, u32[]{:S(2)}, u32[]{:S(2)}) collective-permute-start(bf16[384,1536]{1,0:T(8,128)(2,1)S(1)} %collective-permute-done.11.others_1_.others_6_), channel_id=1, source_target_pairs={{0,4},{4,0},{8,12},{12,8},{16,20},{20,16},{24,28},{28,24},{1,5},{5... | collective-permute-start | bytes 3538952 | tf_op jit(solution)/shard_map/ppermute | solution.py:1024
  108.4 16.8 %collective-permute-start.17 = (bf16[384,1536]{1,0:T(8,128)(2,1)S(1)}, bf16[384,1536]{1,0:T(8,128)(2,1)}, u32[]{:S(2)}, u32[]{:S(2)}) collective-permute-start(bf16[384,1536]{1,0:T(8,128)(2,1)S(1)} %collective-permute-done.12.others_2_.others_7_), channel_id=1, source_target_pairs={{0,4},{4,0},{8,12},{12,8},{16,20},{20,16},{24,28},{28,24},{1,5},{5... | collective-permute-start | bytes 3538952 | tf_op jit(solution)/shard_map/ppermute | solution.py:1024
  109.0 15.5 %collective-permute-start.14 = (bf16[192,1536]{1,0:T(8,128)(2,1)S(1)}, bf16[192,1536]{1,0:T(8,128)(2,1)}, u32[]{:S(2)}, u32[]{:S(2)}) collective-permute-start(bf16[192,1536]{1,0:T(8,128)(2,1)S(1)} %slice.141), channel_id=1, source_target_pairs={{0,16},{4,20},{8,24},{12,28},{16,0},{20,4},{24,8},{28,12},{1,17},{... | collective-permute-start | bytes 1769480 | tf_op jit(solution)/shard_map/ppermute | solution.py:1024
  110.0 15.1 %collective-permute-start.15 = (bf16[192,1536]{1,0:T(8,128)(2,1)S(1)}, bf16[192,1536]{1,0:T(8,128)(2,1)}, u32[]{:S(2)}, u32[]{:S(2)}) collective-permute-start(bf16[192,1536]{1,0:T(8,128)(2,1)S(1)} %slice.142), channel_id=1, source_target_pairs={{0,8},{4,12},{8,0},{12,4},{16,24},{20,28},{24,16},{28,20},{1,9},{5... | collective-permute-start | bytes 1769480 | tf_op jit(solution)/shard_map/ppermute | solution.py:1024
  125.2 21.4 %collective-permute-start.21 = (bf16[192,1536]{1,0:T(8,128)(2,1)}, bf16[192,1536]{1,0:T(8,128)(2,1)S(1)}, u32[]{:S(2)}, u32[]{:S(2)}) collective-permute-start(bf16[192,1536]{1,0:T(8,128)(2,1)} %collective-permute-done.14.others_0_.others_8_), channel_id=1, source_target_pairs={{0,4},{4,0},{8,12},{12,8},{16,20},{20,16},{24,28},{28,24},{1,5},{5... | collective-permute-start | bytes 1769480 | tf_op jit(solution)/shard_map/ppermute | solution.py:1024
  125.2 22.8 %collective-permute-start.22 = (bf16[192,1536]{1,0:T(8,128)(2,1)}, bf16[192,1536]{1,0:T(8,128)(2,1)S(1)}, u32[]{:S(2)}, u32[]{:S(2)}) collective-permute-start(bf16[192,1536]{1,0:T(8,128)(2,1)} %collective-permute-done.15.others_1_.others_9_), channel_id=1, source_target_pairs={{0,4},{4,0},{8,12},{12,8},{16,20},{20,16},{24,28},{28,24},{1,5},{5... | collective-permute-start | bytes 1769480 | tf_op jit(solution)/shard_map/ppermute | solution.py:1024
  128.2 15.9 %collective-permute-start.19 = (bf16[96,3072]{1,0:T(8,128)(2,1)}, bf16[96,3072]{1,0:T(8,128)(2,1)S(1)}, u32[]{:S(2)}, u32[]{:S(2)}) collective-permute-start(bf16[96,3072]{1,0:T(8,128)(2,1)} %shard_map.176.others_0_), channel_id=1, source_target_pairs={{0,16},{4,20},{8,24},{12,28},{16,0},{20,4},{24,8},{28,12},{1,17},{... | collective-permute-start | bytes 1769480 | tf_op jit(solution)/shard_map/ppermute | solution.py:1024
  129.3 15.6 %collective-permute-start.18 = (bf16[96,3072]{1,0:T(8,128)(2,1)}, bf16[96,3072]{1,0:T(8,128)(2,1)S(1)}, u32[]{:S(2)}, u32[]{:S(2)}) collective-permute-start(bf16[96,3072]{1,0:T(8,128)(2,1)} %shard_map.176.others_0_), channel_id=1, source_target_pairs={{0,8},{4,12},{8,0},{12,4},{16,24},{20,28},{24,16},{28,20},{1,9},{5... | collective-permute-start | bytes 1769480 | tf_op jit(solution)/shard_map/ppermute | solution.py:1024
  144.9 15.0 %collective-permute-start.25 = (bf16[96,3072]{1,0:T(8,128)(2,1)S(1)}, bf16[96,3072]{1,0:T(8,128)(2,1)S(1)}, u32[]{:S(2)}, u32[]{:S(2)}) collective-permute-start(bf16[96,3072]{1,0:T(8,128)(2,1)S(1)} %collective-permute-done.18.others_1_), channel_id=1, source_target_pairs={{0,4},{4,0},{8,12},{12,8},{16,20},{20,16},{24,28},{28,24},{1,5},{5... | collective-permute-start | bytes 1769480 | tf_op jit(solution)/shard_map/ppermute | solution.py:1024
  145.0 15.9 %collective-permute-start.26 = (bf16[96,3072]{1,0:T(8,128)(2,1)S(1)}, bf16[96,3072]{1,0:T(8,128)(2,1)}, u32[]{:S(2)}, u32[]{:S(2)}) collective-permute-start(bf16[96,3072]{1,0:T(8,128)(2,1)S(1)} %collective-permute-done.19.others_2_), channel_id=1, source_target_pairs={{0,4},{4,0},{8,12},{12,8},{16,20},{20,16},{24,28},{28,24},{1,5},{5... | collective-permute-start | bytes 1769480 | tf_op jit(solution)/shard_map/ppermute | solution.py:1024
  159.8 24.3 %collective-permute-start.31 = (bf16[384,1536]{1,0:T(8,128)(2,1)}, bf16[384,1536]{1,0:T(8,128)(2,1)}, u32[]{:S(2)}, u32[]{:S(2)}) collective-permute-start(bf16[384,1536]{1,0:T(8,128)(2,1)} %shard_map.179.others_0_.others_4_), channel_id=1, source_target_pairs={{0,4},{4,0},{8,12},{12,8},{16,20},{20,16},{24,28},{28,24},{1,5},{5... | collective-permute-start | bytes 3538952 | tf_op jit(solution)/shard_map/ppermute | solution.py:1024
  159.9 28.5 %collective-permute-start.30 = (bf16[384,1536]{1,0:T(8,128)(2,1)}, bf16[384,1536]{1,0:T(8,128)(2,1)S(1)}, u32[]{:S(2)}, u32[]{:S(2)}) collective-permute-start(bf16[384,1536]{1,0:T(8,128)(2,1)} %shard_map.179.others_0_.others_4_), channel_id=1, source_target_pairs={{0,16},{4,20},{8,24},{12,28},{16,0},{20,4},{24,8},{28,12},{1,17},{... | collective-permute-start | bytes 3538952 | tf_op jit(solution)/shard_map/ppermute | solution.py:1024
  161.0 28.3 %collective-permute-start.29 = (bf16[384,1536]{1,0:T(8,128)(2,1)}, bf16[384,1536]{1,0:T(8,128)(2,1)S(1)}, u32[]{:S(2)}, u32[]{:S(2)}) collective-permute-start(bf16[384,1536]{1,0:T(8,128)(2,1)} %shard_map.179.others_0_.others_4_), channel_id=1, source_target_pairs={{0,8},{4,12},{8,0},{12,4},{16,24},{20,28},{24,16},{28,20},{1,9},{5... | collective-permute-start | bytes 3538952 | tf_op jit(solution)/shard_map/ppermute | solution.py:1024
  189.3 16.8 %collective-permute-start.34 = (bf16[384,1536]{1,0:T(8,128)(2,1)S(1)}, bf16[384,1536]{1,0:T(8,128)(2,1)}, u32[]{:S(2)}, u32[]{:S(2)}) collective-permute-start(bf16[384,1536]{1,0:T(8,128)(2,1)S(1)} %collective-permute-done.29.others_1_.others_5_), channel_id=1, source_target_pairs={{0,4},{4,0},{8,12},{12,8},{16,20},{20,16},{24,28},{28,24},{1,5},{5... | collective-permute-start | bytes 3538952 | tf_op jit(solution)/shard_map/ppermute | solution.py:1024
  189.3 16.8 %collective-permute-start.35 = (bf16[384,1536]{1,0:T(8,128)(2,1)S(1)}, bf16[384,1536]{1,0:T(8,128)(2,1)}, u32[]{:S(2)}, u32[]{:S(2)}) collective-permute-start(bf16[384,1536]{1,0:T(8,128)(2,1)S(1)} %collective-permute-done.30.others_2_.others_6_), channel_id=1, source_target_pairs={{0,4},{4,0},{8,12},{12,8},{16,20},{20,16},{24,28},{28,24},{1,5},{5... | collective-permute-start | bytes 3538952 | tf_op jit(solution)/shard_map/ppermute | solution.py:1024
  189.9 15.3 %collective-permute-start.32 = (bf16[192,1536]{1,0:T(8,128)(2,1)S(1)}, bf16[192,1536]{1,0:T(8,128)(2,1)S(1)}, u32[]{:S(2)}, u32[]{:S(2)}) collective-permute-start(bf16[192,1536]{1,0:T(8,128)(2,1)S(1)} %slice.145), channel_id=1, source_target_pairs={{0,16},{4,20},{8,24},{12,28},{16,0},{20,4},{24,8},{28,12},{1,17},{... | collective-permute-start | bytes 1769480 | tf_op jit(solution)/shard_map/ppermute | solution.py:1024
  191.0 15.1 %collective-permute-start.33 = (bf16[192,1536]{1,0:T(8,128)(2,1)S(1)}, bf16[192,1536]{1,0:T(8,128)(2,1)}, u32[]{:S(2)}, u32[]{:S(2)}) collective-permute-start(bf16[192,1536]{1,0:T(8,128)(2,1)S(1)} %slice.146), channel_id=1, source_target_pairs={{0,8},{4,12},{8,0},{12,4},{16,24},{20,28},{24,16},{28,20},{1,9},{5... | collective-permute-start | bytes 1769480 | tf_op jit(solution)/shard_map/ppermute | solution.py:1024
  244.5 181.0 %reduce-scatter.6.cloned.1.call-start = ((), (), s32[]{:S(2)}) async-start(), calls=%async_computation.7 | async-start | bytes 1474560 | tf_op jit(solution)/shard_map/reduce_scatter | solution.py:1579
  276.3 13.3 %collective-permute-start.38 = (bf16[384,3072]{1,0:T(8,128)(2,1)}, bf16[384,3072]{1,0:T(8,128)(2,1)S(1)}, u32[]{:S(2)}, u32[]{:S(2)}) collective-permute-start(bf16[384,3072]{1,0:T(8,128)(2,1)} %get-tuple-element.342), channel_id=1, source_target_pairs={{0,4},{4,0},{8,12},{12,8},{16,20},{20,16},{24,28},{28,24},{1,5},{5... | collective-permute-start | bytes 7077896 | tf_op jit(solution)/shard_map/ppermute | solution.py:1024
  293.1 16.5 %collective-permute-start.41 = (bf16[1536,1536]{1,0:T(8,128)(2,1)}, bf16[1536,1536]{1,0:T(8,128)(2,1)}, u32[]{:S(2)}, u32[]{:S(2)}) collective-permute-start(bf16[1536,1536]{1,0:T(8,128)(2,1)} %get-tuple-element.354), channel_id=1, source_target_pairs={{0,4},{4,0},{8,12},{12,8},{16,20},{20,16},{24,28},{28,24},{1,5},{5... | collective-permute-start | bytes 14155784 | tf_op jit(solution)/shard_map/ppermute | solution.py:1024
  293.8 15.7 %collective-permute-start.39 = (bf16[48,3072]{1,0:T(8,128)(2,1)}, bf16[48,3072]{1,0:T(8,128)(2,1)S(1)}, u32[]{:S(2)}, u32[]{:S(2)}) collective-permute-start(bf16[48,3072]{1,0:T(8,128)(2,1)} %get-tuple-element.352), channel_id=1, source_target_pairs={{0,8},{4,12},{8,0},{12,4},{16,24},{20,28},{24,16},{28,20},{1,9},{5... | collective-permute-start | bytes 884744 | tf_op jit(solution)/shard_map/ppermute | solution.py:1024
  293.8 15.7 %collective-permute-start.40 = (bf16[48,3072]{1,0:T(8,128)(2,1)}, bf16[48,3072]{1,0:T(8,128)(2,1)S(1)}, u32[]{:S(2)}, u32[]{:S(2)}) collective-permute-start(bf16[48,3072]{1,0:T(8,128)(2,1)} %get-tuple-element.353), channel_id=1, source_target_pairs={{0,16},{4,20},{8,24},{12,28},{16,0},{20,4},{24,8},{28,12},{1,17},{... | collective-permute-start | bytes 884744 | tf_op jit(solution)/shard_map/ppermute | solution.py:1024
  314.4 27.8 %collective-permute-start.42 = (bf16[96,3072]{1,0:T(8,128)(2,1)}, bf16[96,3072]{1,0:T(8,128)(2,1)S(1)}, u32[]{:S(2)}, u32[]{:S(2)}) collective-permute-start(bf16[96,3072]{1,0:T(8,128)(2,1)} %get-tuple-element.379), channel_id=1, source_target_pairs={{0,8},{4,12},{8,0},{12,4},{16,24},{20,28},{24,16},{28,20},{1,9},{5... | collective-permute-start | bytes 1769480 | tf_op jit(solution)/shard_map/ppermute | solution.py:1024
  315.6 26.6 %collective-permute-start.43 = (bf16[96,3072]{1,0:T(8,128)(2,1)}, bf16[96,3072]{1,0:T(8,128)(2,1)S(1)}, u32[]{:S(2)}, u32[]{:S(2)}) collective-permute-start(bf16[96,3072]{1,0:T(8,128)(2,1)} %get-tuple-element.380), channel_id=1, source_target_pairs={{0,16},{4,20},{8,24},{12,28},{16,0},{20,4},{24,8},{28,12},{1,17},{... | collective-permute-start | bytes 1769480 | tf_op jit(solution)/shard_map/ppermute | solution.py:1024
  317.5 29.7 %collective-permute-start.44 = (bf16[192,1536]{1,0:T(8,128)(2,1)}, bf16[192,1536]{1,0:T(8,128)(2,1)S(1)}, u32[]{:S(2)}, u32[]{:S(2)}) collective-permute-start(bf16[192,1536]{1,0:T(8,128)(2,1)} %get-tuple-element.381), channel_id=1, source_target_pairs={{0,8},{4,12},{8,0},{12,4},{16,24},{20,28},{24,16},{28,20},{1,9},{5... | collective-permute-start | bytes 1769480 | tf_op jit(solution)/shard_map/ppermute | solution.py:1024
  317.5 29.7 %collective-permute-start.45 = (bf16[192,1536]{1,0:T(8,128)(2,1)}, bf16[192,1536]{1,0:T(8,128)(2,1)}, u32[]{:S(2)}, u32[]{:S(2)}) collective-permute-start(bf16[192,1536]{1,0:T(8,128)(2,1)} %get-tuple-element.382), channel_id=1, source_target_pairs={{0,16},{4,20},{8,24},{12,28},{16,0},{20,4},{24,8},{28,12},{1,17},{... | collective-permute-start | bytes 1769480 | tf_op jit(solution)/shard_map/ppermute | solution.py:1024
  339.5 34.0 %collective-permute-start.48 = (bf16[384,2048]{1,0:T(8,128)(2,1)}, bf16[384,2048]{1,0:T(8,128)(2,1)S(1)}, u32[]{:S(2)}, u32[]{:S(2)}) collective-permute-start(bf16[384,2048]{1,0:T(8,128)(2,1)} %get-tuple-element.402), channel_id=1, source_target_pairs={{0,4},{4,0},{8,12},{12,8},{16,20},{20,16},{24,28},{28,24},{1,5},{5... | collective-permute-start | bytes 4718600 | tf_op jit(solution)/shard_map/ppermute | solution.py:1024
  355.6 27.8 %collective-permute-start.46 = (bf16[384,1536]{1,0:T(8,128)(2,1)}, bf16[384,1536]{1,0:T(8,128)(2,1)S(1)}, u32[]{:S(2)}, u32[]{:S(2)}) collective-permute-start(bf16[384,1536]{1,0:T(8,128)(2,1)} %get-tuple-element.400), channel_id=1, source_target_pairs={{0,8},{4,12},{8,0},{12,4},{16,24},{20,28},{24,16},{28,20},{1,9},{5... | collective-permute-start | bytes 3538952 | tf_op jit(solution)/shard_map/ppermute | solution.py:1024
  356.4 27.5 %collective-permute-start.47 = (bf16[384,1536]{1,0:T(8,128)(2,1)}, bf16[384,1536]{1,0:T(8,128)(2,1)}, u32[]{:S(2)}, u32[]{:S(2)}) collective-permute-start(bf16[384,1536]{1,0:T(8,128)(2,1)} %get-tuple-element.401), channel_id=1, source_target_pairs={{0,16},{4,20},{8,24},{12,28},{16,0},{20,4},{24,8},{28,12},{1,17},{... | collective-permute-start | bytes 3538952 | tf_op jit(solution)/shard_map/ppermute | solution.py:1024
  390.9 35.4 %all-to-all-start.1 = ((bf16[4,384,384]{2,1,0:T(8,128)(2,1)}), bf16[4,384,384]{2,1,0:T(8,128)(2,1)S(1)}, u32[]{:S(2)}, u32[]{:S(2)}) async-start(bf16[4,384,384]{2,1,0:T(8,128)(2,1)} %shard_map.194), calls=%async_computation.3 | async-start | bytes 2359296 | tf_op jit(solution)/shard_map/all_to_all | solution.py:1028
  395.6 64.1 %reduce-scatter.8.cloned.1.call-start = ((), (), s32[]{:S(2)}) async-start(), calls=%async_computation.8 | async-start | bytes 737280 | tf_op jit(solution)/shard_map/reduce_scatter | solution.py:1612
  409.3 16.3 %collective-permute-start.57 = (bf16[96,2048]{1,0:T(8,128)(2,1)}, bf16[96,2048]{1,0:T(8,128)(2,1)S(1)}, u32[]{:S(2)}, u32[]{:S(2)}) collective-permute-start(bf16[96,2048]{1,0:T(8,128)(2,1)} %get-tuple-element.442), channel_id=1, source_target_pairs={{0,8},{4,12},{8,0},{12,4},{16,24},{20,28},{24,16},{28,20},{1,9},{5... | collective-permute-start | bytes 1179656 | tf_op jit(solution)/shard_map/ppermute | solution.py:1024
  410.1 15.5 %collective-permute-start.58 = (bf16[96,2048]{1,0:T(8,128)(2,1)}, bf16[96,2048]{1,0:T(8,128)(2,1)}, u32[]{:S(2)}, u32[]{:S(2)}) collective-permute-start(bf16[96,2048]{1,0:T(8,128)(2,1)} %get-tuple-element.443), channel_id=1, source_target_pairs={{0,16},{4,20},{8,24},{12,28},{16,0},{20,4},{24,8},{28,12},{1,17},{... | collective-permute-start | bytes 1179656 | tf_op jit(solution)/shard_map/ppermute | solution.py:1024
  411.4 14.1 %collective-permute-start.59 = (bf16[96,1024]{1,0:T(8,128)(2,1)}, bf16[96,1024]{1,0:T(8,128)(2,1)}, u32[]{:S(2)}, u32[]{:S(2)}) collective-permute-start(bf16[96,1024]{1,0:T(8,128)(2,1)} %get-tuple-element.444), channel_id=1, source_target_pairs={{0,8},{4,12},{8,0},{12,4},{16,24},{20,28},{24,16},{28,20},{1,9},{5... | collective-permute-start | bytes 589832 | tf_op jit(solution)/shard_map/ppermute | solution.py:1024
  412.7 12.9 %collective-permute-start.60 = (bf16[96,1024]{1,0:T(8,128)(2,1)}, bf16[96,1024]{1,0:T(8,128)(2,1)}, u32[]{:S(2)}, u32[]{:S(2)}) collective-permute-start(bf16[96,1024]{1,0:T(8,128)(2,1)} %get-tuple-element.445), channel_id=1, source_target_pairs={{0,16},{4,20},{8,24},{12,28},{16,0},{20,4},{24,8},{28,12},{1,17},{... | collective-permute-start | bytes 589832 | tf_op jit(solution)/shard_map/ppermute | solution.py:1024
  429.7 30.0 %all-to-all-start.2 = ((bf16[4,112,768]{2,1,0:T(8,128)(2,1)}), bf16[4,112,768]{2,1,0:T(8,128)(2,1)S(1)}, u32[]{:S(2)}, u32[]{:S(2)}) async-start(bf16[4,112,768]{2,1,0:T(8,128)(2,1)} %shard_map.197), calls=%async_computation.4 | async-start | bytes 1376256 | tf_op jit(solution)/shard_map/all_to_all | solution.py:1028
  (70 other events, 411.4 us)
Sparse Core Ops, SparseCore 0:
  41.2 32.2 all-gather.4
  78.6 40.1 all-gather.6
  244.6 83.5 reduce-scatter.3
  372.9 30.7 reduce-scatter.5
  425.7 28.3 reduce-scatter.7

commit v5 on v4

--- a/solution.py
+++ b/solution.py
@@ -595,7 +595,10 @@
         begin = end
 
 
-def joining(parts, begin, group_width, source, joined):
+def joining(parts, begin, group_width, source_in, joined, source, arrived):
+    copy = pltpu.make_async_copy(source_in, source, arrived)
+    copy.start()
+    copy.wait()
     rows = joined.shape[0]
     count = source.shape[0]
     width = joined.shape[1] // parts // count
@@ -1045,10 +1048,10 @@
     return kernel_call(
         functools.partial(joining, parts, begin, group_width(parts, count * width, wide)),
         1,
-        [whole(source.shape)],
+        [ANYWHERE],
         whole((rows, parts * count * width)),
         struct((rows, parts * count * width), BF16),
-        [],
+        [pltpu.VMEM(source.shape, BF16), pltpu.SemaphoreType.DMA],
         1_000_000,
     )(source)
 
@@ -1575,16 +1578,14 @@
                 for index, (later, feed_part, attention_sum) in enumerate(summing):
                     carried, feed_part = together(carried, feed_part)
                     parted = part_columns([[feed_part]], 2, wide)
-                    carried, parted = together(carried, parted)
-                    parted = lax.psum_scatter(parted, "head", scatter_dimension=0, tiled=True)
-                    summing[index] = later, parted, attention_sum
+                    share = Sharing([], 2, wide, 2)
+                    carried, share.sent = together(carried, parted)
+                    share.send()
+                    traffic.moving.append(share)
+                    summing[index] = later, share, attention_sum
             branch, grad_middle, carried = traffic.slot((branch, grad_middle, carried))
             if attention_sums:
                 traffic.moving.append(attention_sums[-1])
-                for later, parted, attention_sum in summing:
-                    attention_part = part_columns([attention_sum.arrays()], 4, wide)
-                    carried, attention_part = together(carried, attention_part)
-                    shares[later] = parted, attention_part
             carried, *gain_a, far, near = attend_back(
                 call_groups, carried, grad_middle=grad_middle, branch=branch, places=grad_places
             )
@@ -1601,20 +1602,21 @@
         gain_all = jnp.concatenate(gains)
         input_grad = gradient[own_place]
         gain_all = traffic.slot(gain_all)
+        attention_parts = []
+        for later, share, attention_sum in reversed(summing):
+            parted = part_columns([attention_sum.arrays()], 4, wide)
+            gain_all, parted = together(gain_all, parted)
+            parted = lax.psum_scatter(parted, "head", scatter_dimension=0, tiled=True)
+            attention_parts.append(parted)
+            shares[later] = share, parted
         gain_all = shared_gain(shared_gain(gain_all, CORE), X)
         gain_all = traffic.slot(gain_all)
         gain_all, outputs, input_grad = together(gain_all, outputs, input_grad)
         gain_all = shared_gain(gain_all, Y)
-        gain_all, parted, attention_parts = together(
-            gain_all, [share[0] for share in shares[1:]], [share[1] for share in shares[1:]]
-        )
-        attention_parts = [
-            lax.psum_scatter(part, "head", scatter_dimension=0, tiled=True)
-            for part in attention_parts
-        ]
         attention_share.gain = gain_all
-        parted = traffic.slot(parted)
-        turned = finish([shares[0][0].came] + parted, (1, 1), up_weight.shape[1], turned=True)
+        attention_parts = traffic.slot(attention_parts)
+        feed_shares = [share[0].came for share in shares]
+        turned = finish(feed_shares, (1, 1), up_weight.shape[1], turned=True)
         up_grad, down_grad = traffic.slot(turned)
         up_grad, down_grad = up_grad.swapaxes(1, 2), down_grad.swapaxes(1, 2)
         assert not traffic.moving

time: 481 us -> 478 us (level)
  waiting for transfers between devices: 92.4 us -> 87 us
    all_to_all x3 -> x4, waiting for transfers between devices: 22.8 us -> 16.4 us  [exchange(): lax.all_to_all(values, 'head', split_axis=0, concat_axis=0, tiled=True)]
    all_to_all x3 -> x4, starting transfers between devices: 16 us -> 19.2 us  [exchange(): lax.all_to_all(values, 'head', split_axis=0, concat_axis=0, tiled=True)]
    unnamed x103 -> x111, local copies, waits for them, and re-layouts: 11.3 us -> 10.7 us
  transfers between devices with their start and end apart: 69 -> 69, of which waited for: 27 -> 28; matrix products, arithmetic and copies ran while one was open for 5% -> 5% of each run, Pallas kernels for 47% -> 45%
where the time goes in v5:
time: 478 us; the launch traced here: 469 us
  Pallas kernels  258 us (54%)
  waiting for transfers between devices  87 us (18%)
  starting transfers between devices  66.7 us (14%)
  local copies, waits for them, and re-layouts  34.3 us (7%)
  between operations  15 us (3%)
  other arithmetic  7.36 us (2%)
    ppermute x59, waiting for transfers between devices, hop(): return lax.ppermute(values, 'dp', [(i, i ^ bit) for i in range(count)])  69.6 us
    pallas_call x3, Pallas kernels, run_attention_backward(): kernel_call(functools.partial(attention_backward, first, last, scale, gro...  66.8 us
    pallas_call x3, Pallas kernels, run_feed_back(): kernel_call(functools.partial(feed_back, first, last, segments, len(piece...  49.6 us
    pallas_call x5, Pallas kernels, run_feed_forward(): kernel_call(functools.partial(feed_forward, len(pieces)), 1, [ANYWHERE] *...  49.3 us
    pallas_call x2, Pallas kernels, run_attention_forward(): kernel_call(functools.partial(attention_forward, scale, len(pieces)), gro...  42 us
    ppermute x59, starting transfers between devices, hop(): return lax.ppermute(values, 'dp', [(i, i ^ bit) for i in range(count)])  41.2 us
    all_to_all x4, starting transfers between devices, exchange(): lax.all_to_all(values, 'head', split_axis=0, concat_axis=0, tiled=True)  19.2 us
    all_to_all x4, waiting for transfers between devices, exchange(): lax.all_to_all(values, 'head', split_axis=0, concat_axis=0, tiled=True)  16.4 us
  transfers between devices with their start and end apart: 69, of which 28 were waited for; matrix products, arithmetic and copies ran while one was open for 5% of the time, Pallas kernels for 45%

profile of v5, /device:TPU:0, one launch (start us, length us, event | category | flops | bytes accessed | tf_op | source)
XLA Modules:
  0.0 468.7 jit_solution(15239468228338912940)
XLA Ops:
  12.6 6.3 %all-to-all-start = ((bf16[4,112,768]{2,1,0:T(8,128)(2,1)}), bf16[4,112,768]{2,1,0:T(8,128)(2,1)S(1)}, u32[]{:S(2)}, u32[]{:S(2)}) async-start(bf16[4,112,768]{2,1,0:T(8,128)(2,1)} %broadcast_in_dim.13), calls=%async_computation | async-start | bytes 1376256 | tf_op jit(solution)/shard_map/all_to_all | solution.py:1031
  21.0 4.6 collective-permute-start
  31.8 2.8 shard_map.170
  48.3 3.4 shard_map.173
  51.7 8.4 %collective-permute-done.3.others_2_ = bf16[96,3072]{1,0:T(8,128)(2,1)} collective-permute-done((bf16[96,3072]{1,0:T(8,128)(2,1)}, bf16[96,3072]{1,0:T(8,128)(2,1)}, u32[]{:S(2)}, u32[]{:S(2)}) %collective-permute-start.3) | collective-permute-done | bytes 589856 | tf_op jit(solution)/shard_map/ppermute | solution.py:1027
  65.9 4.7 collective-permute-done.6.others_4_
  70.6 2.3 collective-permute-done.5.others_3_
  73.5 2.4 copy.56
  75.8 2.6 shard_map.171.others_0_.others_5_
  81.6 21.2 %shard_map.174 = (bf16[768,3072]{1,0:T(8,128)(2,1)}, bf16[640,768]{1,0:T(8,128)(2,1)}, f32[640,768]{1,0:T(8,128)}, f32[640,768]{1,0:T(8,128)}, bf16[640,768]{1,0...) custom-call(s32[10]{0:T(128)} %stack.123.places, ...), custom_call_target="tpu_custom_call" | custom-call | flops 28999999488 | bytes 48333332 | tf_op jit(solution)/shard_map/pallas_call | solution.py:791
  102.9 4.3 collective-permute-done.12.others_2_.others_7_
  111.5 9.5 %shard_map.175 = (bf16[640,1152]{1,0:T(8,128)(2,1)}, bf16[640,1152]{1,0:T(8,128)(2,1)}, f32[640,768]{1,0:T(8,128)}) custom-call(f32[640,768]{1,0:T(8,128)} %get-tuple-element.267.carried_in.middle, bf16[640,768]{1,0:T(8,128)(2,1)} %get-tuple-element.268.normed_in, bf16[384,1536]{1,0:T(8,128)(2,1)} %shard_map.171.others_0_.others_5_, ...), custom_call_target="tpu_custom_call" | custom-call | flops 9666666496 | bytes 16111111 | tf_op jit(solution)/shard_map/pallas_call | solution.py:926
  121.1 3.4 collective-permute-done.14.others_0_.others_8_
  125.7 2.5 shard_map.176.others_0_
  130.8 9.5 %shard_map.177 = (bf16[640,1152]{1,0:T(8,128)(2,1)}, bf16[640,1152]{1,0:T(8,128)(2,1)}, f32[640,768]{1,0:T(8,128)}) custom-call(f32[640,768]{1,0:T(8,128)} %get-tuple-element.277.carried_in, bf16[640,768]{1,0:T(8,128)(2,1)} %get-tuple-element.268.normed_in, bf16[384,1536]{1,0:T(8,128)(2,1)} %copy-done.35, ...), custom_call_target="tpu_custom_call" | custom-call | flops 9666666496 | bytes 16111111 | tf_op jit(solution)/shard_map/pallas_call | solution.py:926
  140.3 3.9 collective-permute-done.19.others_2_
  148.9 7.6 %shard_map.178 = (bf16[640,768]{1,0:T(8,128)(2,1)}, bf16[640,768]{1,0:T(8,128)(2,1)}, f32[640,768]{1,0:T(8,128)}) custom-call(f32[640,768]{1,0:T(8,128)} %get-tuple-element.286.carried_in, bf16[640,768]{1,0:T(8,128)(2,1)} %get-tuple-element.268.normed_in, bf16[192,1536]{1,0:T(8,128)(2,1)} %collective-permute-done.14.others_0_.others_8_, ...), custom_call_target="tpu_custom_call" | custom-call | flops 9666666496 | bytes 16111111 | tf_op jit(solution)/shard_map/pallas_call | solution.py:926
  157.2 2.8 shard_map.179.others_0_.others_4_
  163.4 20.8 %shard_map.180 = (bf16[768,3072]{1,0:T(8,128)(2,1)}, bf16[640,768]{1,0:T(8,128)(2,1)}, f32[640,768]{1,0:T(8,128)}, f32[640,768]{1,0:T(8,128)}, bf16[640,768]{1,0...) custom-call(s32[10]{0:T(128)} %stack.123.places, ...), custom_call_target="tpu_custom_call" | custom-call | flops 28999999488 | bytes 48333332 | tf_op jit(solution)/shard_map/pallas_call | solution.py:791
  184.3 4.3 collective-permute-done.30.others_2_.others_6_
  192.0 9.5 %shard_map.181 = (bf16[640,1152]{1,0:T(8,128)(2,1)}, bf16[640,1152]{1,0:T(8,128)(2,1)}, f32[640,768]{1,0:T(8,128)}) custom-call(f32[640,768]{1,0:T(8,128)} %get-tuple-element.307.carried_in.middle, bf16[640,768]{1,0:T(8,128)(2,1)} %get-tuple-element.304.normed_in, bf16[384,1536]{1,0:T(8,128)(2,1)} %shard_map.179.others_0_.others_4_, ...), custom_call_target="tpu_custom_call" | custom-call | flops 9666666496 | bytes 16111111 | tf_op jit(solution)/shard_map/pallas_call | solution.py:926
  201.5 3.8 collective-permute-done.32.others_3_.others_10_
  210.1 13.2 %shard_map.182 = (bf16[640,1920]{1,0:T(8,128)(2,1)}, bf16[640,1920]{1,0:T(8,128)(2,1)}, f32[640,768]{1,0:T(8,128)}) custom-call(f32[640,768]{1,0:T(8,128)} %get-tuple-element.314.carried_in, bf16[640,768]{1,0:T(8,128)(2,1)} %get-tuple-element.304.normed_in, bf16[384,1536]{1,0:T(8,128)(2,1)} %collective-permute-done.31.others_0_.others_7_, ...), custom_call_target="tpu_custom_call" | custom-call | flops 9666666496 | bytes 16111111 | tf_op jit(solution)/shard_map/pallas_call | solution.py:926
  223.3 21.3 %shard_map.183 = (bf16[3072,1536]{1,0:T(8,128)(2,1)}, f32[640,768]{1,0:T(8,128)}, f32[1,768]{1,0:T(1,128)}, bf16[640,768]{1,0:T(8,128)(2,1)}) custom-call(s32[10]{0:T(128)} %stack.114.places, f32[640,768]{1,0:T(8,128)} %get-tuple-element.241.gradient_in, f32[640,768]{1,0:T(8,128)} %get-tuple-element.307.carried_in.middle, ...), custom_call_target="tpu_custom_call" | custom-call | flops 14499999744 | bytes 24166666 | tf_op jit(solution)/shard_map/pallas_call | solution.py:967
  245.3 30.8 %shard_map.184 = (f32[640,768]{1,0:T(8,128)}, f32[1,768]{1,0:T(1,128)}, bf16[384,3072]{1,0:T(8,128)(2,1)}, bf16[384,3072]{1,0:T(8,128)(2,1)}) custom-call(s32[8]{0:T(128)} %stack.103.places, bf16[640,768]{1,0:T(8,128)(2,1)} %get-tuple-element.322.branch_in, bf16[768,3072]{1,0:T(8,128)(2,1)} %get-tuple-element.323.weights_in, ...), custom_call_target="tpu_custom_call" | custom-call | flops 40000000000 | bytes 66666664 | tf_op jit(solution)/shard_map/pallas_call | solution.py:868
  276.1 13.5 %shard_map.185 = (bf16[1536,1536]{1,0:T(8,128)(2,1)}, f32[640,768]{1,0:T(8,128)}) custom-call(s32[5]{0:T(128)} %constant.47.clone.places, f32[640,768]{1,0:T(8,128)} %get-tuple-element.331.gradient_in, f32[640,768]{1,0:T(8,128)} %get-tuple-element.267.carried_in.middle, f32[1,768]{1,0:T(1,128)} %get-tuple-element.253.gain_2, ...), custom_call_target="tpu_custom_call" | custom-call | flops 14499999744 | bytes 24166666 | tf_op jit(solution)/shard_map/pallas_call | solution.py:967
  294.9 14.8 %shard_map.187 = (bf16[1536,1536]{1,0:T(8,128)(2,1)}, f32[640,768]{1,0:T(8,128)}, f32[1,768]{1,0:T(1,128)}, bf16[640,768]{1,0:T(8,128)(2,1)}) custom-call(s32[5]{0:T(128)} %constant.47.clone.places, f32[640,768]{1,0:T(8,128)} %get-tuple-element.331.gradient_in, f32[640,768]{1,0:T(8,128)} %get-tuple-element.267.carried_in.middle, ...), custom_call_target="tpu_custom_call" | custom-call | flops 14499999744 | bytes 24166666 | tf_op jit(solution)/shard_map/pallas_call | solution.py:967
  310.5 4.1 shard_map.188
  318.7 21.0 %shard_map.189 = (f32[640,768]{1,0:T(8,128)}, bf16[384,2048]{1,0:T(8,128)(2,1)}, bf16[384,2048]{1,0:T(8,128)(2,1)}) custom-call(s32[8]{0:T(128)} %stack.103.places, bf16[640,768]{1,0:T(8,128)(2,1)} %get-tuple-element.388.branch_in, bf16[768,3072]{1,0:T(8,128)(2,1)} %get-tuple-element.365.weights_in, bf16[640,768]{1,0:T(8,128)(2,1)} %get-tuple-element.366.mixed_in, ...), custom_call_target="tpu_custom_call" | custom-call | flops 26666665984 | bytes 44444444 | tf_op jit(solution)/shard_map/pallas_call | solution.py:868
  339.8 2.6 shard_map.190
  342.4 4.9 %collective-permute-done.44.others_4_ = bf16[192,1536]{1,0:T(8,128)(2,1)S(1)} collective-permute-done((bf16[192,1536]{1,0:T(8,128)(2,1)}, bf16[192,1536]{1,0:T(8,128)(2,1)S(1)}, u32[]{:S(2)}, u32[]{:S(2)}) %collective-permute-start.44) | collective-permute-done | bytes 589856 | tf_op jit(solution)/shard_map/ppermute | solution.py:1027
  347.4 4.6 all-to-all-start.1
  352.0 4.4 shard_map.191
  358.5 15.0 %shard_map.192 = (f32[640,768]{1,0:T(8,128)}, f32[1,768]{1,0:T(1,128)}, bf16[384,1024]{1,0:T(8,128)(2,1)}, bf16[384,1024]{1,0:T(8,128)(2,1)}) custom-call(s32[8]{0:T(128)} %stack.103.places, bf16[640,768]{1,0:T(8,128)(2,1)} %get-tuple-element.388.branch_in, bf16[768,3072]{1,0:T(8,128)(2,1)} %get-tuple-element.365.weights_in, ...), custom_call_target="tpu_custom_call" | custom-call | flops 13333332992 | bytes 22222222 | tf_op jit(solution)/shard_map/pallas_call | solution.py:868
  376.1 7.9 %collective-permute-done.46.others_2_ = bf16[384,1536]{1,0:T(8,128)(2,1)} collective-permute-done((bf16[384,1536]{1,0:T(8,128)(2,1)}, bf16[384,1536]{1,0:T(8,128)(2,1)}, u32[]{:S(2)}, u32[]{:S(2)}) %collective-permute-start.46) | collective-permute-done | bytes 1179680 | tf_op jit(solution)/shard_map/ppermute | solution.py:1027
  385.1 4.6 shard_map.193
  391.8 4.8 %all-to-all-start.2 = ((bf16[4,384,384]{2,1,0:T(8,128)(2,1)}), bf16[4,384,384]{2,1,0:T(8,128)(2,1)S(1)}, u32[]{:S(2)}, u32[]{:S(2)}) async-start(bf16[4,384,384]{2,1,0:T(8,128)(2,1)} %shard_map.193), calls=%async_computation.4 | async-start | bytes 2359296 | tf_op jit(solution)/shard_map/all_to_all | solution.py:1031
  396.9 2.9 shard_map.195
  405.8 3.0 collective-permute-done.51
  410.2 3.0 shard_map.196
  417.3 2.4 slice.167
  421.6 7.1 %collective-permute-done.60 = f32[4,768]{1,0:T(4,128)S(1)} collective-permute-done((f32[4,768]{1,0:T(4,128)S(1)}, f32[4,768]{1,0:T(4,128)S(1)}, u32[]{:S(2)}, u32[]{:S(2)}) %collective-permute-start.60) | collective-permute-done | bytes 12320 | tf_op jit(solution)/shard_map/ppermute | solution.py:1027
  430.3 2.2 all-to-all-done.2.others_0_
  432.5 3.4 shard_map.198
  435.9 3.5 all-to-all-start.3
  439.4 3.2 shard_map.197
  442.6 14.2 %all-to-all-done.3.others_0_ = bf16[4,112,768]{2,1,0:T(8,128)(2,1)S(1)} async-done(((bf16[4,112,768]{2,1,0:T(8,128)(2,1)}), bf16[4,112,768]{2,1,0:T(8,128)(2,1)S(1)}, u32[]{:S(2)}, u32[]{:S(2)}) %all-to-all-start.3) | async-done | bytes 688160 | tf_op jit(solution)/shard_map/all_to_all | solution.py:1031
  457.7 2.1 shard_map.199
  (282 shorter events, 98.8 us)
Async XLA Ops:
  12.6 28.4 %all-to-all-start = ((bf16[4,112,768]{2,1,0:T(8,128)(2,1)}), bf16[4,112,768]{2,1,0:T(8,128)(2,1)S(1)}, u32[]{:S(2)}, u32[]{:S(2)}) async-start(bf16[4,112,768]{2,1,0:T(8,128)(2,1)} %broadcast_in_dim.13), calls=%async_computation | async-start | bytes 1376256 | tf_op jit(solution)/shard_map/all_to_all | solution.py:1031
  18.9 54.5 %all-gather.5.cloned.1.call-start = ((), (), s32[]{:S(2)}) async-start(), calls=%async_computation.8 | async-start | bytes 1474560 | tf_op jit(solution)/shard_map/all_gather | solution.py:1366
  21.0 16.2 %collective-permute-start = (bf16[64,1536]{1,0:T(8,128)(2,1)}, bf16[64,1536]{1,0:T(8,128)(2,1)}, u32[]{:S(2)}, u32[]{:S(2)}) collective-permute-start(bf16[64,1536]{1,0:T(8,128)(2,1)} %get-tuple-element.464), channel_id=1, source_target_pairs={{0,1},{1,2},{2,3},{4,5},{5,6},{6,7},{8,9},{9,10},{10,11},{12,13},{... | collective-permute-start | bytes 589832 | tf_op jit(solution)/shard_map/ppermute | solution.py:1280
  41.0 84.7 %all-gather.7.cloned.1.call-start = ((), (), s32[]{:S(2)}) async-start(), calls=%async_computation.9 | async-start | bytes 2211840 | tf_op jit(solution)/shard_map/all_gather | solution.py:1366
  44.0 16.1 %collective-permute-start.3 = (bf16[96,3072]{1,0:T(8,128)(2,1)}, bf16[96,3072]{1,0:T(8,128)(2,1)}, u32[]{:S(2)}, u32[]{:S(2)}) collective-permute-start(bf16[96,3072]{1,0:T(8,128)(2,1)} %shard_map.172.others_0_), channel_id=1, source_target_pairs={{0,16},{4,20},{8,24},{12,28},{16,0},{20,4},{24,8},{28,12},{1,17},{... | collective-permute-start | bytes 1769480 | tf_op jit(solution)/shard_map/ppermute | solution.py:1027
  45.6 15.7 %collective-permute-start.2 = (bf16[96,3072]{1,0:T(8,128)(2,1)}, bf16[96,3072]{1,0:T(8,128)(2,1)}, u32[]{:S(2)}, u32[]{:S(2)}) collective-permute-start(bf16[96,3072]{1,0:T(8,128)(2,1)} %shard_map.172.others_0_), channel_id=1, source_target_pairs={{0,8},{4,12},{8,0},{12,4},{16,24},{20,28},{24,16},{28,20},{1,9},{5... | collective-permute-start | bytes 1769480 | tf_op jit(solution)/shard_map/ppermute | solution.py:1027
  65.4 16.2 %collective-permute-start.7 = (bf16[96,3072]{1,0:T(8,128)(2,1)}, bf16[96,3072]{1,0:T(8,128)(2,1)}, u32[]{:S(2)}, u32[]{:S(2)}) collective-permute-start(bf16[96,3072]{1,0:T(8,128)(2,1)} %collective-permute-done.2.others_1_), channel_id=1, source_target_pairs={{0,4},{4,0},{8,12},{12,8},{16,20},{20,16},{24,28},{28,24},{1,5},{5... | collective-permute-start | bytes 1769480 | tf_op jit(solution)/shard_map/ppermute | solution.py:1027
  65.4 16.2 %collective-permute-start.8 = (bf16[96,3072]{1,0:T(8,128)(2,1)}, bf16[96,3072]{1,0:T(8,128)(2,1)}, u32[]{:S(2)}, u32[]{:S(2)}) collective-permute-start(bf16[96,3072]{1,0:T(8,128)(2,1)} %collective-permute-done.3.others_2_), channel_id=1, source_target_pairs={{0,4},{4,0},{8,12},{12,8},{16,20},{20,16},{24,28},{28,24},{1,5},{5... | collective-permute-start | bytes 1769480 | tf_op jit(solution)/shard_map/ppermute | solution.py:1027
  78.5 261.3 %reduce-scatter.3.cloned.1.call-start = ((), (), s32[]{:S(2)}) async-start(), calls=%async_computation.6 | async-start | bytes 10616832 | tf_op jit(solution)/shard_map/reduce_scatter | solution.py:1527
  78.5 24.3 %collective-permute-start.13 = (bf16[384,1536]{1,0:T(8,128)(2,1)}, bf16[384,1536]{1,0:T(8,128)(2,1)S(1)}, u32[]{:S(2)}, u32[]{:S(2)}) collective-permute-start(bf16[384,1536]{1,0:T(8,128)(2,1)} %shard_map.171.others_0_.others_5_), channel_id=1, source_target_pairs={{0,4},{4,0},{8,12},{12,8},{16,20},{20,16},{24,28},{28,24},{1,5},{5... | collective-permute-start | bytes 3538952 | tf_op jit(solution)/shard_map/ppermute | solution.py:1027
  78.6 28.6 %collective-permute-start.12 = (bf16[384,1536]{1,0:T(8,128)(2,1)}, bf16[384,1536]{1,0:T(8,128)(2,1)S(1)}, u32[]{:S(2)}, u32[]{:S(2)}) collective-permute-start(bf16[384,1536]{1,0:T(8,128)(2,1)} %shard_map.171.others_0_.others_5_), channel_id=1, source_target_pairs={{0,16},{4,20},{8,24},{12,28},{16,0},{20,4},{24,8},{28,12},{1,17},{... | collective-permute-start | bytes 3538952 | tf_op jit(solution)/shard_map/ppermute | solution.py:1027
  80.2 28.2 %collective-permute-start.11 = (bf16[384,1536]{1,0:T(8,128)(2,1)}, bf16[384,1536]{1,0:T(8,128)(2,1)S(1)}, u32[]{:S(2)}, u32[]{:S(2)}) collective-permute-start(bf16[384,1536]{1,0:T(8,128)(2,1)} %shard_map.171.others_0_.others_5_), channel_id=1, source_target_pairs={{0,8},{4,12},{8,0},{12,4},{16,24},{20,28},{24,16},{28,20},{1,9},{5... | collective-permute-start | bytes 3538952 | tf_op jit(solution)/shard_map/ppermute | solution.py:1027
  108.4 16.8 %collective-permute-start.16 = (bf16[384,1536]{1,0:T(8,128)(2,1)S(1)}, bf16[384,1536]{1,0:T(8,128)(2,1)}, u32[]{:S(2)}, u32[]{:S(2)}) collective-permute-start(bf16[384,1536]{1,0:T(8,128)(2,1)S(1)} %collective-permute-done.11.others_1_.others_6_), channel_id=1, source_target_pairs={{0,4},{4,0},{8,12},{12,8},{16,20},{20,16},{24,28},{28,24},{1,5},{5... | collective-permute-start | bytes 3538952 | tf_op jit(solution)/shard_map/ppermute | solution.py:1027
  108.4 16.8 %collective-permute-start.17 = (bf16[384,1536]{1,0:T(8,128)(2,1)S(1)}, bf16[384,1536]{1,0:T(8,128)(2,1)}, u32[]{:S(2)}, u32[]{:S(2)}) collective-permute-start(bf16[384,1536]{1,0:T(8,128)(2,1)S(1)} %collective-permute-done.12.others_2_.others_7_), channel_id=1, source_target_pairs={{0,4},{4,0},{8,12},{12,8},{16,20},{20,16},{24,28},{28,24},{1,5},{5... | collective-permute-start | bytes 3538952 | tf_op jit(solution)/shard_map/ppermute | solution.py:1027
  109.0 15.5 %collective-permute-start.14 = (bf16[192,1536]{1,0:T(8,128)(2,1)S(1)}, bf16[192,1536]{1,0:T(8,128)(2,1)}, u32[]{:S(2)}, u32[]{:S(2)}) collective-permute-start(bf16[192,1536]{1,0:T(8,128)(2,1)S(1)} %slice.141), channel_id=1, source_target_pairs={{0,16},{4,20},{8,24},{12,28},{16,0},{20,4},{24,8},{28,12},{1,17},{... | collective-permute-start | bytes 1769480 | tf_op jit(solution)/shard_map/ppermute | solution.py:1027
  110.0 15.1 %collective-permute-start.15 = (bf16[192,1536]{1,0:T(8,128)(2,1)S(1)}, bf16[192,1536]{1,0:T(8,128)(2,1)}, u32[]{:S(2)}, u32[]{:S(2)}) collective-permute-start(bf16[192,1536]{1,0:T(8,128)(2,1)S(1)} %slice.142), channel_id=1, source_target_pairs={{0,8},{4,12},{8,0},{12,4},{16,24},{20,28},{24,16},{28,20},{1,9},{5... | collective-permute-start | bytes 1769480 | tf_op jit(solution)/shard_map/ppermute | solution.py:1027
  125.2 21.5 %collective-permute-start.21 = (bf16[192,1536]{1,0:T(8,128)(2,1)}, bf16[192,1536]{1,0:T(8,128)(2,1)S(1)}, u32[]{:S(2)}, u32[]{:S(2)}) collective-permute-start(bf16[192,1536]{1,0:T(8,128)(2,1)} %collective-permute-done.14.others_0_.others_8_), channel_id=1, source_target_pairs={{0,4},{4,0},{8,12},{12,8},{16,20},{20,16},{24,28},{28,24},{1,5},{5... | collective-permute-start | bytes 1769480 | tf_op jit(solution)/shard_map/ppermute | solution.py:1027
  125.2 22.9 %collective-permute-start.22 = (bf16[192,1536]{1,0:T(8,128)(2,1)}, bf16[192,1536]{1,0:T(8,128)(2,1)S(1)}, u32[]{:S(2)}, u32[]{:S(2)}) collective-permute-start(bf16[192,1536]{1,0:T(8,128)(2,1)} %collective-permute-done.15.others_1_.others_9_), channel_id=1, source_target_pairs={{0,4},{4,0},{8,12},{12,8},{16,20},{20,16},{24,28},{28,24},{1,5},{5... | collective-permute-start | bytes 1769480 | tf_op jit(solution)/shard_map/ppermute | solution.py:1027
  128.3 15.9 %collective-permute-start.19 = (bf16[96,3072]{1,0:T(8,128)(2,1)}, bf16[96,3072]{1,0:T(8,128)(2,1)S(1)}, u32[]{:S(2)}, u32[]{:S(2)}) collective-permute-start(bf16[96,3072]{1,0:T(8,128)(2,1)} %shard_map.176.others_0_), channel_id=1, source_target_pairs={{0,16},{4,20},{8,24},{12,28},{16,0},{20,4},{24,8},{28,12},{1,17},{... | collective-permute-start | bytes 1769480 | tf_op jit(solution)/shard_map/ppermute | solution.py:1027
  129.4 15.6 %collective-permute-start.18 = (bf16[96,3072]{1,0:T(8,128)(2,1)}, bf16[96,3072]{1,0:T(8,128)(2,1)S(1)}, u32[]{:S(2)}, u32[]{:S(2)}) collective-permute-start(bf16[96,3072]{1,0:T(8,128)(2,1)} %shard_map.176.others_0_), channel_id=1, source_target_pairs={{0,8},{4,12},{8,0},{12,4},{16,24},{20,28},{24,16},{28,20},{1,9},{5... | collective-permute-start | bytes 1769480 | tf_op jit(solution)/shard_map/ppermute | solution.py:1027
  145.0 15.1 %collective-permute-start.25 = (bf16[96,3072]{1,0:T(8,128)(2,1)S(1)}, bf16[96,3072]{1,0:T(8,128)(2,1)S(1)}, u32[]{:S(2)}, u32[]{:S(2)}) collective-permute-start(bf16[96,3072]{1,0:T(8,128)(2,1)S(1)} %collective-permute-done.18.others_1_), channel_id=1, source_target_pairs={{0,4},{4,0},{8,12},{12,8},{16,20},{20,16},{24,28},{28,24},{1,5},{5... | collective-permute-start | bytes 1769480 | tf_op jit(solution)/shard_map/ppermute | solution.py:1027
  145.1 16.0 %collective-permute-start.26 = (bf16[96,3072]{1,0:T(8,128)(2,1)S(1)}, bf16[96,3072]{1,0:T(8,128)(2,1)}, u32[]{:S(2)}, u32[]{:S(2)}) collective-permute-start(bf16[96,3072]{1,0:T(8,128)(2,1)S(1)} %collective-permute-done.19.others_2_), channel_id=1, source_target_pairs={{0,4},{4,0},{8,12},{12,8},{16,20},{20,16},{24,28},{28,24},{1,5},{5... | collective-permute-start | bytes 1769480 | tf_op jit(solution)/shard_map/ppermute | solution.py:1027
  159.9 24.3 %collective-permute-start.31 = (bf16[384,1536]{1,0:T(8,128)(2,1)}, bf16[384,1536]{1,0:T(8,128)(2,1)}, u32[]{:S(2)}, u32[]{:S(2)}) collective-permute-start(bf16[384,1536]{1,0:T(8,128)(2,1)} %shard_map.179.others_0_.others_4_), channel_id=1, source_target_pairs={{0,4},{4,0},{8,12},{12,8},{16,20},{20,16},{24,28},{28,24},{1,5},{5... | collective-permute-start | bytes 3538952 | tf_op jit(solution)/shard_map/ppermute | solution.py:1027
  160.1 28.5 %collective-permute-start.30 = (bf16[384,1536]{1,0:T(8,128)(2,1)}, bf16[384,1536]{1,0:T(8,128)(2,1)S(1)}, u32[]{:S(2)}, u32[]{:S(2)}) collective-permute-start(bf16[384,1536]{1,0:T(8,128)(2,1)} %shard_map.179.others_0_.others_4_), channel_id=1, source_target_pairs={{0,16},{4,20},{8,24},{12,28},{16,0},{20,4},{24,8},{28,12},{1,17},{... | collective-permute-start | bytes 3538952 | tf_op jit(solution)/shard_map/ppermute | solution.py:1027
  161.2 28.3 %collective-permute-start.29 = (bf16[384,1536]{1,0:T(8,128)(2,1)}, bf16[384,1536]{1,0:T(8,128)(2,1)S(1)}, u32[]{:S(2)}, u32[]{:S(2)}) collective-permute-start(bf16[384,1536]{1,0:T(8,128)(2,1)} %shard_map.179.others_0_.others_4_), channel_id=1, source_target_pairs={{0,8},{4,12},{8,0},{12,4},{16,24},{20,28},{24,16},{28,20},{1,9},{5... | collective-permute-start | bytes 3538952 | tf_op jit(solution)/shard_map/ppermute | solution.py:1027
  189.4 16.8 %collective-permute-start.34 = (bf16[384,1536]{1,0:T(8,128)(2,1)S(1)}, bf16[384,1536]{1,0:T(8,128)(2,1)}, u32[]{:S(2)}, u32[]{:S(2)}) collective-permute-start(bf16[384,1536]{1,0:T(8,128)(2,1)S(1)} %collective-permute-done.29.others_1_.others_5_), channel_id=1, source_target_pairs={{0,4},{4,0},{8,12},{12,8},{16,20},{20,16},{24,28},{28,24},{1,5},{5... | collective-permute-start | bytes 3538952 | tf_op jit(solution)/shard_map/ppermute | solution.py:1027
  189.4 16.8 %collective-permute-start.35 = (bf16[384,1536]{1,0:T(8,128)(2,1)S(1)}, bf16[384,1536]{1,0:T(8,128)(2,1)}, u32[]{:S(2)}, u32[]{:S(2)}) collective-permute-start(bf16[384,1536]{1,0:T(8,128)(2,1)S(1)} %collective-permute-done.30.others_2_.others_6_), channel_id=1, source_target_pairs={{0,4},{4,0},{8,12},{12,8},{16,20},{20,16},{24,28},{28,24},{1,5},{5... | collective-permute-start | bytes 3538952 | tf_op jit(solution)/shard_map/ppermute | solution.py:1027
  190.0 15.3 %collective-permute-start.32 = (bf16[192,1536]{1,0:T(8,128)(2,1)S(1)}, bf16[192,1536]{1,0:T(8,128)(2,1)S(1)}, u32[]{:S(2)}, u32[]{:S(2)}) collective-permute-start(bf16[192,1536]{1,0:T(8,128)(2,1)S(1)} %slice.145), channel_id=1, source_target_pairs={{0,16},{4,20},{8,24},{12,28},{16,0},{20,4},{24,8},{28,12},{1,17},{... | collective-permute-start | bytes 1769480 | tf_op jit(solution)/shard_map/ppermute | solution.py:1027
  191.2 15.1 %collective-permute-start.33 = (bf16[192,1536]{1,0:T(8,128)(2,1)S(1)}, bf16[192,1536]{1,0:T(8,128)(2,1)}, u32[]{:S(2)}, u32[]{:S(2)}) collective-permute-start(bf16[192,1536]{1,0:T(8,128)(2,1)S(1)} %slice.146), channel_id=1, source_target_pairs={{0,8},{4,12},{8,0},{12,4},{16,24},{20,28},{24,16},{28,20},{1,9},{5... | collective-permute-start | bytes 1769480 | tf_op jit(solution)/shard_map/ppermute | solution.py:1027
  276.0 13.6 %collective-permute-start.38 = (bf16[384,3072]{1,0:T(8,128)(2,1)}, bf16[384,3072]{1,0:T(8,128)(2,1)S(1)}, u32[]{:S(2)}, u32[]{:S(2)}) collective-permute-start(bf16[384,3072]{1,0:T(8,128)(2,1)} %get-tuple-element.340), channel_id=1, source_target_pairs={{0,4},{4,0},{8,12},{12,8},{16,20},{20,16},{24,28},{28,24},{1,5},{5... | collective-permute-start | bytes 7077896 | tf_op jit(solution)/shard_map/ppermute | solution.py:1027
  293.2 16.5 %collective-permute-start.41 = (bf16[1536,1536]{1,0:T(8,128)(2,1)}, bf16[1536,1536]{1,0:T(8,128)(2,1)}, u32[]{:S(2)}, u32[]{:S(2)}) collective-permute-start(bf16[1536,1536]{1,0:T(8,128)(2,1)} %get-tuple-element.352), channel_id=1, source_target_pairs={{0,4},{4,0},{8,12},{12,8},{16,20},{20,16},{24,28},{28,24},{1,5},{5... | collective-permute-start | bytes 14155784 | tf_op jit(solution)/shard_map/ppermute | solution.py:1027
  293.7 16.0 %collective-permute-start.39 = (bf16[48,3072]{1,0:T(8,128)(2,1)}, bf16[48,3072]{1,0:T(8,128)(2,1)S(1)}, u32[]{:S(2)}, u32[]{:S(2)}) collective-permute-start(bf16[48,3072]{1,0:T(8,128)(2,1)} %get-tuple-element.350), channel_id=1, source_target_pairs={{0,8},{4,12},{8,0},{12,4},{16,24},{20,28},{24,16},{28,20},{1,9},{5... | collective-permute-start | bytes 884744 | tf_op jit(solution)/shard_map/ppermute | solution.py:1027
  294.0 15.8 %collective-permute-start.40 = (bf16[48,3072]{1,0:T(8,128)(2,1)}, bf16[48,3072]{1,0:T(8,128)(2,1)S(1)}, u32[]{:S(2)}, u32[]{:S(2)}) collective-permute-start(bf16[48,3072]{1,0:T(8,128)(2,1)} %get-tuple-element.351), channel_id=1, source_target_pairs={{0,16},{4,20},{8,24},{12,28},{16,0},{20,4},{24,8},{28,12},{1,17},{... | collective-permute-start | bytes 884744 | tf_op jit(solution)/shard_map/ppermute | solution.py:1027
  314.6 27.8 %collective-permute-start.42 = (bf16[96,3072]{1,0:T(8,128)(2,1)}, bf16[96,3072]{1,0:T(8,128)(2,1)S(1)}, u32[]{:S(2)}, u32[]{:S(2)}) collective-permute-start(bf16[96,3072]{1,0:T(8,128)(2,1)} %get-tuple-element.377), channel_id=1, source_target_pairs={{0,8},{4,12},{8,0},{12,4},{16,24},{20,28},{24,16},{28,20},{1,9},{5... | collective-permute-start | bytes 1769480 | tf_op jit(solution)/shard_map/ppermute | solution.py:1027
  315.9 26.5 %collective-permute-start.43 = (bf16[96,3072]{1,0:T(8,128)(2,1)}, bf16[96,3072]{1,0:T(8,128)(2,1)S(1)}, u32[]{:S(2)}, u32[]{:S(2)}) collective-permute-start(bf16[96,3072]{1,0:T(8,128)(2,1)} %get-tuple-element.378), channel_id=1, source_target_pairs={{0,16},{4,20},{8,24},{12,28},{16,0},{20,4},{24,8},{28,12},{1,17},{... | collective-permute-start | bytes 1769480 | tf_op jit(solution)/shard_map/ppermute | solution.py:1027
  317.4 29.9 %collective-permute-start.44 = (bf16[192,1536]{1,0:T(8,128)(2,1)}, bf16[192,1536]{1,0:T(8,128)(2,1)S(1)}, u32[]{:S(2)}, u32[]{:S(2)}) collective-permute-start(bf16[192,1536]{1,0:T(8,128)(2,1)} %get-tuple-element.379), channel_id=1, source_target_pairs={{0,8},{4,12},{8,0},{12,4},{16,24},{20,28},{24,16},{28,20},{1,9},{5... | collective-permute-start | bytes 1769480 | tf_op jit(solution)/shard_map/ppermute | solution.py:1027
  317.7 29.7 %collective-permute-start.45 = (bf16[192,1536]{1,0:T(8,128)(2,1)}, bf16[192,1536]{1,0:T(8,128)(2,1)}, u32[]{:S(2)}, u32[]{:S(2)}) collective-permute-start(bf16[192,1536]{1,0:T(8,128)(2,1)} %get-tuple-element.380), channel_id=1, source_target_pairs={{0,16},{4,20},{8,24},{12,28},{16,0},{20,4},{24,8},{28,12},{1,17},{... | collective-permute-start | bytes 1769480 | tf_op jit(solution)/shard_map/ppermute | solution.py:1027
  339.7 34.6 %collective-permute-start.48 = (bf16[384,2048]{1,0:T(8,128)(2,1)}, bf16[384,2048]{1,0:T(8,128)(2,1)S(1)}, u32[]{:S(2)}, u32[]{:S(2)}) collective-permute-start(bf16[384,2048]{1,0:T(8,128)(2,1)} %get-tuple-element.398), channel_id=1, source_target_pairs={{0,4},{4,0},{8,12},{12,8},{16,20},{20,16},{24,28},{28,24},{1,5},{5... | collective-permute-start | bytes 4718600 | tf_op jit(solution)/shard_map/ppermute | solution.py:1027
  347.4 37.7 %all-to-all-start.1 = ((bf16[4,384,384]{2,1,0:T(8,128)(2,1)}), bf16[4,384,384]{2,1,0:T(8,128)(2,1)S(1)}, u32[]{:S(2)}, u32[]{:S(2)}) async-start(bf16[4,384,384]{2,1,0:T(8,128)(2,1)} %shard_map.190), calls=%async_computation.2 | async-start | bytes 2359296 | tf_op jit(solution)/shard_map/all_to_all | solution.py:1031
  356.4 27.6 %collective-permute-start.46 = (bf16[384,1536]{1,0:T(8,128)(2,1)}, bf16[384,1536]{1,0:T(8,128)(2,1)}, u32[]{:S(2)}, u32[]{:S(2)}) collective-permute-start(bf16[384,1536]{1,0:T(8,128)(2,1)} %get-tuple-element.395), channel_id=1, source_target_pairs={{0,8},{4,12},{8,0},{12,4},{16,24},{20,28},{24,16},{28,20},{1,9},{5... | collective-permute-start | bytes 3538952 | tf_op jit(solution)/shard_map/ppermute | solution.py:1027
  357.9 27.1 %collective-permute-start.47 = (bf16[384,1536]{1,0:T(8,128)(2,1)}, bf16[384,1536]{1,0:T(8,128)(2,1)}, u32[]{:S(2)}, u32[]{:S(2)}) collective-permute-start(bf16[384,1536]{1,0:T(8,128)(2,1)} %get-tuple-element.396), channel_id=1, source_target_pairs={{0,16},{4,20},{8,24},{12,28},{16,0},{20,4},{24,8},{28,12},{1,17},{... | collective-permute-start | bytes 3538952 | tf_op jit(solution)/shard_map/ppermute | solution.py:1027
  391.8 40.7 %all-to-all-start.2 = ((bf16[4,384,384]{2,1,0:T(8,128)(2,1)}), bf16[4,384,384]{2,1,0:T(8,128)(2,1)S(1)}, u32[]{:S(2)}, u32[]{:S(2)}) async-start(bf16[4,384,384]{2,1,0:T(8,128)(2,1)} %shard_map.193), calls=%async_computation.4 | async-start | bytes 2359296 | tf_op jit(solution)/shard_map/all_to_all | solution.py:1031
  396.6 33.7 %reduce-scatter.5.cloned.1.call-start = ((), (), s32[]{:S(2)}) async-start(), calls=%async_computation.7 | async-start | bytes 737280 | tf_op jit(solution)/shard_map/reduce_scatter | solution.py:1609
  413.3 16.0 %collective-permute-start.56 = (bf16[96,2048]{1,0:T(8,128)(2,1)}, bf16[96,2048]{1,0:T(8,128)(2,1)S(1)}, u32[]{:S(2)}, u32[]{:S(2)}) collective-permute-start(bf16[96,2048]{1,0:T(8,128)(2,1)} %get-tuple-element.438), channel_id=1, source_target_pairs={{0,8},{4,12},{8,0},{12,4},{16,24},{20,28},{24,16},{28,20},{1,9},{5... | collective-permute-start | bytes 1179656 | tf_op jit(solution)/shard_map/ppermute | solution.py:1027
  413.9 16.1 %collective-permute-start.57 = (bf16[96,2048]{1,0:T(8,128)(2,1)}, bf16[96,2048]{1,0:T(8,128)(2,1)}, u32[]{:S(2)}, u32[]{:S(2)}) collective-permute-start(bf16[96,2048]{1,0:T(8,128)(2,1)} %get-tuple-element.439), channel_id=1, source_target_pairs={{0,16},{4,20},{8,24},{12,28},{16,0},{20,4},{24,8},{28,12},{1,17},{... | collective-permute-start | bytes 1179656 | tf_op jit(solution)/shard_map/ppermute | solution.py:1027
  415.3 13.9 %collective-permute-start.58 = (bf16[96,1024]{1,0:T(8,128)(2,1)}, bf16[96,1024]{1,0:T(8,128)(2,1)S(1)}, u32[]{:S(2)}, u32[]{:S(2)}) collective-permute-start(bf16[96,1024]{1,0:T(8,128)(2,1)} %get-tuple-element.440), channel_id=1, source_target_pairs={{0,8},{4,12},{8,0},{12,4},{16,24},{20,28},{24,16},{28,20},{1,9},{5... | collective-permute-start | bytes 589832 | tf_op jit(solution)/shard_map/ppermute | solution.py:1027
  415.9 13.3 %collective-permute-start.59 = (bf16[96,1024]{1,0:T(8,128)(2,1)}, bf16[96,1024]{1,0:T(8,128)(2,1)S(1)}, u32[]{:S(2)}, u32[]{:S(2)}) collective-permute-start(bf16[96,1024]{1,0:T(8,128)(2,1)} %get-tuple-element.441), channel_id=1, source_target_pairs={{0,16},{4,20},{8,24},{12,28},{16,0},{20,4},{24,8},{28,12},{1,17},{... | collective-permute-start | bytes 589832 | tf_op jit(solution)/shard_map/ppermute | solution.py:1027
  435.9 21.0 %all-to-all-start.3 = ((bf16[4,112,768]{2,1,0:T(8,128)(2,1)}), bf16[4,112,768]{2,1,0:T(8,128)(2,1)S(1)}, u32[]{:S(2)}, u32[]{:S(2)}) async-start(bf16[4,112,768]{2,1,0:T(8,128)(2,1)} %shard_map.198), calls=%async_computation.5 | async-start | bytes 1376256 | tf_op jit(solution)/shard_map/all_to_all | solution.py:1031
  (74 other events, 439.0 us)
Sparse Core Ops, SparseCore 0:
  41.1 32.2 all-gather.4
  78.6 40.2 all-gather.6
  244.7 83.6 reduce-scatter.2
  400.0 30.2 reduce-scatter.4

commit v6 on v5

--- a/solution.py
+++ b/solution.py
@@ -1367,8 +1367,11 @@
 
         sent = jnp.concatenate([jnp.concatenate(chunks[0][1:], axis=1), feature_rows])
         sent = jnp.broadcast_to(sent[None], (HEAD_DEVICES,) + sent.shape)
+        first_feed = jnp.concatenate(chunks[1][1:], axis=1)
         sent, inputs, cotangent = together(sent, inputs, cotangent)
         came = exchange(sent)
+        first_feed, inputs, cotangent = together(first_feed, inputs, cotangent)
+        came_feed = gathered_columns(first_feed)
         state, gradient = with_halo(inputs, cotangent)
         position, ids = window_ids(segment_ids, own_rows)
         tables, ids = rotary_tables(position, ids, head_width)
@@ -1383,13 +1386,11 @@
                     ]
                 )
             )
-        first_feed = jnp.concatenate(chunks[1][1:], axis=1)
-        came, state, gradient, tables, ids, first_feed, gain_rows, attention_places = together(
-            came, state, gradient, tables, ids, first_feed, gain_rows, attention_places
+        came, state, gradient, tables, ids, gain_rows, attention_places = together(
+            came, state, gradient, tables, ids, gain_rows, attention_places
         )
         attend = functools.partial(run_attention_forward, tables=tables, ids=ids, scale=scale)
         own = join(0, came)
-        came_feed = gathered_columns(first_feed)
         over_x, over_y, over_core = next_chips(own)
         made = feature_tables(came, in_rows, table_shapes)
         over_x, over_y, over_core, made, both = together(over_x, over_y, over_core, made, both)

time: 478 us -> 495 us (1.036)
  waiting for transfers between devices: 87 us -> 106 us
    reduce_scatter x1, waiting for transfers between devices: 0.02 us -> 6.4 us  [body(): lax.psum_scatter(feed_grad, 'dp', scatter_dimension=0, tiled=True)]
    all_gather x2, waiting for transfers between devices: 0.59 us -> 6.87 us  [gathered_columns(): return lax.all_gather(sent, 'head', axis=0, tiled=False)]
    unnamed x111 -> x107, local copies, waits for them, and re-layouts: 10.7 us -> 11.4 us
  transfers between devices with their start and end apart: 69 -> 69, of which waited for: 28 -> 32; matrix products, arithmetic and copies ran while one was open for 5% -> 5% of each run, Pallas kernels for 45% -> 44%
where the time goes in v6:
time: 495 us; the launch traced here: 486 us
  Pallas kernels  258 us (52%)
  waiting for transfers between devices  106 us (21%)
  starting transfers between devices  65.7 us (13%)
  local copies, waits for them, and re-layouts  34.5 us (7%)
  between operations  15 us (3%)
  other arithmetic  6.33 us (1%)
    ppermute x59, waiting for transfers between devices, hop(): return lax.ppermute(values, 'dp', [(i, i ^ bit) for i in range(count)])  72.6 us
    pallas_call x3, Pallas kernels, run_attention_backward(): kernel_call(functools.partial(attention_backward, first, last, scale, gro...  66.2 us
    pallas_call x3, Pallas kernels, run_feed_back(): kernel_call(functools.partial(feed_back, first, last, segments, len(piece...  49.7 us
    pallas_call x5, Pallas kernels, run_feed_forward(): kernel_call(functools.partial(feed_forward, len(pieces)), 1, [ANYWHERE] *...  49.4 us
    pallas_call x2, Pallas kernels, run_attention_forward(): kernel_call(functools.partial(attention_forward, scale, len(pieces)), gro...  42.1 us
    ppermute x59, starting transfers between devices, hop(): return lax.ppermute(values, 'dp', [(i, i ^ bit) for i in range(count)])  40.2 us
    all_to_all x4, starting transfers between devices, exchange(): lax.all_to_all(values, 'head', split_axis=0, concat_axis=0, tiled=True)  20 us
    all_to_all x4, waiting for transfers between devices, exchange(): lax.all_to_all(values, 'head', split_axis=0, concat_axis=0, tiled=True)  18.9 us
  transfers between devices with their start and end apart: 69, of which 32 were waited for; matrix products, arithmetic and copies ran while one was open for 5% of the time, Pallas kernels for 44%

profile of v6, /device:TPU:0, one launch (start us, length us, event | category | flops | bytes accessed | tf_op | source)
XLA Modules:
  0.0 485.9 jit_solution(315716276189720414)
XLA Ops:
  11.4 6.4 %all-to-all-start = ((bf16[4,112,768]{2,1,0:T(8,128)(2,1)}), bf16[4,112,768]{2,1,0:T(8,128)(2,1)S(1)}, u32[]{:S(2)}, u32[]{:S(2)}) async-start(bf16[4,112,768]{2,1,0:T(8,128)(2,1)} %broadcast_in_dim.13), calls=%async_computation | async-start | bytes 1376256 | tf_op jit(solution)/shard_map/all_to_all | solution.py:1031
  20.1 3.9 collective-permute-start
  31.9 2.8 shard_map.170
  39.9 2.4 all-to-all-done.source_in.source
  49.6 3.4 shard_map.173
  53.0 8.3 %collective-permute-done.3.others_2_ = bf16[96,3072]{1,0:T(8,128)(2,1)} collective-permute-done((bf16[96,3072]{1,0:T(8,128)(2,1)}, bf16[96,3072]{1,0:T(8,128)(2,1)}, u32[]{:S(2)}, u32[]{:S(2)}) %collective-permute-start.3) | collective-permute-done | bytes 589856 | tf_op jit(solution)/shard_map/ppermute | solution.py:1027
  67.2 4.7 collective-permute-done.6.others_4_
  74.2 2.5 copy.56
  76.7 2.6 shard_map.171.others_0_.others_5_
  81.8 21.1 %shard_map.174 = (bf16[768,3072]{1,0:T(8,128)(2,1)}, bf16[640,768]{1,0:T(8,128)(2,1)}, f32[640,768]{1,0:T(8,128)}, f32[640,768]{1,0:T(8,128)}, bf16[640,768]{1,0...) custom-call(s32[10]{0:T(128)} %stack.123.places, ...), custom_call_target="tpu_custom_call" | custom-call | flops 28999999488 | bytes 48333332 | tf_op jit(solution)/shard_map/pallas_call | solution.py:791
  102.9 5.1 %collective-permute-done.12.others_2_.others_7_ = bf16[384,1536]{1,0:T(8,128)(2,1)S(1)} collective-permute-done((bf16[384,1536]{1,0:T(8,128)(2,1)}, bf16[384,1536]{1,0:T(8,128)(2,1)S(1)}, u32[]{:S(2)}, u32[]{:S(2)}) %collective-permute-start.12) | collective-permute-done | bytes 1179680 | tf_op jit(solution)/shard_map/ppermute | solution.py:1027
  111.0 9.6 %shard_map.175 = (bf16[640,1152]{1,0:T(8,128)(2,1)}, bf16[640,1152]{1,0:T(8,128)(2,1)}, f32[640,768]{1,0:T(8,128)}) custom-call(f32[640,768]{1,0:T(8,128)} %get-tuple-element.271.carried_in.middle, bf16[640,768]{1,0:T(8,128)(2,1)} %get-tuple-element.272.normed_in, bf16[384,1536]{1,0:T(8,128)(2,1)} %shard_map.171.others_0_.others_5_, ...), custom_call_target="tpu_custom_call" | custom-call | flops 9666666496 | bytes 16111111 | tf_op jit(solution)/shard_map/pallas_call | solution.py:926
  120.5 3.9 collective-permute-done.14.others_0_.others_8_
  126.1 6.9 %all-gather.7.cloned.1.call-done = bf16[2304,384]{1,0:T(8,128)(2,1)} async-done(((bf16[576,384]{1,0:T(8,128)(2,1)}), bf16[2304,384]{1,0:T(8,128)(2,1)}) %all-gather.7.cloned.1.call-update) | async-done | bytes 1769488 | tf_op jit(solution)/shard_map/all_gather | solution.py:1366
  132.9 2.5 shard_map.176.others_0_
  138.5 9.5 %shard_map.177 = (bf16[640,1152]{1,0:T(8,128)(2,1)}, bf16[640,1152]{1,0:T(8,128)(2,1)}, f32[640,768]{1,0:T(8,128)}) custom-call(f32[640,768]{1,0:T(8,128)} %get-tuple-element.281.carried_in, bf16[640,768]{1,0:T(8,128)(2,1)} %get-tuple-element.272.normed_in, bf16[384,1536]{1,0:T(8,128)(2,1)} %copy-done.33, ...), custom_call_target="tpu_custom_call" | custom-call | flops 9666666496 | bytes 16111111 | tf_op jit(solution)/shard_map/pallas_call | solution.py:926
  148.0 3.4 collective-permute-done.19.others_2_
  156.2 7.6 %shard_map.178 = (bf16[640,768]{1,0:T(8,128)(2,1)}, bf16[640,768]{1,0:T(8,128)(2,1)}, f32[640,768]{1,0:T(8,128)}) custom-call(f32[640,768]{1,0:T(8,128)} %get-tuple-element.290.carried_in, bf16[640,768]{1,0:T(8,128)(2,1)} %get-tuple-element.272.normed_in, bf16[192,1536]{1,0:T(8,128)(2,1)} %collective-permute-done.14.others_0_.others_8_, ...), custom_call_target="tpu_custom_call" | custom-call | flops 9666666496 | bytes 16111111 | tf_op jit(solution)/shard_map/pallas_call | solution.py:926
  164.4 2.8 shard_map.179.others_0_.others_4_
  171.1 21.0 %shard_map.180 = (bf16[768,3072]{1,0:T(8,128)(2,1)}, bf16[640,768]{1,0:T(8,128)(2,1)}, f32[640,768]{1,0:T(8,128)}, f32[640,768]{1,0:T(8,128)}, bf16[640,768]{1,0...) custom-call(s32[10]{0:T(128)} %stack.123.places, ...), custom_call_target="tpu_custom_call" | custom-call | flops 28999999488 | bytes 48333332 | tf_op jit(solution)/shard_map/pallas_call | solution.py:791
  192.1 3.8 collective-permute-done.30.others_2_.others_6_
  199.7 9.5 %shard_map.181 = (bf16[640,1152]{1,0:T(8,128)(2,1)}, bf16[640,1152]{1,0:T(8,128)(2,1)}, f32[640,768]{1,0:T(8,128)}) custom-call(f32[640,768]{1,0:T(8,128)} %get-tuple-element.311.carried_in.middle, bf16[640,768]{1,0:T(8,128)(2,1)} %get-tuple-element.308.normed_in, bf16[384,1536]{1,0:T(8,128)(2,1)} %shard_map.179.others_0_.others_4_, ...), custom_call_target="tpu_custom_call" | custom-call | flops 9666666496 | bytes 16111111 | tf_op jit(solution)/shard_map/pallas_call | solution.py:926
  209.2 3.8 collective-permute-done.32.others_3_.others_10_
  217.8 13.2 %shard_map.182 = (bf16[640,1920]{1,0:T(8,128)(2,1)}, bf16[640,1920]{1,0:T(8,128)(2,1)}, f32[640,768]{1,0:T(8,128)}) custom-call(f32[640,768]{1,0:T(8,128)} %get-tuple-element.318.carried_in, bf16[640,768]{1,0:T(8,128)(2,1)} %get-tuple-element.308.normed_in, bf16[384,1536]{1,0:T(8,128)(2,1)} %collective-permute-done.31.others_0_.others_7_, ...), custom_call_target="tpu_custom_call" | custom-call | flops 9666666496 | bytes 16111111 | tf_op jit(solution)/shard_map/pallas_call | solution.py:926
  231.0 21.2 %shard_map.183 = (bf16[3072,1536]{1,0:T(8,128)(2,1)}, f32[640,768]{1,0:T(8,128)}, f32[1,768]{1,0:T(1,128)}, bf16[640,768]{1,0:T(8,128)(2,1)}) custom-call(s32[10]{0:T(128)} %stack.114.places, f32[640,768]{1,0:T(8,128)} %get-tuple-element.245.gradient_in, f32[640,768]{1,0:T(8,128)} %get-tuple-element.311.carried_in.middle, ...), custom_call_target="tpu_custom_call" | custom-call | flops 14499999744 | bytes 24166666 | tf_op jit(solution)/shard_map/pallas_call | solution.py:967
  252.9 30.2 %shard_map.184 = (f32[640,768]{1,0:T(8,128)}, f32[1,768]{1,0:T(1,128)}, bf16[384,3072]{1,0:T(8,128)(2,1)}, bf16[384,3072]{1,0:T(8,128)(2,1)}) custom-call(s32[8]{0:T(128)} %stack.103.places, bf16[640,768]{1,0:T(8,128)(2,1)} %get-tuple-element.326.branch_in, bf16[768,3072]{1,0:T(8,128)(2,1)} %get-tuple-element.327.weights_in, ...), custom_call_target="tpu_custom_call" | custom-call | flops 40000000000 | bytes 66666664 | tf_op jit(solution)/shard_map/pallas_call | solution.py:868
  283.4 13.7 %shard_map.185 = (bf16[1536,1536]{1,0:T(8,128)(2,1)}, f32[640,768]{1,0:T(8,128)}) custom-call(s32[5]{0:T(128)} %constant.47.clone.places, f32[640,768]{1,0:T(8,128)} %get-tuple-element.335.gradient_in, f32[640,768]{1,0:T(8,128)} %get-tuple-element.271.carried_in.middle, f32[1,768]{1,0:T(1,128)} %get-tuple-element.257.gain_2, ...), custom_call_target="tpu_custom_call" | custom-call | flops 14499999744 | bytes 24166666 | tf_op jit(solution)/shard_map/pallas_call | solution.py:967
  302.7 14.7 %shard_map.187 = (bf16[1536,1536]{1,0:T(8,128)(2,1)}, f32[640,768]{1,0:T(8,128)}, f32[1,768]{1,0:T(1,128)}, bf16[640,768]{1,0:T(8,128)(2,1)}) custom-call(s32[5]{0:T(128)} %constant.47.clone.places, f32[640,768]{1,0:T(8,128)} %get-tuple-element.335.gradient_in, f32[640,768]{1,0:T(8,128)} %get-tuple-element.271.carried_in.middle, ...), custom_call_target="tpu_custom_call" | custom-call | flops 14499999744 | bytes 24166666 | tf_op jit(solution)/shard_map/pallas_call | solution.py:967
  318.3 4.2 shard_map.188
  326.6 21.0 %shard_map.189 = (f32[640,768]{1,0:T(8,128)}, bf16[384,2048]{1,0:T(8,128)(2,1)}, bf16[384,2048]{1,0:T(8,128)(2,1)}) custom-call(s32[8]{0:T(128)} %stack.103.places, bf16[640,768]{1,0:T(8,128)(2,1)} %get-tuple-element.392.branch_in, bf16[768,3072]{1,0:T(8,128)(2,1)} %get-tuple-element.369.weights_in, bf16[640,768]{1,0:T(8,128)(2,1)} %get-tuple-element.370.mixed_in, ...), custom_call_target="tpu_custom_call" | custom-call | flops 26666665984 | bytes 44444444 | tf_op jit(solution)/shard_map/pallas_call | solution.py:868
  347.6 6.4 %reduce-scatter.3.cloned.1.call-done.others_0_ = bf16[384,1536]{1,0:T(8,128)(2,1)} async-done(((bf16[3072,1536]{1,0:T(8,128)(2,1)}), bf16[384,1536]{1,0:T(8,128)(2,1)}) %reduce-scatter.3.cloned.1.call-update) | async-done | bytes 1179664 | tf_op jit(solution)/shard_map/reduce_scatter | solution.py:1528
  354.1 2.6 shard_map.190
  356.7 6.2 %collective-permute-done.44.others_4_ = bf16[192,1536]{1,0:T(8,128)(2,1)S(1)} collective-permute-done((bf16[192,1536]{1,0:T(8,128)(2,1)}, bf16[192,1536]{1,0:T(8,128)(2,1)S(1)}, u32[]{:S(2)}, u32[]{:S(2)}) %collective-permute-start.44) | collective-permute-done | bytes 589856 | tf_op jit(solution)/shard_map/ppermute | solution.py:1027
  363.7 5.2 %all-to-all-start.1 = ((bf16[4,384,384]{2,1,0:T(8,128)(2,1)}), bf16[4,384,384]{2,1,0:T(8,128)(2,1)S(1)}, u32[]{:S(2)}, u32[]{:S(2)}) async-start(bf16[4,384,384]{2,1,0:T(8,128)(2,1)} %shard_map.190), calls=%async_computation.2 | async-start | bytes 2359296 | tf_op jit(solution)/shard_map/all_to_all | solution.py:1031
  368.9 4.4 shard_map.191
  375.4 15.0 %shard_map.192 = (f32[640,768]{1,0:T(8,128)}, f32[1,768]{1,0:T(1,128)}, bf16[384,1024]{1,0:T(8,128)(2,1)}, bf16[384,1024]{1,0:T(8,128)(2,1)}) custom-call(s32[8]{0:T(128)} %stack.103.places, bf16[640,768]{1,0:T(8,128)(2,1)} %get-tuple-element.392.branch_in, bf16[768,3072]{1,0:T(8,128)(2,1)} %get-tuple-element.369.weights_in, ...), custom_call_target="tpu_custom_call" | custom-call | flops 13333332992 | bytes 22222222 | tf_op jit(solution)/shard_map/pallas_call | solution.py:868
  393.0 8.1 %collective-permute-done.46.others_2_ = bf16[384,1536]{1,0:T(8,128)(2,1)} collective-permute-done((bf16[384,1536]{1,0:T(8,128)(2,1)}, bf16[384,1536]{1,0:T(8,128)(2,1)}, u32[]{:S(2)}, u32[]{:S(2)}) %collective-permute-start.46) | collective-permute-done | bytes 1179680 | tf_op jit(solution)/shard_map/ppermute | solution.py:1027
  402.1 4.6 shard_map.193
  408.8 4.8 all-to-all-start.2
  413.9 2.9 shard_map.195
  422.8 3.0 collective-permute-done.51
  427.3 3.0 shard_map.196
  434.4 2.4 slice.167
  438.6 7.1 %collective-permute-done.60 = f32[4,768]{1,0:T(4,128)S(1)} collective-permute-done((f32[4,768]{1,0:T(4,128)S(1)}, f32[4,768]{1,0:T(4,128)S(1)}, u32[]{:S(2)}, u32[]{:S(2)}) %collective-permute-start.60) | collective-permute-done | bytes 12320 | tf_op jit(solution)/shard_map/ppermute | solution.py:1027
  449.7 3.3 shard_map.198
  453.1 3.5 all-to-all-start.3
  456.5 3.2 shard_map.197
  459.8 14.2 %all-to-all-done.3.others_0_ = bf16[4,112,768]{2,1,0:T(8,128)(2,1)S(1)} async-done(((bf16[4,112,768]{2,1,0:T(8,128)(2,1)}), bf16[4,112,768]{2,1,0:T(8,128)(2,1)S(1)}, u32[]{:S(2)}, u32[]{:S(2)}) %all-to-all-start.3) | async-done | bytes 688160 | tf_op jit(solution)/shard_map/all_to_all | solution.py:1031
  (278 shorter events, 105.3 us)
Async XLA Ops:
  11.4 30.9 %all-to-all-start = ((bf16[4,112,768]{2,1,0:T(8,128)(2,1)}), bf16[4,112,768]{2,1,0:T(8,128)(2,1)S(1)}, u32[]{:S(2)}, u32[]{:S(2)}) async-start(bf16[4,112,768]{2,1,0:T(8,128)(2,1)} %broadcast_in_dim.13), calls=%async_computation | async-start | bytes 1376256 | tf_op jit(solution)/shard_map/all_to_all | solution.py:1031
  17.8 56.4 %all-gather.5.cloned.1.call-start = ((), (), s32[]{:S(2)}) async-start(), calls=%async_computation.8 | async-start | bytes 1474560 | tf_op jit(solution)/shard_map/all_gather | solution.py:1366
  18.7 114.2 %all-gather.7.cloned.1.call-start = ((), (), s32[]{:S(2)}) async-start(), calls=%async_computation.9 | async-start | bytes 2211840 | tf_op jit(solution)/shard_map/all_gather | solution.py:1366
  20.1 17.2 %collective-permute-start = (bf16[64,1536]{1,0:T(8,128)(2,1)S(1)}, bf16[64,1536]{1,0:T(8,128)(2,1)S(1)}, u32[]{:S(2)}, u32[]{:S(2)}) collective-permute-start(bf16[64,1536]{1,0:T(8,128)(2,1)S(1)} %get-tuple-element.468), channel_id=1, source_target_pairs={{0,1},{1,2},{2,3},{4,5},{5,6},{6,7},{8,9},{9,10},{10,11},{12,13},{... | collective-permute-start | bytes 589832 | tf_op jit(solution)/shard_map/ppermute | solution.py:1280
  45.3 16.1 %collective-permute-start.3 = (bf16[96,3072]{1,0:T(8,128)(2,1)}, bf16[96,3072]{1,0:T(8,128)(2,1)}, u32[]{:S(2)}, u32[]{:S(2)}) collective-permute-start(bf16[96,3072]{1,0:T(8,128)(2,1)} %shard_map.172.others_0_), channel_id=1, source_target_pairs={{0,16},{4,20},{8,24},{12,28},{16,0},{20,4},{24,8},{28,12},{1,17},{... | collective-permute-start | bytes 1769480 | tf_op jit(solution)/shard_map/ppermute | solution.py:1027
  46.9 15.7 %collective-permute-start.2 = (bf16[96,3072]{1,0:T(8,128)(2,1)}, bf16[96,3072]{1,0:T(8,128)(2,1)}, u32[]{:S(2)}, u32[]{:S(2)}) collective-permute-start(bf16[96,3072]{1,0:T(8,128)(2,1)} %shard_map.172.others_0_), channel_id=1, source_target_pairs={{0,8},{4,12},{8,0},{12,4},{16,24},{20,28},{24,16},{28,20},{1,9},{5... | collective-permute-start | bytes 1769480 | tf_op jit(solution)/shard_map/ppermute | solution.py:1027
  66.7 14.2 %collective-permute-start.7 = (bf16[96,3072]{1,0:T(8,128)(2,1)}, bf16[96,3072]{1,0:T(8,128)(2,1)S(1)}, u32[]{:S(2)}, u32[]{:S(2)}) collective-permute-start(bf16[96,3072]{1,0:T(8,128)(2,1)} %collective-permute-done.2.others_1_), channel_id=1, source_target_pairs={{0,4},{4,0},{8,12},{12,8},{16,20},{20,16},{24,28},{28,24},{1,5},{5... | collective-permute-start | bytes 1769480 | tf_op jit(solution)/shard_map/ppermute | solution.py:1027
  66.7 14.2 %collective-permute-start.8 = (bf16[96,3072]{1,0:T(8,128)(2,1)}, bf16[96,3072]{1,0:T(8,128)(2,1)}, u32[]{:S(2)}, u32[]{:S(2)}) collective-permute-start(bf16[96,3072]{1,0:T(8,128)(2,1)} %collective-permute-done.3.others_2_), channel_id=1, source_target_pairs={{0,4},{4,0},{8,12},{12,8},{16,20},{20,16},{24,28},{28,24},{1,5},{5... | collective-permute-start | bytes 1769480 | tf_op jit(solution)/shard_map/ppermute | solution.py:1027
  79.3 274.8 %reduce-scatter.3.cloned.1.call-start = ((), (), s32[]{:S(2)}) async-start(), calls=%async_computation.6 | async-start | bytes 10616832 | tf_op jit(solution)/shard_map/reduce_scatter | solution.py:1528
  79.3 23.6 %collective-permute-start.13 = (bf16[384,1536]{1,0:T(8,128)(2,1)}, bf16[384,1536]{1,0:T(8,128)(2,1)S(1)}, u32[]{:S(2)}, u32[]{:S(2)}) collective-permute-start(bf16[384,1536]{1,0:T(8,128)(2,1)} %shard_map.171.others_0_.others_5_), channel_id=1, source_target_pairs={{0,4},{4,0},{8,12},{12,8},{16,20},{20,16},{24,28},{28,24},{1,5},{5... | collective-permute-start | bytes 3538952 | tf_op jit(solution)/shard_map/ppermute | solution.py:1027
  79.8 28.2 %collective-permute-start.12 = (bf16[384,1536]{1,0:T(8,128)(2,1)}, bf16[384,1536]{1,0:T(8,128)(2,1)S(1)}, u32[]{:S(2)}, u32[]{:S(2)}) collective-permute-start(bf16[384,1536]{1,0:T(8,128)(2,1)} %shard_map.171.others_0_.others_5_), channel_id=1, source_target_pairs={{0,16},{4,20},{8,24},{12,28},{16,0},{20,4},{24,8},{28,12},{1,17},{... | collective-permute-start | bytes 3538952 | tf_op jit(solution)/shard_map/ppermute | solution.py:1027
  80.4 27.9 %collective-permute-start.11 = (bf16[384,1536]{1,0:T(8,128)(2,1)}, bf16[384,1536]{1,0:T(8,128)(2,1)S(1)}, u32[]{:S(2)}, u32[]{:S(2)}) collective-permute-start(bf16[384,1536]{1,0:T(8,128)(2,1)} %shard_map.171.others_0_.others_5_), channel_id=1, source_target_pairs={{0,8},{4,12},{8,0},{12,4},{16,24},{20,28},{24,16},{28,20},{1,9},{5... | collective-permute-start | bytes 3538952 | tf_op jit(solution)/shard_map/ppermute | solution.py:1027
  108.3 17.2 %collective-permute-start.16 = (bf16[384,1536]{1,0:T(8,128)(2,1)S(1)}, bf16[384,1536]{1,0:T(8,128)(2,1)}, u32[]{:S(2)}, u32[]{:S(2)}) collective-permute-start(bf16[384,1536]{1,0:T(8,128)(2,1)S(1)} %collective-permute-done.11.others_1_.others_6_), channel_id=1, source_target_pairs={{0,4},{4,0},{8,12},{12,8},{16,20},{20,16},{24,28},{28,24},{1,5},{5... | collective-permute-start | bytes 3538952 | tf_op jit(solution)/shard_map/ppermute | solution.py:1027
  108.4 17.2 %collective-permute-start.17 = (bf16[384,1536]{1,0:T(8,128)(2,1)S(1)}, bf16[384,1536]{1,0:T(8,128)(2,1)}, u32[]{:S(2)}, u32[]{:S(2)}) collective-permute-start(bf16[384,1536]{1,0:T(8,128)(2,1)S(1)} %collective-permute-done.12.others_2_.others_7_), channel_id=1, source_target_pairs={{0,4},{4,0},{8,12},{12,8},{16,20},{20,16},{24,28},{28,24},{1,5},{5... | collective-permute-start | bytes 3538952 | tf_op jit(solution)/shard_map/ppermute | solution.py:1027
  108.9 15.5 %collective-permute-start.14 = (bf16[192,1536]{1,0:T(8,128)(2,1)S(1)}, bf16[192,1536]{1,0:T(8,128)(2,1)}, u32[]{:S(2)}, u32[]{:S(2)}) collective-permute-start(bf16[192,1536]{1,0:T(8,128)(2,1)S(1)} %slice.141), channel_id=1, source_target_pairs={{0,16},{4,20},{8,24},{12,28},{16,0},{20,4},{24,8},{28,12},{1,17},{... | collective-permute-start | bytes 1769480 | tf_op jit(solution)/shard_map/ppermute | solution.py:1027
  110.4 15.1 %collective-permute-start.15 = (bf16[192,1536]{1,0:T(8,128)(2,1)S(1)}, bf16[192,1536]{1,0:T(8,128)(2,1)}, u32[]{:S(2)}, u32[]{:S(2)}) collective-permute-start(bf16[192,1536]{1,0:T(8,128)(2,1)S(1)} %slice.142), channel_id=1, source_target_pairs={{0,8},{4,12},{8,0},{12,4},{16,24},{20,28},{24,16},{28,20},{1,9},{5... | collective-permute-start | bytes 1769480 | tf_op jit(solution)/shard_map/ppermute | solution.py:1027
  125.6 28.3 %collective-permute-start.21 = (bf16[192,1536]{1,0:T(8,128)(2,1)}, bf16[192,1536]{1,0:T(8,128)(2,1)S(1)}, u32[]{:S(2)}, u32[]{:S(2)}) collective-permute-start(bf16[192,1536]{1,0:T(8,128)(2,1)} %collective-permute-done.14.others_0_.others_8_), channel_id=1, source_target_pairs={{0,4},{4,0},{8,12},{12,8},{16,20},{20,16},{24,28},{28,24},{1,5},{5... | collective-permute-start | bytes 1769480 | tf_op jit(solution)/shard_map/ppermute | solution.py:1027
  125.6 29.8 %collective-permute-start.22 = (bf16[192,1536]{1,0:T(8,128)(2,1)}, bf16[192,1536]{1,0:T(8,128)(2,1)S(1)}, u32[]{:S(2)}, u32[]{:S(2)}) collective-permute-start(bf16[192,1536]{1,0:T(8,128)(2,1)} %collective-permute-done.15.others_1_.others_9_), channel_id=1, source_target_pairs={{0,4},{4,0},{8,12},{12,8},{16,20},{20,16},{24,28},{28,24},{1,5},{5... | collective-permute-start | bytes 1769480 | tf_op jit(solution)/shard_map/ppermute | solution.py:1027
  135.5 16.0 %collective-permute-start.19 = (bf16[96,3072]{1,0:T(8,128)(2,1)}, bf16[96,3072]{1,0:T(8,128)(2,1)S(1)}, u32[]{:S(2)}, u32[]{:S(2)}) collective-permute-start(bf16[96,3072]{1,0:T(8,128)(2,1)} %shard_map.176.others_0_), channel_id=1, source_target_pairs={{0,16},{4,20},{8,24},{12,28},{16,0},{20,4},{24,8},{28,12},{1,17},{... | collective-permute-start | bytes 1769480 | tf_op jit(solution)/shard_map/ppermute | solution.py:1027
  137.0 15.6 %collective-permute-start.18 = (bf16[96,3072]{1,0:T(8,128)(2,1)}, bf16[96,3072]{1,0:T(8,128)(2,1)S(1)}, u32[]{:S(2)}, u32[]{:S(2)}) collective-permute-start(bf16[96,3072]{1,0:T(8,128)(2,1)} %shard_map.176.others_0_), channel_id=1, source_target_pairs={{0,8},{4,12},{8,0},{12,4},{16,24},{20,28},{24,16},{28,20},{1,9},{5... | collective-permute-start | bytes 1769480 | tf_op jit(solution)/shard_map/ppermute | solution.py:1027
  152.7 14.7 %collective-permute-start.25 = (bf16[96,3072]{1,0:T(8,128)(2,1)S(1)}, bf16[96,3072]{1,0:T(8,128)(2,1)S(1)}, u32[]{:S(2)}, u32[]{:S(2)}) collective-permute-start(bf16[96,3072]{1,0:T(8,128)(2,1)S(1)} %collective-permute-done.18.others_1_), channel_id=1, source_target_pairs={{0,4},{4,0},{8,12},{12,8},{16,20},{20,16},{24,28},{28,24},{1,5},{5... | collective-permute-start | bytes 1769480 | tf_op jit(solution)/shard_map/ppermute | solution.py:1027
  152.8 16.1 %collective-permute-start.26 = (bf16[96,3072]{1,0:T(8,128)(2,1)S(1)}, bf16[96,3072]{1,0:T(8,128)(2,1)}, u32[]{:S(2)}, u32[]{:S(2)}) collective-permute-start(bf16[96,3072]{1,0:T(8,128)(2,1)S(1)} %collective-permute-done.19.others_2_), channel_id=1, source_target_pairs={{0,4},{4,0},{8,12},{12,8},{16,20},{20,16},{24,28},{28,24},{1,5},{5... | collective-permute-start | bytes 1769480 | tf_op jit(solution)/shard_map/ppermute | solution.py:1027
  167.2 24.9 %collective-permute-start.31 = (bf16[384,1536]{1,0:T(8,128)(2,1)}, bf16[384,1536]{1,0:T(8,128)(2,1)}, u32[]{:S(2)}, u32[]{:S(2)}) collective-permute-start(bf16[384,1536]{1,0:T(8,128)(2,1)} %shard_map.179.others_0_.others_4_), channel_id=1, source_target_pairs={{0,4},{4,0},{8,12},{12,8},{16,20},{20,16},{24,28},{28,24},{1,5},{5... | collective-permute-start | bytes 3538952 | tf_op jit(solution)/shard_map/ppermute | solution.py:1027
  167.3 28.5 %collective-permute-start.30 = (bf16[384,1536]{1,0:T(8,128)(2,1)}, bf16[384,1536]{1,0:T(8,128)(2,1)S(1)}, u32[]{:S(2)}, u32[]{:S(2)}) collective-permute-start(bf16[384,1536]{1,0:T(8,128)(2,1)} %shard_map.179.others_0_.others_4_), channel_id=1, source_target_pairs={{0,16},{4,20},{8,24},{12,28},{16,0},{20,4},{24,8},{28,12},{1,17},{... | collective-permute-start | bytes 3538952 | tf_op jit(solution)/shard_map/ppermute | solution.py:1027
  168.8 28.2 %collective-permute-start.29 = (bf16[384,1536]{1,0:T(8,128)(2,1)}, bf16[384,1536]{1,0:T(8,128)(2,1)S(1)}, u32[]{:S(2)}, u32[]{:S(2)}) collective-permute-start(bf16[384,1536]{1,0:T(8,128)(2,1)} %shard_map.179.others_0_.others_4_), channel_id=1, source_target_pairs={{0,8},{4,12},{8,0},{12,4},{16,24},{20,28},{24,16},{28,20},{1,9},{5... | collective-permute-start | bytes 3538952 | tf_op jit(solution)/shard_map/ppermute | solution.py:1027
  197.1 16.8 %collective-permute-start.34 = (bf16[384,1536]{1,0:T(8,128)(2,1)S(1)}, bf16[384,1536]{1,0:T(8,128)(2,1)}, u32[]{:S(2)}, u32[]{:S(2)}) collective-permute-start(bf16[384,1536]{1,0:T(8,128)(2,1)S(1)} %collective-permute-done.29.others_1_.others_5_), channel_id=1, source_target_pairs={{0,4},{4,0},{8,12},{12,8},{16,20},{20,16},{24,28},{28,24},{1,5},{5... | collective-permute-start | bytes 3538952 | tf_op jit(solution)/shard_map/ppermute | solution.py:1027
  197.1 16.8 %collective-permute-start.35 = (bf16[384,1536]{1,0:T(8,128)(2,1)S(1)}, bf16[384,1536]{1,0:T(8,128)(2,1)}, u32[]{:S(2)}, u32[]{:S(2)}) collective-permute-start(bf16[384,1536]{1,0:T(8,128)(2,1)S(1)} %collective-permute-done.30.others_2_.others_6_), channel_id=1, source_target_pairs={{0,4},{4,0},{8,12},{12,8},{16,20},{20,16},{24,28},{28,24},{1,5},{5... | collective-permute-start | bytes 3538952 | tf_op jit(solution)/shard_map/ppermute | solution.py:1027
  197.7 15.3 %collective-permute-start.32 = (bf16[192,1536]{1,0:T(8,128)(2,1)S(1)}, bf16[192,1536]{1,0:T(8,128)(2,1)S(1)}, u32[]{:S(2)}, u32[]{:S(2)}) collective-permute-start(bf16[192,1536]{1,0:T(8,128)(2,1)S(1)} %slice.145), channel_id=1, source_target_pairs={{0,16},{4,20},{8,24},{12,28},{16,0},{20,4},{24,8},{28,12},{1,17},{... | collective-permute-start | bytes 1769480 | tf_op jit(solution)/shard_map/ppermute | solution.py:1027
  198.9 15.1 %collective-permute-start.33 = (bf16[192,1536]{1,0:T(8,128)(2,1)S(1)}, bf16[192,1536]{1,0:T(8,128)(2,1)}, u32[]{:S(2)}, u32[]{:S(2)}) collective-permute-start(bf16[192,1536]{1,0:T(8,128)(2,1)S(1)} %slice.146), channel_id=1, source_target_pairs={{0,8},{4,12},{8,0},{12,4},{16,24},{20,28},{24,16},{28,20},{1,9},{5... | collective-permute-start | bytes 1769480 | tf_op jit(solution)/shard_map/ppermute | solution.py:1027
  283.2 14.0 %collective-permute-start.38 = (bf16[384,3072]{1,0:T(8,128)(2,1)}, bf16[384,3072]{1,0:T(8,128)(2,1)S(1)}, u32[]{:S(2)}, u32[]{:S(2)}) collective-permute-start(bf16[384,3072]{1,0:T(8,128)(2,1)} %get-tuple-element.344), channel_id=1, source_target_pairs={{0,4},{4,0},{8,12},{12,8},{16,20},{20,16},{24,28},{28,24},{1,5},{5... | collective-permute-start | bytes 7077896 | tf_op jit(solution)/shard_map/ppermute | solution.py:1027
  300.6 16.9 %collective-permute-start.41 = (bf16[1536,1536]{1,0:T(8,128)(2,1)}, bf16[1536,1536]{1,0:T(8,128)(2,1)}, u32[]{:S(2)}, u32[]{:S(2)}) collective-permute-start(bf16[1536,1536]{1,0:T(8,128)(2,1)} %get-tuple-element.356), channel_id=1, source_target_pairs={{0,4},{4,0},{8,12},{12,8},{16,20},{20,16},{24,28},{28,24},{1,5},{5... | collective-permute-start | bytes 14155784 | tf_op jit(solution)/shard_map/ppermute | solution.py:1027
  301.0 16.4 %collective-permute-start.39 = (bf16[48,3072]{1,0:T(8,128)(2,1)}, bf16[48,3072]{1,0:T(8,128)(2,1)S(1)}, u32[]{:S(2)}, u32[]{:S(2)}) collective-permute-start(bf16[48,3072]{1,0:T(8,128)(2,1)} %get-tuple-element.354), channel_id=1, source_target_pairs={{0,8},{4,12},{8,0},{12,4},{16,24},{20,28},{24,16},{28,20},{1,9},{5... | collective-permute-start | bytes 884744 | tf_op jit(solution)/shard_map/ppermute | solution.py:1027
  301.6 16.0 %collective-permute-start.40 = (bf16[48,3072]{1,0:T(8,128)(2,1)}, bf16[48,3072]{1,0:T(8,128)(2,1)S(1)}, u32[]{:S(2)}, u32[]{:S(2)}) collective-permute-start(bf16[48,3072]{1,0:T(8,128)(2,1)} %get-tuple-element.355), channel_id=1, source_target_pairs={{0,16},{4,20},{8,24},{12,28},{16,0},{20,4},{24,8},{28,12},{1,17},{... | collective-permute-start | bytes 884744 | tf_op jit(solution)/shard_map/ppermute | solution.py:1027
  322.5 34.1 %collective-permute-start.42 = (bf16[96,3072]{1,0:T(8,128)(2,1)}, bf16[96,3072]{1,0:T(8,128)(2,1)S(1)}, u32[]{:S(2)}, u32[]{:S(2)}) collective-permute-start(bf16[96,3072]{1,0:T(8,128)(2,1)} %get-tuple-element.381), channel_id=1, source_target_pairs={{0,8},{4,12},{8,0},{12,4},{16,24},{20,28},{24,16},{28,20},{1,9},{5... | collective-permute-start | bytes 1769480 | tf_op jit(solution)/shard_map/ppermute | solution.py:1027
  324.0 32.7 %collective-permute-start.43 = (bf16[96,3072]{1,0:T(8,128)(2,1)}, bf16[96,3072]{1,0:T(8,128)(2,1)S(1)}, u32[]{:S(2)}, u32[]{:S(2)}) collective-permute-start(bf16[96,3072]{1,0:T(8,128)(2,1)} %get-tuple-element.382), channel_id=1, source_target_pairs={{0,16},{4,20},{8,24},{12,28},{16,0},{20,4},{24,8},{28,12},{1,17},{... | collective-permute-start | bytes 1769480 | tf_op jit(solution)/shard_map/ppermute | solution.py:1027
  324.8 38.1 %collective-permute-start.44 = (bf16[192,1536]{1,0:T(8,128)(2,1)}, bf16[192,1536]{1,0:T(8,128)(2,1)S(1)}, u32[]{:S(2)}, u32[]{:S(2)}) collective-permute-start(bf16[192,1536]{1,0:T(8,128)(2,1)} %get-tuple-element.383), channel_id=1, source_target_pairs={{0,8},{4,12},{8,0},{12,4},{16,24},{20,28},{24,16},{28,20},{1,9},{5... | collective-permute-start | bytes 1769480 | tf_op jit(solution)/shard_map/ppermute | solution.py:1027
  325.5 38.2 %collective-permute-start.45 = (bf16[192,1536]{1,0:T(8,128)(2,1)}, bf16[192,1536]{1,0:T(8,128)(2,1)}, u32[]{:S(2)}, u32[]{:S(2)}) collective-permute-start(bf16[192,1536]{1,0:T(8,128)(2,1)} %get-tuple-element.384), channel_id=1, source_target_pairs={{0,16},{4,20},{8,24},{12,28},{16,0},{20,4},{24,8},{28,12},{1,17},{... | collective-permute-start | bytes 1769480 | tf_op jit(solution)/shard_map/ppermute | solution.py:1027
  347.6 43.7 %collective-permute-start.48 = (bf16[384,2048]{1,0:T(8,128)(2,1)}, bf16[384,2048]{1,0:T(8,128)(2,1)S(1)}, u32[]{:S(2)}, u32[]{:S(2)}) collective-permute-start(bf16[384,2048]{1,0:T(8,128)(2,1)} %get-tuple-element.402), channel_id=1, source_target_pairs={{0,4},{4,0},{8,12},{12,8},{16,20},{20,16},{24,28},{28,24},{1,5},{5... | collective-permute-start | bytes 4718600 | tf_op jit(solution)/shard_map/ppermute | solution.py:1027
  363.7 38.5 %all-to-all-start.1 = ((bf16[4,384,384]{2,1,0:T(8,128)(2,1)}), bf16[4,384,384]{2,1,0:T(8,128)(2,1)S(1)}, u32[]{:S(2)}, u32[]{:S(2)}) async-start(bf16[4,384,384]{2,1,0:T(8,128)(2,1)} %shard_map.190), calls=%async_computation.2 | async-start | bytes 2359296 | tf_op jit(solution)/shard_map/all_to_all | solution.py:1031
  373.3 27.8 %collective-permute-start.46 = (bf16[384,1536]{1,0:T(8,128)(2,1)}, bf16[384,1536]{1,0:T(8,128)(2,1)}, u32[]{:S(2)}, u32[]{:S(2)}) collective-permute-start(bf16[384,1536]{1,0:T(8,128)(2,1)} %get-tuple-element.399), channel_id=1, source_target_pairs={{0,8},{4,12},{8,0},{12,4},{16,24},{20,28},{24,16},{28,20},{1,9},{5... | collective-permute-start | bytes 3538952 | tf_op jit(solution)/shard_map/ppermute | solution.py:1027
  374.8 27.3 %collective-permute-start.47 = (bf16[384,1536]{1,0:T(8,128)(2,1)}, bf16[384,1536]{1,0:T(8,128)(2,1)}, u32[]{:S(2)}, u32[]{:S(2)}) collective-permute-start(bf16[384,1536]{1,0:T(8,128)(2,1)} %get-tuple-element.400), channel_id=1, source_target_pairs={{0,16},{4,20},{8,24},{12,28},{16,0},{20,4},{24,8},{28,12},{1,17},{... | collective-permute-start | bytes 3538952 | tf_op jit(solution)/shard_map/ppermute | solution.py:1027
  408.8 40.9 %all-to-all-start.2 = ((bf16[4,384,384]{2,1,0:T(8,128)(2,1)}), bf16[4,384,384]{2,1,0:T(8,128)(2,1)S(1)}, u32[]{:S(2)}, u32[]{:S(2)}) async-start(bf16[4,384,384]{2,1,0:T(8,128)(2,1)} %shard_map.193), calls=%async_computation.4 | async-start | bytes 2359296 | tf_op jit(solution)/shard_map/all_to_all | solution.py:1031
  413.6 33.7 %reduce-scatter.5.cloned.1.call-start = ((), (), s32[]{:S(2)}) async-start(), calls=%async_computation.7 | async-start | bytes 737280 | tf_op jit(solution)/shard_map/reduce_scatter | solution.py:1610
  430.3 16.0 %collective-permute-start.56 = (bf16[96,2048]{1,0:T(8,128)(2,1)}, bf16[96,2048]{1,0:T(8,128)(2,1)S(1)}, u32[]{:S(2)}, u32[]{:S(2)}) collective-permute-start(bf16[96,2048]{1,0:T(8,128)(2,1)} %get-tuple-element.442), channel_id=1, source_target_pairs={{0,8},{4,12},{8,0},{12,4},{16,24},{20,28},{24,16},{28,20},{1,9},{5... | collective-permute-start | bytes 1179656 | tf_op jit(solution)/shard_map/ppermute | solution.py:1027
  431.0 16.1 %collective-permute-start.57 = (bf16[96,2048]{1,0:T(8,128)(2,1)}, bf16[96,2048]{1,0:T(8,128)(2,1)}, u32[]{:S(2)}, u32[]{:S(2)}) collective-permute-start(bf16[96,2048]{1,0:T(8,128)(2,1)} %get-tuple-element.443), channel_id=1, source_target_pairs={{0,16},{4,20},{8,24},{12,28},{16,0},{20,4},{24,8},{28,12},{1,17},{... | collective-permute-start | bytes 1179656 | tf_op jit(solution)/shard_map/ppermute | solution.py:1027
  432.4 13.9 %collective-permute-start.58 = (bf16[96,1024]{1,0:T(8,128)(2,1)}, bf16[96,1024]{1,0:T(8,128)(2,1)S(1)}, u32[]{:S(2)}, u32[]{:S(2)}) collective-permute-start(bf16[96,1024]{1,0:T(8,128)(2,1)} %get-tuple-element.444), channel_id=1, source_target_pairs={{0,8},{4,12},{8,0},{12,4},{16,24},{20,28},{24,16},{28,20},{1,9},{5... | collective-permute-start | bytes 589832 | tf_op jit(solution)/shard_map/ppermute | solution.py:1027
  433.0 13.4 %collective-permute-start.59 = (bf16[96,1024]{1,0:T(8,128)(2,1)}, bf16[96,1024]{1,0:T(8,128)(2,1)S(1)}, u32[]{:S(2)}, u32[]{:S(2)}) collective-permute-start(bf16[96,1024]{1,0:T(8,128)(2,1)} %get-tuple-element.445), channel_id=1, source_target_pairs={{0,16},{4,20},{8,24},{12,28},{16,0},{20,4},{24,8},{28,12},{1,17},{... | collective-permute-start | bytes 589832 | tf_op jit(solution)/shard_map/ppermute | solution.py:1027
  453.1 21.0 %all-to-all-start.3 = ((bf16[4,112,768]{2,1,0:T(8,128)(2,1)}), bf16[4,112,768]{2,1,0:T(8,128)(2,1)S(1)}, u32[]{:S(2)}, u32[]{:S(2)}) async-start(bf16[4,112,768]{2,1,0:T(8,128)(2,1)} %shard_map.198), calls=%async_computation.5 | async-start | bytes 1376256 | tf_op jit(solution)/shard_map/all_to_all | solution.py:1031
  (72 other events, 419.5 us)
Sparse Core Ops, SparseCore 0:
  20.8 38.5 all-gather.4
  79.4 53.4 all-gather.6
  252.4 101.6 reduce-scatter.2
  417.0 30.2 reduce-scatter.4
